TPU v7x, 32 devices: a whole 2x2x4 slice. The times are simulated.
32 devices in a mesh: ctx: 8 (over z, x), dp: 4 (over y, core).
Axes of the slice: x: 2, y: 2, z: 4, core: 2. Of those that a mesh axis runs over, the one named last changes fastest.
Arguments:
- xbc_raw: bfloat16 [4, 2048, 512], P('dp', 'ctx'), may hold values from -6 to 6
- conv_weight: float32 [4, 512], replicated, may hold values from -3 to 3
- conv_bias: float32 [512], replicated, may hold values from -3 to 3
- dt_raw: float32 [4, 2048, 4], P('dp', 'ctx'), may hold values from -1 to 10
- dt_bias: float32 [4], replicated, may hold values from -7.3 to -0.15
- a_log: float32 [4], replicated, may hold values from -3.5 to -2.5
- d_skip: float32 [4], replicated, may hold values from 0.5 to 1.5
- grad_out: bfloat16 [4, 2048, 256], P('dp', 'ctx'), may hold values from -6 to 6
Outputs:
- grad_xbc: bfloat16 [4, 2048, 512], P('dp', 'ctx')
- grad_dt: float32 [4, 2048, 4], P('dp', 'ctx')
- grad_conv_weight: float32 [4, 512], replicated
- grad_conv_bias: float32 [512], replicated
- grad_dt_bias: float32 [4], replicated
- grad_a_log: float32 [4], replicated
- grad_d_skip: float32 [4], replicated
All inputs are finite; a program needn't handle non-finite values.
Results may differ from a plain program's by a relative error of at most 0.0025.
The roundings to bfloat16 on the way count: a program that leaves them out, or rounds other values in their place, can miss the bound.
Values may be sent and summed in bfloat16 or wider, within the bound.
No kernel may reach another device: no remote copies, remote signals or barrier semaphores. Data moves between devices by JAX's collectives and lax.ppermute only.
A program may use at most 64 MiB of HBM per device.

v0:
```python
import jax
import jax.numpy as jnp
from jax import lax
from jax.sharding import PartitionSpec as P

H = 4
P_SIZE = 64
N = 128
K = 4


highest = lax.Precision.HIGHEST


def prefix(part, axis, combine, identity, reverse):
    count = lax.axis_size(axis)
    place = lax.axis_index(axis)
    ahead = count - 1 - place if reverse else place
    gathered = jax.tree.map(lambda a: lax.all_gather(a, axis), part)
    state = jax.tree.map(lambda a, e: jnp.zeros_like(a) + jnp.asarray(e, a.dtype), part, identity)

    def one(turn, state):
        source = count - 1 - turn if reverse else turn
        return combine(
            state, jax.tree.map(lambda a: lax.dynamic_index_in_dim(a, source, 0, False), gathered)
        )

    return lax.fori_loop(0, ahead, one, state)


def from_behind(block, axis, distance):
    devices = range(lax.axis_size(axis))
    route = [(i - distance, i) for i in devices if i - distance in devices]
    return lax.ppermute(block, axis, route)


def chain_step(earlier, later):
    return (earlier[0] * later[0], later[1] + later[0][:, None, None] * earlier[1])


def carry_forward(block_decay, local_state):
    identity_pair = (jnp.ones_like(block_decay), jnp.zeros_like(local_state))
    result_pair = prefix((block_decay, local_state), "ctx", chain_step, identity_pair, False)
    carried = result_pair[1]
    return carried


def carry_back(block_decay, local_grad):
    identity_pair = (jnp.ones_like(block_decay), jnp.zeros_like(local_grad))
    result_pair = prefix((block_decay, local_grad), "ctx", chain_step, identity_pair, True)
    carried = result_pair[1]
    return carried


def reduce_grads(weight_grad, bias_grad, grad_bias, grad_alog, skip_grad):
    totals = lax.psum((weight_grad, bias_grad, grad_bias, grad_alog, skip_grad), ("ctx", "dp"))
    return totals


def on_device(xbc_raw, conv_weight, conv_bias, dt_raw, dt_bias, a_log, d_skip, grad_out):
    raw_rows = xbc_raw[0]
    tok_rows = raw_rows.shape[0]
    prior_rows = from_behind(raw_rows[tok_rows - K + 1 :], "ctx", 1)
    padded = jnp.concatenate([prior_rows, raw_rows], 0).astype(jnp.float32)
    pre_conv = conv_bias + sum(
        (conv_weight[tap_idx] * padded[tap_idx : tap_idx + tok_rows] for tap_idx in range(K))
    )
    xbc_low = lax.optimization_barrier(jax.nn.silu(pre_conv).astype(jnp.bfloat16))
    xbc = xbc_low.astype(jnp.float32)
    inner_width = H * P_SIZE
    values = xbc[:, :inner_width].reshape(tok_rows, H, P_SIZE)
    b_proj = xbc[:, inner_width : inner_width + N]
    c_proj = xbc[:, inner_width + N :]
    dt_pre = dt_raw[0] + dt_bias
    step_size = jax.nn.softplus(dt_pre)
    decay_rate = -jnp.exp(a_log)
    cum_log = jnp.cumsum(step_size * decay_rate, axis=0)
    cum_log_t = cum_log.T
    step_t = step_size.T
    causal = jnp.tril(jnp.ones((tok_rows, tok_rows), dtype=jnp.bool_))
    log_gaps = cum_log_t[:, :, None] - cum_log_t[:, None, :]
    within = jnp.where(causal, jnp.exp(jnp.where(causal, log_gaps, 0.0)), 0.0)
    gram_mat = jnp.dot(c_proj, b_proj.T, precision=highest)
    mixing = gram_mat[None] * within * step_t[:, None, :]
    tail_w = jnp.exp(cum_log_t[:, -1:] - cum_log_t) * step_t
    weighted = values * tail_w.T[:, :, None]
    local_state = jnp.einsum("shp,sn->hpn", weighted, b_proj, precision=highest)
    block_decay = jnp.exp(cum_log[-1])
    upstream = jnp.exp(cum_log)
    cotangent = grad_out[0].astype(jnp.float32).reshape(tok_rows, H, P_SIZE)
    scaled_cotan = cotangent * upstream[:, :, None]
    local_grad = jnp.einsum("thp,tn->hpn", scaled_cotan, c_proj, precision=highest)
    state_in = carry_forward(block_decay, local_state)
    grad_after = carry_back(block_decay, local_grad)
    dmix = jnp.where(causal, jnp.einsum("thp,shp->hts", cotangent, values, precision=highest), 0.0)
    state_back = jnp.einsum("hpn,sn->shp", grad_after, b_proj, precision=highest)
    grad_vals = jnp.einsum("hts,thp->shp", mixing, cotangent, precision=highest)
    grad_vals = grad_vals + d_skip[:, None] * cotangent + tail_w.T[:, :, None] * state_back
    skip_grad = jnp.sum(cotangent * values, axis=(0, 2))
    dgram = jnp.sum(dmix * within * step_t[:, None, :], axis=0)
    grad_c = jnp.einsum("thp,hpn->tn", scaled_cotan, state_in, precision=highest)
    grad_c = grad_c + jnp.dot(dgram, b_proj, precision=highest)
    grad_b = jnp.dot(dgram.T, c_proj, precision=highest)
    grad_b = grad_b + jnp.einsum("shp,hpn->sn", weighted, grad_after, precision=highest)
    grad_step = jnp.sum(dmix * gram_mat[None] * within, axis=1).T
    tail_grad = jnp.sum(values * state_back, axis=2)
    grad_step = grad_step + tail_grad * jnp.exp(cum_log[-1:] - cum_log)
    pair_terms = dmix * mixing
    grad_cum = jnp.sum(pair_terms, axis=2).T - jnp.sum(pair_terms, axis=1).T
    state_proj = jnp.einsum("tn,hpn->thp", c_proj, state_in, precision=highest)
    grad_cum = grad_cum + jnp.sum(scaled_cotan * state_proj, axis=2)
    tail_term = tail_grad * tail_w.T
    last_extra = jnp.sum(tail_term, axis=0) + block_decay * jnp.sum(
        grad_after * state_in, axis=(1, 2)
    )
    grad_cum = grad_cum - tail_term
    grad_cum = grad_cum.at[-1].add(last_extra)
    grad_log = jnp.flip(jnp.cumsum(jnp.flip(grad_cum, 0), axis=0), 0)
    grad_step = grad_step + decay_rate * grad_log
    grad_alog = jnp.sum(grad_log * step_size, axis=0) * decay_rate
    grad_pre = grad_step * jax.nn.sigmoid(dt_pre)
    grad_bias = jnp.sum(grad_pre, axis=0)
    grad_mid = jnp.concatenate([grad_vals.reshape(tok_rows, inner_width), grad_b, grad_c], 1)
    grad_low = lax.optimization_barrier(grad_mid.astype(jnp.bfloat16))
    grad_act = grad_low.astype(jnp.float32)
    sigmoid_z = jax.nn.sigmoid(pre_conv)
    grad_conv = grad_act * sigmoid_z * (1.0 + pre_conv * (1.0 - sigmoid_z))
    grad_padded = sum(
        (
            jnp.pad(conv_weight[tap_idx] * grad_conv, ((tap_idx, K - 1 - tap_idx), (0, 0)))
            for tap_idx in range(K)
        )
    )
    weight_grad = jnp.stack(
        [jnp.sum(grad_conv * padded[tap_idx : tap_idx + tok_rows], axis=0) for tap_idx in range(K)]
    )
    bias_grad = jnp.sum(grad_conv, axis=0)
    spill_rows = from_behind(grad_padded[: K - 1], "ctx", -1)
    grad_rows = grad_padded[K - 1 :]
    grad_rows = grad_rows.at[tok_rows - K + 1 :].add(spill_rows)
    grad_input = grad_rows.astype(jnp.bfloat16)[None]
    totals = reduce_grads(weight_grad, bias_grad, grad_bias, grad_alog, skip_grad)
    return (grad_input, grad_pre[None], totals[0], totals[1], totals[2], totals[3], totals[4])


def solution(mesh):
    in_specs = (
        P("dp", "ctx", None),
        P(),
        P(),
        P("dp", "ctx", None),
        P(),
        P(),
        P(),
        P("dp", "ctx", None),
    )
    out_specs = (P("dp", "ctx", None), P("dp", "ctx", None), P(), P(), P(), P(), P())
    return jax.shard_map(
        on_device, mesh=mesh, in_specs=in_specs, out_specs=out_specs, check_vma=False
    )
```

profile of v0, /device:TPU:1, one launch (start us, length us, event | category | flops | bytes accessed | tf_op | source)
XLA Modules:
  0.0 167.6 jit_solution(6240087384232924659)
XLA Ops:
  7.2 0.7 slice_bitcast_fusion
  8.0 3.9 %collective-permute-start = (bf16[3,512]{1,0:T(4,128)(2,1)S(1)}, bf16[3,512]{1,0:T(4,128)(2,1)S(1)}, u32[]{:S(2)}, u32[]{:S(2)}) collective-permute-start(bf16[3,512]{1,0:T(4,128)(2,1)S(1)} %slice_bitcast_fusion), channel_id=1, source_target_pairs={{0,4},{4,8},{8,12},{12,16},{16,20},{20,24},{24,28},{1,5},{5,9},{9,... | collective-permute-start | bytes 9224 | tf_op jit(solution)/shard_map/ppermute | solution.py:34
  11.9 0.9 fusion.47
  12.8 0.7 exponential_negate_fusion
  13.4 0.8 multiply_bitcast_fusion.1
  14.2 1.2 reduce-window.14
  15.9 1.0 copy.103
  17.0 0.7 copy-done.4
  18.0 0.9 fusion.16
  19.2 15.1 %all-gather.2 = f32[8,1,4]{2,1,0:T(1,128)S(1)} all-gather(f32[1,1,4]{2,1,0:T(1,128)S(1)} %bitcast.180), channel_id=1, replica_groups=mesh['ctx'=8,'dp'=4] {'ctx'}, dimensions={0}, use_global_device_ids=true | all-gather | bytes 144 | tf_op jit(solution)/shard_map/all_gather | solution.py:19
  34.8 24.0 %all-gather.6.cloned.1.call-done = f32[32,64,128]{2,1,0:T(8,128)} async-done(((f32[4,64,128]{2,1,0:T(8,128)}), f32[32,64,128]{2,1,0:T(8,128)}) %all-gather.6.cloned.1.call-update) | async-done | bytes 1048592 | tf_op jit(solution)/shard_map/all_gather | solution.py:19
  58.8 7.3 %while.28 = (s32[]{:T(128)}, f32[4,64,128]{2,1,0:T(8,128)S(1)}, s32[]{:T(128)}, f32[8,4,64,128]{3,2,1,0:T(8,128)}, f32[8,4]{1,0:T(8,128)S(1)}, /*index=5*/s32[]{:T(128)}, s32[]{:T(128)}, s32[]{:T(128)}, s32[]{:T(128)}) while((s32[]{:T(128)}, f32[4,64,128]{2,1,0:T(8,128)S(1)}, s32[]{:T(128)}, f32[8,4,64,128]{3,2,1,0:T(8,128)}, ...), condition=%wide.region_3.4_spmd, body=%wide.region_2.3_spmd.sunk | while | flops 65542 | bytes 393411 | solution.py:28
  58.9 1.0 bitcast_add_fusion.7
  59.9 1.0 bitcast_add_fusion.7
  61.0 1.0 bitcast_add_fusion.7
  62.0 1.0 bitcast_add_fusion.7
  63.0 1.0 bitcast_add_fusion.7
  64.1 1.0 bitcast_add_fusion.7
  65.1 1.0 bitcast_add_fusion.7
  66.6 0.9 fusion.18
  67.7 0.8 copy-done
  69.0 0.9 fusion.8
  69.9 0.7 copy-done.6
  70.6 0.9 fusion.3
  71.6 0.6 convolution_bitcast_fusion.3
  72.6 32.5 %all-gather.8.cloned.1.call-done = f32[32,64,128]{2,1,0:T(8,128)} async-done(((f32[4,64,128]{2,1,0:T(8,128)}), f32[32,64,128]{2,1,0:T(8,128)}) %all-gather.8.cloned.1.call-update) | async-done | bytes 1048592 | tf_op jit(solution)/shard_map/all_gather | solution.py:19
  108.0 1.2 reduce-window.16
  110.5 0.8 fusion.45
  111.3 0.7 copy-done.7
  111.9 1.3 collective-permute-start.1
  113.3 46.5 %all-reduce.4 = (f32[4,512]{1,0:T(4,128)}, f32[512]{0:T(512)}, f32[4]{0:T(128)}, f32[4]{0:T(128)}, f32[4]{0:T(128)}) all-reduce(f32[4,512]{1,0:T(4,128)S(1)} %pad_maximum_fusion.1, f32[512]{0:T(512)S(1)} %get-tuple-element.233, f32[4]{0:T(128)S(1)} %get-tuple-element.261, ...), channel_id=1, replica_groups=mesh['ctx'=8,'dp'=4] {'ctx','dp'}, use_global_device_ids=true, to_apply=%region_20.21 | all-reduce | flops 2572 | bytes 20576 | tf_op jit(solution)/shard_map/psum | solution.py:56
  160.0 0.7 copy-done.2
  (83 shorter events, 7.7 us)
Async XLA Ops:
  7.2 9.7 %copy-start.1 = (bf16[1,256,512]{2,1,0:T(8,128)(2,1)S(1)}, bf16[1,256,512]{2,1,0:T(8,128)(2,1)}, u32[]{:S(2)}) copy-start(bf16[1,256,512]{2,1,0:T(8,128)(2,1)} %param.16) | copy-start | bytes 786436
  7.2 51.7 %all-gather.6.cloned.1.call-start = ((), (), s32[]{:S(2)}) async-start(), calls=%async_computation | async-start | bytes 1179648 | tf_op jit(solution)/shard_map/all_gather | solution.py:19
  8.0 8.9 %collective-permute-start = (bf16[3,512]{1,0:T(4,128)(2,1)S(1)}, bf16[3,512]{1,0:T(4,128)(2,1)S(1)}, u32[]{:S(2)}, u32[]{:S(2)}) collective-permute-start(bf16[3,512]{1,0:T(4,128)(2,1)S(1)} %slice_bitcast_fusion), channel_id=1, source_target_pairs={{0,4},{4,8},{8,12},{12,16},{16,20},{20,24},{24,28},{1,5},{5,9},{9,... | collective-permute-start | bytes 9224 | tf_op jit(solution)/shard_map/ppermute | solution.py:34
  17.0 0.7 copy-start.4
  19.0 86.2 %all-gather.8.cloned.1.call-start = ((), (), s32[]{:S(2)}) async-start(), calls=%async_computation.1 | async-start | bytes 1179648 | tf_op jit(solution)/shard_map/all_gather | solution.py:19
  67.6 0.9 copy-start
  69.9 0.7 copy-start.6
  109.6 0.7 copy-start.3
  109.8 0.7 copy-start.5
  111.3 0.7 copy-start.7
  111.9 47.9 %collective-permute-start.1 = (f32[3,512]{1,0:T(4,128)S(1)}, f32[3,512]{1,0:T(4,128)S(1)}, u32[]{:S(2)}, u32[]{:S(2)}) collective-permute-start(f32[3,512]{1,0:T(4,128)S(1)} %pad_add_fusion.1), channel_id=1, source_target_pairs={{4,0},{8,4},{12,8},{16,12},{20,16},{24,20},{28,24},{5,1},{9,5},{13... | collective-permute-start | bytes 18440 | tf_op jit(solution)/shard_map/ppermute | solution.py:34
  160.0 0.7 copy-start.2
Sparse Core Ops, SparseCore 0:
  19.1 39.7 all-gather.5
  67.7 37.3 all-gather.7
where the time goes:
time: 169 us; the launch traced here: 168 us
  blocking collectives  61.6 us (36%)
  waiting for transfers between devices  56.5 us (33%)
  between operations  14.3 us (8%)
  other arithmetic  14 us (8%)
  local copies, waits for them, and re-layouts  9.24 us (5%)
  matrix products  6.26 us (4%)
  starting transfers between devices  5.3 us (3%)
    all_gather x2, waiting for transfers between devices, prefix(): gathered = jax.tree.map(lambda a: lax.all_gather(a, axis), part)  56.5 us
    psum x1, blocking collectives, reduce_grads(): lax.psum((weight_grad, bias_grad, grad_bias, grad_alog, skip_grad), ('ctx...  46.5 us
    all_gather x1, blocking collectives, prefix(): gathered = jax.tree.map(lambda a: lax.all_gather(a, axis), part)  15.1 us
    add x7, other arithmetic, chain_step(): later[1] + later[0][:, None, None] * earlier[1]  6.97 us
    ppermute x2, starting transfers between devices, from_behind(): return lax.ppermute(block, axis, route)  5.22 us
    unnamed x19, local copies, waits for them, and re-layouts  5.16 us
  transfers between devices with their start and end apart: 4, of which 2 were waited for; matrix products, arithmetic and copies ran while one was open for 6% of the time, Pallas kernels for 0%

commit v1 on v0

v1 whole, which is shorter than its diff:
```python
import functools

import jax
import jax.numpy as jnp
from jax import lax
from jax.experimental import pallas as pl
from jax.experimental.pallas import tpu as pltpu
from jax.sharding import PartitionSpec as P

H = 4
P_SIZE = 64
N = 128
K = 4
INNER = H * P_SIZE
HEAD_ROWS = 8
TAIL_ROWS = 16
HALO_ROWS = 16
END_ROWS = 16
LANE_BLOCKS = (INNER + 2 * N) // 128
TOTAL_ROWS = 24

f32 = jnp.float32
bf16 = jnp.bfloat16

VMEM = pl.BlockSpec(memory_space=pltpu.VMEM)
SMEM = pl.BlockSpec(memory_space=pltpu.SMEM)
HBM = pl.BlockSpec(memory_space=pltpu.HBM)


def dot(a, b, a_dim=1, b_dim=0):
    return lax.dot_general(a, b, (((a_dim,), (b_dim,)), ((), ())), preferred_element_type=f32)


def split2(x):
    high = x.astype(bf16)
    return high, (x - high.astype(f32)).astype(bf16)


def split3(x):
    high = x.astype(bf16).astype(f32)
    rest = x - high
    middle = rest.astype(bf16).astype(f32)
    return high, middle, rest - middle


def iota(shape, dim):
    return lax.broadcasted_iota(jnp.int32, shape, dim)


def stacked(rows):
    return jnp.concatenate([*split3(rows), jnp.zeros_like(rows)], 0).astype(bf16)


def unstacked(rows):
    return rows[0:8] + rows[8:16] + rows[16:24]


def head_selector(rows):
    shape = (rows, INNER)
    return jnp.where(iota(shape, 1) // P_SIZE == iota(shape, 0) % HEAD_ROWS, 1.0, 0.0).astype(bf16)


def over_channels(rows):
    return dot(stacked(rows), head_selector(4 * HEAD_ROWS), 0, 0)


def head_sums(x):
    high, low = split2(x)
    selector = head_selector(HEAD_ROWS * 2)
    return (dot(selector, high, 1, 1) + dot(selector, low, 1, 1))[:HEAD_ROWS]


def by_head(ref, width):
    row = iota((HEAD_ROWS, width), 0)
    out = jnp.zeros((HEAD_ROWS, width), f32)
    for h in range(H):
        out = jnp.where(row == h, ref[h], out)
    return out


def shifted_down(x, first, count):
    moved = pltpu.roll(x, count, 0)
    top = jnp.where(iota(first.shape, 0) < count, pltpu.roll(first, count, 0), moved[:8])
    return jnp.concatenate([top, moved[8:]], 0)


def quantized_log(size):
    return jnp.log(jnp.maximum(size, 1e-30)).astype(bf16).astype(f32)


def scaled_columns(x):
    log_size = quantized_log(jnp.max(jnp.abs(x), axis=0, keepdims=True))
    return x * jnp.exp(-log_size), log_size


def write_message(msg_ref, state, grad, log_decay, last, upper):
    row = iota((TAIL_ROWS, INNER), 0)
    if last:
        body, log_size = scaled_columns(jnp.where(upper, grad, state))
        msg_ref[0:N] = body
        msg_ref[N : N + TAIL_ROWS] = jnp.where(row == 0, log_size, 0.0)
        return
    state, state_size = scaled_columns(state)
    grad, grad_size = scaled_columns(grad)
    high, middle, low = split3(log_decay)
    tail = jnp.where(row == 2, state_size, jnp.where(row == 3, grad_size, 0.0))
    tail = jnp.where(row == 4, high, jnp.where(row == 5, middle * 256.0, jnp.where(row == 6, low * 65536.0, tail)))
    msg_ref[0:N] = state
    msg_ref[N : 2 * N] = grad
    msg_ref[2 * N : 2 * N + TAIL_ROWS] = tail


def pack_totals(x):
    log_size = quantized_log(jnp.max(jnp.abs(x), axis=1, keepdims=True))
    shape = x.shape
    logs = jnp.sum(jnp.where(iota(shape, 0) == iota(shape, 1), log_size, 0.0), axis=0, keepdims=True)
    return jnp.where(iota(shape, 0) == shape[0] - 1, logs, x * jnp.exp(-log_size))


def start_kernel(
    raw_hbm, cot_hbm, weight_hbm, bias_hbm, dt_hbm, dt_bias_hbm, alog_hbm, skip_hbm,
    raw_ref, cot_ref, weight_ref, pre_ref, scaled_ref, tail_ref, rows_ref, logs_ref,
    bias_ref, dt_ref, dt8_ref, dt_bias_ref, alog_ref, skip_ref, sems,
):
    pairs = [
        (dt_hbm, dt_ref), (dt_bias_hbm, dt_bias_ref), (alog_hbm, alog_ref), (skip_hbm, skip_ref),
        (cot_hbm, cot_ref), (raw_hbm, raw_ref), (weight_hbm, weight_ref), (bias_hbm, bias_ref),
    ]
    copies = [pltpu.make_async_copy(src, dst, sems.at[i]) for i, (src, dst) in enumerate(pairs)]
    for copy in copies:
        copy.start()
    tok = raw_ref.shape[0]
    dt8_ref[...] = jnp.zeros_like(dt8_ref)
    for copy in copies[:4]:
        copy.wait()
    dt8_ref[0:H] = dt_ref[...]
    dt_pre = dt8_ref[...] + by_head(dt_bias_ref, tok)
    step = jnp.maximum(dt_pre, 0.0) + jnp.log1p(jnp.exp(-jnp.abs(dt_pre)))
    decay_rate = -jnp.exp(by_head(alog_ref, tok))
    until = jnp.where(iota((tok, tok), 0) <= iota((tok, tok), 1), 1.0, 0.0).astype(bf16)
    cum = unstacked(dot(stacked(step * decay_rate), until))
    left = jnp.exp(cum[:, tok - 1 : tok] - cum)
    reach = jnp.exp(cum)
    rows_ref[0:8] = cum
    rows_ref[8:16] = step
    rows_ref[16:24] = left
    rows_ref[24:32] = reach
    rows_ref[32:40] = 1.0 / (1.0 + jnp.exp(-dt_pre))
    rows_ref[40:48] = decay_rate
    tail_ref[...] = over_channels(left * step)
    log_total = over_channels(cum)[tok - 1 : tok]
    skip = jnp.zeros((1, INNER), f32)
    for h in range(H):
        skip = jnp.where(iota((1, INNER), 1) // P_SIZE == h, skip_ref[h], skip)
    row = iota((8, INNER), 0)
    logs_ref[...] = jnp.where(row == 2, log_total, jnp.where(row == 3, skip, 0.0))
    copies[4].wait()
    scaled_ref[...] = jnp.concatenate(split2(cot_ref[...].astype(f32) * over_channels(reach)), 1)
    for copy in copies[5:]:
        copy.wait()
    raw = raw_ref[...].astype(f32)
    zeros = jnp.zeros((8, raw.shape[1]), f32)
    pre = bias_ref[...] + weight_ref[K - 1 : K] * raw
    for back in range(1, K):
        pre = pre + weight_ref[K - 1 - back : K - back] * shifted_down(raw, zeros, back)
    pre_ref[...] = pre


def enter_kernel(
    last, pre_ref, halo_ref, weight_ref, scaled_ref, tail_ref, logs_ref, upper_ref,
    xbc_ref, slope_ref, weighted_ref, state_ref, grad_ref, msg_ref,
):
    tok = pre_ref.shape[0]
    halo = halo_ref[HALO_ROWS - 8 :].astype(f32)
    top = pre_ref[0:8]
    for back in range(1, K):
        tap = weight_ref[K - 1 - back : K - back]
        top = top + jnp.where(iota(top.shape, 0) < back, tap * pltpu.roll(halo, back, 0), 0.0)
    pre = jnp.concatenate([top, pre_ref[8:]], 0)
    gate = 1.0 / (1.0 + jnp.exp(-pre))
    xbc = (pre * gate).astype(bf16)
    xbc_ref[...] = xbc
    slope_ref[...] = gate * (1.0 + pre * (1.0 - gate))
    weighted = jnp.concatenate(split2(xbc[:, :INNER].astype(f32) * tail_ref[...]), 1)
    weighted_ref[...] = weighted
    state = dot(xbc[:, INNER : INNER + N], weighted, 0, 0)
    state = state[:, :INNER] + state[:, INNER:]
    grad = dot(xbc[:, INNER + N :], scaled_ref[...], 0, 0)
    grad = grad[:, :INNER] + grad[:, INNER:]
    state_ref[...] = state
    grad_ref[...] = grad
    write_message(msg_ref, state, grad, logs_ref[2:3], last, upper_ref[0] == 1)


def merge_kernel(first, last, state_ref, grad_ref, logs_ref, got_ref, upper_ref, *refs):
    if first:
        prior = after = 0.0
    else:
        prior, after = refs[0][...], refs[1][...]
        refs = refs[2:]
    logs_out, msg_ref, prior_out, after_out, *refs = refs
    upper = upper_ref[0] == 1
    log_prior, log_after, log_total = logs_ref[0:1], logs_ref[1:2], logs_ref[2:3]
    tail = got_ref[2 * N : 2 * N + TAIL_ROWS]
    got_state = got_ref[0:N] * jnp.exp(tail[2:3])
    got_grad = got_ref[N : 2 * N] * jnp.exp(tail[3:4])
    got_log = tail[4:5] + tail[5:6] * (1 / 256.0) + tail[6:7] * (1 / 65536.0)
    mine, theirs = jnp.exp(log_total), jnp.exp(got_log)
    own_state, own_grad = state_ref[...], grad_ref[...]
    state = jnp.where(upper, own_state + mine * got_state, got_state + theirs * own_state)
    grad = jnp.where(upper, got_grad + theirs * own_grad, own_grad + mine * got_grad)
    prior_out[...] = prior + jnp.where(upper, jnp.exp(log_prior) * got_state, 0.0)
    after_out[...] = after + jnp.where(upper, 0.0, jnp.exp(log_after) * got_grad)
    log_prior = jnp.where(upper, log_prior + got_log, log_prior)
    log_after = jnp.where(upper, log_after, log_after + got_log)
    log_total = log_total + got_log
    row = iota((8, INNER), 0)
    logs_out[...] = jnp.where(row == 0, log_prior, jnp.where(row == 1, log_after, jnp.where(row == 2, log_total, 0.0)))
    if refs:
        refs[0][...] = state
        refs[1][...] = grad
    write_message(msg_ref, state, grad, log_total, last, upper_ref[1] == 1)


def local_kernel(xbc_ref, cot_ref, rows_ref, logs_ref, local_ref, sums_ref):
    tok = xbc_ref.shape[0]
    cot = cot_ref[...]
    values = xbc_ref[:, :INNER]
    b_proj = xbc_ref[:, INNER : INNER + N]
    c_proj = xbc_ref[:, INNER + N :]
    cum, step = rows_ref[0:8], rows_ref[8:16]
    step_wide = over_channels(step)
    values_f = values.astype(f32)
    cot_f = cot.astype(f32)
    stepped = split2(values_f * step_wide)
    gram = dot(b_proj, c_proj, 1, 1)
    reached = iota((tok, tok), 0) <= iota((tok, tok), 1)
    pieces = stacked(cum)
    piece_head = iota((4 * HEAD_ROWS, tok), 0) % HEAD_ROWS
    dgram = jnp.zeros((tok, tok), f32)
    grads, sums = [], []
    for h in range(H):
        of = slice(h * P_SIZE, (h + 1) * P_SIZE)
        column = dot(pieces, jnp.where(piece_head == h, 1.0, 0.0).astype(bf16), 0, 0)
        within = jnp.exp(jnp.where(reached, cum[h : h + 1] - column, -1e30))
        cot_h = cot[:, of]
        high, low = split2(gram * within)
        grads.append(dot(high, cot_h) + dot(low, cot_h))
        dmix = dot(stepped[0][:, of], cot_h, 1, 1) + dot(stepped[1][:, of], cot_h, 1, 1)
        dmix = dmix * within
        dgram = dgram + dmix
        sums.append(jnp.sum(dmix * gram, axis=0, keepdims=True))
    grad_stepped = jnp.concatenate(grads, 1)
    local_ref[:, :INNER] = grad_stepped * step_wide + logs_ref[3:4] * cot_f
    high, low = split2(dgram)
    local_ref[:, INNER : INNER + N] = dot(high, c_proj) + dot(low, c_proj)
    local_ref[:, INNER + N :] = dot(high, b_proj, 0, 0) + dot(low, b_proj, 0, 0)
    row = iota((HEAD_ROWS, tok), 0)
    pairs = jnp.zeros((HEAD_ROWS, tok), f32)
    for h in range(H):
        pairs = jnp.where(row == h, sums[h], pairs)
    sums_ref[0:8] = pairs
    sums_ref[8:16] = head_sums(values_f * grad_stepped)
    sums_ref[16:24] = head_sums(values_f * cot_f)


def leave_kernel(
    raw_ref, halo_ref, weight_ref, xbc_ref, slope_ref, scaled_ref, weighted_ref, tail_ref, rows_ref, local_ref, sums_ref,
    logs_ref, got_ref, upper_ref, *refs
):
    prior, after = 0.0, 0.0
    if len(refs) > 8:
        prior, after = refs[0][...], refs[1][...]
        refs = refs[2:]
    out_hbm, dt_out_ref, end_ref, spill_ref, totals_ref, out_ref, totals_scratch, sem = refs
    tok = raw_ref.shape[0]
    upper = upper_ref[0] == 1
    got = got_ref[0:N] * jnp.exp(got_ref[N : N + 1])
    prior = prior + jnp.where(upper, jnp.exp(logs_ref[0:1]) * got, 0.0)
    after = after + jnp.where(upper, 0.0, jnp.exp(logs_ref[1:2]) * got)

    step, left, reach = rows_ref[8:16], rows_ref[16:24], rows_ref[24:32]
    dt_gate, decay_rate = rows_ref[32:40], rows_ref[40:48]
    b_proj = xbc_ref[:, INNER : INNER + N]
    c_proj = xbc_ref[:, INNER + N :]
    prior2 = jnp.concatenate(split2(prior), 0)
    after2 = jnp.concatenate(split2(after), 0)
    seen = dot(jnp.concatenate([c_proj, c_proj], 1), prior2)
    back = dot(jnp.concatenate([b_proj, b_proj], 1), after2)
    grad_c = dot(scaled_ref[:, :INNER], prior2, 1, 1)
    grad_c = grad_c[:, :N] + grad_c[:, N:] + dot(scaled_ref[:, INNER:], prior2[:N], 1, 1)
    grad_b = dot(weighted_ref[:, :INNER], after2, 1, 1)
    grad_b = grad_b[:, :N] + grad_b[:, N:] + dot(weighted_ref[:, INNER:], after2[:N], 1, 1)
    grad_low = (local_ref[...] + jnp.concatenate([tail_ref[...] * back, grad_b, grad_c], 1)).astype(bf16)
    grad_conv = grad_low.astype(f32) * slope_ref[...]

    raw = raw_ref[...].astype(f32)
    halo = halo_ref[HALO_ROWS - 8 :].astype(f32)
    sums = [None] * (K + 1)
    sums[K - 1] = jnp.sum(grad_conv * raw, axis=0, keepdims=True)
    sums[K] = jnp.sum(grad_conv, axis=0, keepdims=True)
    grad_in = weight_ref[K - 1 : K] * grad_conv
    spill = jnp.zeros((8, raw.shape[1]), f32)
    row8 = iota(spill.shape, 0)
    for ahead in range(1, K):
        tap = weight_ref[K - 1 - ahead : K - ahead]
        sums[K - 1 - ahead] = jnp.sum(grad_conv * shifted_down(raw, halo, ahead), axis=0, keepdims=True)
        moved = pltpu.roll(grad_conv, tok - ahead, 0)
        last8 = moved[tok - 8 :]
        inside = row8 < 8 - ahead
        grad_in = grad_in + tap * jnp.concatenate([moved[: tok - 8], jnp.where(inside, last8, 0.0)], 0)
        spill = spill + tap * jnp.where(inside, 0.0, last8)
    out_ref[...] = grad_in.astype(bf16)
    copy = pltpu.make_async_copy(out_ref, out_hbm, sem)
    copy.start()
    end_ref[...] = grad_in[tok - END_ROWS :]
    spill_ref[...] = spill
    totals_scratch[...] = jnp.zeros_like(totals_scratch)
    for k in range(K + 1):
        for j in range(LANE_BLOCKS):
            at = k * LANE_BLOCKS + j
            totals_scratch[at : at + 1] = sums[k][:, j * 128 : (j + 1) * 128]

    values = xbc_ref[:, :INNER].astype(f32)
    pairs, from_values, skip_rows = sums_ref[0:8], sums_ref[8:16], sums_ref[16:24]
    scaled_f = scaled_ref[:, :INNER].astype(f32) + scaled_ref[:, INNER:].astype(f32)
    seen_rows = head_sums(scaled_f * seen)
    tail_rows = head_sums(values * back)
    tail_term = tail_rows * left * step
    selector = head_selector(HEAD_ROWS * 2)[:HEAD_ROWS].astype(f32)
    through = jnp.sum(prior * after, axis=0, keepdims=True)
    through = jnp.sum(selector * through, axis=1, keepdims=True) * reach[:, tok - 1 : tok]
    last_extra = jnp.sum(tail_term, axis=1, keepdims=True) + through
    from_on = jnp.where(iota((tok, tok), 0) >= iota((tok, tok), 1), 1.0, 0.0).astype(bf16)
    grad_cum = pairs - from_values * step + seen_rows - tail_term
    grad_log = unstacked(dot(stacked(grad_cum), from_on)) + last_extra
    grad_step = from_values + tail_rows * left + decay_rate * grad_log
    grad_pre = grad_step * dt_gate
    dt_out_ref[...] = grad_pre[0:H]
    row, lane = iota((HEAD_ROWS, 128), 0), iota((HEAD_ROWS, 128), 1)
    small = jnp.zeros((HEAD_ROWS, 128), f32)
    for i, each in enumerate((grad_pre, grad_log * step * decay_rate, skip_rows)):
        column = jnp.sum(each, axis=1, keepdims=True)
        small = jnp.where((row < H) & (lane == row + i * H), column, small)
    at = (K + 1) * LANE_BLOCKS
    totals_scratch[at : at + 1] = jnp.sum(small, axis=0, keepdims=True)
    totals_ref[...] = pack_totals(totals_scratch[...])
    copy.wait()


def summed(parts):
    shape = parts.shape
    logs = parts[:, shape[1] - 1 :]
    logs = jnp.sum(jnp.where(iota(shape, 1) == iota(shape, 2), logs, 0.0), axis=2, keepdims=True)
    return jnp.sum(parts * jnp.exp(logs), axis=0)


def repack_kernel(parts_ref, out_ref):
    total = summed(parts_ref[...])
    out_ref[...] = pack_totals(jnp.where(iota(total.shape, 0) == total.shape[0] - 1, 0.0, total))


def finish_kernel(
    parts_ref, end_ref, spilled_ref, main_hbm, out_hbm, weight_ref, bias_ref, dt_bias_ref, alog_ref, skip_ref, rows_ref, sem
):
    end = end_ref[...]
    fixed = end[END_ROWS - 8 :] + spilled_ref[...]
    rows_ref[...] = jnp.concatenate([end[: END_ROWS - 8], fixed], 0).astype(bf16)
    tok = out_hbm.shape[0]
    copy = pltpu.make_async_copy(rows_ref, out_hbm.at[pl.ds(tok - END_ROWS, END_ROWS)], sem)
    copy.start()
    total = summed(parts_ref[...])
    for k in range(K + 1):
        for j in range(LANE_BLOCKS):
            at = k * LANE_BLOCKS + j
            if k < K:
                weight_ref[k : k + 1, j * 128 : (j + 1) * 128] = total[at : at + 1]
            else:
                bias_ref[:, j * 128 : (j + 1) * 128] = total[at : at + 1]
    at = (K + 1) * LANE_BLOCKS
    for i, ref in enumerate((dt_bias_ref, alog_ref, skip_ref)):
        ref[...] = total[at : at + 1, i * H : (i + 1) * H]
    copy.wait()


def call(kernel, outs, in_specs, out_specs=None, scratch=(), flops=0, limit=16 << 20, aliases=None):
    return pl.pallas_call(
        kernel,
        out_shape=outs,
        in_specs=in_specs,
        out_specs=out_specs or jax.tree.map(lambda _: VMEM, outs),
        scratch_shapes=list(scratch),
        input_output_aliases=aliases or {},
        compiler_params=pltpu.CompilerParams(vmem_limit_bytes=limit),
        cost_estimate=pl.CostEstimate(flops=flops, bytes_accessed=1 << 20, transcendentals=0),
    )


def struct(shape, dtype=f32):
    return jax.ShapeDtypeStruct(shape, dtype)


def exchange(message, distance, slabs):
    message = message.astype(jnp.float16)
    return lax.ppermute(message, "ctx", [(i, i ^ distance) for i in range(slabs)]).astype(f32)


def everyones(packed, axes, count):
    packed = jnp.broadcast_to(packed.astype(jnp.float16)[None], (count, *packed.shape))
    return lax.all_to_all(packed, axes, 0, 0).astype(f32)


def on_device(xbc_raw, conv_weight, conv_bias, dt_raw, dt_bias, a_log, d_skip, grad_out):
    raw = xbc_raw[0]
    tok, channels = raw.shape
    slabs = lax.axis_size("ctx")
    rounds = slabs.bit_length() - 1
    assert slabs == 1 << rounds and rounds > 0
    place = lax.axis_index("ctx")
    bits = [(place >> r) & 1 for r in range(rounds)]

    halo = lax.ppermute(raw[tok - HALO_ROWS :], "ctx", [(i, i + 1) for i in range(slabs - 1)])

    def message(r):
        return struct((N + TAIL_ROWS if r == rounds - 1 else 2 * N + TAIL_ROWS, INNER))

    state_like = struct((N, INNER))
    logs_like = struct((8, INNER))
    raw_near, cot, weight, pre, scaled, tail, rows, logs = call(
        start_kernel,
        (
            struct((tok, channels), bf16), struct((tok, INNER), bf16), struct((K, channels)), struct((tok, channels)),
            struct((tok, 2 * INNER), bf16), struct((tok, INNER)), struct((6 * HEAD_ROWS, tok)), logs_like,
        ),
        [HBM] * 8,
        scratch=[
            pltpu.VMEM((1, channels), f32), pltpu.VMEM((H, tok), f32), pltpu.VMEM((HEAD_ROWS, tok), f32),
            pltpu.SMEM((H,), f32), pltpu.SMEM((H,), f32), pltpu.SMEM((H,), f32), pltpu.SemaphoreType.DMA((8,)),
        ],
        flops=100_000_000,
    )(raw, grad_out[0], conv_weight, conv_bias[None], dt_raw[0].T, dt_bias, a_log, d_skip)

    xbc, slope, weighted, state, grad, msg = call(
        functools.partial(enter_kernel, rounds == 1),
        (
            struct((tok, channels), bf16), struct((tok, channels)), struct((tok, 2 * INNER), bf16),
            state_like, state_like, message(0),
        ),
        [VMEM] * 6 + [SMEM],
        flops=200_000_000,
    )(pre, halo, weight, scaled, tail, logs, jnp.stack([bits[0]]))

    local, sums = call(
        local_kernel,
        (struct((tok, channels)), struct((3 * HEAD_ROWS, tok))),
        [VMEM] * 4,
        flops=1_000_000_000,
    )(xbc, cot, rows, logs)

    carried = ()
    for r in range(rounds - 1):
        got = exchange(msg, 1 << r, slabs)
        if r == 0:
            got, local, sums = lax.optimization_barrier((got, local, sums))
        last = r + 1 == rounds - 1
        logs, msg, *carried = call(
            functools.partial(merge_kernel, r == 0, last),
            (logs_like, message(r + 1)) + (state_like,) * (2 if last else 4),
            [VMEM] * 4 + [SMEM] + [VMEM] * len(carried),
            flops=1_000_000,
        )(state, grad, logs, got, jnp.stack([bits[r], bits[r + 1]]), *carried)
        if not last:
            *carried, state, grad = carried
    got = exchange(msg, 1 << (rounds - 1), slabs)

    grad_main, grad_dt, end, spill, packed = call(
        leave_kernel,
        (
            struct((tok, channels), bf16), struct((H, tok)), struct((END_ROWS, channels)), struct((8, channels)),
            struct((TOTAL_ROWS, 128)),
        ),
        [VMEM] * 13 + [SMEM] + [VMEM] * len(carried),
        (HBM, VMEM, VMEM, VMEM, VMEM),
        [pltpu.VMEM((tok, channels), bf16), pltpu.VMEM((TOTAL_ROWS, 128), f32), pltpu.SemaphoreType.DMA],
        flops=200_000_000,
    )(raw_near, halo, weight, xbc, slope, scaled, weighted, tail, rows, local, sums, logs, got, jnp.stack([bits[-1]]), *carried)

    spilled = lax.ppermute(spill, "ctx", [(i + 1, i) for i in range(slabs - 1)])

    contexts = lax.axis_size("dp")
    if slabs * contexts <= 64:
        parts = everyones(packed, ("ctx", "dp"), slabs * contexts)
    else:
        packed = call(repack_kernel, struct((TOTAL_ROWS, 128)), [VMEM])(everyones(packed, "ctx", slabs))
        parts = everyones(packed, "dp", contexts)
    grad_input, grad_weight, grad_bias, *small = call(
        finish_kernel,
        (
            struct((tok, channels), bf16), struct((K, channels)), struct((1, channels)),
            struct((1, H)), struct((1, H)), struct((1, H)),
        ),
        [VMEM] * 3 + [HBM],
        (HBM,) + (VMEM,) * 5,
        [pltpu.VMEM((END_ROWS, channels), bf16), pltpu.SemaphoreType.DMA],
        aliases={3: 0},
    )(parts, end, spilled, grad_main)
    return (grad_input[None], grad_dt.T[None], grad_weight, grad_bias[0], *(each[0] for each in small))


def solution(mesh):
    in_specs = (
        P("dp", "ctx", None),
        P(),
        P(),
        P("dp", "ctx", None),
        P(),
        P(),
        P(),
        P("dp", "ctx", None),
    )
    out_specs = (P("dp", "ctx", None), P("dp", "ctx", None), P(), P(), P(), P(), P())
    return jax.shard_map(
        on_device, mesh=mesh, in_specs=in_specs, out_specs=out_specs, check_vma=False
    )
```

time: 169 us -> 47.4 us (0.28)
  blocking collectives: 61.6 us -> 0 us
  waiting for transfers between devices: 56.5 us -> 13.6 us
  starting transfers between devices: 5.3 us -> 19.8 us
  other arithmetic: 14 us -> 0.28 us
  between operations: 14.3 us -> 0.82 us
  Pallas kernels: 0 us -> 8.6 us
  matrix products: 6.26 us -> 0 us
  local copies, waits for them, and re-layouts: 9.24 us -> 3.95 us
    all_gather x2 -> x0, waiting for transfers between devices: 56.5 us -> none  [prefix(): gathered = jax.tree.map(lambda a: lax.all_gather(a, axis), part)]
    psum x1 -> x0, blocking collectives: 46.5 us -> none  [reduce_grads(): lax.psum((weight_grad, bias_grad, grad_bias, grad_alog, skip_grad), ('ctx...]
    all_gather x1 -> x0, blocking collectives: 15.1 us -> none  [prefix(): gathered = jax.tree.map(lambda a: lax.all_gather(a, axis), part)]
    all_to_all x0 -> x1, starting transfers between devices: none -> 9.5 us  [everyones(): return lax.all_to_all(packed, axes, 0, 0).astype(f32)]
    pallas_call x0 -> x7, Pallas kernels: none -> 8.6 us  [the longest x1 2.17 us: on_device(): call(leave_kernel, (struct((tok, channels), bf16), struct((H, tok)), stru...]
    all_to_all x0 -> x1, waiting for transfers between devices: none -> 7.93 us  [everyones(): return lax.all_to_all(packed, axes, 0, 0).astype(f32)]
    add x10 -> x0, other arithmetic: 7.32 us -> none  [the longest x7 6.97 us: chain_step(): later[1] + later[0][:, None, None] * earlier[1]]
    dot_general x11 -> x0, matrix products: 6.26 us -> none  [the longest x1 0.93 us: on_device(): local_state = jnp.einsum('shp,sn->hpn', weighted, b_proj, precision=highest)]
  transfers between devices with their start and end apart: 4 -> 6, of which waited for: 2 -> 4; matrix products, arithmetic and copies ran while one was open for 6% -> 0% of each run, Pallas kernels for 0% -> 7%
where the time goes in v1:
time: 47.4 us; the launch traced here: 47 us
  starting transfers between devices  19.8 us (42%)
  waiting for transfers between devices  13.6 us (29%)
  Pallas kernels  8.6 us (18%)
  local copies, waits for them, and re-layouts  3.95 us (8%)
  between operations  0.82 us (2%)
    all_to_all x1, starting transfers between devices, everyones(): return lax.all_to_all(packed, axes, 0, 0).astype(f32)  9.5 us
    all_to_all x1, waiting for transfers between devices, everyones(): return lax.all_to_all(packed, axes, 0, 0).astype(f32)  7.93 us
    ppermute x3, waiting for transfers between devices, exchange(): lax.ppermute(message, 'ctx', [(i, i ^ distance) for i in range(slabs)])  5.62 us
    ppermute x3, starting transfers between devices, exchange(): lax.ppermute(message, 'ctx', [(i, i ^ distance) for i in range(slabs)])  5.07 us
    ppermute x1, starting transfers between devices, on_device(): lax.ppermute(raw[tok - HALO_ROWS:], 'ctx', [(i, i + 1) for i in range(sla...  3.93 us
    unnamed x16, local copies, waits for them, and re-layouts  2.54 us
    pallas_call x1, Pallas kernels, on_device(): call(leave_kernel, (struct((tok, channels), bf16), struct((H, tok)), stru...  2.17 us
    pallas_call x1, Pallas kernels, on_device(): call(start_kernel, (struct((tok, channels), bf16), struct((tok, INNER), b...  1.64 us
  transfers between devices with their start and end apart: 6, of which 4 were waited for; matrix products, arithmetic and copies ran while one was open for 0% of the time, Pallas kernels for 7%

profile of v1, /device:TPU:1, one launch (start us, length us, event | category | flops | bytes accessed | tf_op | source)
XLA Modules:
  0.0 47.0 jit_solution(12084365111849344912)
XLA Ops:
  0.6 0.7 %slice_bitcast_fusion = bf16[16,512]{1,0:T(8,128)(2,1)S(1)} fusion(bf16[1,256,512]{2,1,0:T(8,128)(2,1)} %param.8), kind=kLoop, calls=%fused_computation | loop fusion | bytes 32768 | tf_op jit(solution)/shard_map/slice | solution.py:422
  1.4 3.9 %collective-permute-start = (bf16[16,512]{1,0:T(8,128)(2,1)S(1)}, bf16[16,512]{1,0:T(8,128)(2,1)S(1)}, u32[]{:S(2)}, u32[]{:S(2)}) collective-permute-start(bf16[16,512]{1,0:T(8,128)(2,1)S(1)} %slice_bitcast_fusion), channel_id=1, source_target_pairs={{0,4},{4,8},{8,12},{12,16},{16,20},{20,24},{24,28},{1,5},{5,9},{9,... | collective-permute-start | bytes 49160 | tf_op jit(solution)/shard_map/ppermute | solution.py:422
  5.3 0.0 copy-start.7
  5.3 0.0 copy-start.2
  5.3 0.0 copy-start.3
  5.3 0.0 copy-start.4
  5.3 0.0 copy-start.5
  5.4 0.6 %copy-done.7 = f32[4]{0:T(128)S(1)} copy-done((f32[4]{0:T(128)S(1)}, f32[4]{0:T(128)}, u32[]{:S(2)}) %copy-start.7) | copy-done | bytes 40
  6.0 0.1 copy-done.2
  6.0 0.0 copy-done.3
  6.0 0.0 copy-done.4
  6.0 0.9 %copy-done = bf16[1,256,512]{2,1,0:T(8,128)(2,1)S(1)} copy-done((bf16[1,256,512]{2,1,0:T(8,128)(2,1)S(1)}, bf16[1,256,512]{2,1,0:T(8,128)(2,1)}, u32[]{:S(2)}) %copy-start) | copy-done | bytes 262168
  7.0 0.9 %copy-done.1 = bf16[1,256,256]{2,1,0:T(8,128)(2,1)S(1)} copy-done((bf16[1,256,256]{2,1,0:T(8,128)(2,1)S(1)}, bf16[1,256,256]{2,1,0:T(8,128)(2,1)}, u32[]{:S(2)}) %copy-start.1) | copy-done | bytes 131096
  7.9 1.6 %shard_map.135 = (bf16[256,512]{1,0:T(8,128)(2,1)S(1)}, bf16[256,256]{1,0:T(8,128)(2,1)S(1)}, f32[4,512]{1,0:T(4,128)S(1)}, f32[256,512]{1,0:T(8,128)S(1)}, bf16...) custom-call(bf16[256,512]{1,0:T(8,128)(2,1)S(1)} %bitcast.19, ...), custom_call_target="tpu_custom_call" | custom-call | flops 100000000 | bytes 1048576 | tf_op jit(solution)/shard_map/pallas_call | solution.py:429
  9.6 0.5 %shard_map.136 = (bf16[256,512]{1,0:T(8,128)(2,1)S(1)}, f32[256,512]{1,0:T(8,128)S(1)}, bf16[256,512]{1,0:T(8,128)(2,1)S(1)}, f32[128,256]{1,0:T(8,128)S(1)}, f3...) custom-call(f32[256,512]{1,0:T(8,128)S(1)} %get-tuple-element.49.pre_ref, ...), custom_call_target="tpu_custom_call" | custom-call | flops 200000000 | bytes 1048576 | tf_op jit(solution)/shard_map/pallas_call | solution.py:443
  10.1 1.3 %collective-permute-start.1 = (f16[272,256]{1,0:T(8,128)(2,1)S(1)}, f16[272,256]{1,0:T(8,128)(2,1)S(1)}, u32[]{:S(2)}, u32[]{:S(2)}) collective-permute-start(f16[272,256]{1,0:T(8,128)(2,1)S(1)} %convert_element_type.24), channel_id=1, source_target_pairs={{0,4},{4,0},{8,12},{12,8},{16,20},{20,16},{24,28},{28,24},{1,5},{5... | collective-permute-start | bytes 417800 | tf_op jit(solution)/shard_map/ppermute | solution.py:405
  11.4 0.1 pad_add_fusion.upper_ref
  11.5 1.6 %shard_map.137 = (f32[256,512]{1,0:T(8,128)S(1)}, f32[24,256]{1,0:T(8,128)S(1)}) custom-call(bf16[256,512]{1,0:T(8,128)(2,1)S(1)} %get-tuple-element.53.xbc_ref, bf16[256,256]{1,0:T(8,128)(2,1)S(1)} %get-tuple-element.58.cot_ref, f32[48,256]{1,0:T(8,128)S(1)} %get-tuple-element.56.rows_ref, f32[8,256]{1,0:T(8,128)S(1)} %get-tuple-element.52.logs_ref), custom_call_target="tpu_custom_call" | custom-call | flops 1000000000 | bytes 1048576 | tf_op jit(solution)/shard_map/pallas_call | solution.py:453
  13.1 1.3 %collective-permute-done.1 = f16[272,256]{1,0:T(8,128)(2,1)S(1)} collective-permute-done((f16[272,256]{1,0:T(8,128)(2,1)S(1)}, f16[272,256]{1,0:T(8,128)(2,1)S(1)}, u32[]{:S(2)}, u32[]{:S(2)}) %collective-permute-start.1) | collective-permute-done | bytes 139296 | tf_op jit(solution)/shard_map/ppermute | solution.py:405
  14.4 0.7 %shard_map.138 = (f32[8,256]{1,0:T(8,128)S(1)}, f32[272,256]{1,0:T(8,128)S(1)}, f32[128,256]{1,0:T(8,128)S(1)}, f32[128,256]{1,0:T(8,128)S(1)}, f32[128,256]{1,0:T(8,128)S(1)}, /*index=5*/f32[128,256]{1,0:T(8,128)S(1)}) custom-call(f32[128,256]{1,0:T(8,128)S(1)} %get-tuple-element.63.state_ref, f32[128,256]{1,0:T(8,128)S(1)} %get-tuple-element.64.grad_ref, ...), custom_call_target="tpu_custom_call" | custom-call | flops 1000000 | bytes 1048576 | tf_op jit(solution)/shard_map/pallas_call | solution.py:466
  15.1 1.4 %collective-permute-start.2 = (f16[272,256]{1,0:T(8,128)(2,1)S(1)}, f16[272,256]{1,0:T(8,128)(2,1)S(1)}, u32[]{:S(2)}, u32[]{:S(2)}) collective-permute-start(f16[272,256]{1,0:T(8,128)(2,1)S(1)} %convert_element_type.26), channel_id=1, source_target_pairs={{0,8},{4,12},{8,0},{12,4},{16,24},{20,28},{24,16},{28,20},{1,9},{5... | collective-permute-start | bytes 417800 | tf_op jit(solution)/shard_map/ppermute | solution.py:405
  16.4 0.1 pad_add_fusion.1.upper_ref
  16.5 2.5 %collective-permute-done.2 = f16[272,256]{1,0:T(8,128)(2,1)S(1)} collective-permute-done((f16[272,256]{1,0:T(8,128)(2,1)S(1)}, f16[272,256]{1,0:T(8,128)(2,1)S(1)}, u32[]{:S(2)}, u32[]{:S(2)}) %collective-permute-start.2) | collective-permute-done | bytes 139296 | tf_op jit(solution)/shard_map/ppermute | solution.py:405
  19.1 0.7 %shard_map.139 = (f32[8,256]{1,0:T(8,128)S(1)}, f32[144,256]{1,0:T(8,128)S(1)}, f32[128,256]{1,0:T(8,128)S(1)}, f32[128,256]{1,0:T(8,128)S(1)}) custom-call(f32[128,256]{1,0:T(8,128)S(1)} %get-tuple-element.66.state_ref, f32[128,256]{1,0:T(8,128)S(1)} %get-tuple-element.67.grad_ref, f32[8,256]{1,0:T(8,128)S(1)} %get-tuple-element.68.logs_ref, ...), custom_call_target="tpu_custom_call" | custom-call | flops 1000000 | bytes 1048576 | tf_op jit(solution)/shard_map/pallas_call | solution.py:466
  19.8 2.4 %collective-permute-start.3 = (f16[144,256]{1,0:T(8,128)(2,1)S(1)}, f16[144,256]{1,0:T(8,128)(2,1)S(1)}, u32[]{:S(2)}, u32[]{:S(2)}) collective-permute-start(f16[144,256]{1,0:T(8,128)(2,1)S(1)} %convert_element_type.28), channel_id=1, source_target_pairs={{0,16},{4,20},{8,24},{12,28},{16,0},{20,4},{24,8},{28,12},{1,17},{... | collective-permute-start | bytes 221192 | tf_op jit(solution)/shard_map/ppermute | solution.py:405
  22.2 1.8 %collective-permute-done.3 = f16[144,256]{1,0:T(8,128)(2,1)S(1)} collective-permute-done((f16[144,256]{1,0:T(8,128)(2,1)S(1)}, f16[144,256]{1,0:T(8,128)(2,1)S(1)}, u32[]{:S(2)}, u32[]{:S(2)}) %collective-permute-start.3) | collective-permute-done | bytes 73760 | tf_op jit(solution)/shard_map/ppermute | solution.py:405
  24.0 2.2 %shard_map.140 = (bf16[256,512]{1,0:T(8,128)(2,1)}, f32[4,256]{1,0:T(4,128)}, f32[16,512]{1,0:T(8,128)S(1)}, f32[8,512]{1,0:T(8,128)S(1)}, f32[24,128]{1,0:T(8,128)S(1)}) custom-call(bf16[256,512]{1,0:T(8,128)(2,1)S(1)} %get-tuple-element.47.raw_ref, bf16[16,512]{1,0:T(8,128)(2,1)S(1)} %collective-permute-done.halo_ref, ...), custom_call_target="tpu_custom_call" | custom-call | flops 200000000 | bytes 1048576 | tf_op jit(solution)/shard_map/pallas_call | solution.py:476
  26.2 0.7 %broadcast_in_dim.16 = f16[32,24,128]{2,1,0:T(8,128)(2,1)} broadcast(f16[24,128]{1,0:T(8,128)(2,1)S(1)} %convert_element_type.30), dimensions={1,2} | broadcast | bytes 202752 | tf_op jit(solution)/shard_map/broadcast_in_dim | solution.py:409
  26.9 9.5 %all-to-all-start = ((f16[32,24,128]{2,1,0:T(8,128)(2,1)}), f16[32,24,128]{2,1,0:T(8,128)(2,1)S(1)}, u32[]{:S(2)}, u32[]{:S(2)}) async-start(f16[32,24,128]{2,1,0:T(8,128)(2,1)} %broadcast_in_dim.16), calls=%async_computation | async-start | bytes 393216 | tf_op jit(solution)/shard_map/all_to_all | solution.py:410
  36.4 1.3 %collective-permute-start.4 = (f32[8,512]{1,0:T(8,128)S(1)}, f32[8,512]{1,0:T(8,128)S(1)}, u32[]{:S(2)}, u32[]{:S(2)}) collective-permute-start(f32[8,512]{1,0:T(8,128)S(1)} %get-tuple-element.78), channel_id=1, source_target_pairs={{4,0},{8,4},{12,8},{16,12},{20,16},{24,20},{28,24},{5,1},{9,5},{13... | collective-permute-start | bytes 49160 | tf_op jit(solution)/shard_map/ppermute | solution.py:488
  37.7 7.9 %all-to-all-done = f16[32,24,128]{2,1,0:T(8,128)(2,1)S(1)} async-done(((f16[32,24,128]{2,1,0:T(8,128)(2,1)}), f16[32,24,128]{2,1,0:T(8,128)(2,1)S(1)}, u32[]{:S(2)}, u32[]{:S(2)}) %all-to-all-start) | async-done | bytes 196640 | tf_op jit(solution)/shard_map/all_to_all | solution.py:410
  45.7 1.3 %shard_map.141 = (bf16[256,512]{1,0:T(8,128)(2,1)}, f32[4,512]{1,0:T(4,128)}, f32[1,512]{1,0:T(1,128)}, f32[1,4]{1,0:T(1,128)}, f32[1,4]{1,0:T(1,128)}, /*index=5*/f32[1,4]{1,0:T(1,128)}) custom-call(f32[32,24,128]{2,1,0:T(8,128)S(1)} %convert_element_type.31.parts_ref, f32[16,512]{1,0:T(8,128)S(1)} %get-tuple-element.77.end_ref, ...), custom_call_target="tpu_custom_call", output_to_operand_aliasing={{0}: (3, {})} | custom-call | bytes 1048576 | tf_op jit(solution)/shard_map/pallas_call | solution.py:496
  (15 shorter events, 0.1 us)
Async XLA Ops:
  1.4 8.2 %collective-permute-start = (bf16[16,512]{1,0:T(8,128)(2,1)S(1)}, bf16[16,512]{1,0:T(8,128)(2,1)S(1)}, u32[]{:S(2)}, u32[]{:S(2)}) collective-permute-start(bf16[16,512]{1,0:T(8,128)(2,1)S(1)} %slice_bitcast_fusion), channel_id=1, source_target_pairs={{0,4},{4,8},{8,12},{12,16},{16,20},{20,24},{24,28},{1,5},{5,9},{9,... | collective-permute-start | bytes 49160 | tf_op jit(solution)/shard_map/ppermute | solution.py:422
  5.3 0.7 %copy-start.7 = (f32[4]{0:T(128)S(1)}, f32[4]{0:T(128)}, u32[]{:S(2)}) copy-start(f32[4]{0:T(128)} %skip_hbm.1) | copy-start | bytes 52
  5.3 0.7 %copy-start.2 = (f32[4,512]{1,0:T(4,128)S(1)}, f32[4,512]{1,0:T(4,128)}, u32[]{:S(2)}) copy-start(f32[4,512]{1,0:T(4,128)} %weight_hbm.1) | copy-start | bytes 24580
  5.3 0.7 %copy-start.3 = (f32[1,256,4]{1,2,0:T(4,128)S(1)}, f32[1,256,4]{1,2,0:T(4,128)}, u32[]{:S(2)}) copy-start(f32[1,256,4]{1,2,0:T(4,128)} %param.11) | copy-start | bytes 12292
  5.3 0.7 %copy-start.4 = (f32[512]{0:T(512)S(1)}, f32[512]{0:T(512)}, u32[]{:S(2)}) copy-start(f32[512]{0:T(512)} %param.10) | copy-start | bytes 6148
  5.3 0.7 %copy-start.5 = (f32[4]{0:T(128)S(1)}, f32[4]{0:T(128)}, u32[]{:S(2)}) copy-start(f32[4]{0:T(128)} %dt_bias_hbm.1) | copy-start | bytes 52
  5.4 0.7 %copy-start.6 = (f32[4]{0:T(128)S(1)}, f32[4]{0:T(128)}, u32[]{:S(2)}) copy-start(f32[4]{0:T(128)} %alog_hbm.1) | copy-start | bytes 52
  6.0 1.0 %copy-start = (bf16[1,256,512]{2,1,0:T(8,128)(2,1)S(1)}, bf16[1,256,512]{2,1,0:T(8,128)(2,1)}, u32[]{:S(2)}) copy-start(bf16[1,256,512]{2,1,0:T(8,128)(2,1)} %param.8) | copy-start | bytes 786436
  7.0 0.9 %copy-start.1 = (bf16[1,256,256]{2,1,0:T(8,128)(2,1)S(1)}, bf16[1,256,256]{2,1,0:T(8,128)(2,1)}, u32[]{:S(2)}) copy-start(bf16[1,256,256]{2,1,0:T(8,128)(2,1)} %param.15) | copy-start | bytes 393220
  10.1 4.3 %collective-permute-start.1 = (f16[272,256]{1,0:T(8,128)(2,1)S(1)}, f16[272,256]{1,0:T(8,128)(2,1)S(1)}, u32[]{:S(2)}, u32[]{:S(2)}) collective-permute-start(f16[272,256]{1,0:T(8,128)(2,1)S(1)} %convert_element_type.24), channel_id=1, source_target_pairs={{0,4},{4,0},{8,12},{12,8},{16,20},{20,16},{24,28},{28,24},{1,5},{5... | collective-permute-start | bytes 417800 | tf_op jit(solution)/shard_map/ppermute | solution.py:405
  15.1 4.0 %collective-permute-start.2 = (f16[272,256]{1,0:T(8,128)(2,1)S(1)}, f16[272,256]{1,0:T(8,128)(2,1)S(1)}, u32[]{:S(2)}, u32[]{:S(2)}) collective-permute-start(f16[272,256]{1,0:T(8,128)(2,1)S(1)} %convert_element_type.26), channel_id=1, source_target_pairs={{0,8},{4,12},{8,0},{12,4},{16,24},{20,28},{24,16},{28,20},{1,9},{5... | collective-permute-start | bytes 417800 | tf_op jit(solution)/shard_map/ppermute | solution.py:405
  19.8 4.2 %collective-permute-start.3 = (f16[144,256]{1,0:T(8,128)(2,1)S(1)}, f16[144,256]{1,0:T(8,128)(2,1)S(1)}, u32[]{:S(2)}, u32[]{:S(2)}) collective-permute-start(f16[144,256]{1,0:T(8,128)(2,1)S(1)} %convert_element_type.28), channel_id=1, source_target_pairs={{0,16},{4,20},{8,24},{12,28},{16,0},{20,4},{24,8},{28,12},{1,17},{... | collective-permute-start | bytes 221192 | tf_op jit(solution)/shard_map/ppermute | solution.py:405
  26.9 18.7 %all-to-all-start = ((f16[32,24,128]{2,1,0:T(8,128)(2,1)}), f16[32,24,128]{2,1,0:T(8,128)(2,1)S(1)}, u32[]{:S(2)}, u32[]{:S(2)}) async-start(f16[32,24,128]{2,1,0:T(8,128)(2,1)} %broadcast_in_dim.16), calls=%async_computation | async-start | bytes 393216 | tf_op jit(solution)/shard_map/all_to_all | solution.py:410
  36.4 9.3 %collective-permute-start.4 = (f32[8,512]{1,0:T(8,128)S(1)}, f32[8,512]{1,0:T(8,128)S(1)}, u32[]{:S(2)}, u32[]{:S(2)}) collective-permute-start(f32[8,512]{1,0:T(8,128)S(1)} %get-tuple-element.78), channel_id=1, source_target_pairs={{4,0},{8,4},{12,8},{16,12},{20,16},{24,20},{28,24},{5,1},{9,5},{13... | collective-permute-start | bytes 49160 | tf_op jit(solution)/shard_map/ppermute | solution.py:488

commit v2 on v1

--- a/solution.py
+++ b/solution.py
@@ -17,13 +17,13 @@
 HALO_ROWS = 16
 END_ROWS = 16
 LANE_BLOCKS = (INNER + 2 * N) // 128
+SMALL_ROW = (K + 1) * LANE_BLOCKS
 TOTAL_ROWS = 24
 
 f32 = jnp.float32
 bf16 = jnp.bfloat16
 
 VMEM = pl.BlockSpec(memory_space=pltpu.VMEM)
-SMEM = pl.BlockSpec(memory_space=pltpu.SMEM)
 HBM = pl.BlockSpec(memory_space=pltpu.HBM)
 
 
@@ -74,7 +74,7 @@
     row = iota((HEAD_ROWS, width), 0)
     out = jnp.zeros((HEAD_ROWS, width), f32)
     for h in range(H):
-        out = jnp.where(row == h, ref[h], out)
+        out = jnp.where(row == h, ref[:, h : h + 1], out)
     return out
 
 
@@ -82,6 +82,10 @@
     moved = pltpu.roll(x, count, 0)
     top = jnp.where(iota(first.shape, 0) < count, pltpu.roll(first, count, 0), moved[:8])
     return jnp.concatenate([top, moved[8:]], 0)
+
+
+def is_upper(bits_ref, r):
+    return bits_ref[8 * r : 8 * r + 1] > 0.5
 
 
 def quantized_log(size):
@@ -111,34 +115,35 @@
 
 
 def pack_totals(x):
-    log_size = quantized_log(jnp.max(jnp.abs(x), axis=1, keepdims=True))
-    shape = x.shape
-    logs = jnp.sum(jnp.where(iota(shape, 0) == iota(shape, 1), log_size, 0.0), axis=0, keepdims=True)
-    return jnp.where(iota(shape, 0) == shape[0] - 1, logs, x * jnp.exp(-log_size))
+    row = iota(x.shape, 0)
+    large = jnp.where(row < SMALL_ROW, x, 0.0)
+    large_size = quantized_log(jnp.max(jnp.abs(large), axis=0, keepdims=True))
+    small = x[SMALL_ROW : SMALL_ROW + 1]
+    small_size = quantized_log(jnp.abs(small))
+    out = jnp.where(row == SMALL_ROW, small * jnp.exp(-small_size), large * jnp.exp(-large_size))
+    return jnp.where(row == SMALL_ROW + 1, large_size, jnp.where(row == SMALL_ROW + 2, small_size, out))
+
+
+def triangle_kernel(until_ref):
+    shape = until_ref.shape
+    until_ref[...] = jnp.where(iota(shape, 0) <= iota(shape, 1), 1.0, 0.0).astype(bf16)
 
 
 def start_kernel(
-    raw_hbm, cot_hbm, weight_hbm, bias_hbm, dt_hbm, dt_bias_hbm, alog_hbm, skip_hbm,
-    raw_ref, cot_ref, weight_ref, pre_ref, scaled_ref, tail_ref, rows_ref, logs_ref,
-    bias_ref, dt_ref, dt8_ref, dt_bias_ref, alog_ref, skip_ref, sems,
+    rounds, raw_ref, cot_ref, weight_ref, bias_ref, dt_ref, dt_bias_ref, alog_ref, skip_ref, until_ref,
+    pre_ref, scaled_ref, tail_ref, rows_ref, logs_ref, bits_ref, dt8_ref,
 ):
-    pairs = [
-        (dt_hbm, dt_ref), (dt_bias_hbm, dt_bias_ref), (alog_hbm, alog_ref), (skip_hbm, skip_ref),
-        (cot_hbm, cot_ref), (raw_hbm, raw_ref), (weight_hbm, weight_ref), (bias_hbm, bias_ref),
-    ]
-    copies = [pltpu.make_async_copy(src, dst, sems.at[i]) for i, (src, dst) in enumerate(pairs)]
-    for copy in copies:
-        copy.start()
     tok = raw_ref.shape[0]
+    place = lax.axis_index("ctx")
+    for r in range(rounds):
+        bits_ref[8 * r : 8 * r + 8] = jnp.full((8, INNER), (place >> r) & 1, jnp.int32).astype(f32)
     dt8_ref[...] = jnp.zeros_like(dt8_ref)
-    for copy in copies[:4]:
-        copy.wait()
     dt8_ref[0:H] = dt_ref[...]
     dt_pre = dt8_ref[...] + by_head(dt_bias_ref, tok)
     step = jnp.maximum(dt_pre, 0.0) + jnp.log1p(jnp.exp(-jnp.abs(dt_pre)))
-    decay_rate = -jnp.exp(by_head(alog_ref, tok))
-    until = jnp.where(iota((tok, tok), 0) <= iota((tok, tok), 1), 1.0, 0.0).astype(bf16)
-    cum = unstacked(dot(stacked(step * decay_rate), until))
+    real = iota((HEAD_ROWS, tok), 0) < H
+    decay_rate = jnp.where(real, -jnp.exp(by_head(alog_ref, tok)), 0.0)
+    cum = unstacked(dot(stacked(step * decay_rate), until_ref[...]))
     left = jnp.exp(cum[:, tok - 1 : tok] - cum)
     reach = jnp.exp(cum)
     rows_ref[0:8] = cum
@@ -149,15 +154,10 @@
     rows_ref[40:48] = decay_rate
     tail_ref[...] = over_channels(left * step)
     log_total = over_channels(cum)[tok - 1 : tok]
-    skip = jnp.zeros((1, INNER), f32)
-    for h in range(H):
-        skip = jnp.where(iota((1, INNER), 1) // P_SIZE == h, skip_ref[h], skip)
+    skip = over_channels(by_head(skip_ref, HEAD_ROWS))[0:1]
     row = iota((8, INNER), 0)
     logs_ref[...] = jnp.where(row == 2, log_total, jnp.where(row == 3, skip, 0.0))
-    copies[4].wait()
     scaled_ref[...] = jnp.concatenate(split2(cot_ref[...].astype(f32) * over_channels(reach)), 1)
-    for copy in copies[5:]:
-        copy.wait()
     raw = raw_ref[...].astype(f32)
     zeros = jnp.zeros((8, raw.shape[1]), f32)
     pre = bias_ref[...] + weight_ref[K - 1 : K] * raw
@@ -167,7 +167,7 @@
 
 
 def enter_kernel(
-    last, pre_ref, halo_ref, weight_ref, scaled_ref, tail_ref, logs_ref, upper_ref,
+    last, pre_ref, halo_ref, weight_ref, scaled_ref, tail_ref, logs_ref, bits_ref,
     xbc_ref, slope_ref, weighted_ref, state_ref, grad_ref, msg_ref,
 ):
     tok = pre_ref.shape[0]
@@ -189,17 +189,17 @@
     grad = grad[:, :INNER] + grad[:, INNER:]
     state_ref[...] = state
     grad_ref[...] = grad
-    write_message(msg_ref, state, grad, logs_ref[2:3], last, upper_ref[0] == 1)
-
-
-def merge_kernel(first, last, state_ref, grad_ref, logs_ref, got_ref, upper_ref, *refs):
+    write_message(msg_ref, state, grad, logs_ref[2:3], last, is_upper(bits_ref, 0))
+
+
+def merge_kernel(r, first, last, state_ref, grad_ref, logs_ref, got_ref, bits_ref, *refs):
     if first:
         prior = after = 0.0
     else:
         prior, after = refs[0][...], refs[1][...]
         refs = refs[2:]
     logs_out, msg_ref, prior_out, after_out, *refs = refs
-    upper = upper_ref[0] == 1
+    upper = is_upper(bits_ref, r)
     log_prior, log_after, log_total = logs_ref[0:1], logs_ref[1:2], logs_ref[2:3]
     tail = got_ref[2 * N : 2 * N + TAIL_ROWS]
     got_state = got_ref[0:N] * jnp.exp(tail[2:3])
@@ -219,7 +219,7 @@
     if refs:
         refs[0][...] = state
         refs[1][...] = grad
-    write_message(msg_ref, state, grad, log_total, last, upper_ref[1] == 1)
+    write_message(msg_ref, state, grad, log_total, last, is_upper(bits_ref, r + 1))
 
 
 def local_kernel(xbc_ref, cot_ref, rows_ref, logs_ref, local_ref, sums_ref):
@@ -264,17 +264,17 @@
     sums_ref[16:24] = head_sums(values_f * cot_f)
 
 
-def leave_kernel(
-    raw_ref, halo_ref, weight_ref, xbc_ref, slope_ref, scaled_ref, weighted_ref, tail_ref, rows_ref, local_ref, sums_ref,
-    logs_ref, got_ref, upper_ref, *refs
+def totals_kernel(
+    r, raw_ref, halo_ref, xbc_ref, slope_ref, scaled_ref, weighted_ref, tail_ref, rows_ref, local_ref, sums_ref,
+    logs_ref, got_ref, bits_ref, until_ref, weight_ref, *refs
 ):
     prior, after = 0.0, 0.0
-    if len(refs) > 8:
+    if len(refs) > 5:
         prior, after = refs[0][...], refs[1][...]
         refs = refs[2:]
-    out_hbm, dt_out_ref, end_ref, spill_ref, totals_ref, out_ref, totals_scratch, sem = refs
+    conv_ref, dt_out_ref, totals_ref, spill_ref, totals_scratch = refs
     tok = raw_ref.shape[0]
-    upper = upper_ref[0] == 1
+    upper = is_upper(bits_ref, r)
     got = got_ref[0:N] * jnp.exp(got_ref[N : N + 1])
     prior = prior + jnp.where(upper, jnp.exp(logs_ref[0:1]) * got, 0.0)
     after = after + jnp.where(upper, 0.0, jnp.exp(logs_ref[1:2]) * got)
@@ -293,33 +293,23 @@
     grad_b = grad_b[:, :N] + grad_b[:, N:] + dot(weighted_ref[:, INNER:], after2[:N], 1, 1)
     grad_low = (local_ref[...] + jnp.concatenate([tail_ref[...] * back, grad_b, grad_c], 1)).astype(bf16)
     grad_conv = grad_low.astype(f32) * slope_ref[...]
+    conv_ref[...] = grad_conv
+    top = grad_conv[:8]
+    spill = jnp.zeros_like(top)
+    for ahead in range(1, K):
+        tap = weight_ref[K - 1 - ahead : K - ahead]
+        spill = spill + tap * jnp.where(iota(top.shape, 0) < 8 - ahead, 0.0, pltpu.roll(top, 8 - ahead, 0))
+    spill_ref[...] = spill
 
     raw = raw_ref[...].astype(f32)
     halo = halo_ref[HALO_ROWS - 8 :].astype(f32)
-    sums = [None] * (K + 1)
-    sums[K - 1] = jnp.sum(grad_conv * raw, axis=0, keepdims=True)
-    sums[K] = jnp.sum(grad_conv, axis=0, keepdims=True)
-    grad_in = weight_ref[K - 1 : K] * grad_conv
-    spill = jnp.zeros((8, raw.shape[1]), f32)
-    row8 = iota(spill.shape, 0)
-    for ahead in range(1, K):
-        tap = weight_ref[K - 1 - ahead : K - ahead]
-        sums[K - 1 - ahead] = jnp.sum(grad_conv * shifted_down(raw, halo, ahead), axis=0, keepdims=True)
-        moved = pltpu.roll(grad_conv, tok - ahead, 0)
-        last8 = moved[tok - 8 :]
-        inside = row8 < 8 - ahead
-        grad_in = grad_in + tap * jnp.concatenate([moved[: tok - 8], jnp.where(inside, last8, 0.0)], 0)
-        spill = spill + tap * jnp.where(inside, 0.0, last8)
-    out_ref[...] = grad_in.astype(bf16)
-    copy = pltpu.make_async_copy(out_ref, out_hbm, sem)
-    copy.start()
-    end_ref[...] = grad_in[tok - END_ROWS :]
-    spill_ref[...] = spill
+    sums = [grad_conv * shifted_down(raw, halo, K - 1 - k) for k in range(K - 1)] + [grad_conv * raw, grad_conv]
     totals_scratch[...] = jnp.zeros_like(totals_scratch)
-    for k in range(K + 1):
+    for k, each in enumerate(sums):
+        each = jnp.sum(each, axis=0, keepdims=True)
         for j in range(LANE_BLOCKS):
             at = k * LANE_BLOCKS + j
-            totals_scratch[at : at + 1] = sums[k][:, j * 128 : (j + 1) * 128]
+            totals_scratch[at : at + 1] = each[:, j * 128 : (j + 1) * 128]
 
     values = xbc_ref[:, :INNER].astype(f32)
     pairs, from_values, skip_rows = sums_ref[0:8], sums_ref[8:16], sums_ref[16:24]
@@ -331,9 +321,8 @@
     through = jnp.sum(prior * after, axis=0, keepdims=True)
     through = jnp.sum(selector * through, axis=1, keepdims=True) * reach[:, tok - 1 : tok]
     last_extra = jnp.sum(tail_term, axis=1, keepdims=True) + through
-    from_on = jnp.where(iota((tok, tok), 0) >= iota((tok, tok), 1), 1.0, 0.0).astype(bf16)
     grad_cum = pairs - from_values * step + seen_rows - tail_term
-    grad_log = unstacked(dot(stacked(grad_cum), from_on)) + last_extra
+    grad_log = unstacked(dot(stacked(grad_cum), until_ref[...], 1, 1)) + last_extra
     grad_step = from_values + tail_rows * left + decay_rate * grad_log
     grad_pre = grad_step * dt_gate
     dt_out_ref[...] = grad_pre[0:H]
@@ -342,45 +331,60 @@
     for i, each in enumerate((grad_pre, grad_log * step * decay_rate, skip_rows)):
         column = jnp.sum(each, axis=1, keepdims=True)
         small = jnp.where((row < H) & (lane == row + i * H), column, small)
-    at = (K + 1) * LANE_BLOCKS
-    totals_scratch[at : at + 1] = jnp.sum(small, axis=0, keepdims=True)
+    totals_scratch[SMALL_ROW : SMALL_ROW + 1] = jnp.sum(small, axis=0, keepdims=True)
     totals_ref[...] = pack_totals(totals_scratch[...])
+
+
+def input_kernel(conv_ref, weight_ref, out_hbm, end_ref, out_ref, sem):
+    grad_conv = conv_ref[...]
+    tok, channels = grad_conv.shape
+    grad_in = weight_ref[K - 1 : K] * grad_conv
+    row8 = iota((8, channels), 0)
+    for ahead in range(1, K):
+        tap = weight_ref[K - 1 - ahead : K - ahead]
+        moved = pltpu.roll(grad_conv, tok - ahead, 0)
+        last8 = moved[tok - 8 :]
+        inside = row8 < 8 - ahead
+        grad_in = grad_in + tap * jnp.concatenate([moved[: tok - 8], jnp.where(inside, last8, 0.0)], 0)
+    out_ref[...] = grad_in.astype(bf16)
+    copy = pltpu.make_async_copy(out_ref, out_hbm, sem)
+    copy.start()
+    end_ref[...] = grad_in[tok - END_ROWS :]
     copy.wait()
 
 
-def summed(parts):
-    shape = parts.shape
-    logs = parts[:, shape[1] - 1 :]
-    logs = jnp.sum(jnp.where(iota(shape, 1) == iota(shape, 2), logs, 0.0), axis=2, keepdims=True)
-    return jnp.sum(parts * jnp.exp(logs), axis=0)
-
-
-def repack_kernel(parts_ref, out_ref):
-    total = summed(parts_ref[...])
-    out_ref[...] = pack_totals(jnp.where(iota(total.shape, 0) == total.shape[0] - 1, 0.0, total))
-
-
-def finish_kernel(
-    parts_ref, end_ref, spilled_ref, main_hbm, out_hbm, weight_ref, bias_ref, dt_bias_ref, alog_ref, skip_ref, rows_ref, sem
-):
+def end_kernel(end_ref, spilled_ref, main_hbm, out_hbm, rows_ref, sem):
     end = end_ref[...]
     fixed = end[END_ROWS - 8 :] + spilled_ref[...]
     rows_ref[...] = jnp.concatenate([end[: END_ROWS - 8], fixed], 0).astype(bf16)
     tok = out_hbm.shape[0]
     copy = pltpu.make_async_copy(rows_ref, out_hbm.at[pl.ds(tok - END_ROWS, END_ROWS)], sem)
     copy.start()
-    total = summed(parts_ref[...])
+    copy.wait()
+
+
+def summed(parts):
+    large = jnp.sum(parts * jnp.exp(parts[:, SMALL_ROW + 1 : SMALL_ROW + 2]), axis=0)
+    small = parts[:, SMALL_ROW : SMALL_ROW + 1] * jnp.exp(parts[:, SMALL_ROW + 2 : SMALL_ROW + 3])
+    return large, jnp.sum(small, axis=0)
+
+
+def repack_kernel(parts_ref, out_ref):
+    large, small = summed(parts_ref[...])
+    out_ref[...] = pack_totals(jnp.where(iota(large.shape, 0) == SMALL_ROW, small, large))
+
+
+def finish_kernel(parts_ref, weight_ref, bias_ref, dt_bias_ref, alog_ref, skip_ref):
+    large, small = summed(parts_ref[...])
     for k in range(K + 1):
         for j in range(LANE_BLOCKS):
             at = k * LANE_BLOCKS + j
             if k < K:
-                weight_ref[k : k + 1, j * 128 : (j + 1) * 128] = total[at : at + 1]
+                weight_ref[k : k + 1, j * 128 : (j + 1) * 128] = large[at : at + 1]
             else:
-                bias_ref[:, j * 128 : (j + 1) * 128] = total[at : at + 1]
-    at = (K + 1) * LANE_BLOCKS
+                bias_ref[:, j * 128 : (j + 1) * 128] = large[at : at + 1]
     for i, ref in enumerate((dt_bias_ref, alog_ref, skip_ref)):
-        ref[...] = total[at : at + 1, i * H : (i + 1) * H]
-    copy.wait()
+        ref[...] = small[:, i * H : (i + 1) * H]
 
 
 def call(kernel, outs, in_specs, out_specs=None, scratch=(), flops=0, limit=16 << 20, aliases=None):
@@ -411,34 +415,32 @@
 
 
 def on_device(xbc_raw, conv_weight, conv_bias, dt_raw, dt_bias, a_log, d_skip, grad_out):
-    raw = xbc_raw[0]
-    tok, channels = raw.shape
+    tok, channels = xbc_raw.shape[1:]
     slabs = lax.axis_size("ctx")
+    contexts = lax.axis_size("dp")
     rounds = slabs.bit_length() - 1
     assert slabs == 1 << rounds and rounds > 0
-    place = lax.axis_index("ctx")
-    bits = [(place >> r) & 1 for r in range(rounds)]
-
-    halo = lax.ppermute(raw[tok - HALO_ROWS :], "ctx", [(i, i + 1) for i in range(slabs - 1)])
+
+    raw, cot, dt_rows = xbc_raw[0], grad_out[0], dt_raw[0].T
+    until = call(triangle_kernel, struct((tok, tok), bf16), [], flops=10**10)()
+    early_raw, until = lax.optimization_barrier((raw, until))
+    halo = lax.ppermute(early_raw[tok - HALO_ROWS :], "ctx", [(i, i + 1) for i in range(slabs - 1)])
 
     def message(r):
         return struct((N + TAIL_ROWS if r == rounds - 1 else 2 * N + TAIL_ROWS, INNER))
 
     state_like = struct((N, INNER))
     logs_like = struct((8, INNER))
-    raw_near, cot, weight, pre, scaled, tail, rows, logs = call(
-        start_kernel,
+    pre, scaled, tail, rows, logs, bits = call(
+        functools.partial(start_kernel, rounds),
         (
-            struct((tok, channels), bf16), struct((tok, INNER), bf16), struct((K, channels)), struct((tok, channels)),
-            struct((tok, 2 * INNER), bf16), struct((tok, INNER)), struct((6 * HEAD_ROWS, tok)), logs_like,
+            struct((tok, channels)), struct((tok, 2 * INNER), bf16), struct((tok, INNER)), struct((6 * HEAD_ROWS, tok)),
+            logs_like, struct((8 * rounds, INNER)),
         ),
-        [HBM] * 8,
-        scratch=[
-            pltpu.VMEM((1, channels), f32), pltpu.VMEM((H, tok), f32), pltpu.VMEM((HEAD_ROWS, tok), f32),
-            pltpu.SMEM((H,), f32), pltpu.SMEM((H,), f32), pltpu.SMEM((H,), f32), pltpu.SemaphoreType.DMA((8,)),
-        ],
+        [VMEM] * 9,
+        scratch=[pltpu.VMEM((HEAD_ROWS, tok), f32)],
         flops=100_000_000,
-    )(raw, grad_out[0], conv_weight, conv_bias[None], dt_raw[0].T, dt_bias, a_log, d_skip)
+    )(raw, cot, conv_weight, conv_bias[None], dt_rows, dt_bias[None], a_log[None], d_skip[None], until)
 
     xbc, slope, weighted, state, grad, msg = call(
         functools.partial(enter_kernel, rounds == 1),
@@ -446,9 +448,9 @@
             struct((tok, channels), bf16), struct((tok, channels)), struct((tok, 2 * INNER), bf16),
             state_like, state_like, message(0),
         ),
-        [VMEM] * 6 + [SMEM],
+        [VMEM] * 7,
         flops=200_000_000,
-    )(pre, halo, weight, scaled, tail, logs, jnp.stack([bits[0]]))
+    )(pre, halo, conv_weight, scaled, tail, logs, bits)
 
     local, sums = call(
         local_kernel,
@@ -464,46 +466,52 @@
             got, local, sums = lax.optimization_barrier((got, local, sums))
         last = r + 1 == rounds - 1
         logs, msg, *carried = call(
-            functools.partial(merge_kernel, r == 0, last),
+            functools.partial(merge_kernel, r, r == 0, last),
             (logs_like, message(r + 1)) + (state_like,) * (2 if last else 4),
-            [VMEM] * 4 + [SMEM] + [VMEM] * len(carried),
+            [VMEM] * (5 + len(carried)),
             flops=1_000_000,
-        )(state, grad, logs, got, jnp.stack([bits[r], bits[r + 1]]), *carried)
+        )(state, grad, logs, got, bits, *carried)
         if not last:
             *carried, state, grad = carried
     got = exchange(msg, 1 << (rounds - 1), slabs)
 
-    grad_main, grad_dt, end, spill, packed = call(
-        leave_kernel,
-        (
-            struct((tok, channels), bf16), struct((H, tok)), struct((END_ROWS, channels)), struct((8, channels)),
-            struct((TOTAL_ROWS, 128)),
-        ),
-        [VMEM] * 13 + [SMEM] + [VMEM] * len(carried),
-        (HBM, VMEM, VMEM, VMEM, VMEM),
-        [pltpu.VMEM((tok, channels), bf16), pltpu.VMEM((TOTAL_ROWS, 128), f32), pltpu.SemaphoreType.DMA],
+    grad_conv, grad_dt, packed, spill = call(
+        functools.partial(totals_kernel, rounds - 1),
+        (struct((tok, channels)), struct((H, tok)), struct((TOTAL_ROWS, 128)), struct((8, channels))),
+        [VMEM] * (15 + len(carried)),
+        scratch=[pltpu.VMEM((TOTAL_ROWS, 128), f32)],
         flops=200_000_000,
-    )(raw_near, halo, weight, xbc, slope, scaled, weighted, tail, rows, local, sums, logs, got, jnp.stack([bits[-1]]), *carried)
+    )(raw, halo, xbc, slope, scaled, weighted, tail, rows, local, sums, logs, got, bits, until, conv_weight, *carried)
 
     spilled = lax.ppermute(spill, "ctx", [(i + 1, i) for i in range(slabs - 1)])
-
-    contexts = lax.axis_size("dp")
     if slabs * contexts <= 64:
         parts = everyones(packed, ("ctx", "dp"), slabs * contexts)
     else:
         packed = call(repack_kernel, struct((TOTAL_ROWS, 128)), [VMEM])(everyones(packed, "ctx", slabs))
         parts = everyones(packed, "dp", contexts)
-    grad_input, grad_weight, grad_bias, *small = call(
+
+    grad_main, end = call(
+        input_kernel,
+        (struct((tok, channels), bf16), struct((END_ROWS, channels))),
+        [VMEM] * 2,
+        (HBM, VMEM),
+        [pltpu.VMEM((tok, channels), bf16), pltpu.SemaphoreType.DMA],
+        flops=1_000_000,
+    )(grad_conv, conv_weight)
+    grad_input = call(
+        end_kernel,
+        struct((tok, channels), bf16),
+        [VMEM] * 2 + [HBM],
+        HBM,
+        [pltpu.VMEM((END_ROWS, channels), bf16), pltpu.SemaphoreType.DMA],
+        aliases={2: 0},
+    )(end, spilled, grad_main)
+
+    grad_weight, grad_bias, *small = call(
         finish_kernel,
-        (
-            struct((tok, channels), bf16), struct((K, channels)), struct((1, channels)),
-            struct((1, H)), struct((1, H)), struct((1, H)),
-        ),
-        [VMEM] * 3 + [HBM],
-        (HBM,) + (VMEM,) * 5,
-        [pltpu.VMEM((END_ROWS, channels), bf16), pltpu.SemaphoreType.DMA],
-        aliases={3: 0},
-    )(parts, end, spilled, grad_main)
+        (struct((K, channels)), struct((1, channels)), struct((1, H)), struct((1, H)), struct((1, H))),
+        [VMEM],
+    )(parts)
     return (grad_input[None], grad_dt.T[None], grad_weight, grad_bias[0], *(each[0] for each in small))
 
 

time: 47.4 us -> 44.3 us (0.935)
  starting transfers between devices: 19.8 us -> 21.6 us
  local copies, waits for them, and re-layouts: 3.95 us -> 2.23 us
  waiting for transfers between devices: 13.6 us -> 11.9 us
  Pallas kernels: 8.6 us -> 7.27 us
    all_to_all x1, waiting for transfers between devices: 7.93 us -> 3.57 us  [everyones(): return lax.all_to_all(packed, axes, 0, 0).astype(f32)]
    ppermute x1, waiting for transfers between devices: 0.01 us -> 2.78 us  [on_device(): spilled = lax.ppermute(spill, 'ctx', [(i + 1, i) for i in range(slabs - 1)])]
    pallas_call x5 -> x8, Pallas kernels: 6.53 us -> 5.19 us  [the longest x1 1.6 us: on_device(): call(functools.partial(totals_kernel, rounds - 1), (struct((tok, channels...]
    all_to_all x1, starting transfers between devices: 9.5 us -> 10.8 us  [everyones(): return lax.all_to_all(packed, axes, 0, 0).astype(f32)]
    unnamed x16, local copies, waits for them, and re-layouts: 2.54 us -> 1.52 us
    slice x1, local copies, waits for them, and re-layouts: 0.72 us -> 0.01 us  [on_device(): early_raw[tok - HALO_ROWS:]]
  transfers between devices with their start and end apart: 6 -> 6, of which waited for: 4 -> 5; matrix products, arithmetic and copies ran while one was open for 0% -> 0% of each run, Pallas kernels for 7% -> 9%
where the time goes in v2:
time: 44.3 us; the launch traced here: 44 us
  starting transfers between devices  21.6 us (49%)
  waiting for transfers between devices  11.9 us (27%)
  Pallas kernels  7.27 us (16%)
  local copies, waits for them, and re-layouts  2.23 us (5%)
  between operations  0.85 us (2%)
    all_to_all x1, starting transfers between devices, everyones(): return lax.all_to_all(packed, axes, 0, 0).astype(f32)  10.8 us
    ppermute x3, waiting for transfers between devices, exchange(): lax.ppermute(message, 'ctx', [(i, i ^ distance) for i in range(slabs)])  5.54 us
    ppermute x3, starting transfers between devices, exchange(): lax.ppermute(message, 'ctx', [(i, i ^ distance) for i in range(slabs)])  5.46 us
    ppermute x1, starting transfers between devices, on_device(): lax.ppermute(early_raw[tok - HALO_ROWS:], 'ctx', [(i, i + 1) for i in ran...  4.06 us
    all_to_all x1, waiting for transfers between devices, everyones(): return lax.all_to_all(packed, axes, 0, 0).astype(f32)  3.57 us
    ppermute x1, waiting for transfers between devices, on_device(): spilled = lax.ppermute(spill, 'ctx', [(i + 1, i) for i in range(slabs - 1)])  2.78 us
    pallas_call x1, Pallas kernels, on_device(): call(functools.partial(totals_kernel, rounds - 1), (struct((tok, channels...  1.6 us
    pallas_call x1, Pallas kernels, on_device(): call(local_kernel, (struct((tok, channels)), struct((3 * HEAD_ROWS, tok))...  1.59 us
  transfers between devices with their start and end apart: 6, of which 5 were waited for; matrix products, arithmetic and copies ran while one was open for 0% of the time, Pallas kernels for 9%

profile of v2, /device:TPU:1, one launch (start us, length us, event | category | flops | bytes accessed | tf_op | source)
XLA Modules:
  0.0 44.0 jit_solution(12655622285601060114)
XLA Ops:
  0.6 0.0 copy-start
  0.6 0.0 copy-start.2
  0.7 0.0 copy-start.3
  0.7 0.0 copy-start.7
  0.7 0.9 %copy-done = bf16[1,256,512]{2,1,0:T(8,128)(2,1)S(1)} copy-done((bf16[1,256,512]{2,1,0:T(8,128)(2,1)S(1)}, bf16[1,256,512]{2,1,0:T(8,128)(2,1)}, u32[]{:S(2)}) %copy-start) | copy-done | bytes 262168
  1.6 4.1 %collective-permute-start = (bf16[16,512]{1,0:T(8,128)(2,1)S(1)}, bf16[16,512]{1,0:T(8,128)(2,1)S(1)}, u32[]{:S(2)}, u32[]{:S(2)}) collective-permute-start(bf16[16,512]{1,0:T(8,128)(2,1)S(1)} %slice.3), channel_id=1, source_target_pairs={{0,4},{4,8},{8,12},{12,16},{16,20},{20,24},{24,28},{1,5},{5,9},{9,... | collective-permute-start | bytes 49160 | tf_op jit(solution)/shard_map/ppermute | solution.py:427
  5.7 0.0 copy-start.4
  5.7 0.0 copy-start.5
  5.7 0.0 copy-start.6
  5.7 0.0 copy-done.2
  5.7 0.6 %copy-done.4 = f32[512]{0:T(512)S(1)} copy-done((f32[512]{0:T(512)S(1)}, f32[512]{0:T(512)}, u32[]{:S(2)}) %copy-start.4) | copy-done | bytes 2072
  6.4 1.0 %shard_map.136 = (f32[256,512]{1,0:T(8,128)S(1)}, bf16[256,512]{1,0:T(8,128)(2,1)S(1)}, f32[256,256]{1,0:T(8,128)S(1)}, f32[48,256]{1,0:T(8,128)S(1)}, f32[8,256]{1,0:T(8,128)S(1)}, /*index=5*/f32[24,256]{1,0:T(8,128)S(1)}) custom-call(bf16[256,512]{1,0:T(8,128)(2,1)S(1)} %bitcast.18, bf16[256,256]{1,0:T(8,128)(2,1)S(1)} %bitcast.20, ...), custom_call_target="tpu_custom_call" | custom-call | flops 100000000 | bytes 1048576 | tf_op jit(solution)/shard_map/pallas_call | solution.py:434
  7.4 0.0 collective-permute-done.halo_ref
  7.4 0.5 %shard_map.137 = (bf16[256,512]{1,0:T(8,128)(2,1)S(1)}, f32[256,512]{1,0:T(8,128)S(1)}, bf16[256,512]{1,0:T(8,128)(2,1)S(1)}, f32[128,256]{1,0:T(8,128)S(1)}, f3...) custom-call(f32[256,512]{1,0:T(8,128)S(1)} %get-tuple-element.49.pre_ref, ...), custom_call_target="tpu_custom_call" | custom-call | flops 200000000 | bytes 1048576 | tf_op jit(solution)/shard_map/pallas_call | solution.py:445
  7.9 1.3 %collective-permute-start.1 = (f16[272,256]{1,0:T(8,128)(2,1)S(1)}, f16[272,256]{1,0:T(8,128)(2,1)S(1)}, u32[]{:S(2)}, u32[]{:S(2)}) collective-permute-start(f16[272,256]{1,0:T(8,128)(2,1)S(1)} %convert_element_type.24), channel_id=1, source_target_pairs={{0,4},{4,0},{8,12},{12,8},{16,20},{20,16},{24,28},{28,24},{1,5},{5... | collective-permute-start | bytes 417800 | tf_op jit(solution)/shard_map/ppermute | solution.py:409
  9.2 1.6 %shard_map.138 = (f32[256,512]{1,0:T(8,128)S(1)}, f32[24,256]{1,0:T(8,128)S(1)}) custom-call(bf16[256,512]{1,0:T(8,128)(2,1)S(1)} %get-tuple-element.54.xbc_ref, bf16[256,256]{1,0:T(8,128)(2,1)S(1)} %bitcast.21, f32[48,256]{1,0:T(8,128)S(1)} %get-tuple-element.57.rows_ref, f32[8,256]{1,0:T(8,128)S(1)} %get-tuple-element.52.logs_ref), custom_call_target="tpu_custom_call" | custom-call | flops 1000000000 | bytes 1048576 | tf_op jit(solution)/shard_map/pallas_call | solution.py:455
  10.8 1.3 %collective-permute-done.1 = f16[272,256]{1,0:T(8,128)(2,1)S(1)} collective-permute-done((f16[272,256]{1,0:T(8,128)(2,1)S(1)}, f16[272,256]{1,0:T(8,128)(2,1)S(1)}, u32[]{:S(2)}, u32[]{:S(2)}) %collective-permute-start.1) | collective-permute-done | bytes 139296 | tf_op jit(solution)/shard_map/ppermute | solution.py:409
  12.2 0.1 shard_map.139
  12.4 1.6 %collective-permute-start.2 = (f16[272,256]{1,0:T(8,128)(2,1)S(1)}, f16[272,256]{1,0:T(8,128)(2,1)S(1)}, u32[]{:S(2)}, u32[]{:S(2)}) collective-permute-start(f16[272,256]{1,0:T(8,128)(2,1)S(1)} %convert_element_type.26), channel_id=1, source_target_pairs={{0,8},{4,12},{8,0},{12,4},{16,24},{20,28},{24,16},{28,20},{1,9},{5... | collective-permute-start | bytes 417800 | tf_op jit(solution)/shard_map/ppermute | solution.py:409
  14.0 2.4 %collective-permute-done.2 = f16[272,256]{1,0:T(8,128)(2,1)S(1)} collective-permute-done((f16[272,256]{1,0:T(8,128)(2,1)S(1)}, f16[272,256]{1,0:T(8,128)(2,1)S(1)}, u32[]{:S(2)}, u32[]{:S(2)}) %collective-permute-start.2) | collective-permute-done | bytes 139296 | tf_op jit(solution)/shard_map/ppermute | solution.py:409
  16.4 0.2 shard_map.140
  16.6 2.5 %collective-permute-start.3 = (f16[144,256]{1,0:T(8,128)(2,1)S(1)}, f16[144,256]{1,0:T(8,128)(2,1)S(1)}, u32[]{:S(2)}, u32[]{:S(2)}) collective-permute-start(f16[144,256]{1,0:T(8,128)(2,1)S(1)} %convert_element_type.28), channel_id=1, source_target_pairs={{0,16},{4,20},{8,24},{12,28},{16,0},{20,4},{24,8},{28,12},{1,17},{... | collective-permute-start | bytes 221192 | tf_op jit(solution)/shard_map/ppermute | solution.py:409
  19.2 1.7 %collective-permute-done.3 = f16[144,256]{1,0:T(8,128)(2,1)S(1)} collective-permute-done((f16[144,256]{1,0:T(8,128)(2,1)S(1)}, f16[144,256]{1,0:T(8,128)(2,1)S(1)}, u32[]{:S(2)}, u32[]{:S(2)}) %collective-permute-start.3) | collective-permute-done | bytes 73760 | tf_op jit(solution)/shard_map/ppermute | solution.py:409
  20.9 1.6 %shard_map.141 = (f32[256,512]{1,0:T(8,128)S(1)}, f32[4,256]{1,0:T(4,128)}, f32[24,128]{1,0:T(8,128)S(1)}, f32[8,512]{1,0:T(8,128)S(1)}) custom-call(bf16[256,512]{1,0:T(8,128)(2,1)S(1)} %bitcast.19, bf16[16,512]{1,0:T(8,128)(2,1)S(1)} %collective-permute-done.halo_ref, bf16[256,512]{1,0:T(8,128)(2,1)S(1)} %get-tuple-element.54.xbc_ref, ...), custom_call_target="tpu_custom_call" | custom-call | flops 200000000 | bytes 1048576 | tf_op jit(solution)/shard_map/pallas_call | solution.py:478
  22.5 0.7 %broadcast_in_dim.30 = f16[32,24,128]{2,1,0:T(8,128)(2,1)} broadcast(f16[24,128]{1,0:T(8,128)(2,1)S(1)} %convert_element_type.30), dimensions={1,2} | broadcast | bytes 202752 | tf_op jit(solution)/shard_map/broadcast_in_dim | solution.py:413
  23.2 10.8 %all-to-all-start = ((f16[32,24,128]{2,1,0:T(8,128)(2,1)}), f16[32,24,128]{2,1,0:T(8,128)(2,1)S(1)}, u32[]{:S(2)}, u32[]{:S(2)}) async-start(f16[32,24,128]{2,1,0:T(8,128)(2,1)} %broadcast_in_dim.30), calls=%async_computation | async-start | bytes 393216 | tf_op jit(solution)/shard_map/all_to_all | solution.py:414
  34.0 1.3 %collective-permute-start.4 = (f32[8,512]{1,0:T(8,128)S(1)}, f32[8,512]{1,0:T(8,128)S(1)}, u32[]{:S(2)}, u32[]{:S(2)}) collective-permute-start(f32[8,512]{1,0:T(8,128)S(1)} %get-tuple-element.78), channel_id=1, source_target_pairs={{4,0},{8,4},{12,8},{16,12},{20,16},{24,20},{28,24},{5,1},{9,5},{13... | collective-permute-start | bytes 49160 | tf_op jit(solution)/shard_map/ppermute | solution.py:486
  35.3 0.9 %shard_map.142 = (bf16[256,512]{1,0:T(8,128)(2,1)}, f32[16,512]{1,0:T(8,128)S(1)}) custom-call(f32[256,512]{1,0:T(8,128)S(1)} %get-tuple-element.76.conv_ref, f32[4,512]{1,0:T(4,128)S(1)} %copy-done.1), custom_call_target="tpu_custom_call" | custom-call | flops 1000000 | bytes 1048576 | tf_op jit(solution)/shard_map/pallas_call | solution.py:493
  36.3 2.8 %collective-permute-done.4.spilled_ref = f32[8,512]{1,0:T(8,128)S(1)} collective-permute-done((f32[8,512]{1,0:T(8,128)S(1)}, f32[8,512]{1,0:T(8,128)S(1)}, u32[]{:S(2)}, u32[]{:S(2)}) %collective-permute-start.4) | collective-permute-done | bytes 16416 | tf_op jit(solution)/shard_map/ppermute | solution.py:486
  39.1 0.6 %shard_map.143 = bf16[256,512]{1,0:T(8,128)(2,1)} custom-call(f32[16,512]{1,0:T(8,128)S(1)} %get-tuple-element.77.end_ref, f32[8,512]{1,0:T(8,128)S(1)} %collective-permute-done.4.spilled_ref, bf16[256,512]{1,0:T(8,128)(2,1)} %get-tuple-element.79.main_hbm), custom_call_target="tpu_custom_call", output_to_operand_aliasing={{}: (2, {})} | custom-call | bytes 1048576 | tf_op jit(solution)/shard_map/pallas_call | solution.py:501
  39.7 3.6 %all-to-all-done = f16[32,24,128]{2,1,0:T(8,128)(2,1)S(1)} async-done(((f16[32,24,128]{2,1,0:T(8,128)(2,1)}), f16[32,24,128]{2,1,0:T(8,128)(2,1)S(1)}, u32[]{:S(2)}, u32[]{:S(2)}) %all-to-all-start) | async-done | bytes 196640 | tf_op jit(solution)/shard_map/all_to_all | solution.py:414
  43.3 0.7 %shard_map.144 = (f32[4,512]{1,0:T(4,128)}, f32[1,512]{1,0:T(1,128)}, f32[1,4]{1,0:T(1,128)}, f32[1,4]{1,0:T(1,128)}, f32[1,4]{1,0:T(1,128)}) custom-call(f32[32,24,128]{2,1,0:T(8,128)S(1)} %convert_element_type.31.parts_ref), custom_call_target="tpu_custom_call" | custom-call | bytes 1048576 | tf_op jit(solution)/shard_map/pallas_call | solution.py:510
  (16 shorter events, 0.2 us)
Async XLA Ops:
  0.6 1.0 %copy-start = (bf16[1,256,512]{2,1,0:T(8,128)(2,1)S(1)}, bf16[1,256,512]{2,1,0:T(8,128)(2,1)}, u32[]{:S(2)}) copy-start(bf16[1,256,512]{2,1,0:T(8,128)(2,1)} %param.8) | copy-start | bytes 786436
  0.6 5.1 %copy-start.2 = (bf16[1,256,256]{2,1,0:T(8,128)(2,1)S(1)}, bf16[1,256,256]{2,1,0:T(8,128)(2,1)}, u32[]{:S(2)}) copy-start(bf16[1,256,256]{2,1,0:T(8,128)(2,1)} %param.15) | copy-start | bytes 393220
  0.7 5.1 %copy-start.3 = (f32[1,256,4]{1,2,0:T(4,128)S(1)}, f32[1,256,4]{1,2,0:T(4,128)}, u32[]{:S(2)}) copy-start(f32[1,256,4]{1,2,0:T(4,128)} %param.11) | copy-start | bytes 12292
  0.7 5.1 %copy-start.7 = (f32[4]{0:T(128)S(1)}, f32[4]{0:T(128)}, u32[]{:S(2)}) copy-start(f32[4]{0:T(128)} %param.14) | copy-start | bytes 52
  1.6 4.1 %copy-start.1 = (f32[4,512]{1,0:T(4,128)S(1)}, f32[4,512]{1,0:T(4,128)}, u32[]{:S(2)}) copy-start(f32[4,512]{1,0:T(4,128)} %weight_ref.7) | copy-start | bytes 24580
  1.6 5.8 %collective-permute-start = (bf16[16,512]{1,0:T(8,128)(2,1)S(1)}, bf16[16,512]{1,0:T(8,128)(2,1)S(1)}, u32[]{:S(2)}, u32[]{:S(2)}) collective-permute-start(bf16[16,512]{1,0:T(8,128)(2,1)S(1)} %slice.3), channel_id=1, source_target_pairs={{0,4},{4,8},{8,12},{12,16},{16,20},{20,24},{24,28},{1,5},{5,9},{9,... | collective-permute-start | bytes 49160 | tf_op jit(solution)/shard_map/ppermute | solution.py:427
  5.7 0.7 %copy-start.4 = (f32[512]{0:T(512)S(1)}, f32[512]{0:T(512)}, u32[]{:S(2)}) copy-start(f32[512]{0:T(512)} %param.10) | copy-start | bytes 6148
  5.7 0.7 %copy-start.5 = (f32[4]{0:T(128)S(1)}, f32[4]{0:T(128)}, u32[]{:S(2)}) copy-start(f32[4]{0:T(128)} %param.12) | copy-start | bytes 52
  5.7 0.7 %copy-start.6 = (f32[4]{0:T(128)S(1)}, f32[4]{0:T(128)}, u32[]{:S(2)}) copy-start(f32[4]{0:T(128)} %param.13) | copy-start | bytes 52
  7.9 4.3 %collective-permute-start.1 = (f16[272,256]{1,0:T(8,128)(2,1)S(1)}, f16[272,256]{1,0:T(8,128)(2,1)S(1)}, u32[]{:S(2)}, u32[]{:S(2)}) collective-permute-start(f16[272,256]{1,0:T(8,128)(2,1)S(1)} %convert_element_type.24), channel_id=1, source_target_pairs={{0,4},{4,0},{8,12},{12,8},{16,20},{20,16},{24,28},{28,24},{1,5},{5... | collective-permute-start | bytes 417800 | tf_op jit(solution)/shard_map/ppermute | solution.py:409
  12.4 4.0 %collective-permute-start.2 = (f16[272,256]{1,0:T(8,128)(2,1)S(1)}, f16[272,256]{1,0:T(8,128)(2,1)S(1)}, u32[]{:S(2)}, u32[]{:S(2)}) collective-permute-start(f16[272,256]{1,0:T(8,128)(2,1)S(1)} %convert_element_type.26), channel_id=1, source_target_pairs={{0,8},{4,12},{8,0},{12,4},{16,24},{20,28},{24,16},{28,20},{1,9},{5... | collective-permute-start | bytes 417800 | tf_op jit(solution)/shard_map/ppermute | solution.py:409
  16.6 4.3 %collective-permute-start.3 = (f16[144,256]{1,0:T(8,128)(2,1)S(1)}, f16[144,256]{1,0:T(8,128)(2,1)S(1)}, u32[]{:S(2)}, u32[]{:S(2)}) collective-permute-start(f16[144,256]{1,0:T(8,128)(2,1)S(1)} %convert_element_type.28), channel_id=1, source_target_pairs={{0,16},{4,20},{8,24},{12,28},{16,0},{20,4},{24,8},{28,12},{1,17},{... | collective-permute-start | bytes 221192 | tf_op jit(solution)/shard_map/ppermute | solution.py:409
  23.2 20.0 %all-to-all-start = ((f16[32,24,128]{2,1,0:T(8,128)(2,1)}), f16[32,24,128]{2,1,0:T(8,128)(2,1)S(1)}, u32[]{:S(2)}, u32[]{:S(2)}) async-start(f16[32,24,128]{2,1,0:T(8,128)(2,1)} %broadcast_in_dim.30), calls=%async_computation | async-start | bytes 393216 | tf_op jit(solution)/shard_map/all_to_all | solution.py:414
  34.0 5.0 %collective-permute-start.4 = (f32[8,512]{1,0:T(8,128)S(1)}, f32[8,512]{1,0:T(8,128)S(1)}, u32[]{:S(2)}, u32[]{:S(2)}) collective-permute-start(f32[8,512]{1,0:T(8,128)S(1)} %get-tuple-element.78), channel_id=1, source_target_pairs={{4,0},{8,4},{12,8},{16,12},{20,16},{24,20},{28,24},{5,1},{9,5},{13... | collective-permute-start | bytes 49160 | tf_op jit(solution)/shard_map/ppermute | solution.py:486

commit v3 on v2

--- a/solution.py
+++ b/solution.py
@@ -84,10 +84,6 @@
     return jnp.concatenate([top, moved[8:]], 0)
 
 
-def is_upper(bits_ref, r):
-    return bits_ref[8 * r : 8 * r + 1] > 0.5
-
-
 def quantized_log(size):
     return jnp.log(jnp.maximum(size, 1e-30)).astype(bf16).astype(f32)
 
@@ -97,21 +93,41 @@
     return x * jnp.exp(-log_size), log_size
 
 
-def write_message(msg_ref, state, grad, log_decay, last, upper):
+def write_messages(msg_refs, state, grad, log_total, place, radix):
     row = iota((TAIL_ROWS, INNER), 0)
-    if last:
-        body, log_size = scaled_columns(jnp.where(upper, grad, state))
-        msg_ref[0:N] = body
-        msg_ref[N : N + TAIL_ROWS] = jnp.where(row == 0, log_size, 0.0)
-        return
+    high, middle, low = split3(log_total)
+    tail = jnp.where(row == 4, high, jnp.where(row == 5, middle * 256.0, jnp.where(row == 6, low * 65536.0, 0.0)))
     state, state_size = scaled_columns(state)
     grad, grad_size = scaled_columns(grad)
-    high, middle, low = split3(log_decay)
-    tail = jnp.where(row == 2, state_size, jnp.where(row == 3, grad_size, 0.0))
-    tail = jnp.where(row == 4, high, jnp.where(row == 5, middle * 256.0, jnp.where(row == 6, low * 65536.0, tail)))
-    msg_ref[0:N] = state
-    msg_ref[N : 2 * N] = grad
-    msg_ref[2 * N : 2 * N + TAIL_ROWS] = tail
+    if radix:
+        for s, msg_ref in enumerate(msg_refs, 1):
+            on = place + s < radix
+            msg_ref[0:N] = jnp.where(on, state, grad)
+            msg_ref[N : N + TAIL_ROWS] = jnp.where(row == 0, jnp.where(on, state_size, grad_size), tail)
+    else:
+        (msg_ref,) = msg_refs
+        msg_ref[0:N] = state
+        msg_ref[N : 2 * N] = grad
+        msg_ref[2 * N : 2 * N + TAIL_ROWS] = jnp.where(row == 0, state_size, jnp.where(row == 1, grad_size, tail))
+
+
+def message_log(got_ref):
+    rows = got_ref.shape[0] - TAIL_ROWS
+    tail = got_ref[rows : rows + 8]
+    return tail[4:5] + tail[5:6] * (1 / 256.0) + tail[6:7] * (1 / 65536.0)
+
+
+def message_block(got_ref, which=0):
+    rows = got_ref.shape[0] - TAIL_ROWS
+    return got_ref[which * N : (which + 1) * N] * jnp.exp(got_ref[rows + which : rows + which + 1])
+
+
+def chained(blocks, logs, used):
+    total, log_sum = 0.0, 0.0
+    for block, log, use in zip(blocks, logs, used):
+        total = total + jnp.where(use, jnp.exp(log_sum) * block, 0.0)
+        log_sum = log_sum + jnp.where(use, log, 0.0)
+    return total, log_sum
 
 
 def pack_totals(x):
@@ -120,7 +136,10 @@
     large_size = quantized_log(jnp.max(jnp.abs(large), axis=0, keepdims=True))
     small = x[SMALL_ROW : SMALL_ROW + 1]
     small_size = quantized_log(jnp.abs(small))
-    out = jnp.where(row == SMALL_ROW, small * jnp.exp(-small_size), large * jnp.exp(-large_size))
+    small = small * jnp.exp(-small_size)
+    small_high = small.astype(bf16).astype(f32)
+    out = jnp.where(row == SMALL_ROW, small_high, large * jnp.exp(-large_size))
+    out = jnp.where(row == SMALL_ROW + 3, (small - small_high) * 256.0, out)
     return jnp.where(row == SMALL_ROW + 1, large_size, jnp.where(row == SMALL_ROW + 2, small_size, out))
 
 
@@ -130,13 +149,13 @@
 
 
 def start_kernel(
-    rounds, raw_ref, cot_ref, weight_ref, bias_ref, dt_ref, dt_bias_ref, alog_ref, skip_ref, until_ref,
-    pre_ref, scaled_ref, tail_ref, rows_ref, logs_ref, bits_ref, dt8_ref,
+    stages, raw_ref, cot_ref, weight_ref, bias_ref, dt_ref, dt_bias_ref, alog_ref, skip_ref, until_ref,
+    pre_ref, scaled_ref, tail_ref, rows_ref, logs_ref, places_ref, dt8_ref,
 ):
     tok = raw_ref.shape[0]
     place = lax.axis_index("ctx")
-    for r in range(rounds):
-        bits_ref[8 * r : 8 * r + 8] = jnp.full((8, INNER), (place >> r) & 1, jnp.int32).astype(f32)
+    for t, (size, radix) in enumerate(stages):
+        places_ref[8 * t : 8 * t + 8] = jnp.full((8, INNER), lax.rem(lax.div(place, size), radix), jnp.int32).astype(f32)
     dt8_ref[...] = jnp.zeros_like(dt8_ref)
     dt8_ref[0:H] = dt_ref[...]
     dt_pre = dt8_ref[...] + by_head(dt_bias_ref, tok)
@@ -167,8 +186,8 @@
 
 
 def enter_kernel(
-    last, pre_ref, halo_ref, weight_ref, scaled_ref, tail_ref, logs_ref, bits_ref,
-    xbc_ref, slope_ref, weighted_ref, state_ref, grad_ref, msg_ref,
+    radix, pre_ref, halo_ref, weight_ref, scaled_ref, tail_ref, logs_ref, places_ref,
+    xbc_ref, slope_ref, weighted_ref, state_ref, grad_ref, *msg_refs
 ):
     tok = pre_ref.shape[0]
     halo = halo_ref[HALO_ROWS - 8 :].astype(f32)
@@ -189,37 +208,43 @@
     grad = grad[:, :INNER] + grad[:, INNER:]
     state_ref[...] = state
     grad_ref[...] = grad
-    write_message(msg_ref, state, grad, logs_ref[2:3], last, is_upper(bits_ref, 0))
-
-
-def merge_kernel(r, first, last, state_ref, grad_ref, logs_ref, got_ref, bits_ref, *refs):
-    if first:
-        prior = after = 0.0
-    else:
+    write_messages(msg_refs, state, grad, logs_ref[2:3], places_ref[0:1], radix)
+
+
+def merge_kernel(t, radix, next_radix, state_ref, grad_ref, logs_ref, places_ref, *refs):
+    got, refs = refs[: radix - 1], refs[radix - 1 :]
+    prior = after = 0.0
+    if t > 0:
         prior, after = refs[0][...], refs[1][...]
         refs = refs[2:]
-    logs_out, msg_ref, prior_out, after_out, *refs = refs
-    upper = is_upper(bits_ref, r)
+    logs_out, prior_out, after_out, *refs = refs
+    if not next_radix:
+        state_out, grad_out, *refs = refs
+    place = places_ref[8 * t : 8 * t + 1]
     log_prior, log_after, log_total = logs_ref[0:1], logs_ref[1:2], logs_ref[2:3]
-    tail = got_ref[2 * N : 2 * N + TAIL_ROWS]
-    got_state = got_ref[0:N] * jnp.exp(tail[2:3])
-    got_grad = got_ref[N : 2 * N] * jnp.exp(tail[3:4])
-    got_log = tail[4:5] + tail[5:6] * (1 / 256.0) + tail[6:7] * (1 / 65536.0)
-    mine, theirs = jnp.exp(log_total), jnp.exp(got_log)
-    own_state, own_grad = state_ref[...], grad_ref[...]
-    state = jnp.where(upper, own_state + mine * got_state, got_state + theirs * own_state)
-    grad = jnp.where(upper, got_grad + theirs * own_grad, own_grad + mine * got_grad)
-    prior_out[...] = prior + jnp.where(upper, jnp.exp(log_prior) * got_state, 0.0)
-    after_out[...] = after + jnp.where(upper, 0.0, jnp.exp(log_after) * got_grad)
-    log_prior = jnp.where(upper, log_prior + got_log, log_prior)
-    log_after = jnp.where(upper, log_after, log_after + got_log)
-    log_total = log_total + got_log
+    states = [message_block(ref, 0) for ref in got]
+    grads = [message_block(ref, 1) for ref in got]
+    logs = [message_log(ref) for ref in got]
+    earlier = [s <= place for s in range(1, radix)]
+    later = [s > place for s in range(1, radix)]
+    before, log_before = chained(states, logs, earlier)
+    beyond, log_beyond = chained(grads[::-1], logs[::-1], later[::-1])
+    above, _ = chained(states, logs, later)
+    below, _ = chained(grads[::-1], logs[::-1], earlier[::-1])
+    mine = jnp.exp(log_total)
+    state = above + jnp.exp(log_beyond) * (state_ref[...] + mine * before)
+    grad = below + jnp.exp(log_before) * (grad_ref[...] + mine * beyond)
+    prior_out[...] = prior + jnp.exp(log_prior) * before
+    after_out[...] = after + jnp.exp(log_after) * beyond
+    log_prior = log_prior + log_before
+    log_after = log_after + log_beyond
+    log_total = log_total + log_before + log_beyond
     row = iota((8, INNER), 0)
     logs_out[...] = jnp.where(row == 0, log_prior, jnp.where(row == 1, log_after, jnp.where(row == 2, log_total, 0.0)))
-    if refs:
-        refs[0][...] = state
-        refs[1][...] = grad
-    write_message(msg_ref, state, grad, log_total, last, is_upper(bits_ref, r + 1))
+    if not next_radix:
+        state_out[...] = state
+        grad_out[...] = grad
+    write_messages(refs, state, grad, log_total, places_ref[8 * t + 8 : 8 * t + 9], next_radix)
 
 
 def local_kernel(xbc_ref, cot_ref, rows_ref, logs_ref, local_ref, sums_ref):
@@ -265,19 +290,23 @@
 
 
 def totals_kernel(
-    r, raw_ref, halo_ref, xbc_ref, slope_ref, scaled_ref, weighted_ref, tail_ref, rows_ref, local_ref, sums_ref,
-    logs_ref, got_ref, bits_ref, until_ref, weight_ref, *refs
+    t, radix, raw_ref, halo_ref, xbc_ref, slope_ref, scaled_ref, weighted_ref, tail_ref, rows_ref, local_ref, sums_ref,
+    logs_ref, places_ref, until_ref, weight_ref, *refs
 ):
-    prior, after = 0.0, 0.0
-    if len(refs) > 5:
+    got, refs = refs[: radix - 1], refs[radix - 1 :]
+    prior = after = 0.0
+    if t > 0:
         prior, after = refs[0][...], refs[1][...]
         refs = refs[2:]
     conv_ref, dt_out_ref, totals_ref, spill_ref, totals_scratch = refs
     tok = raw_ref.shape[0]
-    upper = is_upper(bits_ref, r)
-    got = got_ref[0:N] * jnp.exp(got_ref[N : N + 1])
-    prior = prior + jnp.where(upper, jnp.exp(logs_ref[0:1]) * got, 0.0)
-    after = after + jnp.where(upper, 0.0, jnp.exp(logs_ref[1:2]) * got)
+    place = places_ref[8 * t : 8 * t + 1]
+    blocks = [message_block(ref) for ref in got]
+    logs = [message_log(ref) for ref in got]
+    before, _ = chained(blocks, logs, [s <= place for s in range(1, radix)])
+    beyond, _ = chained(blocks[::-1], logs[::-1], [s > place for s in range(radix - 1, 0, -1)])
+    prior = prior + jnp.exp(logs_ref[0:1]) * before
+    after = after + jnp.exp(logs_ref[1:2]) * beyond
 
     step, left, reach = rows_ref[8:16], rows_ref[16:24], rows_ref[24:32]
     dt_gate, decay_rate = rows_ref[32:40], rows_ref[40:48]
@@ -365,7 +394,8 @@
 
 def summed(parts):
     large = jnp.sum(parts * jnp.exp(parts[:, SMALL_ROW + 1 : SMALL_ROW + 2]), axis=0)
-    small = parts[:, SMALL_ROW : SMALL_ROW + 1] * jnp.exp(parts[:, SMALL_ROW + 2 : SMALL_ROW + 3])
+    small = parts[:, SMALL_ROW : SMALL_ROW + 1] + parts[:, SMALL_ROW + 3 : SMALL_ROW + 4] * (1 / 256.0)
+    small = small * jnp.exp(parts[:, SMALL_ROW + 2 : SMALL_ROW + 3])
     return large, jnp.sum(small, axis=0)
 
 
@@ -404,9 +434,23 @@
     return jax.ShapeDtypeStruct(shape, dtype)
 
 
-def exchange(message, distance, slabs):
-    message = message.astype(jnp.float16)
-    return lax.ppermute(message, "ctx", [(i, i ^ distance) for i in range(slabs)]).astype(f32)
+def from_groups(messages, slabs, size, radix):
+    got = []
+    for s in range(1, radix):
+        message = messages[s - 1 if len(messages) > 1 else 0]
+        route = [(p, p - p % (size * radix) + (p + s * size) % (size * radix)) for p in range(slabs)]
+        got.append(lax.ppermute(message.astype(jnp.float16), "ctx", route).astype(f32))
+    return got
+
+
+def stages_of(slabs):
+    stages, size = [], 1
+    while size < slabs:
+        radix = 2 if (slabs // size).bit_length() % 2 == 0 else 4
+        stages.append((size, radix))
+        size *= radix
+    assert size == slabs and stages
+    return stages
 
 
 def everyones(packed, axes, count):
@@ -418,39 +462,43 @@
     tok, channels = xbc_raw.shape[1:]
     slabs = lax.axis_size("ctx")
     contexts = lax.axis_size("dp")
-    rounds = slabs.bit_length() - 1
-    assert slabs == 1 << rounds and rounds > 0
+    stages = stages_of(slabs)
 
     raw, cot, dt_rows = xbc_raw[0], grad_out[0], dt_raw[0].T
     until = call(triangle_kernel, struct((tok, tok), bf16), [], flops=10**10)()
     early_raw, until = lax.optimization_barrier((raw, until))
     halo = lax.ppermute(early_raw[tok - HALO_ROWS :], "ctx", [(i, i + 1) for i in range(slabs - 1)])
 
-    def message(r):
-        return struct((N + TAIL_ROWS if r == rounds - 1 else 2 * N + TAIL_ROWS, INNER))
+    def last_radix(t):
+        return stages[t][1] if t == len(stages) - 1 else 0
+
+    def messages(t):
+        if last_radix(t):
+            return (struct((N + TAIL_ROWS, INNER)),) * (last_radix(t) - 1)
+        return (struct((2 * N + TAIL_ROWS, INNER)),)
 
     state_like = struct((N, INNER))
     logs_like = struct((8, INNER))
-    pre, scaled, tail, rows, logs, bits = call(
-        functools.partial(start_kernel, rounds),
+    pre, scaled, tail, rows, logs, places = call(
+        functools.partial(start_kernel, stages),
         (
             struct((tok, channels)), struct((tok, 2 * INNER), bf16), struct((tok, INNER)), struct((6 * HEAD_ROWS, tok)),
-            logs_like, struct((8 * rounds, INNER)),
+            logs_like, struct((8 * len(stages), INNER)),
         ),
         [VMEM] * 9,
         scratch=[pltpu.VMEM((HEAD_ROWS, tok), f32)],
         flops=100_000_000,
     )(raw, cot, conv_weight, conv_bias[None], dt_rows, dt_bias[None], a_log[None], d_skip[None], until)
 
-    xbc, slope, weighted, state, grad, msg = call(
-        functools.partial(enter_kernel, rounds == 1),
+    xbc, slope, weighted, state, grad, *outgoing = call(
+        functools.partial(enter_kernel, last_radix(0)),
         (
             struct((tok, channels), bf16), struct((tok, channels)), struct((tok, 2 * INNER), bf16),
-            state_like, state_like, message(0),
+            state_like, state_like, *messages(0),
         ),
         [VMEM] * 7,
         flops=200_000_000,
-    )(pre, halo, conv_weight, scaled, tail, logs, bits)
+    )(pre, halo, conv_weight, scaled, tail, logs, places)
 
     local, sums = call(
         local_kernel,
@@ -460,28 +508,31 @@
     )(xbc, cot, rows, logs)
 
     carried = ()
-    for r in range(rounds - 1):
-        got = exchange(msg, 1 << r, slabs)
-        if r == 0:
+    for t, (size, radix) in enumerate(stages):
+        got = from_groups(outgoing, slabs, size, radix)
+        if t == 0:
             got, local, sums = lax.optimization_barrier((got, local, sums))
-        last = r + 1 == rounds - 1
-        logs, msg, *carried = call(
-            functools.partial(merge_kernel, r, r == 0, last),
-            (logs_like, message(r + 1)) + (state_like,) * (2 if last else 4),
-            [VMEM] * (5 + len(carried)),
+        if t == len(stages) - 1:
+            break
+        last = last_radix(t + 1)
+        outs = (logs_like, state_like, state_like) + (() if last else (state_like, state_like))
+        logs, *outgoing = call(
+            functools.partial(merge_kernel, t, radix, last),
+            outs + messages(t + 1),
+            [VMEM] * (4 + len(got) + len(carried)),
             flops=1_000_000,
-        )(state, grad, logs, got, bits, *carried)
+        )(state, grad, logs, places, *got, *carried)
+        carried, outgoing = outgoing[:2], outgoing[2:]
         if not last:
-            *carried, state, grad = carried
-    got = exchange(msg, 1 << (rounds - 1), slabs)
+            (state, grad), outgoing = outgoing[:2], outgoing[2:]
 
     grad_conv, grad_dt, packed, spill = call(
-        functools.partial(totals_kernel, rounds - 1),
+        functools.partial(totals_kernel, len(stages) - 1, radix),
         (struct((tok, channels)), struct((H, tok)), struct((TOTAL_ROWS, 128)), struct((8, channels))),
-        [VMEM] * (15 + len(carried)),
+        [VMEM] * (14 + len(got) + len(carried)),
         scratch=[pltpu.VMEM((TOTAL_ROWS, 128), f32)],
         flops=200_000_000,
-    )(raw, halo, xbc, slope, scaled, weighted, tail, rows, local, sums, logs, got, bits, until, conv_weight, *carried)
+    )(raw, halo, xbc, slope, scaled, weighted, tail, rows, local, sums, logs, places, until, conv_weight, *got, *carried)
 
     spilled = lax.ppermute(spill, "ctx", [(i + 1, i) for i in range(slabs - 1)])
     if slabs * contexts <= 64:

time: 44.3 us -> 40.4 us (0.912)
  starting transfers between devices: 21.6 us -> 16.9 us
  waiting for transfers between devices: 11.9 us -> 12.9 us
    all_to_all x1, starting transfers between devices: 10.8 us -> 6.1 us  [everyones(): return lax.all_to_all(packed, axes, 0, 0).astype(f32)]
    ppermute x3 -> x4, waiting for transfers between devices: 5.54 us -> 6.4 us  [from_groups(): lax.ppermute(message.astype(jnp.float16), 'ctx', route).astype(f32)]
    pallas_call x5 -> x4, Pallas kernels: 3.4 us -> 3.31 us  [the longest x1 1.67 us: on_device(): call(functools.partial(totals_kernel, len(stages) - 1, radix), (struct((t...]
    ppermute x3 -> x4, starting transfers between devices: 5.46 us -> 5.43 us  [from_groups(): lax.ppermute(message.astype(jnp.float16), 'ctx', route).astype(f32)]
  transfers between devices with their start and end apart: 6 -> 7, of which waited for: 5 -> 6; matrix products, arithmetic and copies ran while one was open for 0% -> 0% of each run, Pallas kernels for 9% -> 10%
where the time goes in v3:
time: 40.4 us; the launch traced here: 40.1 us
  starting transfers between devices  16.9 us (42%)
  waiting for transfers between devices  12.9 us (32%)
  Pallas kernels  7.18 us (18%)
  local copies, waits for them, and re-layouts  2.23 us (6%)
  between operations  0.85 us (2%)
    ppermute x4, waiting for transfers between devices, from_groups(): lax.ppermute(message.astype(jnp.float16), 'ctx', route).astype(f32)  6.4 us
    all_to_all x1, starting transfers between devices, everyones(): return lax.all_to_all(packed, axes, 0, 0).astype(f32)  6.1 us
    ppermute x4, starting transfers between devices, from_groups(): lax.ppermute(message.astype(jnp.float16), 'ctx', route).astype(f32)  5.43 us
    ppermute x1, starting transfers between devices, on_device(): lax.ppermute(early_raw[tok - HALO_ROWS:], 'ctx', [(i, i + 1) for i in ran...  4.06 us
    all_to_all x1, waiting for transfers between devices, everyones(): return lax.all_to_all(packed, axes, 0, 0).astype(f32)  3.73 us
    ppermute x1, waiting for transfers between devices, on_device(): spilled = lax.ppermute(spill, 'ctx', [(i + 1, i) for i in range(slabs - 1)])  2.72 us
    pallas_call x1, Pallas kernels, on_device(): call(functools.partial(totals_kernel, len(stages) - 1, radix), (struct((t...  1.67 us
    pallas_call x1, Pallas kernels, on_device(): call(local_kernel, (struct((tok, channels)), struct((3 * HEAD_ROWS, tok))...  1.59 us
  transfers between devices with their start and end apart: 7, of which 6 were waited for; matrix products, arithmetic and copies ran while one was open for 0% of the time, Pallas kernels for 10%

profile of v3, /device:TPU:1, one launch (start us, length us, event | category | flops | bytes accessed | tf_op | source)
XLA Modules:
  0.0 40.1 jit_solution(3423997641533499782)
XLA Ops:
  0.6 0.0 copy-start
  0.6 0.0 copy-start.2
  0.7 0.0 copy-start.3
  0.7 0.0 copy-start.7
  0.7 0.9 %copy-done = bf16[1,256,512]{2,1,0:T(8,128)(2,1)S(1)} copy-done((bf16[1,256,512]{2,1,0:T(8,128)(2,1)S(1)}, bf16[1,256,512]{2,1,0:T(8,128)(2,1)}, u32[]{:S(2)}) %copy-start) | copy-done | bytes 262168
  1.6 4.1 %collective-permute-start = (bf16[16,512]{1,0:T(8,128)(2,1)S(1)}, bf16[16,512]{1,0:T(8,128)(2,1)S(1)}, u32[]{:S(2)}, u32[]{:S(2)}) collective-permute-start(bf16[16,512]{1,0:T(8,128)(2,1)S(1)} %slice.3), channel_id=1, source_target_pairs={{0,4},{4,8},{8,12},{12,16},{16,20},{20,24},{24,28},{1,5},{5,9},{9,... | collective-permute-start | bytes 49160 | tf_op jit(solution)/shard_map/ppermute | solution.py:470
  5.7 0.0 copy-start.4
  5.7 0.0 copy-start.5
  5.7 0.0 copy-start.6
  5.7 0.6 %copy-done.4 = f32[512]{0:T(512)S(1)} copy-done((f32[512]{0:T(512)S(1)}, f32[512]{0:T(512)}, u32[]{:S(2)}) %copy-start.4) | copy-done | bytes 2072
  6.4 1.0 %shard_map.136 = (f32[256,512]{1,0:T(8,128)S(1)}, bf16[256,512]{1,0:T(8,128)(2,1)S(1)}, f32[256,256]{1,0:T(8,128)S(1)}, f32[48,256]{1,0:T(8,128)S(1)}, f32[8,256]{1,0:T(8,128)S(1)}, /*index=5*/f32[16,256]{1,0:T(8,128)S(1)}) custom-call(bf16[256,512]{1,0:T(8,128)(2,1)S(1)} %bitcast.18, bf16[256,256]{1,0:T(8,128)(2,1)S(1)} %bitcast.20, ...), custom_call_target="tpu_custom_call" | custom-call | flops 100000000 | bytes 1048576 | tf_op jit(solution)/shard_map/pallas_call | solution.py:482
  7.4 0.0 collective-permute-done.halo_ref
  7.4 0.5 %shard_map.137 = (bf16[256,512]{1,0:T(8,128)(2,1)S(1)}, f32[256,512]{1,0:T(8,128)S(1)}, bf16[256,512]{1,0:T(8,128)(2,1)S(1)}, f32[128,256]{1,0:T(8,128)S(1)}, f3...) custom-call(f32[256,512]{1,0:T(8,128)S(1)} %get-tuple-element.45.pre_ref, ...), custom_call_target="tpu_custom_call" | custom-call | flops 200000000 | bytes 1048576 | tf_op jit(solution)/shard_map/pallas_call | solution.py:493
  7.9 1.3 %collective-permute-start.1 = (f16[272,256]{1,0:T(8,128)(2,1)S(1)}, f16[272,256]{1,0:T(8,128)(2,1)S(1)}, u32[]{:S(2)}, u32[]{:S(2)}) collective-permute-start(f16[272,256]{1,0:T(8,128)(2,1)S(1)} %convert_element_type.30), channel_id=1, source_target_pairs={{0,4},{4,0},{8,12},{12,8},{16,20},{20,16},{24,28},{28,24},{1,5},{5... | collective-permute-start | bytes 417800 | tf_op jit(solution)/shard_map/ppermute | solution.py:442
  9.2 1.6 %shard_map.138 = (f32[256,512]{1,0:T(8,128)S(1)}, f32[24,256]{1,0:T(8,128)S(1)}) custom-call(bf16[256,512]{1,0:T(8,128)(2,1)S(1)} %get-tuple-element.50.xbc_ref, bf16[256,256]{1,0:T(8,128)(2,1)S(1)} %bitcast.21, f32[48,256]{1,0:T(8,128)S(1)} %get-tuple-element.53.rows_ref, f32[8,256]{1,0:T(8,128)S(1)} %get-tuple-element.48.logs_ref), custom_call_target="tpu_custom_call" | custom-call | flops 1000000000 | bytes 1048576 | tf_op jit(solution)/shard_map/pallas_call | solution.py:503
  10.8 1.4 %collective-permute-done.1 = f16[272,256]{1,0:T(8,128)(2,1)S(1)} collective-permute-done((f16[272,256]{1,0:T(8,128)(2,1)S(1)}, f16[272,256]{1,0:T(8,128)(2,1)S(1)}, u32[]{:S(2)}, u32[]{:S(2)}) %collective-permute-start.1) | collective-permute-done | bytes 139296 | tf_op jit(solution)/shard_map/ppermute | solution.py:442
  12.2 0.2 shard_map.139
  12.4 3.6 %collective-permute-start.4 = (f16[144,256]{1,0:T(8,128)(2,1)S(1)}, f16[144,256]{1,0:T(8,128)(2,1)S(1)}, u32[]{:S(2)}, u32[]{:S(2)}) collective-permute-start(f16[144,256]{1,0:T(8,128)(2,1)S(1)} %convert_element_type.36), channel_id=1, source_target_pairs={{0,24},{4,28},{8,0},{12,4},{16,8},{20,12},{24,16},{28,20},{1,25},{... | collective-permute-start | bytes 221192 | tf_op jit(solution)/shard_map/ppermute | solution.py:442
  16.0 0.0 collective-permute-start.3
  16.0 0.5 %collective-permute-start.2 = (f16[144,256]{1,0:T(8,128)(2,1)S(1)}, f16[144,256]{1,0:T(8,128)(2,1)S(1)}, u32[]{:S(2)}, u32[]{:S(2)}) collective-permute-start(f16[144,256]{1,0:T(8,128)(2,1)S(1)} %convert_element_type.32), channel_id=1, source_target_pairs={{0,8},{4,12},{8,16},{12,20},{16,24},{20,28},{24,0},{28,4},{1,9},{5... | collective-permute-start | bytes 221192 | tf_op jit(solution)/shard_map/ppermute | solution.py:442
  16.5 0.9 %collective-permute-done.4 = f16[144,256]{1,0:T(8,128)(2,1)S(1)} collective-permute-done((f16[144,256]{1,0:T(8,128)(2,1)S(1)}, f16[144,256]{1,0:T(8,128)(2,1)S(1)}, u32[]{:S(2)}, u32[]{:S(2)}) %collective-permute-start.4) | collective-permute-done | bytes 73760 | tf_op jit(solution)/shard_map/ppermute | solution.py:442
  17.4 3.9 %collective-permute-done.3 = f16[144,256]{1,0:T(8,128)(2,1)S(1)} collective-permute-done((f16[144,256]{1,0:T(8,128)(2,1)S(1)}, f16[144,256]{1,0:T(8,128)(2,1)S(1)}, u32[]{:S(2)}, u32[]{:S(2)}) %collective-permute-start.3) | collective-permute-done | bytes 73760 | tf_op jit(solution)/shard_map/ppermute | solution.py:442
  21.3 0.3 collective-permute-done.2
  21.6 1.7 %shard_map.140 = (f32[256,512]{1,0:T(8,128)S(1)}, f32[4,256]{1,0:T(4,128)}, f32[24,128]{1,0:T(8,128)S(1)}, f32[8,512]{1,0:T(8,128)S(1)}) custom-call(bf16[256,512]{1,0:T(8,128)(2,1)S(1)} %bitcast.19, bf16[16,512]{1,0:T(8,128)(2,1)S(1)} %collective-permute-done.halo_ref, bf16[256,512]{1,0:T(8,128)(2,1)S(1)} %get-tuple-element.50.xbc_ref, ...), custom_call_target="tpu_custom_call" | custom-call | flops 200000000 | bytes 1048576 | tf_op jit(solution)/shard_map/pallas_call | solution.py:529
  23.3 0.7 %broadcast_in_dim.30 = f16[32,24,128]{2,1,0:T(8,128)(2,1)} broadcast(f16[24,128]{1,0:T(8,128)(2,1)S(1)} %convert_element_type.38), dimensions={1,2} | broadcast | bytes 202752 | tf_op jit(solution)/shard_map/broadcast_in_dim | solution.py:457
  24.0 6.1 %all-to-all-start = ((f16[32,24,128]{2,1,0:T(8,128)(2,1)}), f16[32,24,128]{2,1,0:T(8,128)(2,1)S(1)}, u32[]{:S(2)}, u32[]{:S(2)}) async-start(f16[32,24,128]{2,1,0:T(8,128)(2,1)} %broadcast_in_dim.30), calls=%async_computation | async-start | bytes 393216 | tf_op jit(solution)/shard_map/all_to_all | solution.py:458
  30.1 1.3 %collective-permute-start.5 = (f32[8,512]{1,0:T(8,128)S(1)}, f32[8,512]{1,0:T(8,128)S(1)}, u32[]{:S(2)}, u32[]{:S(2)}) collective-permute-start(f32[8,512]{1,0:T(8,128)S(1)} %get-tuple-element.70), channel_id=1, source_target_pairs={{4,0},{8,4},{12,8},{16,12},{20,16},{24,20},{28,24},{5,1},{9,5},{13... | collective-permute-start | bytes 49160 | tf_op jit(solution)/shard_map/ppermute | solution.py:537
  31.4 0.9 %shard_map.141 = (bf16[256,512]{1,0:T(8,128)(2,1)}, f32[16,512]{1,0:T(8,128)S(1)}) custom-call(f32[256,512]{1,0:T(8,128)S(1)} %get-tuple-element.68.conv_ref, f32[4,512]{1,0:T(4,128)S(1)} %copy-done.1), custom_call_target="tpu_custom_call" | custom-call | flops 1000000 | bytes 1048576 | tf_op jit(solution)/shard_map/pallas_call | solution.py:544
  32.3 2.7 %collective-permute-done.5.spilled_ref = f32[8,512]{1,0:T(8,128)S(1)} collective-permute-done((f32[8,512]{1,0:T(8,128)S(1)}, f32[8,512]{1,0:T(8,128)S(1)}, u32[]{:S(2)}, u32[]{:S(2)}) %collective-permute-start.5) | collective-permute-done | bytes 16416 | tf_op jit(solution)/shard_map/ppermute | solution.py:537
  35.1 0.6 %shard_map.142 = bf16[256,512]{1,0:T(8,128)(2,1)} custom-call(f32[16,512]{1,0:T(8,128)S(1)} %get-tuple-element.69.end_ref, f32[8,512]{1,0:T(8,128)S(1)} %collective-permute-done.5.spilled_ref, bf16[256,512]{1,0:T(8,128)(2,1)} %get-tuple-element.71.main_hbm), custom_call_target="tpu_custom_call", output_to_operand_aliasing={{}: (2, {})} | custom-call | bytes 1048576 | tf_op jit(solution)/shard_map/pallas_call | solution.py:552
  35.7 3.7 %all-to-all-done = f16[32,24,128]{2,1,0:T(8,128)(2,1)S(1)} async-done(((f16[32,24,128]{2,1,0:T(8,128)(2,1)}), f16[32,24,128]{2,1,0:T(8,128)(2,1)S(1)}, u32[]{:S(2)}, u32[]{:S(2)}) %all-to-all-start) | async-done | bytes 196640 | tf_op jit(solution)/shard_map/all_to_all | solution.py:458
  39.4 0.7 %shard_map.143 = (f32[4,512]{1,0:T(4,128)}, f32[1,512]{1,0:T(1,128)}, f32[1,4]{1,0:T(1,128)}, f32[1,4]{1,0:T(1,128)}, f32[1,4]{1,0:T(1,128)}) custom-call(f32[32,24,128]{2,1,0:T(8,128)S(1)} %convert_element_type.39.parts_ref), custom_call_target="tpu_custom_call" | custom-call | bytes 1048576 | tf_op jit(solution)/shard_map/pallas_call | solution.py:561
  (19 shorter events, 0.2 us)
Async XLA Ops:
  0.6 1.0 %copy-start = (bf16[1,256,512]{2,1,0:T(8,128)(2,1)S(1)}, bf16[1,256,512]{2,1,0:T(8,128)(2,1)}, u32[]{:S(2)}) copy-start(bf16[1,256,512]{2,1,0:T(8,128)(2,1)} %param.8) | copy-start | bytes 786436
  0.6 5.1 %copy-start.2 = (bf16[1,256,256]{2,1,0:T(8,128)(2,1)S(1)}, bf16[1,256,256]{2,1,0:T(8,128)(2,1)}, u32[]{:S(2)}) copy-start(bf16[1,256,256]{2,1,0:T(8,128)(2,1)} %param.15) | copy-start | bytes 393220
  0.7 5.1 %copy-start.3 = (f32[1,256,4]{1,2,0:T(4,128)S(1)}, f32[1,256,4]{1,2,0:T(4,128)}, u32[]{:S(2)}) copy-start(f32[1,256,4]{1,2,0:T(4,128)} %param.11) | copy-start | bytes 12292
  0.7 5.1 %copy-start.7 = (f32[4]{0:T(128)S(1)}, f32[4]{0:T(128)}, u32[]{:S(2)}) copy-start(f32[4]{0:T(128)} %param.14) | copy-start | bytes 52
  1.6 4.1 %copy-start.1 = (f32[4,512]{1,0:T(4,128)S(1)}, f32[4,512]{1,0:T(4,128)}, u32[]{:S(2)}) copy-start(f32[4,512]{1,0:T(4,128)} %weight_ref.7) | copy-start | bytes 24580
  1.6 5.8 %collective-permute-start = (bf16[16,512]{1,0:T(8,128)(2,1)S(1)}, bf16[16,512]{1,0:T(8,128)(2,1)S(1)}, u32[]{:S(2)}, u32[]{:S(2)}) collective-permute-start(bf16[16,512]{1,0:T(8,128)(2,1)S(1)} %slice.3), channel_id=1, source_target_pairs={{0,4},{4,8},{8,12},{12,16},{16,20},{20,24},{24,28},{1,5},{5,9},{9,... | collective-permute-start | bytes 49160 | tf_op jit(solution)/shard_map/ppermute | solution.py:470
  5.7 0.7 %copy-start.4 = (f32[512]{0:T(512)S(1)}, f32[512]{0:T(512)}, u32[]{:S(2)}) copy-start(f32[512]{0:T(512)} %param.10) | copy-start | bytes 6148
  5.7 0.7 %copy-start.5 = (f32[4]{0:T(128)S(1)}, f32[4]{0:T(128)}, u32[]{:S(2)}) copy-start(f32[4]{0:T(128)} %param.12) | copy-start | bytes 52
  5.7 0.7 %copy-start.6 = (f32[4]{0:T(128)S(1)}, f32[4]{0:T(128)}, u32[]{:S(2)}) copy-start(f32[4]{0:T(128)} %param.13) | copy-start | bytes 52
  7.9 4.3 %collective-permute-start.1 = (f16[272,256]{1,0:T(8,128)(2,1)S(1)}, f16[272,256]{1,0:T(8,128)(2,1)S(1)}, u32[]{:S(2)}, u32[]{:S(2)}) collective-permute-start(f16[272,256]{1,0:T(8,128)(2,1)S(1)} %convert_element_type.30), channel_id=1, source_target_pairs={{0,4},{4,0},{8,12},{12,8},{16,20},{20,16},{24,28},{28,24},{1,5},{5... | collective-permute-start | bytes 417800 | tf_op jit(solution)/shard_map/ppermute | solution.py:442
  12.4 5.0 %collective-permute-start.4 = (f16[144,256]{1,0:T(8,128)(2,1)S(1)}, f16[144,256]{1,0:T(8,128)(2,1)S(1)}, u32[]{:S(2)}, u32[]{:S(2)}) collective-permute-start(f16[144,256]{1,0:T(8,128)(2,1)S(1)} %convert_element_type.36), channel_id=1, source_target_pairs={{0,24},{4,28},{8,0},{12,4},{16,8},{20,12},{24,16},{28,20},{1,25},{... | collective-permute-start | bytes 221192 | tf_op jit(solution)/shard_map/ppermute | solution.py:442
  16.0 5.3 %collective-permute-start.3 = (f16[144,256]{1,0:T(8,128)(2,1)S(1)}, f16[144,256]{1,0:T(8,128)(2,1)S(1)}, u32[]{:S(2)}, u32[]{:S(2)}) collective-permute-start(f16[144,256]{1,0:T(8,128)(2,1)S(1)} %convert_element_type.34), channel_id=1, source_target_pairs={{0,16},{4,20},{8,24},{12,28},{16,0},{20,4},{24,8},{28,12},{1,17},{... | collective-permute-start | bytes 221192 | tf_op jit(solution)/shard_map/ppermute | solution.py:442
  16.0 5.6 %collective-permute-start.2 = (f16[144,256]{1,0:T(8,128)(2,1)S(1)}, f16[144,256]{1,0:T(8,128)(2,1)S(1)}, u32[]{:S(2)}, u32[]{:S(2)}) collective-permute-start(f16[144,256]{1,0:T(8,128)(2,1)S(1)} %convert_element_type.32), channel_id=1, source_target_pairs={{0,8},{4,12},{8,16},{12,20},{16,24},{20,28},{24,0},{28,4},{1,9},{5... | collective-permute-start | bytes 221192 | tf_op jit(solution)/shard_map/ppermute | solution.py:442
  24.0 15.4 %all-to-all-start = ((f16[32,24,128]{2,1,0:T(8,128)(2,1)}), f16[32,24,128]{2,1,0:T(8,128)(2,1)S(1)}, u32[]{:S(2)}, u32[]{:S(2)}) async-start(f16[32,24,128]{2,1,0:T(8,128)(2,1)} %broadcast_in_dim.30), calls=%async_computation | async-start | bytes 393216 | tf_op jit(solution)/shard_map/all_to_all | solution.py:458
  30.1 5.0 %collective-permute-start.5 = (f32[8,512]{1,0:T(8,128)S(1)}, f32[8,512]{1,0:T(8,128)S(1)}, u32[]{:S(2)}, u32[]{:S(2)}) collective-permute-start(f32[8,512]{1,0:T(8,128)S(1)} %get-tuple-element.70), channel_id=1, source_target_pairs={{4,0},{8,4},{12,8},{16,12},{20,16},{24,20},{28,24},{5,1},{9,5},{13... | collective-permute-start | bytes 49160 | tf_op jit(solution)/shard_map/ppermute | solution.py:537

commit v4 on v3

--- a/solution.py
+++ b/solution.py
@@ -156,6 +156,10 @@
     place = lax.axis_index("ctx")
     for t, (size, radix) in enumerate(stages):
         places_ref[8 * t : 8 * t + 8] = jnp.full((8, INNER), lax.rem(lax.div(place, size), radix), jnp.int32).astype(f32)
+    at = 8 * len(stages)
+    slabs = stages[-1][0] * stages[-1][1]
+    places_ref[at : at + 8] = jnp.full((8, INNER), jnp.where(place == 0, 1, 0), jnp.int32).astype(f32)
+    places_ref[at + 8 : at + 16] = jnp.full((8, INNER), jnp.where(place == slabs - 1, 1, 0), jnp.int32).astype(f32)
     dt8_ref[...] = jnp.zeros_like(dt8_ref)
     dt8_ref[0:H] = dt_ref[...]
     dt_pre = dt8_ref[...] + by_head(dt_bias_ref, tok)
@@ -185,12 +189,17 @@
     pre_ref[...] = pre
 
 
+def real_halo(halo_ref, places_ref):
+    first = places_ref[places_ref.shape[0] - 16 :][:1, :1]
+    return jnp.where(first > 0.5, 0.0, halo_ref[HALO_ROWS - 8 :].astype(f32))
+
+
 def enter_kernel(
     radix, pre_ref, halo_ref, weight_ref, scaled_ref, tail_ref, logs_ref, places_ref,
     xbc_ref, slope_ref, weighted_ref, state_ref, grad_ref, *msg_refs
 ):
     tok = pre_ref.shape[0]
-    halo = halo_ref[HALO_ROWS - 8 :].astype(f32)
+    halo = real_halo(halo_ref, places_ref)
     top = pre_ref[0:8]
     for back in range(1, K):
         tap = weight_ref[K - 1 - back : K - back]
@@ -331,7 +340,7 @@
     spill_ref[...] = spill
 
     raw = raw_ref[...].astype(f32)
-    halo = halo_ref[HALO_ROWS - 8 :].astype(f32)
+    halo = real_halo(halo_ref, places_ref)
     sums = [grad_conv * shifted_down(raw, halo, K - 1 - k) for k in range(K - 1)] + [grad_conv * raw, grad_conv]
     totals_scratch[...] = jnp.zeros_like(totals_scratch)
     for k, each in enumerate(sums):
@@ -382,9 +391,10 @@
     copy.wait()
 
 
-def end_kernel(end_ref, spilled_ref, main_hbm, out_hbm, rows_ref, sem):
+def end_kernel(end_ref, spilled_ref, places_ref, main_hbm, out_hbm, rows_ref, sem):
     end = end_ref[...]
-    fixed = end[END_ROWS - 8 :] + spilled_ref[...]
+    last = places_ref[places_ref.shape[0] - 8 :][:1, :1]
+    fixed = end[END_ROWS - 8 :] + jnp.where(last > 0.5, 0.0, spilled_ref[...])
     rows_ref[...] = jnp.concatenate([end[: END_ROWS - 8], fixed], 0).astype(bf16)
     tok = out_hbm.shape[0]
     copy = pltpu.make_async_copy(rows_ref, out_hbm.at[pl.ds(tok - END_ROWS, END_ROWS)], sem)
@@ -467,7 +477,7 @@
     raw, cot, dt_rows = xbc_raw[0], grad_out[0], dt_raw[0].T
     until = call(triangle_kernel, struct((tok, tok), bf16), [], flops=10**10)()
     early_raw, until = lax.optimization_barrier((raw, until))
-    halo = lax.ppermute(early_raw[tok - HALO_ROWS :], "ctx", [(i, i + 1) for i in range(slabs - 1)])
+    halo = lax.ppermute(early_raw[tok - HALO_ROWS :], "ctx", [(i, (i + 1) % slabs) for i in range(slabs)])
 
     def last_radix(t):
         return stages[t][1] if t == len(stages) - 1 else 0
@@ -483,7 +493,7 @@
         functools.partial(start_kernel, stages),
         (
             struct((tok, channels)), struct((tok, 2 * INNER), bf16), struct((tok, INNER)), struct((6 * HEAD_ROWS, tok)),
-            logs_like, struct((8 * len(stages), INNER)),
+            logs_like, struct((8 * len(stages) + 16, INNER)),
         ),
         [VMEM] * 9,
         scratch=[pltpu.VMEM((HEAD_ROWS, tok), f32)],
@@ -534,7 +544,7 @@
         flops=200_000_000,
     )(raw, halo, xbc, slope, scaled, weighted, tail, rows, local, sums, logs, places, until, conv_weight, *got, *carried)
 
-    spilled = lax.ppermute(spill, "ctx", [(i + 1, i) for i in range(slabs - 1)])
+    spilled = lax.ppermute(spill, "ctx", [((i + 1) % slabs, i) for i in range(slabs)])
     if slabs * contexts <= 64:
         parts = everyones(packed, ("ctx", "dp"), slabs * contexts)
     else:
@@ -552,11 +562,11 @@
     grad_input = call(
         end_kernel,
         struct((tok, channels), bf16),
-        [VMEM] * 2 + [HBM],
+        [VMEM] * 3 + [HBM],
         HBM,
         [pltpu.VMEM((END_ROWS, channels), bf16), pltpu.SemaphoreType.DMA],
-        aliases={2: 0},
-    )(end, spilled, grad_main)
+        aliases={3: 0},
+    )(end, spilled, places, grad_main)
 
     grad_weight, grad_bias, *small = call(
         finish_kernel,

time: 40.4 us -> 38.5 us (0.953)
  starting transfers between devices: 16.9 us -> 13.9 us
  waiting for transfers between devices: 12.9 us -> 13.8 us
    ppermute x4, starting transfers between devices: 5.43 us -> 2.06 us  [from_groups(): lax.ppermute(message.astype(jnp.float16), 'ctx', route).astype(f32)]
    ppermute x4, waiting for transfers between devices: 6.4 us -> 7.96 us  [from_groups(): lax.ppermute(message.astype(jnp.float16), 'ctx', route).astype(f32)]
    ppermute x2, starting transfers between devices: 5.36 us -> 6.39 us  [the longest x1 4.34 us: on_device(): lax.ppermute(spill, 'ctx', [((i + 1) % slabs, i) for i in range(slabs)])]
    all_to_all x1, starting transfers between devices: 6.1 us -> 5.5 us  [everyones(): return lax.all_to_all(packed, axes, 0, 0).astype(f32)]
  transfers between devices with their start and end apart: 7 -> 7, of which waited for: 6 -> 5; matrix products, arithmetic and copies ran while one was open for 0% -> 0% of each run, Pallas kernels for 10% -> 11%
where the time goes in v4:
time: 38.5 us; the launch traced here: 38.3 us
  starting transfers between devices  13.9 us (36%)
  waiting for transfers between devices  13.8 us (36%)
  Pallas kernels  7.27 us (19%)
  local copies, waits for them, and re-layouts  2.25 us (6%)
  between operations  0.83 us (2%)
    ppermute x4, waiting for transfers between devices, from_groups(): lax.ppermute(message.astype(jnp.float16), 'ctx', route).astype(f32)  7.96 us
    all_to_all x1, starting transfers between devices, everyones(): return lax.all_to_all(packed, axes, 0, 0).astype(f32)  5.5 us
    ppermute x1, starting transfers between devices, on_device(): lax.ppermute(spill, 'ctx', [((i + 1) % slabs, i) for i in range(slabs)])  4.34 us
    all_to_all x1, waiting for transfers between devices, everyones(): return lax.all_to_all(packed, axes, 0, 0).astype(f32)  3.39 us
    ppermute x1, waiting for transfers between devices, on_device(): lax.ppermute(early_raw[tok - HALO_ROWS:], 'ctx', [(i, (i + 1) % slabs) fo...  2.45 us
    ppermute x4, starting transfers between devices, from_groups(): lax.ppermute(message.astype(jnp.float16), 'ctx', route).astype(f32)  2.06 us
    ppermute x1, starting transfers between devices, on_device(): lax.ppermute(early_raw[tok - HALO_ROWS:], 'ctx', [(i, (i + 1) % slabs) fo...  2.04 us
    pallas_call x1, Pallas kernels, on_device(): call(functools.partial(totals_kernel, len(stages) - 1, radix), (struct((t...  1.69 us
  transfers between devices with their start and end apart: 7, of which 5 were waited for; matrix products, arithmetic and copies ran while one was open for 0% of the time, Pallas kernels for 11%

profile of v4, /device:TPU:1, one launch (start us, length us, event | category | flops | bytes accessed | tf_op | source)
XLA Modules:
  0.0 38.3 jit_solution(5577932625968313004)
XLA Ops:
  0.6 0.0 copy-start
  0.6 0.0 copy-start.2
  0.7 0.0 copy-start.3
  0.7 0.0 copy-start.7
  0.7 0.9 %copy-done = bf16[1,256,512]{2,1,0:T(8,128)(2,1)S(1)} copy-done((bf16[1,256,512]{2,1,0:T(8,128)(2,1)S(1)}, bf16[1,256,512]{2,1,0:T(8,128)(2,1)}, u32[]{:S(2)}) %copy-start) | copy-done | bytes 262168
  1.6 2.0 %collective-permute-start = (bf16[16,512]{1,0:T(8,128)(2,1)S(1)}, bf16[16,512]{1,0:T(8,128)(2,1)S(1)}, u32[]{:S(2)}, u32[]{:S(2)}) collective-permute-start(bf16[16,512]{1,0:T(8,128)(2,1)S(1)} %slice.3), channel_id=1, source_target_pairs={{0,4},{4,8},{8,12},{12,16},{16,20},{20,24},{24,28},{28,0},{1,5},{5... | collective-permute-start | bytes 49160 | tf_op jit(solution)/shard_map/ppermute | solution.py:480
  3.6 0.0 copy-done.2
  3.6 0.0 copy-done.3
  3.7 0.0 copy-done.7
  3.7 0.6 %copy-done.4 = f32[512]{0:T(512)S(1)} copy-done((f32[512]{0:T(512)S(1)}, f32[512]{0:T(512)}, u32[]{:S(2)}) %copy-start.4) | copy-done | bytes 2072
  4.3 1.0 %shard_map.136 = (f32[256,512]{1,0:T(8,128)S(1)}, bf16[256,512]{1,0:T(8,128)(2,1)S(1)}, f32[256,256]{1,0:T(8,128)S(1)}, f32[48,256]{1,0:T(8,128)S(1)}, f32[8,256]{1,0:T(8,128)S(1)}, /*index=5*/f32[32,256]{1,0:T(8,128)S(1)}) custom-call(bf16[256,512]{1,0:T(8,128)(2,1)S(1)} %bitcast.18, bf16[256,256]{1,0:T(8,128)(2,1)S(1)} %bitcast.20, ...), custom_call_target="tpu_custom_call" | custom-call | flops 100000000 | bytes 1048576 | tf_op jit(solution)/shard_map/pallas_call | solution.py:492
  5.3 2.4 %collective-permute-done.halo_ref = bf16[16,512]{1,0:T(8,128)(2,1)S(1)} collective-permute-done((bf16[16,512]{1,0:T(8,128)(2,1)S(1)}, bf16[16,512]{1,0:T(8,128)(2,1)S(1)}, u32[]{:S(2)}, u32[]{:S(2)}) %collective-permute-start) | collective-permute-done | bytes 16416 | tf_op jit(solution)/shard_map/ppermute | solution.py:480
  7.8 0.5 %shard_map.137 = (bf16[256,512]{1,0:T(8,128)(2,1)S(1)}, f32[256,512]{1,0:T(8,128)S(1)}, bf16[256,512]{1,0:T(8,128)(2,1)S(1)}, f32[128,256]{1,0:T(8,128)S(1)}, f3...) custom-call(f32[256,512]{1,0:T(8,128)S(1)} %get-tuple-element.45.pre_ref, ...), custom_call_target="tpu_custom_call" | custom-call | flops 200000000 | bytes 1048576 | tf_op jit(solution)/shard_map/pallas_call | solution.py:503
  8.3 0.1 collective-permute-start.1
  8.4 1.6 %shard_map.138 = (f32[256,512]{1,0:T(8,128)S(1)}, f32[24,256]{1,0:T(8,128)S(1)}) custom-call(bf16[256,512]{1,0:T(8,128)(2,1)S(1)} %get-tuple-element.50.xbc_ref, bf16[256,256]{1,0:T(8,128)(2,1)S(1)} %bitcast.21, f32[48,256]{1,0:T(8,128)S(1)} %get-tuple-element.53.rows_ref, f32[8,256]{1,0:T(8,128)S(1)} %get-tuple-element.48.logs_ref), custom_call_target="tpu_custom_call" | custom-call | flops 1000000000 | bytes 1048576 | tf_op jit(solution)/shard_map/pallas_call | solution.py:513
  10.0 2.3 %collective-permute-done.1 = f16[272,256]{1,0:T(8,128)(2,1)S(1)} collective-permute-done((f16[272,256]{1,0:T(8,128)(2,1)S(1)}, f16[272,256]{1,0:T(8,128)(2,1)S(1)}, u32[]{:S(2)}, u32[]{:S(2)}) %collective-permute-start.1) | collective-permute-done | bytes 139296 | tf_op jit(solution)/shard_map/ppermute | solution.py:452
  12.3 0.2 shard_map.139
  12.5 1.5 %collective-permute-start.4 = (f16[144,256]{1,0:T(8,128)(2,1)S(1)}, f16[144,256]{1,0:T(8,128)(2,1)S(1)}, u32[]{:S(2)}, u32[]{:S(2)}) collective-permute-start(f16[144,256]{1,0:T(8,128)(2,1)S(1)} %convert_element_type.36), channel_id=1, source_target_pairs={{0,24},{4,28},{8,0},{12,4},{16,8},{20,12},{24,16},{28,20},{1,25},{... | collective-permute-start | bytes 221192 | tf_op jit(solution)/shard_map/ppermute | solution.py:452
  14.0 0.0 collective-permute-start.3
  14.0 0.5 %collective-permute-start.2 = (f16[144,256]{1,0:T(8,128)(2,1)S(1)}, f16[144,256]{1,0:T(8,128)(2,1)S(1)}, u32[]{:S(2)}, u32[]{:S(2)}) collective-permute-start(f16[144,256]{1,0:T(8,128)(2,1)S(1)} %convert_element_type.32), channel_id=1, source_target_pairs={{0,8},{4,12},{8,16},{12,20},{16,24},{20,28},{24,0},{28,4},{1,9},{5... | collective-permute-start | bytes 221192 | tf_op jit(solution)/shard_map/ppermute | solution.py:452
  14.5 1.2 %collective-permute-done.4 = f16[144,256]{1,0:T(8,128)(2,1)S(1)} collective-permute-done((f16[144,256]{1,0:T(8,128)(2,1)S(1)}, f16[144,256]{1,0:T(8,128)(2,1)S(1)}, u32[]{:S(2)}, u32[]{:S(2)}) %collective-permute-start.4) | collective-permute-done | bytes 73760 | tf_op jit(solution)/shard_map/ppermute | solution.py:452
  15.8 4.4 %collective-permute-done.3 = f16[144,256]{1,0:T(8,128)(2,1)S(1)} collective-permute-done((f16[144,256]{1,0:T(8,128)(2,1)S(1)}, f16[144,256]{1,0:T(8,128)(2,1)S(1)}, u32[]{:S(2)}, u32[]{:S(2)}) %collective-permute-start.3) | collective-permute-done | bytes 73760 | tf_op jit(solution)/shard_map/ppermute | solution.py:452
  20.2 0.0 collective-permute-done.2
  20.3 1.7 %shard_map.140 = (f32[256,512]{1,0:T(8,128)S(1)}, f32[4,256]{1,0:T(4,128)}, f32[24,128]{1,0:T(8,128)S(1)}, f32[8,512]{1,0:T(8,128)S(1)}) custom-call(bf16[256,512]{1,0:T(8,128)(2,1)S(1)} %bitcast.19, bf16[16,512]{1,0:T(8,128)(2,1)S(1)} %collective-permute-done.halo_ref, bf16[256,512]{1,0:T(8,128)(2,1)S(1)} %get-tuple-element.50.xbc_ref, ...), custom_call_target="tpu_custom_call" | custom-call | flops 200000000 | bytes 1048576 | tf_op jit(solution)/shard_map/pallas_call | solution.py:539
  21.9 0.7 %broadcast_in_dim.30 = f16[32,24,128]{2,1,0:T(8,128)(2,1)} broadcast(f16[24,128]{1,0:T(8,128)(2,1)S(1)} %convert_element_type.38), dimensions={1,2} | broadcast | bytes 202752 | tf_op jit(solution)/shard_map/broadcast_in_dim | solution.py:467
  22.7 5.5 %all-to-all-start = ((f16[32,24,128]{2,1,0:T(8,128)(2,1)}), f16[32,24,128]{2,1,0:T(8,128)(2,1)S(1)}, u32[]{:S(2)}, u32[]{:S(2)}) async-start(f16[32,24,128]{2,1,0:T(8,128)(2,1)} %broadcast_in_dim.30), calls=%async_computation | async-start | bytes 393216 | tf_op jit(solution)/shard_map/all_to_all | solution.py:468
  28.2 4.3 %collective-permute-start.5 = (f32[8,512]{1,0:T(8,128)S(1)}, f32[8,512]{1,0:T(8,128)S(1)}, u32[]{:S(2)}, u32[]{:S(2)}) collective-permute-start(f32[8,512]{1,0:T(8,128)S(1)} %get-tuple-element.70), channel_id=1, source_target_pairs={{4,0},{8,4},{12,8},{16,12},{20,16},{24,20},{28,24},{0,28},{5,1},{9... | collective-permute-start | bytes 49160 | tf_op jit(solution)/shard_map/ppermute | solution.py:547
  32.5 0.9 %shard_map.141 = (bf16[256,512]{1,0:T(8,128)(2,1)}, f32[16,512]{1,0:T(8,128)S(1)}) custom-call(f32[256,512]{1,0:T(8,128)S(1)} %get-tuple-element.68.conv_ref, f32[4,512]{1,0:T(4,128)S(1)} %copy-done.1), custom_call_target="tpu_custom_call" | custom-call | flops 1000000 | bytes 1048576 | tf_op jit(solution)/shard_map/pallas_call | solution.py:554
  33.5 0.0 collective-permute-done.5.spilled_ref
  33.5 0.7 %shard_map.142 = bf16[256,512]{1,0:T(8,128)(2,1)} custom-call(f32[16,512]{1,0:T(8,128)S(1)} %get-tuple-element.69.end_ref, f32[8,512]{1,0:T(8,128)S(1)} %collective-permute-done.5.spilled_ref, f32[32,256]{1,0:T(8,128)S(1)} %get-tuple-element.49.places_ref, bf16[256,512]{1,0:T(8,128)(2,1)} %get-tuple-element.71.main_hbm), custom_call_target="tpu_custom_call", output_to_operand_aliasing={{}: (3, {})} | custom-call | bytes 1048576 | tf_op jit(solution)/shard_map/pallas_call | solution.py:562
  34.1 3.4 %all-to-all-done = f16[32,24,128]{2,1,0:T(8,128)(2,1)S(1)} async-done(((f16[32,24,128]{2,1,0:T(8,128)(2,1)}), f16[32,24,128]{2,1,0:T(8,128)(2,1)S(1)}, u32[]{:S(2)}, u32[]{:S(2)}) %all-to-all-start) | async-done | bytes 196640 | tf_op jit(solution)/shard_map/all_to_all | solution.py:468
  37.6 0.7 %shard_map.143 = (f32[4,512]{1,0:T(4,128)}, f32[1,512]{1,0:T(1,128)}, f32[1,4]{1,0:T(1,128)}, f32[1,4]{1,0:T(1,128)}, f32[1,4]{1,0:T(1,128)}) custom-call(f32[32,24,128]{2,1,0:T(8,128)S(1)} %convert_element_type.39.parts_ref), custom_call_target="tpu_custom_call" | custom-call | bytes 1048576 | tf_op jit(solution)/shard_map/pallas_call | solution.py:571
  (19 shorter events, 0.2 us)
Async XLA Ops:
  0.6 1.0 %copy-start = (bf16[1,256,512]{2,1,0:T(8,128)(2,1)S(1)}, bf16[1,256,512]{2,1,0:T(8,128)(2,1)}, u32[]{:S(2)}) copy-start(bf16[1,256,512]{2,1,0:T(8,128)(2,1)} %param.8) | copy-start | bytes 786436
  0.6 3.0 %copy-start.2 = (bf16[1,256,256]{2,1,0:T(8,128)(2,1)S(1)}, bf16[1,256,256]{2,1,0:T(8,128)(2,1)}, u32[]{:S(2)}) copy-start(bf16[1,256,256]{2,1,0:T(8,128)(2,1)} %param.15) | copy-start | bytes 393220
  0.7 3.0 %copy-start.3 = (f32[1,256,4]{1,2,0:T(4,128)S(1)}, f32[1,256,4]{1,2,0:T(4,128)}, u32[]{:S(2)}) copy-start(f32[1,256,4]{1,2,0:T(4,128)} %param.11) | copy-start | bytes 12292
  0.7 3.0 %copy-start.7 = (f32[4]{0:T(128)S(1)}, f32[4]{0:T(128)}, u32[]{:S(2)}) copy-start(f32[4]{0:T(128)} %param.14) | copy-start | bytes 52
  1.6 2.1 %copy-start.1 = (f32[4,512]{1,0:T(4,128)S(1)}, f32[4,512]{1,0:T(4,128)}, u32[]{:S(2)}) copy-start(f32[4,512]{1,0:T(4,128)} %weight_ref.7) | copy-start | bytes 24580
  1.6 6.2 %collective-permute-start = (bf16[16,512]{1,0:T(8,128)(2,1)S(1)}, bf16[16,512]{1,0:T(8,128)(2,1)S(1)}, u32[]{:S(2)}, u32[]{:S(2)}) collective-permute-start(bf16[16,512]{1,0:T(8,128)(2,1)S(1)} %slice.3), channel_id=1, source_target_pairs={{0,4},{4,8},{8,12},{12,16},{16,20},{20,24},{24,28},{28,0},{1,5},{5... | collective-permute-start | bytes 49160 | tf_op jit(solution)/shard_map/ppermute | solution.py:480
  3.6 0.7 %copy-start.4 = (f32[512]{0:T(512)S(1)}, f32[512]{0:T(512)}, u32[]{:S(2)}) copy-start(f32[512]{0:T(512)} %param.10) | copy-start | bytes 6148
  3.6 0.7 %copy-start.5 = (f32[4]{0:T(128)S(1)}, f32[4]{0:T(128)}, u32[]{:S(2)}) copy-start(f32[4]{0:T(128)} %param.12) | copy-start | bytes 52
  3.6 0.7 %copy-start.6 = (f32[4]{0:T(128)S(1)}, f32[4]{0:T(128)}, u32[]{:S(2)}) copy-start(f32[4]{0:T(128)} %param.13) | copy-start | bytes 52
  8.3 4.0 %collective-permute-start.1 = (f16[272,256]{1,0:T(8,128)(2,1)S(1)}, f16[272,256]{1,0:T(8,128)(2,1)S(1)}, u32[]{:S(2)}, u32[]{:S(2)}) collective-permute-start(f16[272,256]{1,0:T(8,128)(2,1)S(1)} %convert_element_type.30), channel_id=1, source_target_pairs={{0,4},{4,0},{8,12},{12,8},{16,20},{20,16},{24,28},{28,24},{1,5},{5... | collective-permute-start | bytes 417800 | tf_op jit(solution)/shard_map/ppermute | solution.py:452
  12.5 3.3 %collective-permute-start.4 = (f16[144,256]{1,0:T(8,128)(2,1)S(1)}, f16[144,256]{1,0:T(8,128)(2,1)S(1)}, u32[]{:S(2)}, u32[]{:S(2)}) collective-permute-start(f16[144,256]{1,0:T(8,128)(2,1)S(1)} %convert_element_type.36), channel_id=1, source_target_pairs={{0,24},{4,28},{8,0},{12,4},{16,8},{20,12},{24,16},{28,20},{1,25},{... | collective-permute-start | bytes 221192 | tf_op jit(solution)/shard_map/ppermute | solution.py:452
  14.0 6.2 %collective-permute-start.3 = (f16[144,256]{1,0:T(8,128)(2,1)S(1)}, f16[144,256]{1,0:T(8,128)(2,1)S(1)}, u32[]{:S(2)}, u32[]{:S(2)}) collective-permute-start(f16[144,256]{1,0:T(8,128)(2,1)S(1)} %convert_element_type.34), channel_id=1, source_target_pairs={{0,16},{4,20},{8,24},{12,28},{16,0},{20,4},{24,8},{28,12},{1,17},{... | collective-permute-start | bytes 221192 | tf_op jit(solution)/shard_map/ppermute | solution.py:452
  14.0 6.2 %collective-permute-start.2 = (f16[144,256]{1,0:T(8,128)(2,1)S(1)}, f16[144,256]{1,0:T(8,128)(2,1)S(1)}, u32[]{:S(2)}, u32[]{:S(2)}) collective-permute-start(f16[144,256]{1,0:T(8,128)(2,1)S(1)} %convert_element_type.32), channel_id=1, source_target_pairs={{0,8},{4,12},{8,16},{12,20},{16,24},{20,28},{24,0},{28,4},{1,9},{5... | collective-permute-start | bytes 221192 | tf_op jit(solution)/shard_map/ppermute | solution.py:452
  22.7 14.9 %all-to-all-start = ((f16[32,24,128]{2,1,0:T(8,128)(2,1)}), f16[32,24,128]{2,1,0:T(8,128)(2,1)S(1)}, u32[]{:S(2)}, u32[]{:S(2)}) async-start(f16[32,24,128]{2,1,0:T(8,128)(2,1)} %broadcast_in_dim.30), calls=%async_computation | async-start | bytes 393216 | tf_op jit(solution)/shard_map/all_to_all | solution.py:468
  28.2 5.3 %collective-permute-start.5 = (f32[8,512]{1,0:T(8,128)S(1)}, f32[8,512]{1,0:T(8,128)S(1)}, u32[]{:S(2)}, u32[]{:S(2)}) collective-permute-start(f32[8,512]{1,0:T(8,128)S(1)} %get-tuple-element.70), channel_id=1, source_target_pairs={{4,0},{8,4},{12,8},{16,12},{20,16},{24,20},{28,24},{0,28},{5,1},{9... | collective-permute-start | bytes 49160 | tf_op jit(solution)/shard_map/ppermute | solution.py:547

commit v5 on v4

--- a/solution.py
+++ b/solution.py
@@ -15,6 +15,7 @@
 HEAD_ROWS = 8
 TAIL_ROWS = 16
 HALO_ROWS = 16
+FIX_ROWS = 16
 END_ROWS = 16
 LANE_BLOCKS = (INNER + 2 * N) // 128
 SMALL_ROW = (K + 1) * LANE_BLOCKS
@@ -148,9 +149,20 @@
     until_ref[...] = jnp.where(iota(shape, 0) <= iota(shape, 1), 1.0, 0.0).astype(bf16)
 
 
+def heads_kernel(bias_ref, dt_bias_ref, alog_ref, skip_ref, until_in, until_ref, bias_out, heads_ref):
+    bias_out[...] = bias_ref[...]
+    for i, ref in enumerate((dt_bias_ref, alog_ref, skip_ref)):
+        heads_ref[8 * i : 8 * i + 8] = by_head(ref, until_ref.shape[1])
+
+
+def mask_first(x):
+    top = jnp.where(iota((FIX_ROWS, x.shape[1]), 0) < K - 1, 0.0, x[:FIX_ROWS].astype(f32))
+    return jnp.concatenate([top.astype(x.dtype), x[FIX_ROWS:]], 0)
+
+
 def start_kernel(
-    stages, raw_ref, cot_ref, weight_ref, bias_ref, dt_ref, dt_bias_ref, alog_ref, skip_ref, until_ref,
-    pre_ref, scaled_ref, tail_ref, rows_ref, logs_ref, places_ref, dt8_ref,
+    stages, raw_ref, cot_ref, weight_ref, bias_ref, dt_ref, heads_ref, until_ref,
+    top_ref, xbc_ref, slope_ref, weighted_ref, scaled_ref, tail_ref, rows_ref, logs_ref, places_ref, state_ref, grad_ref, msg_ref, dt8_ref,
 ):
     tok = raw_ref.shape[0]
     place = lax.axis_index("ctx")
@@ -162,10 +174,10 @@
     places_ref[at + 8 : at + 16] = jnp.full((8, INNER), jnp.where(place == slabs - 1, 1, 0), jnp.int32).astype(f32)
     dt8_ref[...] = jnp.zeros_like(dt8_ref)
     dt8_ref[0:H] = dt_ref[...]
-    dt_pre = dt8_ref[...] + by_head(dt_bias_ref, tok)
+    dt_pre = dt8_ref[...] + heads_ref[0:8]
     step = jnp.maximum(dt_pre, 0.0) + jnp.log1p(jnp.exp(-jnp.abs(dt_pre)))
     real = iota((HEAD_ROWS, tok), 0) < H
-    decay_rate = jnp.where(real, -jnp.exp(by_head(alog_ref, tok)), 0.0)
+    decay_rate = jnp.where(real, -jnp.exp(heads_ref[8:16]), 0.0)
     cum = unstacked(dot(stacked(step * decay_rate), until_ref[...]))
     left = jnp.exp(cum[:, tok - 1 : tok] - cum)
     reach = jnp.exp(cum)
@@ -175,49 +187,76 @@
     rows_ref[24:32] = reach
     rows_ref[32:40] = 1.0 / (1.0 + jnp.exp(-dt_pre))
     rows_ref[40:48] = decay_rate
-    tail_ref[...] = over_channels(left * step)
+    tail = over_channels(left * step)
+    tail_ref[...] = tail
     log_total = over_channels(cum)[tok - 1 : tok]
-    skip = over_channels(by_head(skip_ref, HEAD_ROWS))[0:1]
+    skip = over_channels(heads_ref[16:24])[0:1]
     row = iota((8, INNER), 0)
     logs_ref[...] = jnp.where(row == 2, log_total, jnp.where(row == 3, skip, 0.0))
-    scaled_ref[...] = jnp.concatenate(split2(cot_ref[...].astype(f32) * over_channels(reach)), 1)
+    scaled = jnp.concatenate(split2(cot_ref[...].astype(f32) * over_channels(reach)), 1)
+    scaled_ref[...] = scaled
+
     raw = raw_ref[...].astype(f32)
     zeros = jnp.zeros((8, raw.shape[1]), f32)
     pre = bias_ref[...] + weight_ref[K - 1 : K] * raw
     for back in range(1, K):
         pre = pre + weight_ref[K - 1 - back : K - back] * shifted_down(raw, zeros, back)
-    pre_ref[...] = pre
-
-
-def real_halo(halo_ref, places_ref):
-    first = places_ref[places_ref.shape[0] - 16 :][:1, :1]
-    return jnp.where(first > 0.5, 0.0, halo_ref[HALO_ROWS - 8 :].astype(f32))
-
-
-def enter_kernel(
-    radix, pre_ref, halo_ref, weight_ref, scaled_ref, tail_ref, logs_ref, places_ref,
-    xbc_ref, slope_ref, weighted_ref, state_ref, grad_ref, *msg_refs
-):
-    tok = pre_ref.shape[0]
-    halo = real_halo(halo_ref, places_ref)
-    top = pre_ref[0:8]
-    for back in range(1, K):
-        tap = weight_ref[K - 1 - back : K - back]
-        top = top + jnp.where(iota(top.shape, 0) < back, tap * pltpu.roll(halo, back, 0), 0.0)
-    pre = jnp.concatenate([top, pre_ref[8:]], 0)
+    top_ref[...] = pre[:FIX_ROWS]
     gate = 1.0 / (1.0 + jnp.exp(-pre))
     xbc = (pre * gate).astype(bf16)
     xbc_ref[...] = xbc
     slope_ref[...] = gate * (1.0 + pre * (1.0 - gate))
-    weighted = jnp.concatenate(split2(xbc[:, :INNER].astype(f32) * tail_ref[...]), 1)
+    weighted = jnp.concatenate(split2(xbc[:, :INNER].astype(f32) * tail), 1)
     weighted_ref[...] = weighted
-    state = dot(xbc[:, INNER : INNER + N], weighted, 0, 0)
+    later = mask_first(xbc[:, INNER:])
+    state = dot(later[:, :N], weighted, 0, 0)
     state = state[:, :INNER] + state[:, INNER:]
-    grad = dot(xbc[:, INNER + N :], scaled_ref[...], 0, 0)
+    grad = dot(later[:, N:], scaled, 0, 0)
     grad = grad[:, :INNER] + grad[:, INNER:]
     state_ref[...] = state
     grad_ref[...] = grad
-    write_messages(msg_refs, state, grad, logs_ref[2:3], places_ref[0:1], radix)
+    write_messages((msg_ref,), state, grad, log_total, places_ref[0:1], 0)
+
+
+def real_halo(halo_ref, places_ref):
+    first = places_ref[places_ref.shape[0] - 16 :][:1, :1]
+    return jnp.where(first > 0.5, 0.0, halo_ref[HALO_ROWS - 8 :].astype(f32))
+
+
+def fix_kernel(
+    top_ref, halo_ref, weight_ref, scaled_ref, tail_ref, places_ref, xbc_in, slope_in, weighted_in,
+    xbc_ref, slope_ref, weighted_ref, factors_ref,
+):
+    halo = real_halo(halo_ref, places_ref)
+    top = top_ref[0:8]
+    for back in range(1, K):
+        tap = weight_ref[K - 1 - back : K - back]
+        top = top + jnp.where(iota(top.shape, 0) < back, tap * pltpu.roll(halo, back, 0), 0.0)
+    pre = jnp.concatenate([top, top_ref[8:]], 0)
+    gate = 1.0 / (1.0 + jnp.exp(-pre))
+    xbc = (pre * gate).astype(bf16)
+    xbc_ref[0:FIX_ROWS] = xbc
+    slope_ref[0:FIX_ROWS] = gate * (1.0 + pre * (1.0 - gate))
+    xbc = xbc.astype(f32)
+    weighted = jnp.concatenate([each.astype(f32) for each in split2(xbc[:, :INNER] * tail_ref[0:FIX_ROWS])], 1)
+    weighted_ref[0:FIX_ROWS] = weighted.astype(bf16)
+    scaled = scaled_ref[0:FIX_ROWS].astype(f32)
+
+    def placed(low, high):
+        row = iota(low.shape, 0)
+        moved = jnp.concatenate([high[8:], high[:8]], 0)
+        return jnp.where(row < K - 1, low, jnp.where((row >= 8) & (row < 8 + K - 1), moved, 0.0)).astype(bf16)
+
+    zero = jnp.zeros((FIX_ROWS, N), f32)
+    factors_ref[:, : 2 * INNER] = placed(weighted, scaled)
+    factors_ref[:, 2 * INNER : 2 * INNER + N] = placed(xbc[:, INNER : INNER + N], zero)
+    factors_ref[:, 2 * INNER + N :] = placed(zero, xbc[:, INNER + N :])
+
+
+def first_parts(factors_ref):
+    both = dot(factors_ref[:, 2 * INNER :], factors_ref[:, : 2 * INNER], 0, 0)
+    both = both[:, :INNER] + both[:, INNER:]
+    return both[:N], both[N:]
 
 
 def merge_kernel(t, radix, next_radix, state_ref, grad_ref, logs_ref, places_ref, *refs):
@@ -226,6 +265,8 @@
     if t > 0:
         prior, after = refs[0][...], refs[1][...]
         refs = refs[2:]
+    else:
+        parts, refs = [first_parts(ref) for ref in refs[:radix]], refs[radix:]
     logs_out, prior_out, after_out, *refs = refs
     if not next_radix:
         state_out, grad_out, *refs = refs
@@ -234,6 +275,11 @@
     states = [message_block(ref, 0) for ref in got]
     grads = [message_block(ref, 1) for ref in got]
     logs = [message_log(ref) for ref in got]
+    own_state, own_grad = state_ref[...], grad_ref[...]
+    if t == 0:
+        own_state, own_grad = own_state + parts[0][0], own_grad + parts[0][1]
+        states = [each + part[0] for each, part in zip(states, parts[1:])]
+        grads = [each + part[1] for each, part in zip(grads, parts[1:])]
     earlier = [s <= place for s in range(1, radix)]
     later = [s > place for s in range(1, radix)]
     before, log_before = chained(states, logs, earlier)
@@ -241,8 +287,8 @@
     above, _ = chained(states, logs, later)
     below, _ = chained(grads[::-1], logs[::-1], earlier[::-1])
     mine = jnp.exp(log_total)
-    state = above + jnp.exp(log_beyond) * (state_ref[...] + mine * before)
-    grad = below + jnp.exp(log_before) * (grad_ref[...] + mine * beyond)
+    state = above + jnp.exp(log_beyond) * (own_state + mine * before)
+    grad = below + jnp.exp(log_before) * (own_grad + mine * beyond)
     prior_out[...] = prior + jnp.exp(log_prior) * before
     after_out[...] = after + jnp.exp(log_after) * beyond
     log_prior = log_prior + log_before
@@ -449,8 +495,13 @@
     for s in range(1, radix):
         message = messages[s - 1 if len(messages) > 1 else 0]
         route = [(p, p - p % (size * radix) + (p + s * size) % (size * radix)) for p in range(slabs)]
-        got.append(lax.ppermute(message.astype(jnp.float16), "ctx", route).astype(f32))
+        got.append(lax.ppermute(message, "ctx", route))
     return got
+
+
+def states_from_groups(messages, slabs, size, radix):
+    got = from_groups([message.astype(jnp.float16) for message in messages], slabs, size, radix)
+    return [each.astype(f32) for each in got]
 
 
 def stages_of(slabs):
@@ -459,7 +510,7 @@
         radix = 2 if (slabs // size).bit_length() % 2 == 0 else 4
         stages.append((size, radix))
         size *= radix
-    assert size == slabs and stages
+    assert size == slabs and len(stages) > 1
     return stages
 
 
@@ -475,7 +526,13 @@
     stages = stages_of(slabs)
 
     raw, cot, dt_rows = xbc_raw[0], grad_out[0], dt_raw[0].T
-    until = call(triangle_kernel, struct((tok, tok), bf16), [], flops=10**10)()
+    until = call(triangle_kernel, struct((tok, tok), bf16), [], flops=10**11)()
+    until, bias, heads = call(
+        heads_kernel,
+        (struct((tok, tok), bf16), struct((1, channels)), struct((3 * HEAD_ROWS, tok))),
+        [VMEM] * 5,
+        aliases={4: 0},
+    )(conv_bias[None], dt_bias[None], a_log[None], d_skip[None], until)
     early_raw, until = lax.optimization_barrier((raw, until))
     halo = lax.ppermute(early_raw[tok - HALO_ROWS :], "ctx", [(i, (i + 1) % slabs) for i in range(slabs)])
 
@@ -489,39 +546,41 @@
 
     state_like = struct((N, INNER))
     logs_like = struct((8, INNER))
-    pre, scaled, tail, rows, logs, places = call(
+    top, xbc, slope, weighted, scaled, tail, rows, logs, places, state, grad, *outgoing = call(
         functools.partial(start_kernel, stages),
         (
-            struct((tok, channels)), struct((tok, 2 * INNER), bf16), struct((tok, INNER)), struct((6 * HEAD_ROWS, tok)),
-            logs_like, struct((8 * len(stages) + 16, INNER)),
+            struct((FIX_ROWS, channels)), struct((tok, channels), bf16), struct((tok, channels)), struct((tok, 2 * INNER), bf16),
+            struct((tok, 2 * INNER), bf16), struct((tok, INNER)), struct((6 * HEAD_ROWS, tok)),
+            logs_like, struct((8 * len(stages) + 16, INNER)), state_like, state_like, *messages(0),
+        ),
+        [VMEM] * 7,
+        scratch=[pltpu.VMEM((HEAD_ROWS, tok), f32)],
+        flops=10**11,
+    )(raw, cot, conv_weight, bias, dt_rows, heads, until)
+    xbc, slope, weighted, factors = call(
+        fix_kernel,
+        (
+            struct((tok, channels), bf16), struct((tok, channels)), struct((tok, 2 * INNER), bf16),
+            struct((FIX_ROWS, 2 * INNER + 2 * N), bf16),
         ),
         [VMEM] * 9,
-        scratch=[pltpu.VMEM((HEAD_ROWS, tok), f32)],
-        flops=100_000_000,
-    )(raw, cot, conv_weight, conv_bias[None], dt_rows, dt_bias[None], a_log[None], d_skip[None], until)
-
-    xbc, slope, weighted, state, grad, *outgoing = call(
-        functools.partial(enter_kernel, last_radix(0)),
-        (
-            struct((tok, channels), bf16), struct((tok, channels)), struct((tok, 2 * INNER), bf16),
-            state_like, state_like, *messages(0),
-        ),
-        [VMEM] * 7,
-        flops=200_000_000,
-    )(pre, halo, conv_weight, scaled, tail, logs, places)
+        flops=1_000_000,
+        aliases={6: 0, 7: 1, 8: 2},
+    )(top, halo, conv_weight, scaled, tail, places, xbc, slope, weighted)
 
     local, sums = call(
         local_kernel,
         (struct((tok, channels)), struct((3 * HEAD_ROWS, tok))),
         [VMEM] * 4,
-        flops=1_000_000_000,
+        flops=10**11,
     )(xbc, cot, rows, logs)
 
     carried = ()
     for t, (size, radix) in enumerate(stages):
-        got = from_groups(outgoing, slabs, size, radix)
+        got = states_from_groups(outgoing, slabs, size, radix)
         if t == 0:
             got, local, sums = lax.optimization_barrier((got, local, sums))
+            carried = [factors] + from_groups([factors], slabs, size, radix)
         if t == len(stages) - 1:
             break
         last = last_radix(t + 1)

time: 38.5 us -> 38.2 us (level)
  starting transfers between devices: 13.9 us -> 16.5 us
  waiting for transfers between devices: 13.8 us -> 11.7 us
  local copies, waits for them, and re-layouts: 2.25 us -> 1.51 us
    ppermute x4 -> x5, starting transfers between devices: 2.06 us -> 3.91 us  [from_groups(): got.append(lax.ppermute(message, 'ctx', route))]
    ppermute x4 -> x5, waiting for transfers between devices: 7.96 us -> 6.49 us  [from_groups(): got.append(lax.ppermute(message, 'ctx', route))]
    all_to_all x1, starting transfers between devices: 5.5 us -> 6.31 us  [everyones(): return lax.all_to_all(packed, axes, 0, 0).astype(f32)]
    unnamed x16, local copies, waits for them, and re-layouts: 1.55 us -> 0.8 us
    ppermute x1, waiting for transfers between devices: 2.45 us -> 1.78 us  [on_device(): lax.ppermute(early_raw[tok - HALO_ROWS:], 'ctx', [(i, (i + 1) % slabs) fo...]
    pallas_call x3 -> x4, Pallas kernels: 1.54 us -> 1.29 us  [the longest x1 1.12 us: on_device(): call(functools.partial(start_kernel, stages), (struct((FIX_ROWS, channels...]
  transfers between devices with their start and end apart: 7 -> 8, of which waited for: 5 -> 6; matrix products, arithmetic and copies ran while one was open for 0% -> 0% of each run, Pallas kernels for 11% -> 12%
where the time goes in v5:
time: 38.2 us; the launch traced here: 37.9 us
  starting transfers between devices  16.5 us (43%)
  waiting for transfers between devices  11.7 us (31%)
  Pallas kernels  7.27 us (19%)
  local copies, waits for them, and re-layouts  1.51 us (4%)
  between operations  0.84 us (2%)
    ppermute x5, waiting for transfers between devices, from_groups(): got.append(lax.ppermute(message, 'ctx', route))  6.49 us
    all_to_all x1, starting transfers between devices, everyones(): return lax.all_to_all(packed, axes, 0, 0).astype(f32)  6.31 us
    ppermute x1, starting transfers between devices, on_device(): lax.ppermute(spill, 'ctx', [((i + 1) % slabs, i) for i in range(slabs)])  4.21 us
    ppermute x5, starting transfers between devices, from_groups(): got.append(lax.ppermute(message, 'ctx', route))  3.91 us
    all_to_all x1, waiting for transfers between devices, everyones(): return lax.all_to_all(packed, axes, 0, 0).astype(f32)  3.39 us
    ppermute x1, starting transfers between devices, on_device(): lax.ppermute(early_raw[tok - HALO_ROWS:], 'ctx', [(i, (i + 1) % slabs) fo...  2.09 us
    ppermute x1, waiting for transfers between devices, on_device(): lax.ppermute(early_raw[tok - HALO_ROWS:], 'ctx', [(i, (i + 1) % slabs) fo...  1.78 us
    pallas_call x1, Pallas kernels, on_device(): call(functools.partial(totals_kernel, len(stages) - 1, radix), (struct((t...  1.69 us
  transfers between devices with their start and end apart: 8, of which 6 were waited for; matrix products, arithmetic and copies ran while one was open for 0% of the time, Pallas kernels for 12%

profile of v5, /device:TPU:1, one launch (start us, length us, event | category | flops | bytes accessed | tf_op | source)
XLA Modules:
  0.0 37.9 jit_solution(14075370957162055789)
XLA Ops:
  0.7 0.0 copy-start.2
  0.7 0.0 copy-start.3
  0.7 0.0 copy-start.4
  0.7 0.0 copy-start.5
  0.7 0.7 %copy-done.2 = f32[512]{0:T(512)S(1)} copy-done((f32[512]{0:T(512)S(1)}, f32[512]{0:T(512)}, u32[]{:S(2)}) %copy-start.2) | copy-done | bytes 2072
  1.5 0.0 copy-done.5
  1.5 0.1 shard_map.136
  1.6 0.0 copy-done
  1.6 0.0 copy-start.7
  1.6 2.1 %collective-permute-start = (bf16[16,512]{1,0:T(8,128)(2,1)S(1)}, bf16[16,512]{1,0:T(8,128)(2,1)S(1)}, u32[]{:S(2)}, u32[]{:S(2)}) collective-permute-start(bf16[16,512]{1,0:T(8,128)(2,1)S(1)} %slice.3), channel_id=1, source_target_pairs={{0,4},{4,8},{8,12},{12,16},{16,20},{20,24},{24,28},{28,0},{1,5},{5... | collective-permute-start | bytes 49160 | tf_op jit(solution)/shard_map/ppermute | solution.py:537
  3.7 1.1 %shard_map.137 = (f32[16,512]{1,0:T(8,128)S(1)}, bf16[256,512]{1,0:T(8,128)(2,1)S(1)}, f32[256,512]{1,0:T(8,128)S(1)}, bf16[256,512]{1,0:T(8,128)(2,1)S(1)}, bf1...) custom-call(bf16[256,512]{1,0:T(8,128)(2,1)S(1)} %bitcast.18, ...), custom_call_target="tpu_custom_call" | custom-call | flops 99999997952 | bytes 1048576 | tf_op jit(solution)/shard_map/pallas_call | solution.py:549
  4.9 1.3 %collective-permute-start.1 = (f16[272,256]{1,0:T(8,128)(2,1)S(1)}, f16[272,256]{1,0:T(8,128)(2,1)S(1)}, u32[]{:S(2)}, u32[]{:S(2)}) collective-permute-start(f16[272,256]{1,0:T(8,128)(2,1)S(1)} %convert_element_type.30), channel_id=1, source_target_pairs={{0,4},{4,0},{8,12},{12,8},{16,20},{20,16},{24,28},{28,24},{1,5},{5... | collective-permute-start | bytes 417800 | tf_op jit(solution)/shard_map/ppermute | solution.py:498
  6.2 1.8 %collective-permute-done.halo_ref = bf16[16,512]{1,0:T(8,128)(2,1)S(1)} collective-permute-done((bf16[16,512]{1,0:T(8,128)(2,1)S(1)}, bf16[16,512]{1,0:T(8,128)(2,1)S(1)}, u32[]{:S(2)}, u32[]{:S(2)}) %collective-permute-start) | collective-permute-done | bytes 16416 | tf_op jit(solution)/shard_map/ppermute | solution.py:537
  8.0 0.1 shard_map.138
  8.0 0.1 collective-permute-start.2
  8.1 1.6 %shard_map.139 = (f32[256,512]{1,0:T(8,128)S(1)}, f32[24,256]{1,0:T(8,128)S(1)}) custom-call(bf16[256,512]{1,0:T(8,128)(2,1)S(1)} %get-tuple-element.62.xbc_ref, bf16[256,256]{1,0:T(8,128)(2,1)S(1)} %bitcast.25, f32[48,256]{1,0:T(8,128)S(1)} %get-tuple-element.65.rows_ref, f32[8,256]{1,0:T(8,128)S(1)} %get-tuple-element.67.logs_ref), custom_call_target="tpu_custom_call" | custom-call | flops 99999997952 | bytes 1048576 | tf_op jit(solution)/shard_map/pallas_call | solution.py:571
  9.7 0.1 collective-permute-done.1
  9.8 1.2 %collective-permute-done.2.refs_2_ = bf16[16,768]{1,0:T(8,128)(2,1)S(1)} collective-permute-done((bf16[16,768]{1,0:T(8,128)(2,1)S(1)}, bf16[16,768]{1,0:T(8,128)(2,1)S(1)}, u32[]{:S(2)}, u32[]{:S(2)}) %collective-permute-start.2) | collective-permute-done | bytes 24608 | tf_op jit(solution)/shard_map/ppermute | solution.py:498
  11.1 0.4 %shard_map.140 = (f32[8,256]{1,0:T(8,128)S(1)}, f32[128,256]{1,0:T(8,128)S(1)}, f32[128,256]{1,0:T(8,128)S(1)}, f32[144,256]{1,0:T(8,128)S(1)}, f32[144,256]{1,0:T(8,128)S(1)}, /*index=5*/f32[144,256]{1,0:T(8,128)S(1)}) custom-call(f32[128,256]{1,0:T(8,128)S(1)} %get-tuple-element.72.state_ref, f32[128,256]{1,0:T(8,128)S(1)} %get-tuple-element.73.grad_ref, ...), custom_call_target="tpu_custom_call" | custom-call | flops 1000000 | bytes 1048576 | tf_op jit(solution)/shard_map/pallas_call | solution.py:588
  11.5 2.0 %collective-permute-start.5 = (f16[144,256]{1,0:T(8,128)(2,1)S(1)}, f16[144,256]{1,0:T(8,128)(2,1)S(1)}, u32[]{:S(2)}, u32[]{:S(2)}) collective-permute-start(f16[144,256]{1,0:T(8,128)(2,1)S(1)} %convert_element_type.36), channel_id=1, source_target_pairs={{0,24},{4,28},{8,0},{12,4},{16,8},{20,12},{24,16},{28,20},{1,25},{... | collective-permute-start | bytes 221192 | tf_op jit(solution)/shard_map/ppermute | solution.py:498
  13.5 0.0 collective-permute-start.4
  13.5 0.5 %collective-permute-start.3 = (f16[144,256]{1,0:T(8,128)(2,1)S(1)}, f16[144,256]{1,0:T(8,128)(2,1)S(1)}, u32[]{:S(2)}, u32[]{:S(2)}) collective-permute-start(f16[144,256]{1,0:T(8,128)(2,1)S(1)} %convert_element_type.32), channel_id=1, source_target_pairs={{0,8},{4,12},{8,16},{12,20},{16,24},{20,28},{24,0},{28,4},{1,9},{5... | collective-permute-start | bytes 221192 | tf_op jit(solution)/shard_map/ppermute | solution.py:498
  14.0 0.9 %collective-permute-done.5 = f16[144,256]{1,0:T(8,128)(2,1)S(1)} collective-permute-done((f16[144,256]{1,0:T(8,128)(2,1)S(1)}, f16[144,256]{1,0:T(8,128)(2,1)S(1)}, u32[]{:S(2)}, u32[]{:S(2)}) %collective-permute-start.5) | collective-permute-done | bytes 73760 | tf_op jit(solution)/shard_map/ppermute | solution.py:498
  15.0 4.3 %collective-permute-done.4 = f16[144,256]{1,0:T(8,128)(2,1)S(1)} collective-permute-done((f16[144,256]{1,0:T(8,128)(2,1)S(1)}, f16[144,256]{1,0:T(8,128)(2,1)S(1)}, u32[]{:S(2)}, u32[]{:S(2)}) %collective-permute-start.4) | collective-permute-done | bytes 73760 | tf_op jit(solution)/shard_map/ppermute | solution.py:498
  19.3 1.7 %shard_map.141 = (f32[256,512]{1,0:T(8,128)S(1)}, f32[4,256]{1,0:T(4,128)}, f32[24,128]{1,0:T(8,128)S(1)}, f32[8,512]{1,0:T(8,128)S(1)}) custom-call(bf16[256,512]{1,0:T(8,128)(2,1)S(1)} %bitcast.19, bf16[16,512]{1,0:T(8,128)(2,1)S(1)} %collective-permute-done.halo_ref, bf16[256,512]{1,0:T(8,128)(2,1)S(1)} %get-tuple-element.62.xbc_ref, ...), custom_call_target="tpu_custom_call" | custom-call | flops 200000000 | bytes 1048576 | tf_op jit(solution)/shard_map/pallas_call | solution.py:598
  21.0 0.7 %broadcast_in_dim.30 = f16[32,24,128]{2,1,0:T(8,128)(2,1)} broadcast(f16[24,128]{1,0:T(8,128)(2,1)S(1)} %convert_element_type.38), dimensions={1,2} | broadcast | bytes 202752 | tf_op jit(solution)/shard_map/broadcast_in_dim | solution.py:518
  21.7 6.3 %all-to-all-start = ((f16[32,24,128]{2,1,0:T(8,128)(2,1)}), f16[32,24,128]{2,1,0:T(8,128)(2,1)S(1)}, u32[]{:S(2)}, u32[]{:S(2)}) async-start(f16[32,24,128]{2,1,0:T(8,128)(2,1)} %broadcast_in_dim.30), calls=%async_computation | async-start | bytes 393216 | tf_op jit(solution)/shard_map/all_to_all | solution.py:519
  28.0 4.2 %collective-permute-start.6 = (f32[8,512]{1,0:T(8,128)S(1)}, f32[8,512]{1,0:T(8,128)S(1)}, u32[]{:S(2)}, u32[]{:S(2)}) collective-permute-start(f32[8,512]{1,0:T(8,128)S(1)} %get-tuple-element.84), channel_id=1, source_target_pairs={{4,0},{8,4},{12,8},{16,12},{20,16},{24,20},{28,24},{0,28},{5,1},{9... | collective-permute-start | bytes 49160 | tf_op jit(solution)/shard_map/ppermute | solution.py:606
  32.2 0.9 %shard_map.142 = (bf16[256,512]{1,0:T(8,128)(2,1)}, f32[16,512]{1,0:T(8,128)S(1)}) custom-call(f32[256,512]{1,0:T(8,128)S(1)} %get-tuple-element.82.conv_ref, f32[4,512]{1,0:T(4,128)S(1)} %copy-done.1), custom_call_target="tpu_custom_call" | custom-call | flops 1000000 | bytes 1048576 | tf_op jit(solution)/shard_map/pallas_call | solution.py:613
  33.2 0.7 %shard_map.143 = bf16[256,512]{1,0:T(8,128)(2,1)} custom-call(f32[16,512]{1,0:T(8,128)S(1)} %get-tuple-element.83.end_ref, f32[8,512]{1,0:T(8,128)S(1)} %collective-permute-done.6.spilled_ref, f32[32,256]{1,0:T(8,128)S(1)} %get-tuple-element.58.places_ref, bf16[256,512]{1,0:T(8,128)(2,1)} %get-tuple-element.85.main_hbm), custom_call_target="tpu_custom_call", output_to_operand_aliasing={{}: (3, {})} | custom-call | bytes 1048576 | tf_op jit(solution)/shard_map/pallas_call | solution.py:621
  33.8 3.4 %all-to-all-done = f16[32,24,128]{2,1,0:T(8,128)(2,1)S(1)} async-done(((f16[32,24,128]{2,1,0:T(8,128)(2,1)}), f16[32,24,128]{2,1,0:T(8,128)(2,1)S(1)}, u32[]{:S(2)}, u32[]{:S(2)}) %all-to-all-start) | async-done | bytes 196640 | tf_op jit(solution)/shard_map/all_to_all | solution.py:519
  37.3 0.7 %shard_map.144 = (f32[4,512]{1,0:T(4,128)}, f32[1,512]{1,0:T(1,128)}, f32[1,4]{1,0:T(1,128)}, f32[1,4]{1,0:T(1,128)}, f32[1,4]{1,0:T(1,128)}) custom-call(f32[32,24,128]{2,1,0:T(8,128)S(1)} %convert_element_type.39.parts_ref), custom_call_target="tpu_custom_call" | custom-call | bytes 1048576 | tf_op jit(solution)/shard_map/pallas_call | solution.py:630
  (22 shorter events, 0.2 us)
Async XLA Ops:
  0.6 1.0 %copy-start = (bf16[1,256,512]{2,1,0:T(8,128)(2,1)S(1)}, bf16[1,256,512]{2,1,0:T(8,128)(2,1)}, u32[]{:S(2)}) copy-start(bf16[1,256,512]{2,1,0:T(8,128)(2,1)} %param.8) | copy-start | bytes 786436
  0.6 3.1 %copy-start.6 = (bf16[1,256,256]{2,1,0:T(8,128)(2,1)S(1)}, bf16[1,256,256]{2,1,0:T(8,128)(2,1)}, u32[]{:S(2)}) copy-start(bf16[1,256,256]{2,1,0:T(8,128)(2,1)} %param.15) | copy-start | bytes 393220
  0.7 0.8 %copy-start.2 = (f32[512]{0:T(512)S(1)}, f32[512]{0:T(512)}, u32[]{:S(2)}) copy-start(f32[512]{0:T(512)} %param.10) | copy-start | bytes 6148
  0.7 0.8 %copy-start.3 = (f32[4]{0:T(128)S(1)}, f32[4]{0:T(128)}, u32[]{:S(2)}) copy-start(f32[4]{0:T(128)} %param.12) | copy-start | bytes 52
  0.7 0.8 %copy-start.4 = (f32[4]{0:T(128)S(1)}, f32[4]{0:T(128)}, u32[]{:S(2)}) copy-start(f32[4]{0:T(128)} %param.13) | copy-start | bytes 52
  0.7 0.8 %copy-start.5 = (f32[4]{0:T(128)S(1)}, f32[4]{0:T(128)}, u32[]{:S(2)}) copy-start(f32[4]{0:T(128)} %param.14) | copy-start | bytes 52
  1.6 2.1 %copy-start.1 = (f32[4,512]{1,0:T(4,128)S(1)}, f32[4,512]{1,0:T(4,128)}, u32[]{:S(2)}) copy-start(f32[4,512]{1,0:T(4,128)} %weight_ref.7) | copy-start | bytes 24580
  1.6 2.1 %copy-start.7 = (f32[1,256,4]{1,2,0:T(4,128)S(1)}, f32[1,256,4]{1,2,0:T(4,128)}, u32[]{:S(2)}) copy-start(f32[1,256,4]{1,2,0:T(4,128)} %param.11) | copy-start | bytes 12292
  1.6 6.4 %collective-permute-start = (bf16[16,512]{1,0:T(8,128)(2,1)S(1)}, bf16[16,512]{1,0:T(8,128)(2,1)S(1)}, u32[]{:S(2)}, u32[]{:S(2)}) collective-permute-start(bf16[16,512]{1,0:T(8,128)(2,1)S(1)} %slice.3), channel_id=1, source_target_pairs={{0,4},{4,8},{8,12},{12,16},{16,20},{20,24},{24,28},{28,0},{1,5},{5... | collective-permute-start | bytes 49160 | tf_op jit(solution)/shard_map/ppermute | solution.py:537
  4.9 4.9 %collective-permute-start.1 = (f16[272,256]{1,0:T(8,128)(2,1)S(1)}, f16[272,256]{1,0:T(8,128)(2,1)S(1)}, u32[]{:S(2)}, u32[]{:S(2)}) collective-permute-start(f16[272,256]{1,0:T(8,128)(2,1)S(1)} %convert_element_type.30), channel_id=1, source_target_pairs={{0,4},{4,0},{8,12},{12,8},{16,20},{20,16},{24,28},{28,24},{1,5},{5... | collective-permute-start | bytes 417800 | tf_op jit(solution)/shard_map/ppermute | solution.py:498
  8.0 3.0 %collective-permute-start.2 = (bf16[16,768]{1,0:T(8,128)(2,1)S(1)}, bf16[16,768]{1,0:T(8,128)(2,1)S(1)}, u32[]{:S(2)}, u32[]{:S(2)}) collective-permute-start(bf16[16,768]{1,0:T(8,128)(2,1)S(1)} %get-tuple-element.75.refs_1_), channel_id=1, source_target_pairs={{0,4},{4,0},{8,12},{12,8},{16,20},{20,16},{24,28},{28,24},{1,5},{5... | collective-permute-start | bytes 73736 | tf_op jit(solution)/shard_map/ppermute | solution.py:498
  11.5 3.4 %collective-permute-start.5 = (f16[144,256]{1,0:T(8,128)(2,1)S(1)}, f16[144,256]{1,0:T(8,128)(2,1)S(1)}, u32[]{:S(2)}, u32[]{:S(2)}) collective-permute-start(f16[144,256]{1,0:T(8,128)(2,1)S(1)} %convert_element_type.36), channel_id=1, source_target_pairs={{0,24},{4,28},{8,0},{12,4},{16,8},{20,12},{24,16},{28,20},{1,25},{... | collective-permute-start | bytes 221192 | tf_op jit(solution)/shard_map/ppermute | solution.py:498
  13.5 5.7 %collective-permute-start.4 = (f16[144,256]{1,0:T(8,128)(2,1)S(1)}, f16[144,256]{1,0:T(8,128)(2,1)S(1)}, u32[]{:S(2)}, u32[]{:S(2)}) collective-permute-start(f16[144,256]{1,0:T(8,128)(2,1)S(1)} %convert_element_type.34), channel_id=1, source_target_pairs={{0,16},{4,20},{8,24},{12,28},{16,0},{20,4},{24,8},{28,12},{1,17},{... | collective-permute-start | bytes 221192 | tf_op jit(solution)/shard_map/ppermute | solution.py:498
  13.5 5.7 %collective-permute-start.3 = (f16[144,256]{1,0:T(8,128)(2,1)S(1)}, f16[144,256]{1,0:T(8,128)(2,1)S(1)}, u32[]{:S(2)}, u32[]{:S(2)}) collective-permute-start(f16[144,256]{1,0:T(8,128)(2,1)S(1)} %convert_element_type.32), channel_id=1, source_target_pairs={{0,8},{4,12},{8,16},{12,20},{16,24},{20,28},{24,0},{28,4},{1,9},{5... | collective-permute-start | bytes 221192 | tf_op jit(solution)/shard_map/ppermute | solution.py:498
  21.7 15.5 %all-to-all-start = ((f16[32,24,128]{2,1,0:T(8,128)(2,1)}), f16[32,24,128]{2,1,0:T(8,128)(2,1)S(1)}, u32[]{:S(2)}, u32[]{:S(2)}) async-start(f16[32,24,128]{2,1,0:T(8,128)(2,1)} %broadcast_in_dim.30), calls=%async_computation | async-start | bytes 393216 | tf_op jit(solution)/shard_map/all_to_all | solution.py:519
  28.0 5.2 %collective-permute-start.6 = (f32[8,512]{1,0:T(8,128)S(1)}, f32[8,512]{1,0:T(8,128)S(1)}, u32[]{:S(2)}, u32[]{:S(2)}) collective-permute-start(f32[8,512]{1,0:T(8,128)S(1)} %get-tuple-element.84), channel_id=1, source_target_pairs={{4,0},{8,4},{12,8},{16,12},{20,16},{24,20},{28,24},{0,28},{5,1},{9... | collective-permute-start | bytes 49160 | tf_op jit(solution)/shard_map/ppermute | solution.py:606

commit v6 on v5

--- a/solution.py
+++ b/solution.py
@@ -13,7 +13,7 @@
 K = 4
 INNER = H * P_SIZE
 HEAD_ROWS = 8
-TAIL_ROWS = 16
+TAIL_ROWS = 8
 HALO_ROWS = 16
 FIX_ROWS = 16
 END_ROWS = 16

time: 38.2 us -> 37.8 us (0.990)
  waiting for transfers between devices: 11.7 us -> 11.3 us
    ppermute x5, waiting for transfers between devices: 6.49 us -> 6.1 us  [from_groups(): got.append(lax.ppermute(message, 'ctx', route))]
  transfers between devices with their start and end apart: 8 -> 8, of which waited for: 6 -> 5; matrix products, arithmetic and copies ran while one was open for 0% -> 0% of each run, Pallas kernels for 12% -> 12%
where the time goes in v6:
time: 37.8 us; the launch traced here: 37.5 us
  starting transfers between devices  16.5 us (44%)
  waiting for transfers between devices  11.3 us (30%)
  Pallas kernels  7.28 us (19%)
  local copies, waits for them, and re-layouts  1.51 us (4%)
  between operations  0.84 us (2%)
    all_to_all x1, starting transfers between devices, everyones(): return lax.all_to_all(packed, axes, 0, 0).astype(f32)  6.24 us
    ppermute x5, waiting for transfers between devices, from_groups(): got.append(lax.ppermute(message, 'ctx', route))  6.1 us
    ppermute x1, starting transfers between devices, on_device(): lax.ppermute(spill, 'ctx', [((i + 1) % slabs, i) for i in range(slabs)])  4.21 us
    ppermute x5, starting transfers between devices, from_groups(): got.append(lax.ppermute(message, 'ctx', route))  3.96 us
    all_to_all x1, waiting for transfers between devices, everyones(): return lax.all_to_all(packed, axes, 0, 0).astype(f32)  3.39 us
    ppermute x1, starting transfers between devices, on_device(): lax.ppermute(early_raw[tok - HALO_ROWS:], 'ctx', [(i, (i + 1) % slabs) fo...  2.09 us
    ppermute x1, waiting for transfers between devices, on_device(): lax.ppermute(early_raw[tok - HALO_ROWS:], 'ctx', [(i, (i + 1) % slabs) fo...  1.77 us
    pallas_call x1, Pallas kernels, on_device(): call(functools.partial(totals_kernel, len(stages) - 1, radix), (struct((t...  1.68 us
  transfers between devices with their start and end apart: 8, of which 5 were waited for; matrix products, arithmetic and copies ran while one was open for 0% of the time, Pallas kernels for 12%

profile of v6, /device:TPU:1, one launch (start us, length us, event | category | flops | bytes accessed | tf_op | source)
XLA Modules:
  0.0 37.5 jit_solution(11454349144256041094)
XLA Ops:
  0.7 0.0 copy-start.2
  0.7 0.0 copy-start.3
  0.7 0.0 copy-start.4
  0.7 0.0 copy-start.5
  0.7 0.7 %copy-done.2 = f32[512]{0:T(512)S(1)} copy-done((f32[512]{0:T(512)S(1)}, f32[512]{0:T(512)}, u32[]{:S(2)}) %copy-start.2) | copy-done | bytes 2072
  1.5 0.0 copy-done.5
  1.5 0.1 shard_map.136
  1.6 0.0 copy-done
  1.6 0.0 copy-start.7
  1.6 2.1 %collective-permute-start = (bf16[16,512]{1,0:T(8,128)(2,1)S(1)}, bf16[16,512]{1,0:T(8,128)(2,1)S(1)}, u32[]{:S(2)}, u32[]{:S(2)}) collective-permute-start(bf16[16,512]{1,0:T(8,128)(2,1)S(1)} %slice.3), channel_id=1, source_target_pairs={{0,4},{4,8},{8,12},{12,16},{16,20},{20,24},{24,28},{28,0},{1,5},{5... | collective-permute-start | bytes 49160 | tf_op jit(solution)/shard_map/ppermute | solution.py:537
  3.7 1.1 %shard_map.137 = (f32[16,512]{1,0:T(8,128)S(1)}, bf16[256,512]{1,0:T(8,128)(2,1)S(1)}, f32[256,512]{1,0:T(8,128)S(1)}, bf16[256,512]{1,0:T(8,128)(2,1)S(1)}, bf1...) custom-call(bf16[256,512]{1,0:T(8,128)(2,1)S(1)} %bitcast.18, ...), custom_call_target="tpu_custom_call" | custom-call | flops 99999997952 | bytes 1048576 | tf_op jit(solution)/shard_map/pallas_call | solution.py:549
  4.9 1.3 %collective-permute-start.1 = (f16[264,256]{1,0:T(8,128)(2,1)S(1)}, f16[264,256]{1,0:T(8,128)(2,1)S(1)}, u32[]{:S(2)}, u32[]{:S(2)}) collective-permute-start(f16[264,256]{1,0:T(8,128)(2,1)S(1)} %convert_element_type.30), channel_id=1, source_target_pairs={{0,4},{4,0},{8,12},{12,8},{16,20},{20,16},{24,28},{28,24},{1,5},{5... | collective-permute-start | bytes 405512 | tf_op jit(solution)/shard_map/ppermute | solution.py:498
  6.2 1.8 %collective-permute-done.halo_ref = bf16[16,512]{1,0:T(8,128)(2,1)S(1)} collective-permute-done((bf16[16,512]{1,0:T(8,128)(2,1)S(1)}, bf16[16,512]{1,0:T(8,128)(2,1)S(1)}, u32[]{:S(2)}, u32[]{:S(2)}) %collective-permute-start) | collective-permute-done | bytes 16416 | tf_op jit(solution)/shard_map/ppermute | solution.py:537
  8.0 0.1 shard_map.138
  8.0 0.1 collective-permute-start.2
  8.1 1.6 %shard_map.139 = (f32[256,512]{1,0:T(8,128)S(1)}, f32[24,256]{1,0:T(8,128)S(1)}) custom-call(bf16[256,512]{1,0:T(8,128)(2,1)S(1)} %get-tuple-element.62.xbc_ref, bf16[256,256]{1,0:T(8,128)(2,1)S(1)} %bitcast.25, f32[48,256]{1,0:T(8,128)S(1)} %get-tuple-element.65.rows_ref, f32[8,256]{1,0:T(8,128)S(1)} %get-tuple-element.67.logs_ref), custom_call_target="tpu_custom_call" | custom-call | flops 99999997952 | bytes 1048576 | tf_op jit(solution)/shard_map/pallas_call | solution.py:571
  9.7 0.0 collective-permute-done.1
  9.8 1.1 %collective-permute-done.2.refs_2_ = bf16[16,768]{1,0:T(8,128)(2,1)S(1)} collective-permute-done((bf16[16,768]{1,0:T(8,128)(2,1)S(1)}, bf16[16,768]{1,0:T(8,128)(2,1)S(1)}, u32[]{:S(2)}, u32[]{:S(2)}) %collective-permute-start.2) | collective-permute-done | bytes 24608 | tf_op jit(solution)/shard_map/ppermute | solution.py:498
  10.9 0.4 %shard_map.140 = (f32[8,256]{1,0:T(8,128)S(1)}, f32[128,256]{1,0:T(8,128)S(1)}, f32[128,256]{1,0:T(8,128)S(1)}, f32[136,256]{1,0:T(8,128)S(1)}, f32[136,256]{1,0:T(8,128)S(1)}, /*index=5*/f32[136,256]{1,0:T(8,128)S(1)}) custom-call(f32[128,256]{1,0:T(8,128)S(1)} %get-tuple-element.72.state_ref, f32[128,256]{1,0:T(8,128)S(1)} %get-tuple-element.73.grad_ref, ...), custom_call_target="tpu_custom_call" | custom-call | flops 1000000 | bytes 1048576 | tf_op jit(solution)/shard_map/pallas_call | solution.py:588
  11.4 2.1 %collective-permute-start.5 = (f16[136,256]{1,0:T(8,128)(2,1)S(1)}, f16[136,256]{1,0:T(8,128)(2,1)S(1)}, u32[]{:S(2)}, u32[]{:S(2)}) collective-permute-start(f16[136,256]{1,0:T(8,128)(2,1)S(1)} %convert_element_type.36), channel_id=1, source_target_pairs={{0,24},{4,28},{8,0},{12,4},{16,8},{20,12},{24,16},{28,20},{1,25},{... | collective-permute-start | bytes 208904 | tf_op jit(solution)/shard_map/ppermute | solution.py:498
  13.4 0.0 collective-permute-start.4
  13.4 0.5 %collective-permute-start.3 = (f16[136,256]{1,0:T(8,128)(2,1)S(1)}, f16[136,256]{1,0:T(8,128)(2,1)S(1)}, u32[]{:S(2)}, u32[]{:S(2)}) collective-permute-start(f16[136,256]{1,0:T(8,128)(2,1)S(1)} %convert_element_type.32), channel_id=1, source_target_pairs={{0,8},{4,12},{8,16},{12,20},{16,24},{20,28},{24,0},{28,4},{1,9},{5... | collective-permute-start | bytes 208904 | tf_op jit(solution)/shard_map/ppermute | solution.py:498
  13.9 0.9 %collective-permute-done.5 = f16[136,256]{1,0:T(8,128)(2,1)S(1)} collective-permute-done((f16[136,256]{1,0:T(8,128)(2,1)S(1)}, f16[136,256]{1,0:T(8,128)(2,1)S(1)}, u32[]{:S(2)}, u32[]{:S(2)}) %collective-permute-start.5) | collective-permute-done | bytes 69664 | tf_op jit(solution)/shard_map/ppermute | solution.py:498
  14.8 4.1 %collective-permute-done.4 = f16[136,256]{1,0:T(8,128)(2,1)S(1)} collective-permute-done((f16[136,256]{1,0:T(8,128)(2,1)S(1)}, f16[136,256]{1,0:T(8,128)(2,1)S(1)}, u32[]{:S(2)}, u32[]{:S(2)}) %collective-permute-start.4) | collective-permute-done | bytes 69664 | tf_op jit(solution)/shard_map/ppermute | solution.py:498
  18.9 1.7 %shard_map.141 = (f32[256,512]{1,0:T(8,128)S(1)}, f32[4,256]{1,0:T(4,128)}, f32[24,128]{1,0:T(8,128)S(1)}, f32[8,512]{1,0:T(8,128)S(1)}) custom-call(bf16[256,512]{1,0:T(8,128)(2,1)S(1)} %bitcast.19, bf16[16,512]{1,0:T(8,128)(2,1)S(1)} %collective-permute-done.halo_ref, bf16[256,512]{1,0:T(8,128)(2,1)S(1)} %get-tuple-element.62.xbc_ref, ...), custom_call_target="tpu_custom_call" | custom-call | flops 200000000 | bytes 1048576 | tf_op jit(solution)/shard_map/pallas_call | solution.py:598
  20.6 0.7 %broadcast_in_dim.30 = f16[32,24,128]{2,1,0:T(8,128)(2,1)} broadcast(f16[24,128]{1,0:T(8,128)(2,1)S(1)} %convert_element_type.38), dimensions={1,2} | broadcast | bytes 202752 | tf_op jit(solution)/shard_map/broadcast_in_dim | solution.py:518
  21.3 6.2 %all-to-all-start = ((f16[32,24,128]{2,1,0:T(8,128)(2,1)}), f16[32,24,128]{2,1,0:T(8,128)(2,1)S(1)}, u32[]{:S(2)}, u32[]{:S(2)}) async-start(f16[32,24,128]{2,1,0:T(8,128)(2,1)} %broadcast_in_dim.30), calls=%async_computation | async-start | bytes 393216 | tf_op jit(solution)/shard_map/all_to_all | solution.py:519
  27.6 4.2 %collective-permute-start.6 = (f32[8,512]{1,0:T(8,128)S(1)}, f32[8,512]{1,0:T(8,128)S(1)}, u32[]{:S(2)}, u32[]{:S(2)}) collective-permute-start(f32[8,512]{1,0:T(8,128)S(1)} %get-tuple-element.84), channel_id=1, source_target_pairs={{4,0},{8,4},{12,8},{16,12},{20,16},{24,20},{28,24},{0,28},{5,1},{9... | collective-permute-start | bytes 49160 | tf_op jit(solution)/shard_map/ppermute | solution.py:606
  31.8 0.9 %shard_map.142 = (bf16[256,512]{1,0:T(8,128)(2,1)}, f32[16,512]{1,0:T(8,128)S(1)}) custom-call(f32[256,512]{1,0:T(8,128)S(1)} %get-tuple-element.82.conv_ref, f32[4,512]{1,0:T(4,128)S(1)} %copy-done.1), custom_call_target="tpu_custom_call" | custom-call | flops 1000000 | bytes 1048576 | tf_op jit(solution)/shard_map/pallas_call | solution.py:613
  32.8 0.7 %shard_map.143 = bf16[256,512]{1,0:T(8,128)(2,1)} custom-call(f32[16,512]{1,0:T(8,128)S(1)} %get-tuple-element.83.end_ref, f32[8,512]{1,0:T(8,128)S(1)} %collective-permute-done.6.spilled_ref, f32[32,256]{1,0:T(8,128)S(1)} %get-tuple-element.58.places_ref, bf16[256,512]{1,0:T(8,128)(2,1)} %get-tuple-element.85.main_hbm), custom_call_target="tpu_custom_call", output_to_operand_aliasing={{}: (3, {})} | custom-call | bytes 1048576 | tf_op jit(solution)/shard_map/pallas_call | solution.py:621
  33.4 3.4 %all-to-all-done = f16[32,24,128]{2,1,0:T(8,128)(2,1)S(1)} async-done(((f16[32,24,128]{2,1,0:T(8,128)(2,1)}), f16[32,24,128]{2,1,0:T(8,128)(2,1)S(1)}, u32[]{:S(2)}, u32[]{:S(2)}) %all-to-all-start) | async-done | bytes 196640 | tf_op jit(solution)/shard_map/all_to_all | solution.py:519
  36.8 0.7 %shard_map.144 = (f32[4,512]{1,0:T(4,128)}, f32[1,512]{1,0:T(1,128)}, f32[1,4]{1,0:T(1,128)}, f32[1,4]{1,0:T(1,128)}, f32[1,4]{1,0:T(1,128)}) custom-call(f32[32,24,128]{2,1,0:T(8,128)S(1)} %convert_element_type.39.parts_ref), custom_call_target="tpu_custom_call" | custom-call | bytes 1048576 | tf_op jit(solution)/shard_map/pallas_call | solution.py:630
  (22 shorter events, 0.2 us)
Async XLA Ops:
  0.6 1.0 %copy-start = (bf16[1,256,512]{2,1,0:T(8,128)(2,1)S(1)}, bf16[1,256,512]{2,1,0:T(8,128)(2,1)}, u32[]{:S(2)}) copy-start(bf16[1,256,512]{2,1,0:T(8,128)(2,1)} %param.8) | copy-start | bytes 786436
  0.6 3.1 %copy-start.6 = (bf16[1,256,256]{2,1,0:T(8,128)(2,1)S(1)}, bf16[1,256,256]{2,1,0:T(8,128)(2,1)}, u32[]{:S(2)}) copy-start(bf16[1,256,256]{2,1,0:T(8,128)(2,1)} %param.15) | copy-start | bytes 393220
  0.7 0.8 %copy-start.2 = (f32[512]{0:T(512)S(1)}, f32[512]{0:T(512)}, u32[]{:S(2)}) copy-start(f32[512]{0:T(512)} %param.10) | copy-start | bytes 6148
  0.7 0.8 %copy-start.3 = (f32[4]{0:T(128)S(1)}, f32[4]{0:T(128)}, u32[]{:S(2)}) copy-start(f32[4]{0:T(128)} %param.12) | copy-start | bytes 52
  0.7 0.8 %copy-start.4 = (f32[4]{0:T(128)S(1)}, f32[4]{0:T(128)}, u32[]{:S(2)}) copy-start(f32[4]{0:T(128)} %param.13) | copy-start | bytes 52
  0.7 0.8 %copy-start.5 = (f32[4]{0:T(128)S(1)}, f32[4]{0:T(128)}, u32[]{:S(2)}) copy-start(f32[4]{0:T(128)} %param.14) | copy-start | bytes 52
  1.6 2.1 %copy-start.1 = (f32[4,512]{1,0:T(4,128)S(1)}, f32[4,512]{1,0:T(4,128)}, u32[]{:S(2)}) copy-start(f32[4,512]{1,0:T(4,128)} %weight_ref.7) | copy-start | bytes 24580
  1.6 2.1 %copy-start.7 = (f32[1,256,4]{1,2,0:T(4,128)S(1)}, f32[1,256,4]{1,2,0:T(4,128)}, u32[]{:S(2)}) copy-start(f32[1,256,4]{1,2,0:T(4,128)} %param.11) | copy-start | bytes 12292
  1.6 6.4 %collective-permute-start = (bf16[16,512]{1,0:T(8,128)(2,1)S(1)}, bf16[16,512]{1,0:T(8,128)(2,1)S(1)}, u32[]{:S(2)}, u32[]{:S(2)}) collective-permute-start(bf16[16,512]{1,0:T(8,128)(2,1)S(1)} %slice.3), channel_id=1, source_target_pairs={{0,4},{4,8},{8,12},{12,16},{16,20},{20,24},{24,28},{28,0},{1,5},{5... | collective-permute-start | bytes 49160 | tf_op jit(solution)/shard_map/ppermute | solution.py:537
  4.9 4.8 %collective-permute-start.1 = (f16[264,256]{1,0:T(8,128)(2,1)S(1)}, f16[264,256]{1,0:T(8,128)(2,1)S(1)}, u32[]{:S(2)}, u32[]{:S(2)}) collective-permute-start(f16[264,256]{1,0:T(8,128)(2,1)S(1)} %convert_element_type.30), channel_id=1, source_target_pairs={{0,4},{4,0},{8,12},{12,8},{16,20},{20,16},{24,28},{28,24},{1,5},{5... | collective-permute-start | bytes 405512 | tf_op jit(solution)/shard_map/ppermute | solution.py:498
  8.0 2.9 %collective-permute-start.2 = (bf16[16,768]{1,0:T(8,128)(2,1)S(1)}, bf16[16,768]{1,0:T(8,128)(2,1)S(1)}, u32[]{:S(2)}, u32[]{:S(2)}) collective-permute-start(bf16[16,768]{1,0:T(8,128)(2,1)S(1)} %get-tuple-element.75.refs_1_), channel_id=1, source_target_pairs={{0,4},{4,0},{8,12},{12,8},{16,20},{20,16},{24,28},{28,24},{1,5},{5... | collective-permute-start | bytes 73736 | tf_op jit(solution)/shard_map/ppermute | solution.py:498
  11.4 3.4 %collective-permute-start.5 = (f16[136,256]{1,0:T(8,128)(2,1)S(1)}, f16[136,256]{1,0:T(8,128)(2,1)S(1)}, u32[]{:S(2)}, u32[]{:S(2)}) collective-permute-start(f16[136,256]{1,0:T(8,128)(2,1)S(1)} %convert_element_type.36), channel_id=1, source_target_pairs={{0,24},{4,28},{8,0},{12,4},{16,8},{20,12},{24,16},{28,20},{1,25},{... | collective-permute-start | bytes 208904 | tf_op jit(solution)/shard_map/ppermute | solution.py:498
  13.4 5.5 %collective-permute-start.4 = (f16[136,256]{1,0:T(8,128)(2,1)S(1)}, f16[136,256]{1,0:T(8,128)(2,1)S(1)}, u32[]{:S(2)}, u32[]{:S(2)}) collective-permute-start(f16[136,256]{1,0:T(8,128)(2,1)S(1)} %convert_element_type.34), channel_id=1, source_target_pairs={{0,16},{4,20},{8,24},{12,28},{16,0},{20,4},{24,8},{28,12},{1,17},{... | collective-permute-start | bytes 208904 | tf_op jit(solution)/shard_map/ppermute | solution.py:498
  13.4 5.5 %collective-permute-start.3 = (f16[136,256]{1,0:T(8,128)(2,1)S(1)}, f16[136,256]{1,0:T(8,128)(2,1)S(1)}, u32[]{:S(2)}, u32[]{:S(2)}) collective-permute-start(f16[136,256]{1,0:T(8,128)(2,1)S(1)} %convert_element_type.32), channel_id=1, source_target_pairs={{0,8},{4,12},{8,16},{12,20},{16,24},{20,28},{24,0},{28,4},{1,9},{5... | collective-permute-start | bytes 208904 | tf_op jit(solution)/shard_map/ppermute | solution.py:498
  21.3 15.5 %all-to-all-start = ((f16[32,24,128]{2,1,0:T(8,128)(2,1)}), f16[32,24,128]{2,1,0:T(8,128)(2,1)S(1)}, u32[]{:S(2)}, u32[]{:S(2)}) async-start(f16[32,24,128]{2,1,0:T(8,128)(2,1)} %broadcast_in_dim.30), calls=%async_computation | async-start | bytes 393216 | tf_op jit(solution)/shard_map/all_to_all | solution.py:519
  27.6 5.2 %collective-permute-start.6 = (f32[8,512]{1,0:T(8,128)S(1)}, f32[8,512]{1,0:T(8,128)S(1)}, u32[]{:S(2)}, u32[]{:S(2)}) collective-permute-start(f32[8,512]{1,0:T(8,128)S(1)} %get-tuple-element.84), channel_id=1, source_target_pairs={{4,0},{8,4},{12,8},{16,12},{20,16},{24,20},{28,24},{0,28},{5,1},{9... | collective-permute-start | bytes 49160 | tf_op jit(solution)/shard_map/ppermute | solution.py:606

commit v7 on v6

--- a/solution.py
+++ b/solution.py
@@ -162,7 +162,7 @@
 
 def start_kernel(
     stages, raw_ref, cot_ref, weight_ref, bias_ref, dt_ref, heads_ref, until_ref,
-    top_ref, xbc_ref, slope_ref, weighted_ref, scaled_ref, tail_ref, rows_ref, logs_ref, places_ref, state_ref, grad_ref, msg_ref, dt8_ref,
+    pre_ref, xbc_ref, weighted_ref, scaled_ref, tail_ref, rows_ref, logs_ref, places_ref, state_ref, grad_ref, msg_ref, dt8_ref,
 ):
     tok = raw_ref.shape[0]
     place = lax.axis_index("ctx")
@@ -201,11 +201,10 @@
     pre = bias_ref[...] + weight_ref[K - 1 : K] * raw
     for back in range(1, K):
         pre = pre + weight_ref[K - 1 - back : K - back] * shifted_down(raw, zeros, back)
-    top_ref[...] = pre[:FIX_ROWS]
+    pre_ref[...] = pre
     gate = 1.0 / (1.0 + jnp.exp(-pre))
     xbc = (pre * gate).astype(bf16)
     xbc_ref[...] = xbc
-    slope_ref[...] = gate * (1.0 + pre * (1.0 - gate))
     weighted = jnp.concatenate(split2(xbc[:, :INNER].astype(f32) * tail), 1)
     weighted_ref[...] = weighted
     later = mask_first(xbc[:, INNER:])
@@ -224,19 +223,19 @@
 
 
 def fix_kernel(
-    top_ref, halo_ref, weight_ref, scaled_ref, tail_ref, places_ref, xbc_in, slope_in, weighted_in,
-    xbc_ref, slope_ref, weighted_ref, factors_ref,
+    halo_ref, weight_ref, scaled_ref, tail_ref, places_ref, pre_in, xbc_in, weighted_in,
+    pre_ref, xbc_ref, weighted_ref, factors_ref,
 ):
     halo = real_halo(halo_ref, places_ref)
-    top = top_ref[0:8]
+    top = pre_in[0:8]
     for back in range(1, K):
         tap = weight_ref[K - 1 - back : K - back]
         top = top + jnp.where(iota(top.shape, 0) < back, tap * pltpu.roll(halo, back, 0), 0.0)
-    pre = jnp.concatenate([top, top_ref[8:]], 0)
+    pre = jnp.concatenate([top, pre_in[8:FIX_ROWS]], 0)
+    pre_ref[0:FIX_ROWS] = pre
     gate = 1.0 / (1.0 + jnp.exp(-pre))
     xbc = (pre * gate).astype(bf16)
     xbc_ref[0:FIX_ROWS] = xbc
-    slope_ref[0:FIX_ROWS] = gate * (1.0 + pre * (1.0 - gate))
     xbc = xbc.astype(f32)
     weighted = jnp.concatenate([each.astype(f32) for each in split2(xbc[:, :INNER] * tail_ref[0:FIX_ROWS])], 1)
     weighted_ref[0:FIX_ROWS] = weighted.astype(bf16)
@@ -266,7 +265,7 @@
         prior, after = refs[0][...], refs[1][...]
         refs = refs[2:]
     else:
-        parts, refs = [first_parts(ref) for ref in refs[:radix]], refs[radix:]
+        parts, refs = [first_parts(ref) for ref in refs[: radix - 1]], refs[radix - 1 :]
     logs_out, prior_out, after_out, *refs = refs
     if not next_radix:
         state_out, grad_out, *refs = refs
@@ -277,9 +276,8 @@
     logs = [message_log(ref) for ref in got]
     own_state, own_grad = state_ref[...], grad_ref[...]
     if t == 0:
-        own_state, own_grad = own_state + parts[0][0], own_grad + parts[0][1]
-        states = [each + part[0] for each, part in zip(states, parts[1:])]
-        grads = [each + part[1] for each, part in zip(grads, parts[1:])]
+        states = [each + part[0] for each, part in zip(states, parts)]
+        grads = [each + part[1] for each, part in zip(grads, parts)]
     earlier = [s <= place for s in range(1, radix)]
     later = [s > place for s in range(1, radix)]
     before, log_before = chained(states, logs, earlier)
@@ -302,7 +300,16 @@
     write_messages(refs, state, grad, log_total, places_ref[8 * t + 8 : 8 * t + 9], next_radix)
 
 
-def local_kernel(xbc_ref, cot_ref, rows_ref, logs_ref, local_ref, sums_ref):
+def local_kernel(
+    xbc_ref, cot_ref, rows_ref, logs_ref, raw_ref, halo_ref, places_ref, scaled_ref, until_ref, pre_ref, factors_ref, state_in, grad_in,
+    local_ref, sums_ref, weights_ref, moved_ref, slope_ref, state_ref, grad_ref,
+):
+    state, grad = first_parts(factors_ref)
+    state_ref[...] = state_in[...] + state
+    grad_ref[...] = grad_in[...] + grad
+    pre = pre_ref[...]
+    sigmoid = 1.0 / (1.0 + jnp.exp(-pre))
+    slope_ref[...] = sigmoid * (1.0 + pre * (1.0 - sigmoid))
     tok = xbc_ref.shape[0]
     cot = cot_ref[...]
     values = xbc_ref[:, :INNER]
@@ -339,21 +346,47 @@
     pairs = jnp.zeros((HEAD_ROWS, tok), f32)
     for h in range(H):
         pairs = jnp.where(row == h, sums[h], pairs)
-    sums_ref[0:8] = pairs
-    sums_ref[8:16] = head_sums(values_f * grad_stepped)
-    sums_ref[16:24] = head_sums(values_f * cot_f)
+    left, gate, decay_rate = rows_ref[16:24], rows_ref[32:40], rows_ref[40:48]
+    from_values = head_sums(values_f * grad_stepped)
+    skip_rows = head_sums(values_f * cot_f)
+    base = pairs - from_values * step
+    sums_ref[0:8] = base
+    sums_ref[8:16] = from_values
+
+    bias_weight = decay_rate * unstacked(dot(stacked(gate), until_ref[...]))
+    cum_last, bias_last = cum[:, tok - 1 : tok], bias_weight[:, tok - 1 : tok]
+    tail = left * step
+    scaled_f = scaled_ref[:, :INNER].astype(f32) + scaled_ref[:, INNER:].astype(f32)
+    weights_ref[:, :INNER] = scaled_f * over_channels(cum)
+    weights_ref[:, INNER : 2 * INNER] = values_f * over_channels(tail * (cum_last - cum))
+    weights_ref[:, 2 * INNER : 3 * INNER] = scaled_f * over_channels(bias_weight)
+    weights_ref[:, 3 * INNER :] = values_f * over_channels(left * gate + tail * (bias_last - bias_weight))
+    lane = iota((HEAD_ROWS, tok), 1)
+    fixed = jnp.zeros((HEAD_ROWS, tok), f32)
+    for i, column in enumerate((
+        jnp.sum(from_values * gate + base * bias_weight, axis=1, keepdims=True),
+        jnp.sum(base * cum, axis=1, keepdims=True),
+        jnp.sum(skip_rows, axis=1, keepdims=True),
+        bias_last, cum_last,
+    )):
+        fixed = jnp.where(lane == i, column, fixed)
+    sums_ref[16:24] = fixed
+    raw = raw_ref[...].astype(f32)
+    halo = real_halo(halo_ref, places_ref)
+    for back in range(1, K):
+        moved_ref[(back - 1) * tok : back * tok] = shifted_down(raw, halo, back)
 
 
 def totals_kernel(
-    t, radix, raw_ref, halo_ref, xbc_ref, slope_ref, scaled_ref, weighted_ref, tail_ref, rows_ref, local_ref, sums_ref,
-    logs_ref, places_ref, until_ref, weight_ref, *refs
+    t, radix, raw_ref, moved_ref, xbc_ref, slope_ref, scaled_ref, weighted_ref, tail_ref, rows_ref, local_ref, sums_ref, weights_ref,
+    logs_ref, places_ref, weight_ref, *refs
 ):
     got, refs = refs[: radix - 1], refs[radix - 1 :]
     prior = after = 0.0
     if t > 0:
         prior, after = refs[0][...], refs[1][...]
         refs = refs[2:]
-    conv_ref, dt_out_ref, totals_ref, spill_ref, totals_scratch = refs
+    conv_ref, states_ref, totals_ref, spill_ref, totals_scratch = refs
     tok = raw_ref.shape[0]
     place = places_ref[8 * t : 8 * t + 1]
     blocks = [message_block(ref) for ref in got]
@@ -363,8 +396,6 @@
     prior = prior + jnp.exp(logs_ref[0:1]) * before
     after = after + jnp.exp(logs_ref[1:2]) * beyond
 
-    step, left, reach = rows_ref[8:16], rows_ref[16:24], rows_ref[24:32]
-    dt_gate, decay_rate = rows_ref[32:40], rows_ref[40:48]
     b_proj = xbc_ref[:, INNER : INNER + N]
     c_proj = xbc_ref[:, INNER + N :]
     prior2 = jnp.concatenate(split2(prior), 0)
@@ -385,9 +416,8 @@
         spill = spill + tap * jnp.where(iota(top.shape, 0) < 8 - ahead, 0.0, pltpu.roll(top, 8 - ahead, 0))
     spill_ref[...] = spill
 
-    raw = raw_ref[...].astype(f32)
-    halo = real_halo(halo_ref, places_ref)
-    sums = [grad_conv * shifted_down(raw, halo, K - 1 - k) for k in range(K - 1)] + [grad_conv * raw, grad_conv]
+    sums = [grad_conv * moved_ref[back * tok : (back + 1) * tok] for back in range(K - 2, -1, -1)]
+    sums += [grad_conv * raw_ref[...].astype(f32), grad_conv]
     totals_scratch[...] = jnp.zeros_like(totals_scratch)
     for k, each in enumerate(sums):
         each = jnp.sum(each, axis=0, keepdims=True)
@@ -395,31 +425,33 @@
             at = k * LANE_BLOCKS + j
             totals_scratch[at : at + 1] = each[:, j * 128 : (j + 1) * 128]
 
-    values = xbc_ref[:, :INNER].astype(f32)
-    pairs, from_values, skip_rows = sums_ref[0:8], sums_ref[8:16], sums_ref[16:24]
-    scaled_f = scaled_ref[:, :INNER].astype(f32) + scaled_ref[:, INNER:].astype(f32)
-    seen_rows = head_sums(scaled_f * seen)
-    tail_rows = head_sums(values * back)
-    tail_term = tail_rows * left * step
+    states_ref[:tok, :INNER] = seen
+    states_ref[:tok, INNER:] = back
+    through = jnp.sum(prior * after, axis=0, keepdims=True)
+    grad_bias = jnp.sum(seen * weights_ref[:, 2 * INNER : 3 * INNER] + back * weights_ref[:, 3 * INNER :], axis=0, keepdims=True)
+    grad_alog = jnp.sum(seen * weights_ref[:, :INNER] + back * weights_ref[:, INNER : 2 * INNER], axis=0, keepdims=True)
     selector = head_selector(HEAD_ROWS * 2)[:HEAD_ROWS].astype(f32)
-    through = jnp.sum(prior * after, axis=0, keepdims=True)
-    through = jnp.sum(selector * through, axis=1, keepdims=True) * reach[:, tok - 1 : tok]
-    last_extra = jnp.sum(tail_term, axis=1, keepdims=True) + through
-    grad_cum = pairs - from_values * step + seen_rows - tail_term
-    grad_log = unstacked(dot(stacked(grad_cum), until_ref[...], 1, 1)) + last_extra
-    grad_step = from_values + tail_rows * left + decay_rate * grad_log
-    grad_pre = grad_step * dt_gate
-    dt_out_ref[...] = grad_pre[0:H]
+    grad_bias, grad_alog, through = (
+        jnp.sum(selector * each, axis=1, keepdims=True) for each in (grad_bias, grad_alog, through)
+    )
+    through = through * rows_ref[24:32][:, tok - 1 : tok]
+    states_ref[tok:] = jnp.broadcast_to(through, (HEAD_ROWS, 2 * INNER))
+    fixed = sums_ref[16:24]
     row, lane = iota((HEAD_ROWS, 128), 0), iota((HEAD_ROWS, 128), 1)
     small = jnp.zeros((HEAD_ROWS, 128), f32)
-    for i, each in enumerate((grad_pre, grad_log * step * decay_rate, skip_rows)):
-        column = jnp.sum(each, axis=1, keepdims=True)
+    for i, column in enumerate((
+        fixed[:, 0:1] + grad_bias + through * fixed[:, 3:4],
+        fixed[:, 1:2] + grad_alog + through * fixed[:, 4:5],
+        fixed[:, 2:3],
+    )):
         small = jnp.where((row < H) & (lane == row + i * H), column, small)
     totals_scratch[SMALL_ROW : SMALL_ROW + 1] = jnp.sum(small, axis=0, keepdims=True)
     totals_ref[...] = pack_totals(totals_scratch[...])
 
 
-def input_kernel(conv_ref, weight_ref, out_hbm, end_ref, out_ref, sem):
+def input_kernel(
+    conv_ref, weight_ref, states_ref, xbc_ref, scaled_ref, rows_ref, sums_ref, until_ref, out_hbm, dt_out_ref, end_ref, out_ref, sem
+):
     grad_conv = conv_ref[...]
     tok, channels = grad_conv.shape
     grad_in = weight_ref[K - 1 : K] * grad_conv
@@ -434,6 +466,17 @@
     copy = pltpu.make_async_copy(out_ref, out_hbm, sem)
     copy.start()
     end_ref[...] = grad_in[tok - END_ROWS :]
+
+    step, left, gate, decay_rate = rows_ref[8:16], rows_ref[16:24], rows_ref[32:40], rows_ref[40:48]
+    scaled_f = scaled_ref[:, :INNER].astype(f32) + scaled_ref[:, INNER:].astype(f32)
+    seen_rows = head_sums(scaled_f * states_ref[:tok, :INNER])
+    tail_rows = head_sums(xbc_ref[:, :INNER].astype(f32) * states_ref[:tok, INNER:])
+    tail_term = tail_rows * left * step
+    last_extra = jnp.sum(tail_term, axis=1, keepdims=True) + states_ref[tok:][:, :1]
+    grad_cum = sums_ref[0:8] + seen_rows - tail_term
+    grad_log = unstacked(dot(stacked(grad_cum), until_ref[...], 1, 1)) + last_extra
+    grad_step = sums_ref[8:16] + tail_rows * left + decay_rate * grad_log
+    dt_out_ref[...] = (grad_step * gate)[0:H]
     copy.wait()
 
 
@@ -546,10 +589,10 @@
 
     state_like = struct((N, INNER))
     logs_like = struct((8, INNER))
-    top, xbc, slope, weighted, scaled, tail, rows, logs, places, state, grad, *outgoing = call(
+    pre, xbc, weighted, scaled, tail, rows, logs, places, state, grad, *outgoing = call(
         functools.partial(start_kernel, stages),
         (
-            struct((FIX_ROWS, channels)), struct((tok, channels), bf16), struct((tok, channels)), struct((tok, 2 * INNER), bf16),
+            struct((tok, channels)), struct((tok, channels), bf16), struct((tok, 2 * INNER), bf16),
             struct((tok, 2 * INNER), bf16), struct((tok, INNER)), struct((6 * HEAD_ROWS, tok)),
             logs_like, struct((8 * len(stages) + 16, INNER)), state_like, state_like, *messages(0),
         ),
@@ -557,30 +600,34 @@
         scratch=[pltpu.VMEM((HEAD_ROWS, tok), f32)],
         flops=10**11,
     )(raw, cot, conv_weight, bias, dt_rows, heads, until)
-    xbc, slope, weighted, factors = call(
+    pre, xbc, weighted, factors = call(
         fix_kernel,
         (
-            struct((tok, channels), bf16), struct((tok, channels)), struct((tok, 2 * INNER), bf16),
+            struct((tok, channels)), struct((tok, channels), bf16), struct((tok, 2 * INNER), bf16),
             struct((FIX_ROWS, 2 * INNER + 2 * N), bf16),
         ),
-        [VMEM] * 9,
+        [VMEM] * 8,
         flops=1_000_000,
-        aliases={6: 0, 7: 1, 8: 2},
-    )(top, halo, conv_weight, scaled, tail, places, xbc, slope, weighted)
-
-    local, sums = call(
+        aliases={5: 0, 6: 1, 7: 2},
+    )(halo, conv_weight, scaled, tail, places, pre, xbc, weighted)
+
+    local, sums, weights, moved, slope, state, grad = call(
         local_kernel,
-        (struct((tok, channels)), struct((3 * HEAD_ROWS, tok))),
-        [VMEM] * 4,
+        (
+            struct((tok, channels)), struct((3 * HEAD_ROWS, tok)), struct((tok, 4 * INNER)), struct(((K - 1) * tok, channels)),
+            struct((tok, channels)), state_like, state_like,
+        ),
+        [VMEM] * 13,
         flops=10**11,
-    )(xbc, cot, rows, logs)
+        aliases={11: 5, 12: 6},
+    )(xbc, cot, rows, logs, raw, halo, places, scaled, until, pre, factors, state, grad)
 
     carried = ()
     for t, (size, radix) in enumerate(stages):
         got = states_from_groups(outgoing, slabs, size, radix)
         if t == 0:
-            got, local, sums = lax.optimization_barrier((got, local, sums))
-            carried = [factors] + from_groups([factors], slabs, size, radix)
+            got, local, sums, weights, moved, slope = lax.optimization_barrier((got, local, sums, weights, moved, slope))
+            carried = from_groups([factors], slabs, size, radix)
         if t == len(stages) - 1:
             break
         last = last_radix(t + 1)
@@ -595,13 +642,13 @@
         if not last:
             (state, grad), outgoing = outgoing[:2], outgoing[2:]
 
-    grad_conv, grad_dt, packed, spill = call(
+    grad_conv, states, packed, spill = call(
         functools.partial(totals_kernel, len(stages) - 1, radix),
-        (struct((tok, channels)), struct((H, tok)), struct((TOTAL_ROWS, 128)), struct((8, channels))),
+        (struct((tok, channels)), struct((tok + HEAD_ROWS, 2 * INNER)), struct((TOTAL_ROWS, 128)), struct((8, channels))),
         [VMEM] * (14 + len(got) + len(carried)),
         scratch=[pltpu.VMEM((TOTAL_ROWS, 128), f32)],
         flops=200_000_000,
-    )(raw, halo, xbc, slope, scaled, weighted, tail, rows, local, sums, logs, places, until, conv_weight, *got, *carried)
+    )(raw, moved, xbc, slope, scaled, weighted, tail, rows, local, sums, weights, logs, places, conv_weight, *got, *carried)
 
     spilled = lax.ppermute(spill, "ctx", [((i + 1) % slabs, i) for i in range(slabs)])
     if slabs * contexts <= 64:
@@ -610,14 +657,14 @@
         packed = call(repack_kernel, struct((TOTAL_ROWS, 128)), [VMEM])(everyones(packed, "ctx", slabs))
         parts = everyones(packed, "dp", contexts)
 
-    grad_main, end = call(
+    grad_main, grad_dt, end = call(
         input_kernel,
-        (struct((tok, channels), bf16), struct((END_ROWS, channels))),
-        [VMEM] * 2,
-        (HBM, VMEM),
+        (struct((tok, channels), bf16), struct((H, tok)), struct((END_ROWS, channels))),
+        [VMEM] * 8,
+        (HBM, VMEM, VMEM),
         [pltpu.VMEM((tok, channels), bf16), pltpu.SemaphoreType.DMA],
         flops=1_000_000,
-    )(grad_conv, conv_weight)
+    )(grad_conv, conv_weight, states, xbc, scaled, rows, sums, until)
     grad_input = call(
         end_kernel,
         struct((tok, channels), bf16),

time: 37.8 us -> 36.6 us (0.968)
  waiting for transfers between devices: 11.3 us -> 9.74 us
  Pallas kernels: 7.28 us -> 7.8 us
    all_to_all x1, waiting for transfers between devices: 3.39 us -> 2.48 us  [everyones(): return lax.all_to_all(packed, axes, 0, 0).astype(f32)]
    pallas_call x1, Pallas kernels: 1.68 us -> 0.83 us  [on_device(): call(functools.partial(totals_kernel, len(stages) - 1, radix), (struct((t...]
    pallas_call x3, Pallas kernels: 2.14 us -> 2.98 us  [the longest x1 1.86 us: on_device(): call(input_kernel, (struct((tok, channels), bf16), struct((H, tok)), stru...]
    ppermute x5, waiting for transfers between devices: 6.1 us -> 5.42 us  [from_groups(): got.append(lax.ppermute(message, 'ctx', route))]
    pallas_call x1, Pallas kernels: 1.59 us -> 2.19 us  [on_device(): call(local_kernel, (struct((tok, channels)), struct((3 * HEAD_ROWS, tok))...]
  transfers between devices with their start and end apart: 8 -> 8, of which waited for: 5 -> 5; matrix products, arithmetic and copies ran while one was open for 0% -> 0% of each run, Pallas kernels for 12% -> 16%
where the time goes in v7:
time: 36.6 us; the launch traced here: 36.4 us
  starting transfers between devices  16.3 us (45%)
  waiting for transfers between devices  9.74 us (27%)
  Pallas kernels  7.8 us (21%)
  local copies, waits for them, and re-layouts  1.55 us (4%)
  between operations  0.87 us (2%)
    all_to_all x1, starting transfers between devices, everyones(): return lax.all_to_all(packed, axes, 0, 0).astype(f32)  6.1 us
    ppermute x5, waiting for transfers between devices, from_groups(): got.append(lax.ppermute(message, 'ctx', route))  5.42 us
    ppermute x1, starting transfers between devices, on_device(): lax.ppermute(spill, 'ctx', [((i + 1) % slabs, i) for i in range(slabs)])  4.21 us
    ppermute x5, starting transfers between devices, from_groups(): got.append(lax.ppermute(message, 'ctx', route))  3.97 us
    all_to_all x1, waiting for transfers between devices, everyones(): return lax.all_to_all(packed, axes, 0, 0).astype(f32)  2.48 us
    pallas_call x1, Pallas kernels, on_device(): call(local_kernel, (struct((tok, channels)), struct((3 * HEAD_ROWS, tok))...  2.19 us
    ppermute x1, starting transfers between devices, on_device(): lax.ppermute(early_raw[tok - HALO_ROWS:], 'ctx', [(i, (i + 1) % slabs) fo...  2.04 us
    pallas_call x1, Pallas kernels, on_device(): call(input_kernel, (struct((tok, channels), bf16), struct((H, tok)), stru...  1.86 us
  transfers between devices with their start and end apart: 8, of which 5 were waited for; matrix products, arithmetic and copies ran while one was open for 0% of the time, Pallas kernels for 16%

profile of v7, /device:TPU:1, one launch (start us, length us, event | category | flops | bytes accessed | tf_op | source)
XLA Modules:
  0.0 36.4 jit_solution(13857772291239032680)
XLA Ops:
  0.6 0.0 copy-start.5
  0.7 0.5 %copy-done.5 = f32[4]{0:T(128)S(1)} copy-done((f32[4]{0:T(128)S(1)}, f32[4]{0:T(128)}, u32[]{:S(2)}) %copy-start.5) | copy-done | bytes 40
  1.3 0.0 copy-done.4
  1.3 0.0 copy-done.3
  1.3 0.0 copy-done.2
  1.4 0.1 shard_map.136
  1.4 0.2 copy-done
  1.7 2.0 %collective-permute-start.1 = (bf16[16,512]{1,0:T(8,128)(2,1)S(1)}, bf16[16,512]{1,0:T(8,128)(2,1)S(1)}, u32[]{:S(2)}, u32[]{:S(2)}) collective-permute-start(bf16[16,512]{1,0:T(8,128)(2,1)S(1)} %slice.3), channel_id=1, source_target_pairs={{0,4},{4,8},{8,12},{12,16},{16,20},{20,24},{24,28},{28,0},{1,5},{5... | collective-permute-start | bytes 49160 | tf_op jit(solution)/shard_map/ppermute | solution.py:580
  3.7 1.1 %shard_map.137 = (f32[256,512]{1,0:T(8,128)S(1)}, bf16[256,512]{1,0:T(8,128)(2,1)S(1)}, bf16[256,512]{1,0:T(8,128)(2,1)S(1)}, bf16[256,512]{1,0:T(8,128)(2,1)S(1...) custom-call(bf16[256,512]{1,0:T(8,128)(2,1)S(1)} %bitcast.18, ...), custom_call_target="tpu_custom_call" | custom-call | flops 99999997952 | bytes 1048576 | tf_op jit(solution)/shard_map/pallas_call | solution.py:592
  4.8 1.3 %collective-permute-start = (f16[264,256]{1,0:T(8,128)(2,1)S(1)}, f16[264,256]{1,0:T(8,128)(2,1)S(1)}, u32[]{:S(2)}, u32[]{:S(2)}) collective-permute-start(f16[264,256]{1,0:T(8,128)(2,1)S(1)} %convert_element_type.30), channel_id=1, source_target_pairs={{0,4},{4,0},{8,12},{12,8},{16,20},{20,16},{24,28},{28,24},{1,5},{5... | collective-permute-start | bytes 405512 | tf_op jit(solution)/shard_map/ppermute | solution.py:541
  6.1 1.8 %collective-permute-done.1.halo_ref = bf16[16,512]{1,0:T(8,128)(2,1)S(1)} collective-permute-done((bf16[16,512]{1,0:T(8,128)(2,1)S(1)}, bf16[16,512]{1,0:T(8,128)(2,1)S(1)}, u32[]{:S(2)}, u32[]{:S(2)}) %collective-permute-start.1) | collective-permute-done | bytes 16416 | tf_op jit(solution)/shard_map/ppermute | solution.py:580
  8.0 0.1 shard_map.138
  8.0 0.1 collective-permute-start.2
  8.1 2.2 %shard_map.139 = (f32[256,512]{1,0:T(8,128)S(1)}, f32[24,256]{1,0:T(8,128)S(1)}, f32[256,1024]{1,0:T(8,128)S(1)}, f32[768,512]{1,0:T(8,128)S(1)}, f32[256,512]{1...) custom-call(bf16[256,512]{1,0:T(8,128)(2,1)S(1)} %get-tuple-element., ...), custom_call_target="tpu_custom_call", output_to_operand_aliasing={{5}: (11, {}), {6}: (12, {})} | custom-call | flops 99999997952 | bytes 1048576 | tf_op jit(solution)/shard_map/pallas_call | solution.py:614
  10.3 0.0 collective-permute-done
  10.4 0.5 %collective-permute-done.2.refs_1_ = bf16[16,768]{1,0:T(8,128)(2,1)S(1)} collective-permute-done((bf16[16,768]{1,0:T(8,128)(2,1)S(1)}, bf16[16,768]{1,0:T(8,128)(2,1)S(1)}, u32[]{:S(2)}, u32[]{:S(2)}) %collective-permute-start.2) | collective-permute-done | bytes 24608 | tf_op jit(solution)/shard_map/ppermute | solution.py:541
  10.8 0.3 shard_map.140
  11.2 2.1 %collective-permute-start.5 = (f16[136,256]{1,0:T(8,128)(2,1)S(1)}, f16[136,256]{1,0:T(8,128)(2,1)S(1)}, u32[]{:S(2)}, u32[]{:S(2)}) collective-permute-start(f16[136,256]{1,0:T(8,128)(2,1)S(1)} %convert_element_type.36), channel_id=1, source_target_pairs={{0,24},{4,28},{8,0},{12,4},{16,8},{20,12},{24,16},{28,20},{1,25},{... | collective-permute-start | bytes 208904 | tf_op jit(solution)/shard_map/ppermute | solution.py:541
  13.3 0.0 collective-permute-start.4
  13.3 0.5 %collective-permute-start.3 = (f16[136,256]{1,0:T(8,128)(2,1)S(1)}, f16[136,256]{1,0:T(8,128)(2,1)S(1)}, u32[]{:S(2)}, u32[]{:S(2)}) collective-permute-start(f16[136,256]{1,0:T(8,128)(2,1)S(1)} %convert_element_type.32), channel_id=1, source_target_pairs={{0,8},{4,12},{8,16},{12,20},{16,24},{20,28},{24,0},{28,4},{1,9},{5... | collective-permute-start | bytes 208904 | tf_op jit(solution)/shard_map/ppermute | solution.py:541
  13.8 0.9 %collective-permute-done.5 = f16[136,256]{1,0:T(8,128)(2,1)S(1)} collective-permute-done((f16[136,256]{1,0:T(8,128)(2,1)S(1)}, f16[136,256]{1,0:T(8,128)(2,1)S(1)}, u32[]{:S(2)}, u32[]{:S(2)}) %collective-permute-start.5) | collective-permute-done | bytes 69664 | tf_op jit(solution)/shard_map/ppermute | solution.py:541
  14.6 4.1 %collective-permute-done.4 = f16[136,256]{1,0:T(8,128)(2,1)S(1)} collective-permute-done((f16[136,256]{1,0:T(8,128)(2,1)S(1)}, f16[136,256]{1,0:T(8,128)(2,1)S(1)}, u32[]{:S(2)}, u32[]{:S(2)}) %collective-permute-start.4) | collective-permute-done | bytes 69664 | tf_op jit(solution)/shard_map/ppermute | solution.py:541
  18.8 0.0 collective-permute-done.3
  18.8 0.8 %shard_map.141 = (f32[256,512]{1,0:T(8,128)S(1)}, f32[264,512]{1,0:T(8,128)S(1)}, f32[24,128]{1,0:T(8,128)S(1)}, f32[8,512]{1,0:T(8,128)S(1)}) custom-call(bf16[256,512]{1,0:T(8,128)(2,1)S(1)} %bitcast.20, f32[768,512]{1,0:T(8,128)S(1)} %get-tuple-element.82.moved_ref, bf16[256,512]{1,0:T(8,128)(2,1)S(1)} %get-tuple-element.70.xbc_ref, ...), custom_call_target="tpu_custom_call" | custom-call | flops 200000000 | bytes 1048576 | tf_op jit(solution)/shard_map/pallas_call | solution.py:645
  19.7 0.7 %broadcast_in_dim.30 = f16[32,24,128]{2,1,0:T(8,128)(2,1)} broadcast(f16[24,128]{1,0:T(8,128)(2,1)S(1)} %convert_element_type.38), dimensions={1,2} | broadcast | bytes 202752 | tf_op jit(solution)/shard_map/broadcast_in_dim | solution.py:561
  20.4 6.1 %all-to-all-start = ((f16[32,24,128]{2,1,0:T(8,128)(2,1)}), f16[32,24,128]{2,1,0:T(8,128)(2,1)S(1)}, u32[]{:S(2)}, u32[]{:S(2)}) async-start(f16[32,24,128]{2,1,0:T(8,128)(2,1)} %broadcast_in_dim.30), calls=%async_computation | async-start | bytes 393216 | tf_op jit(solution)/shard_map/all_to_all | solution.py:562
  26.5 4.2 %collective-permute-start.6 = (f32[8,512]{1,0:T(8,128)S(1)}, f32[8,512]{1,0:T(8,128)S(1)}, u32[]{:S(2)}, u32[]{:S(2)}) collective-permute-start(f32[8,512]{1,0:T(8,128)S(1)} %get-tuple-element.100), channel_id=1, source_target_pairs={{4,0},{8,4},{12,8},{16,12},{20,16},{24,20},{28,24},{0,28},{5,1},{9... | collective-permute-start | bytes 49160 | tf_op jit(solution)/shard_map/ppermute | solution.py:653
  30.7 1.9 %shard_map.142 = (bf16[256,512]{1,0:T(8,128)(2,1)}, f32[4,256]{1,0:T(4,128)}, f32[16,512]{1,0:T(8,128)S(1)}) custom-call(f32[256,512]{1,0:T(8,128)S(1)} %get-tuple-element.97.conv_ref, f32[4,512]{1,0:T(4,128)S(1)} %copy-done.1, f32[264,512]{1,0:T(8,128)S(1)} %get-tuple-element.98.states_ref, bf16[256,512]{1,0:T(8,128)(2,1)S(1)} %get-tuple-element.70.xbc_ref, ...), custom_call_target="tpu_custom_call" | custom-call | flops 1000000 | bytes 1048576 | tf_op jit(solution)/shard_map/pallas_call | solution.py:660
  32.5 0.0 collective-permute-done.6.spilled_ref
  32.6 0.7 %shard_map.143 = bf16[256,512]{1,0:T(8,128)(2,1)} custom-call(f32[16,512]{1,0:T(8,128)S(1)} %get-tuple-element.99.end_ref, f32[8,512]{1,0:T(8,128)S(1)} %collective-permute-done.6.spilled_ref, f32[32,256]{1,0:T(8,128)S(1)} %get-tuple-element.66.places_ref, bf16[256,512]{1,0:T(8,128)(2,1)} %get-tuple-element.101.main_hbm), custom_call_target="tpu_custom_call", output_to_operand_aliasing={{}: (3, {})} | custom-call | bytes 1048576 | tf_op jit(solution)/shard_map/pallas_call | solution.py:668
  33.2 2.5 %all-to-all-done = f16[32,24,128]{2,1,0:T(8,128)(2,1)S(1)} async-done(((f16[32,24,128]{2,1,0:T(8,128)(2,1)}), f16[32,24,128]{2,1,0:T(8,128)(2,1)S(1)}, u32[]{:S(2)}, u32[]{:S(2)}) %all-to-all-start) | async-done | bytes 196640 | tf_op jit(solution)/shard_map/all_to_all | solution.py:562
  35.7 0.7 %shard_map.144 = (f32[4,512]{1,0:T(4,128)}, f32[1,512]{1,0:T(1,128)}, f32[1,4]{1,0:T(1,128)}, f32[1,4]{1,0:T(1,128)}, f32[1,4]{1,0:T(1,128)}) custom-call(f32[32,24,128]{2,1,0:T(8,128)S(1)} %convert_element_type.39.parts_ref), custom_call_target="tpu_custom_call" | custom-call | bytes 1048576 | tf_op jit(solution)/shard_map/pallas_call | solution.py:677
  (22 shorter events, 0.2 us)
Async XLA Ops:
  0.6 0.7 %copy-start.5 = (f32[4]{0:T(128)S(1)}, f32[4]{0:T(128)}, u32[]{:S(2)}) copy-start(f32[4]{0:T(128)} %param.14) | copy-start | bytes 52
  0.6 0.7 %copy-start.4 = (f32[4]{0:T(128)S(1)}, f32[4]{0:T(128)}, u32[]{:S(2)}) copy-start(f32[4]{0:T(128)} %param.13) | copy-start | bytes 52
  0.7 0.7 %copy-start.3 = (f32[4]{0:T(128)S(1)}, f32[4]{0:T(128)}, u32[]{:S(2)}) copy-start(f32[4]{0:T(128)} %param.12) | copy-start | bytes 52
  0.7 0.7 %copy-start.2 = (f32[512]{0:T(512)S(1)}, f32[512]{0:T(512)}, u32[]{:S(2)}) copy-start(f32[512]{0:T(512)} %param.10) | copy-start | bytes 6148
  0.7 1.0 %copy-start = (bf16[1,256,512]{2,1,0:T(8,128)(2,1)S(1)}, bf16[1,256,512]{2,1,0:T(8,128)(2,1)}, u32[]{:S(2)}) copy-start(bf16[1,256,512]{2,1,0:T(8,128)(2,1)} %param.8) | copy-start | bytes 786436
  0.7 3.0 %copy-start.1 = (f32[4,512]{1,0:T(4,128)S(1)}, f32[4,512]{1,0:T(4,128)}, u32[]{:S(2)}) copy-start(f32[4,512]{1,0:T(4,128)} %weight_ref.7) | copy-start | bytes 24580
  0.7 3.0 %copy-start.6 = (bf16[1,256,256]{2,1,0:T(8,128)(2,1)S(1)}, bf16[1,256,256]{2,1,0:T(8,128)(2,1)}, u32[]{:S(2)}) copy-start(bf16[1,256,256]{2,1,0:T(8,128)(2,1)} %param.15) | copy-start | bytes 393220
  0.7 3.0 %copy-start.7 = (f32[1,256,4]{1,2,0:T(4,128)S(1)}, f32[1,256,4]{1,2,0:T(4,128)}, u32[]{:S(2)}) copy-start(f32[1,256,4]{1,2,0:T(4,128)} %param.11) | copy-start | bytes 12292
  1.7 6.3 %collective-permute-start.1 = (bf16[16,512]{1,0:T(8,128)(2,1)S(1)}, bf16[16,512]{1,0:T(8,128)(2,1)S(1)}, u32[]{:S(2)}, u32[]{:S(2)}) collective-permute-start(bf16[16,512]{1,0:T(8,128)(2,1)S(1)} %slice.3), channel_id=1, source_target_pairs={{0,4},{4,8},{8,12},{12,16},{16,20},{20,24},{24,28},{28,0},{1,5},{5... | collective-permute-start | bytes 49160 | tf_op jit(solution)/shard_map/ppermute | solution.py:580
  4.8 5.5 %collective-permute-start = (f16[264,256]{1,0:T(8,128)(2,1)S(1)}, f16[264,256]{1,0:T(8,128)(2,1)S(1)}, u32[]{:S(2)}, u32[]{:S(2)}) collective-permute-start(f16[264,256]{1,0:T(8,128)(2,1)S(1)} %convert_element_type.30), channel_id=1, source_target_pairs={{0,4},{4,0},{8,12},{12,8},{16,20},{20,16},{24,28},{28,24},{1,5},{5... | collective-permute-start | bytes 405512 | tf_op jit(solution)/shard_map/ppermute | solution.py:541
  8.0 2.8 %collective-permute-start.2 = (bf16[16,768]{1,0:T(8,128)(2,1)S(1)}, bf16[16,768]{1,0:T(8,128)(2,1)S(1)}, u32[]{:S(2)}, u32[]{:S(2)}) collective-permute-start(bf16[16,768]{1,0:T(8,128)(2,1)S(1)} %get-tuple-element.74.factors_ref), channel_id=1, source_target_pairs={{0,4},{4,0},{8,12},{12,8},{16,20},{20,16},{24,28},{28,24},{1,5},{5... | collective-permute-start | bytes 73736 | tf_op jit(solution)/shard_map/ppermute | solution.py:541
  11.2 3.4 %collective-permute-start.5 = (f16[136,256]{1,0:T(8,128)(2,1)S(1)}, f16[136,256]{1,0:T(8,128)(2,1)S(1)}, u32[]{:S(2)}, u32[]{:S(2)}) collective-permute-start(f16[136,256]{1,0:T(8,128)(2,1)S(1)} %convert_element_type.36), channel_id=1, source_target_pairs={{0,24},{4,28},{8,0},{12,4},{16,8},{20,12},{24,16},{28,20},{1,25},{... | collective-permute-start | bytes 208904 | tf_op jit(solution)/shard_map/ppermute | solution.py:541
  13.3 5.5 %collective-permute-start.4 = (f16[136,256]{1,0:T(8,128)(2,1)S(1)}, f16[136,256]{1,0:T(8,128)(2,1)S(1)}, u32[]{:S(2)}, u32[]{:S(2)}) collective-permute-start(f16[136,256]{1,0:T(8,128)(2,1)S(1)} %convert_element_type.34), channel_id=1, source_target_pairs={{0,16},{4,20},{8,24},{12,28},{16,0},{20,4},{24,8},{28,12},{1,17},{... | collective-permute-start | bytes 208904 | tf_op jit(solution)/shard_map/ppermute | solution.py:541
  13.3 5.5 %collective-permute-start.3 = (f16[136,256]{1,0:T(8,128)(2,1)S(1)}, f16[136,256]{1,0:T(8,128)(2,1)S(1)}, u32[]{:S(2)}, u32[]{:S(2)}) collective-permute-start(f16[136,256]{1,0:T(8,128)(2,1)S(1)} %convert_element_type.32), channel_id=1, source_target_pairs={{0,8},{4,12},{8,16},{12,20},{16,24},{20,28},{24,0},{28,4},{1,9},{5... | collective-permute-start | bytes 208904 | tf_op jit(solution)/shard_map/ppermute | solution.py:541
  20.4 15.3 %all-to-all-start = ((f16[32,24,128]{2,1,0:T(8,128)(2,1)}), f16[32,24,128]{2,1,0:T(8,128)(2,1)S(1)}, u32[]{:S(2)}, u32[]{:S(2)}) async-start(f16[32,24,128]{2,1,0:T(8,128)(2,1)} %broadcast_in_dim.30), calls=%async_computation | async-start | bytes 393216 | tf_op jit(solution)/shard_map/all_to_all | solution.py:562
  26.5 6.1 %collective-permute-start.6 = (f32[8,512]{1,0:T(8,128)S(1)}, f32[8,512]{1,0:T(8,128)S(1)}, u32[]{:S(2)}, u32[]{:S(2)}) collective-permute-start(f32[8,512]{1,0:T(8,128)S(1)} %get-tuple-element.100), channel_id=1, source_target_pairs={{4,0},{8,4},{12,8},{16,12},{20,16},{24,20},{28,24},{0,28},{5,1},{9... | collective-permute-start | bytes 49160 | tf_op jit(solution)/shard_map/ppermute | solution.py:653

commit v8 on v7

--- a/solution.py
+++ b/solution.py
@@ -14,8 +14,9 @@
 INNER = H * P_SIZE
 HEAD_ROWS = 8
 TAIL_ROWS = 8
-HALO_ROWS = 16
+HALO_ROWS = 8
 FIX_ROWS = 16
+FACTOR_ROWS = 8
 END_ROWS = 16
 LANE_BLOCKS = (INNER + 2 * N) // 128
 SMALL_ROW = (K + 1) * LANE_BLOCKS
@@ -242,11 +243,11 @@
     scaled = scaled_ref[0:FIX_ROWS].astype(f32)
 
     def placed(low, high):
-        row = iota(low.shape, 0)
-        moved = jnp.concatenate([high[8:], high[:8]], 0)
-        return jnp.where(row < K - 1, low, jnp.where((row >= 8) & (row < 8 + K - 1), moved, 0.0)).astype(bf16)
-
-    zero = jnp.zeros((FIX_ROWS, N), f32)
+        row = iota((FACTOR_ROWS, low.shape[1]), 0)
+        moved = pltpu.roll(high[:FACTOR_ROWS], 4, 0)
+        return jnp.where(row < K - 1, low[:FACTOR_ROWS], jnp.where((row >= 4) & (row < 4 + K - 1), moved, 0.0)).astype(bf16)
+
+    zero = jnp.zeros((FACTOR_ROWS, N), f32)
     factors_ref[:, : 2 * INNER] = placed(weighted, scaled)
     factors_ref[:, 2 * INNER : 2 * INNER + N] = placed(xbc[:, INNER : INNER + N], zero)
     factors_ref[:, 2 * INNER + N :] = placed(zero, xbc[:, INNER + N :])
@@ -604,7 +605,7 @@
         fix_kernel,
         (
             struct((tok, channels)), struct((tok, channels), bf16), struct((tok, 2 * INNER), bf16),
-            struct((FIX_ROWS, 2 * INNER + 2 * N), bf16),
+            struct((FACTOR_ROWS, 2 * INNER + 2 * N), bf16),
         ),
         [VMEM] * 8,
         flops=1_000_000,

time: 36.6 us -> 36.5 us (level)
  no operation moved by 1% of the time
where the time goes in v8:
time: 36.5 us; the launch traced here: 36.2 us
  starting transfers between devices  16.2 us (44%)
  waiting for transfers between devices  9.63 us (26%)
  Pallas kernels  7.8 us (21%)
  local copies, waits for them, and re-layouts  1.55 us (4%)
  between operations  0.87 us (2%)
    all_to_all x1, starting transfers between devices, everyones(): return lax.all_to_all(packed, axes, 0, 0).astype(f32)  6.12 us
    ppermute x5, waiting for transfers between devices, from_groups(): got.append(lax.ppermute(message, 'ctx', route))  5.4 us
    ppermute x1, starting transfers between devices, on_device(): lax.ppermute(spill, 'ctx', [((i + 1) % slabs, i) for i in range(slabs)])  4.21 us
    ppermute x5, starting transfers between devices, from_groups(): got.append(lax.ppermute(message, 'ctx', route))  3.88 us
    all_to_all x1, waiting for transfers between devices, everyones(): return lax.all_to_all(packed, axes, 0, 0).astype(f32)  2.48 us
    pallas_call x1, Pallas kernels, on_device(): call(local_kernel, (struct((tok, channels)), struct((3 * HEAD_ROWS, tok))...  2.2 us
    ppermute x1, starting transfers between devices, on_device(): lax.ppermute(early_raw[tok - HALO_ROWS:], 'ctx', [(i, (i + 1) % slabs) fo...  2.04 us
    pallas_call x1, Pallas kernels, on_device(): call(input_kernel, (struct((tok, channels), bf16), struct((H, tok)), stru...  1.86 us
  transfers between devices with their start and end apart: 8, of which 5 were waited for; matrix products, arithmetic and copies ran while one was open for 0% of the time, Pallas kernels for 16%

profile of v8, /device:TPU:1, one launch (start us, length us, event | category | flops | bytes accessed | tf_op | source)
XLA Modules:
  0.0 36.2 jit_solution(4704969821479323392)
XLA Ops:
  0.7 0.5 %copy-done.5 = f32[4]{0:T(128)S(1)} copy-done((f32[4]{0:T(128)S(1)}, f32[4]{0:T(128)}, u32[]{:S(2)}) %copy-start.5) | copy-done | bytes 40
  1.3 0.0 copy-done.4
  1.3 0.0 copy-done.3
  1.3 0.0 copy-done.2
  1.4 0.1 shard_map.136
  1.4 0.2 copy-done
  1.7 2.0 %collective-permute-start.1 = (bf16[8,512]{1,0:T(8,128)(2,1)S(1)}, bf16[8,512]{1,0:T(8,128)(2,1)S(1)}, u32[]{:S(2)}, u32[]{:S(2)}) collective-permute-start(bf16[8,512]{1,0:T(8,128)(2,1)S(1)} %slice.3), channel_id=1, source_target_pairs={{0,4},{4,8},{8,12},{12,16},{16,20},{20,24},{24,28},{28,0},{1,5},{5... | collective-permute-start | bytes 24584 | tf_op jit(solution)/shard_map/ppermute | solution.py:581
  3.7 0.0 copy-done.1
  3.7 1.1 %shard_map.137 = (f32[256,512]{1,0:T(8,128)S(1)}, bf16[256,512]{1,0:T(8,128)(2,1)S(1)}, bf16[256,512]{1,0:T(8,128)(2,1)S(1)}, bf16[256,512]{1,0:T(8,128)(2,1)S(1...) custom-call(bf16[256,512]{1,0:T(8,128)(2,1)S(1)} %bitcast.18, ...), custom_call_target="tpu_custom_call" | custom-call | flops 99999997952 | bytes 1048576 | tf_op jit(solution)/shard_map/pallas_call | solution.py:593
  4.8 1.3 %collective-permute-start = (f16[264,256]{1,0:T(8,128)(2,1)S(1)}, f16[264,256]{1,0:T(8,128)(2,1)S(1)}, u32[]{:S(2)}, u32[]{:S(2)}) collective-permute-start(f16[264,256]{1,0:T(8,128)(2,1)S(1)} %convert_element_type.30), channel_id=1, source_target_pairs={{0,4},{4,0},{8,12},{12,8},{16,20},{20,16},{24,28},{28,24},{1,5},{5... | collective-permute-start | bytes 405512 | tf_op jit(solution)/shard_map/ppermute | solution.py:542
  6.1 1.7 %collective-permute-done.1.halo_ref = bf16[8,512]{1,0:T(8,128)(2,1)S(1)} collective-permute-done((bf16[8,512]{1,0:T(8,128)(2,1)S(1)}, bf16[8,512]{1,0:T(8,128)(2,1)S(1)}, u32[]{:S(2)}, u32[]{:S(2)}) %collective-permute-start.1) | collective-permute-done | bytes 8224 | tf_op jit(solution)/shard_map/ppermute | solution.py:581
  7.9 0.1 shard_map.138
  8.0 0.1 collective-permute-start.2
  8.0 2.2 %shard_map.139 = (f32[256,512]{1,0:T(8,128)S(1)}, f32[24,256]{1,0:T(8,128)S(1)}, f32[256,1024]{1,0:T(8,128)S(1)}, f32[768,512]{1,0:T(8,128)S(1)}, f32[256,512]{1...) custom-call(bf16[256,512]{1,0:T(8,128)(2,1)S(1)} %get-tuple-element., ...), custom_call_target="tpu_custom_call", output_to_operand_aliasing={{5}: (11, {}), {6}: (12, {})} | custom-call | flops 99999997952 | bytes 1048576 | tf_op jit(solution)/shard_map/pallas_call | solution.py:615
  10.2 0.0 collective-permute-done
  10.3 0.4 %collective-permute-done.2.refs_1_ = bf16[8,768]{1,0:T(8,128)(2,1)S(1)} collective-permute-done((bf16[8,768]{1,0:T(8,128)(2,1)S(1)}, bf16[8,768]{1,0:T(8,128)(2,1)S(1)}, u32[]{:S(2)}, u32[]{:S(2)}) %collective-permute-start.2) | collective-permute-done | bytes 12320 | tf_op jit(solution)/shard_map/ppermute | solution.py:542
  10.6 0.3 shard_map.140
  11.0 2.0 %collective-permute-start.5 = (f16[136,256]{1,0:T(8,128)(2,1)S(1)}, f16[136,256]{1,0:T(8,128)(2,1)S(1)}, u32[]{:S(2)}, u32[]{:S(2)}) collective-permute-start(f16[136,256]{1,0:T(8,128)(2,1)S(1)} %convert_element_type.36), channel_id=1, source_target_pairs={{0,24},{4,28},{8,0},{12,4},{16,8},{20,12},{24,16},{28,20},{1,25},{... | collective-permute-start | bytes 208904 | tf_op jit(solution)/shard_map/ppermute | solution.py:542
  13.0 0.0 collective-permute-start.4
  13.0 0.5 %collective-permute-start.3 = (f16[136,256]{1,0:T(8,128)(2,1)S(1)}, f16[136,256]{1,0:T(8,128)(2,1)S(1)}, u32[]{:S(2)}, u32[]{:S(2)}) collective-permute-start(f16[136,256]{1,0:T(8,128)(2,1)S(1)} %convert_element_type.32), channel_id=1, source_target_pairs={{0,8},{4,12},{8,16},{12,20},{16,24},{20,28},{24,0},{28,4},{1,9},{5... | collective-permute-start | bytes 208904 | tf_op jit(solution)/shard_map/ppermute | solution.py:542
  13.5 0.9 %collective-permute-done.5 = f16[136,256]{1,0:T(8,128)(2,1)S(1)} collective-permute-done((f16[136,256]{1,0:T(8,128)(2,1)S(1)}, f16[136,256]{1,0:T(8,128)(2,1)S(1)}, u32[]{:S(2)}, u32[]{:S(2)}) %collective-permute-start.5) | collective-permute-done | bytes 69664 | tf_op jit(solution)/shard_map/ppermute | solution.py:542
  14.4 4.2 %collective-permute-done.4 = f16[136,256]{1,0:T(8,128)(2,1)S(1)} collective-permute-done((f16[136,256]{1,0:T(8,128)(2,1)S(1)}, f16[136,256]{1,0:T(8,128)(2,1)S(1)}, u32[]{:S(2)}, u32[]{:S(2)}) %collective-permute-start.4) | collective-permute-done | bytes 69664 | tf_op jit(solution)/shard_map/ppermute | solution.py:542
  18.6 0.0 collective-permute-done.3
  18.6 0.8 %shard_map.141 = (f32[256,512]{1,0:T(8,128)S(1)}, f32[264,512]{1,0:T(8,128)S(1)}, f32[24,128]{1,0:T(8,128)S(1)}, f32[8,512]{1,0:T(8,128)S(1)}) custom-call(bf16[256,512]{1,0:T(8,128)(2,1)S(1)} %bitcast.20, f32[768,512]{1,0:T(8,128)S(1)} %get-tuple-element.82.moved_ref, bf16[256,512]{1,0:T(8,128)(2,1)S(1)} %get-tuple-element.70.xbc_ref, ...), custom_call_target="tpu_custom_call" | custom-call | flops 200000000 | bytes 1048576 | tf_op jit(solution)/shard_map/pallas_call | solution.py:646
  19.4 0.7 %broadcast_in_dim.30 = f16[32,24,128]{2,1,0:T(8,128)(2,1)} broadcast(f16[24,128]{1,0:T(8,128)(2,1)S(1)} %convert_element_type.38), dimensions={1,2} | broadcast | bytes 202752 | tf_op jit(solution)/shard_map/broadcast_in_dim | solution.py:562
  20.2 6.1 %all-to-all-start = ((f16[32,24,128]{2,1,0:T(8,128)(2,1)}), f16[32,24,128]{2,1,0:T(8,128)(2,1)S(1)}, u32[]{:S(2)}, u32[]{:S(2)}) async-start(f16[32,24,128]{2,1,0:T(8,128)(2,1)} %broadcast_in_dim.30), calls=%async_computation | async-start | bytes 393216 | tf_op jit(solution)/shard_map/all_to_all | solution.py:563
  26.3 4.2 %collective-permute-start.6 = (f32[8,512]{1,0:T(8,128)S(1)}, f32[8,512]{1,0:T(8,128)S(1)}, u32[]{:S(2)}, u32[]{:S(2)}) collective-permute-start(f32[8,512]{1,0:T(8,128)S(1)} %get-tuple-element.100), channel_id=1, source_target_pairs={{4,0},{8,4},{12,8},{16,12},{20,16},{24,20},{28,24},{0,28},{5,1},{9... | collective-permute-start | bytes 49160 | tf_op jit(solution)/shard_map/ppermute | solution.py:654
  30.5 1.9 %shard_map.142 = (bf16[256,512]{1,0:T(8,128)(2,1)}, f32[4,256]{1,0:T(4,128)}, f32[16,512]{1,0:T(8,128)S(1)}) custom-call(f32[256,512]{1,0:T(8,128)S(1)} %get-tuple-element.97.conv_ref, f32[4,512]{1,0:T(4,128)S(1)} %copy-done.1, f32[264,512]{1,0:T(8,128)S(1)} %get-tuple-element.98.states_ref, bf16[256,512]{1,0:T(8,128)(2,1)S(1)} %get-tuple-element.70.xbc_ref, ...), custom_call_target="tpu_custom_call" | custom-call | flops 1000000 | bytes 1048576 | tf_op jit(solution)/shard_map/pallas_call | solution.py:661
  32.4 0.0 collective-permute-done.6.spilled_ref
  32.4 0.7 %shard_map.143 = bf16[256,512]{1,0:T(8,128)(2,1)} custom-call(f32[16,512]{1,0:T(8,128)S(1)} %get-tuple-element.99.end_ref, f32[8,512]{1,0:T(8,128)S(1)} %collective-permute-done.6.spilled_ref, f32[32,256]{1,0:T(8,128)S(1)} %get-tuple-element.66.places_ref, bf16[256,512]{1,0:T(8,128)(2,1)} %get-tuple-element.101.main_hbm), custom_call_target="tpu_custom_call", output_to_operand_aliasing={{}: (3, {})} | custom-call | bytes 1048576 | tf_op jit(solution)/shard_map/pallas_call | solution.py:669
  33.0 2.5 %all-to-all-done = f16[32,24,128]{2,1,0:T(8,128)(2,1)S(1)} async-done(((f16[32,24,128]{2,1,0:T(8,128)(2,1)}), f16[32,24,128]{2,1,0:T(8,128)(2,1)S(1)}, u32[]{:S(2)}, u32[]{:S(2)}) %all-to-all-start) | async-done | bytes 196640 | tf_op jit(solution)/shard_map/all_to_all | solution.py:563
  35.5 0.7 %shard_map.144 = (f32[4,512]{1,0:T(4,128)}, f32[1,512]{1,0:T(1,128)}, f32[1,4]{1,0:T(1,128)}, f32[1,4]{1,0:T(1,128)}, f32[1,4]{1,0:T(1,128)}) custom-call(f32[32,24,128]{2,1,0:T(8,128)S(1)} %convert_element_type.39.parts_ref), custom_call_target="tpu_custom_call" | custom-call | bytes 1048576 | tf_op jit(solution)/shard_map/pallas_call | solution.py:678
  (22 shorter events, 0.2 us)
Async XLA Ops:
  0.6 0.7 %copy-start.5 = (f32[4]{0:T(128)S(1)}, f32[4]{0:T(128)}, u32[]{:S(2)}) copy-start(f32[4]{0:T(128)} %param.14) | copy-start | bytes 52
  0.6 0.7 %copy-start.4 = (f32[4]{0:T(128)S(1)}, f32[4]{0:T(128)}, u32[]{:S(2)}) copy-start(f32[4]{0:T(128)} %param.13) | copy-start | bytes 52
  0.7 0.7 %copy-start.3 = (f32[4]{0:T(128)S(1)}, f32[4]{0:T(128)}, u32[]{:S(2)}) copy-start(f32[4]{0:T(128)} %param.12) | copy-start | bytes 52
  0.7 0.7 %copy-start.2 = (f32[512]{0:T(512)S(1)}, f32[512]{0:T(512)}, u32[]{:S(2)}) copy-start(f32[512]{0:T(512)} %param.10) | copy-start | bytes 6148
  0.7 1.0 %copy-start = (bf16[1,256,512]{2,1,0:T(8,128)(2,1)S(1)}, bf16[1,256,512]{2,1,0:T(8,128)(2,1)}, u32[]{:S(2)}) copy-start(bf16[1,256,512]{2,1,0:T(8,128)(2,1)} %param.8) | copy-start | bytes 786436
  0.7 3.0 %copy-start.1 = (f32[4,512]{1,0:T(4,128)S(1)}, f32[4,512]{1,0:T(4,128)}, u32[]{:S(2)}) copy-start(f32[4,512]{1,0:T(4,128)} %weight_ref.7) | copy-start | bytes 24580
  0.7 3.0 %copy-start.6 = (bf16[1,256,256]{2,1,0:T(8,128)(2,1)S(1)}, bf16[1,256,256]{2,1,0:T(8,128)(2,1)}, u32[]{:S(2)}) copy-start(bf16[1,256,256]{2,1,0:T(8,128)(2,1)} %param.15) | copy-start | bytes 393220
  0.7 3.0 %copy-start.7 = (f32[1,256,4]{1,2,0:T(4,128)S(1)}, f32[1,256,4]{1,2,0:T(4,128)}, u32[]{:S(2)}) copy-start(f32[1,256,4]{1,2,0:T(4,128)} %param.11) | copy-start | bytes 12292
  1.7 6.2 %collective-permute-start.1 = (bf16[8,512]{1,0:T(8,128)(2,1)S(1)}, bf16[8,512]{1,0:T(8,128)(2,1)S(1)}, u32[]{:S(2)}, u32[]{:S(2)}) collective-permute-start(bf16[8,512]{1,0:T(8,128)(2,1)S(1)} %slice.3), channel_id=1, source_target_pairs={{0,4},{4,8},{8,12},{12,16},{16,20},{20,24},{24,28},{28,0},{1,5},{5... | collective-permute-start | bytes 24584 | tf_op jit(solution)/shard_map/ppermute | solution.py:581
  4.8 5.4 %collective-permute-start = (f16[264,256]{1,0:T(8,128)(2,1)S(1)}, f16[264,256]{1,0:T(8,128)(2,1)S(1)}, u32[]{:S(2)}, u32[]{:S(2)}) collective-permute-start(f16[264,256]{1,0:T(8,128)(2,1)S(1)} %convert_element_type.30), channel_id=1, source_target_pairs={{0,4},{4,0},{8,12},{12,8},{16,20},{20,16},{24,28},{28,24},{1,5},{5... | collective-permute-start | bytes 405512 | tf_op jit(solution)/shard_map/ppermute | solution.py:542
  8.0 2.7 %collective-permute-start.2 = (bf16[8,768]{1,0:T(8,128)(2,1)S(1)}, bf16[8,768]{1,0:T(8,128)(2,1)S(1)}, u32[]{:S(2)}, u32[]{:S(2)}) collective-permute-start(bf16[8,768]{1,0:T(8,128)(2,1)S(1)} %get-tuple-element.74.factors_ref), channel_id=1, source_target_pairs={{0,4},{4,0},{8,12},{12,8},{16,20},{20,16},{24,28},{28,24},{1,5},{5... | collective-permute-start | bytes 36872 | tf_op jit(solution)/shard_map/ppermute | solution.py:542
  11.0 3.4 %collective-permute-start.5 = (f16[136,256]{1,0:T(8,128)(2,1)S(1)}, f16[136,256]{1,0:T(8,128)(2,1)S(1)}, u32[]{:S(2)}, u32[]{:S(2)}) collective-permute-start(f16[136,256]{1,0:T(8,128)(2,1)S(1)} %convert_element_type.36), channel_id=1, source_target_pairs={{0,24},{4,28},{8,0},{12,4},{16,8},{20,12},{24,16},{28,20},{1,25},{... | collective-permute-start | bytes 208904 | tf_op jit(solution)/shard_map/ppermute | solution.py:542
  13.0 5.6 %collective-permute-start.4 = (f16[136,256]{1,0:T(8,128)(2,1)S(1)}, f16[136,256]{1,0:T(8,128)(2,1)S(1)}, u32[]{:S(2)}, u32[]{:S(2)}) collective-permute-start(f16[136,256]{1,0:T(8,128)(2,1)S(1)} %convert_element_type.34), channel_id=1, source_target_pairs={{0,16},{4,20},{8,24},{12,28},{16,0},{20,4},{24,8},{28,12},{1,17},{... | collective-permute-start | bytes 208904 | tf_op jit(solution)/shard_map/ppermute | solution.py:542
  13.0 5.6 %collective-permute-start.3 = (f16[136,256]{1,0:T(8,128)(2,1)S(1)}, f16[136,256]{1,0:T(8,128)(2,1)S(1)}, u32[]{:S(2)}, u32[]{:S(2)}) collective-permute-start(f16[136,256]{1,0:T(8,128)(2,1)S(1)} %convert_element_type.32), channel_id=1, source_target_pairs={{0,8},{4,12},{8,16},{12,20},{16,24},{20,28},{24,0},{28,4},{1,9},{5... | collective-permute-start | bytes 208904 | tf_op jit(solution)/shard_map/ppermute | solution.py:542
  20.2 15.4 %all-to-all-start = ((f16[32,24,128]{2,1,0:T(8,128)(2,1)}), f16[32,24,128]{2,1,0:T(8,128)(2,1)S(1)}, u32[]{:S(2)}, u32[]{:S(2)}) async-start(f16[32,24,128]{2,1,0:T(8,128)(2,1)} %broadcast_in_dim.30), calls=%async_computation | async-start | bytes 393216 | tf_op jit(solution)/shard_map/all_to_all | solution.py:563
  26.3 6.1 %collective-permute-start.6 = (f32[8,512]{1,0:T(8,128)S(1)}, f32[8,512]{1,0:T(8,128)S(1)}, u32[]{:S(2)}, u32[]{:S(2)}) collective-permute-start(f32[8,512]{1,0:T(8,128)S(1)} %get-tuple-element.100), channel_id=1, source_target_pairs={{4,0},{8,4},{12,8},{16,12},{20,16},{24,20},{28,24},{0,28},{5,1},{9... | collective-permute-start | bytes 49160 | tf_op jit(solution)/shard_map/ppermute | solution.py:654

commit v9 on v7

--- a/solution.py
+++ b/solution.py
@@ -65,10 +65,13 @@
     return dot(stacked(rows), head_selector(4 * HEAD_ROWS), 0, 0)
 
 
-def head_sums(x):
-    high, low = split2(x)
+def pieces3(x):
+    return [each.astype(bf16) for each in split3(x)]
+
+
+def head_sums(x, split=split2):
     selector = head_selector(HEAD_ROWS * 2)
-    return (dot(selector, high, 1, 1) + dot(selector, low, 1, 1))[:HEAD_ROWS]
+    return sum(dot(selector, each, 1, 1) for each in split(x))[:HEAD_ROWS]
 
 
 def by_head(ref, width):
@@ -319,7 +322,7 @@
     step_wide = over_channels(step)
     values_f = values.astype(f32)
     cot_f = cot.astype(f32)
-    stepped = split2(values_f * step_wide)
+    stepped = pieces3(values_f * step_wide)
     gram = dot(b_proj, c_proj, 1, 1)
     reached = iota((tok, tok), 0) <= iota((tok, tok), 1)
     pieces = stacked(cum)
@@ -331,10 +334,8 @@
         column = dot(pieces, jnp.where(piece_head == h, 1.0, 0.0).astype(bf16), 0, 0)
         within = jnp.exp(jnp.where(reached, cum[h : h + 1] - column, -1e30))
         cot_h = cot[:, of]
-        high, low = split2(gram * within)
-        grads.append(dot(high, cot_h) + dot(low, cot_h))
-        dmix = dot(stepped[0][:, of], cot_h, 1, 1) + dot(stepped[1][:, of], cot_h, 1, 1)
-        dmix = dmix * within
+        grads.append(sum(dot(each, cot_h) for each in pieces3(gram * within)))
+        dmix = sum(dot(each[:, of], cot_h, 1, 1) for each in stepped) * within
         dgram = dgram + dmix
         sums.append(jnp.sum(dmix * gram, axis=0, keepdims=True))
     grad_stepped = jnp.concatenate(grads, 1)
@@ -347,7 +348,7 @@
     for h in range(H):
         pairs = jnp.where(row == h, sums[h], pairs)
     left, gate, decay_rate = rows_ref[16:24], rows_ref[32:40], rows_ref[40:48]
-    from_values = head_sums(values_f * grad_stepped)
+    from_values = head_sums(values_f * grad_stepped, pieces3)
     skip_rows = head_sums(values_f * cot_f)
     base = pairs - from_values * step
     sums_ref[0:8] = base

time: 36.6 us -> 36.8 us (level)
  transfers between devices with their start and end apart: 8 -> 8, of which waited for: 5 -> 5; matrix products, arithmetic and copies ran while one was open for 0% -> 0% of each run, Pallas kernels for 16% -> 17%
where the time goes in v9:
time: 36.8 us; the launch traced here: 36.6 us
  starting transfers between devices  16.5 us (45%)
  waiting for transfers between devices  9.4 us (26%)
  Pallas kernels  8.14 us (22%)
  local copies, waits for them, and re-layouts  1.55 us (4%)
  between operations  0.87 us (2%)
    all_to_all x1, starting transfers between devices, everyones(): return lax.all_to_all(packed, axes, 0, 0).astype(f32)  6.24 us
    ppermute x5, waiting for transfers between devices, from_groups(): got.append(lax.ppermute(message, 'ctx', route))  5.08 us
    ppermute x1, starting transfers between devices, on_device(): lax.ppermute(spill, 'ctx', [((i + 1) % slabs, i) for i in range(slabs)])  4.21 us
    ppermute x5, starting transfers between devices, from_groups(): got.append(lax.ppermute(message, 'ctx', route))  3.97 us
    pallas_call x1, Pallas kernels, on_device(): call(local_kernel, (struct((tok, channels)), struct((3 * HEAD_ROWS, tok))...  2.53 us
    all_to_all x1, waiting for transfers between devices, everyones(): return lax.all_to_all(packed, axes, 0, 0).astype(f32)  2.48 us
    ppermute x1, starting transfers between devices, on_device(): lax.ppermute(early_raw[tok - HALO_ROWS:], 'ctx', [(i, (i + 1) % slabs) fo...  2.04 us
    pallas_call x1, Pallas kernels, on_device(): call(input_kernel, (struct((tok, channels), bf16), struct((H, tok)), stru...  1.86 us
  transfers between devices with their start and end apart: 8, of which 5 were waited for; matrix products, arithmetic and copies ran while one was open for 0% of the time, Pallas kernels for 17%

profile of v9, /device:TPU:1, one launch (start us, length us, event | category | flops | bytes accessed | tf_op | source)
XLA Modules:
  0.0 36.6 jit_solution(8483027854913330024)
XLA Ops:
  0.6 0.0 copy-start.5
  0.7 0.5 %copy-done.5 = f32[4]{0:T(128)S(1)} copy-done((f32[4]{0:T(128)S(1)}, f32[4]{0:T(128)}, u32[]{:S(2)}) %copy-start.5) | copy-done | bytes 40
  1.3 0.0 copy-done.4
  1.3 0.0 copy-done.3
  1.3 0.0 copy-done.2
  1.4 0.1 shard_map.136
  1.4 0.2 copy-done
  1.7 2.0 %collective-permute-start.1 = (bf16[16,512]{1,0:T(8,128)(2,1)S(1)}, bf16[16,512]{1,0:T(8,128)(2,1)S(1)}, u32[]{:S(2)}, u32[]{:S(2)}) collective-permute-start(bf16[16,512]{1,0:T(8,128)(2,1)S(1)} %slice.3), channel_id=1, source_target_pairs={{0,4},{4,8},{8,12},{12,16},{16,20},{20,24},{24,28},{28,0},{1,5},{5... | collective-permute-start | bytes 49160 | tf_op jit(solution)/shard_map/ppermute | solution.py:581
  3.7 1.1 %shard_map.137 = (f32[256,512]{1,0:T(8,128)S(1)}, bf16[256,512]{1,0:T(8,128)(2,1)S(1)}, bf16[256,512]{1,0:T(8,128)(2,1)S(1)}, bf16[256,512]{1,0:T(8,128)(2,1)S(1...) custom-call(bf16[256,512]{1,0:T(8,128)(2,1)S(1)} %bitcast.18, ...), custom_call_target="tpu_custom_call" | custom-call | flops 99999997952 | bytes 1048576 | tf_op jit(solution)/shard_map/pallas_call | solution.py:593
  4.8 1.3 %collective-permute-start = (f16[264,256]{1,0:T(8,128)(2,1)S(1)}, f16[264,256]{1,0:T(8,128)(2,1)S(1)}, u32[]{:S(2)}, u32[]{:S(2)}) collective-permute-start(f16[264,256]{1,0:T(8,128)(2,1)S(1)} %convert_element_type.30), channel_id=1, source_target_pairs={{0,4},{4,0},{8,12},{12,8},{16,20},{20,16},{24,28},{28,24},{1,5},{5... | collective-permute-start | bytes 405512 | tf_op jit(solution)/shard_map/ppermute | solution.py:542
  6.1 1.8 %collective-permute-done.1.halo_ref = bf16[16,512]{1,0:T(8,128)(2,1)S(1)} collective-permute-done((bf16[16,512]{1,0:T(8,128)(2,1)S(1)}, bf16[16,512]{1,0:T(8,128)(2,1)S(1)}, u32[]{:S(2)}, u32[]{:S(2)}) %collective-permute-start.1) | collective-permute-done | bytes 16416 | tf_op jit(solution)/shard_map/ppermute | solution.py:581
  8.0 0.1 shard_map.138
  8.0 0.1 collective-permute-start.2
  8.1 2.5 %shard_map.139 = (f32[256,512]{1,0:T(8,128)S(1)}, f32[24,256]{1,0:T(8,128)S(1)}, f32[256,1024]{1,0:T(8,128)S(1)}, f32[768,512]{1,0:T(8,128)S(1)}, f32[256,512]{1...) custom-call(bf16[256,512]{1,0:T(8,128)(2,1)S(1)} %get-tuple-element., ...), custom_call_target="tpu_custom_call", output_to_operand_aliasing={{5}: (11, {}), {6}: (12, {})} | custom-call | flops 99999997952 | bytes 1048576 | tf_op jit(solution)/shard_map/pallas_call | solution.py:615
  10.7 0.0 collective-permute-done
  10.7 0.1 collective-permute-done.2.refs_1_
  10.8 0.3 shard_map.140
  11.2 2.1 %collective-permute-start.5 = (f16[136,256]{1,0:T(8,128)(2,1)S(1)}, f16[136,256]{1,0:T(8,128)(2,1)S(1)}, u32[]{:S(2)}, u32[]{:S(2)}) collective-permute-start(f16[136,256]{1,0:T(8,128)(2,1)S(1)} %convert_element_type.36), channel_id=1, source_target_pairs={{0,24},{4,28},{8,0},{12,4},{16,8},{20,12},{24,16},{28,20},{1,25},{... | collective-permute-start | bytes 208904 | tf_op jit(solution)/shard_map/ppermute | solution.py:542
  13.3 0.0 collective-permute-start.4
  13.3 0.5 %collective-permute-start.3 = (f16[136,256]{1,0:T(8,128)(2,1)S(1)}, f16[136,256]{1,0:T(8,128)(2,1)S(1)}, u32[]{:S(2)}, u32[]{:S(2)}) collective-permute-start(f16[136,256]{1,0:T(8,128)(2,1)S(1)} %convert_element_type.32), channel_id=1, source_target_pairs={{0,8},{4,12},{8,16},{12,20},{16,24},{20,28},{24,0},{28,4},{1,9},{5... | collective-permute-start | bytes 208904 | tf_op jit(solution)/shard_map/ppermute | solution.py:542
  13.8 0.9 %collective-permute-done.5 = f16[136,256]{1,0:T(8,128)(2,1)S(1)} collective-permute-done((f16[136,256]{1,0:T(8,128)(2,1)S(1)}, f16[136,256]{1,0:T(8,128)(2,1)S(1)}, u32[]{:S(2)}, u32[]{:S(2)}) %collective-permute-start.5) | collective-permute-done | bytes 69664 | tf_op jit(solution)/shard_map/ppermute | solution.py:542
  14.6 4.1 %collective-permute-done.4 = f16[136,256]{1,0:T(8,128)(2,1)S(1)} collective-permute-done((f16[136,256]{1,0:T(8,128)(2,1)S(1)}, f16[136,256]{1,0:T(8,128)(2,1)S(1)}, u32[]{:S(2)}, u32[]{:S(2)}) %collective-permute-start.4) | collective-permute-done | bytes 69664 | tf_op jit(solution)/shard_map/ppermute | solution.py:542
  18.8 0.0 collective-permute-done.3
  18.8 0.8 %shard_map.141 = (f32[256,512]{1,0:T(8,128)S(1)}, f32[264,512]{1,0:T(8,128)S(1)}, f32[24,128]{1,0:T(8,128)S(1)}, f32[8,512]{1,0:T(8,128)S(1)}) custom-call(bf16[256,512]{1,0:T(8,128)(2,1)S(1)} %bitcast.20, f32[768,512]{1,0:T(8,128)S(1)} %get-tuple-element.82.moved_ref, bf16[256,512]{1,0:T(8,128)(2,1)S(1)} %get-tuple-element.70.xbc_ref, ...), custom_call_target="tpu_custom_call" | custom-call | flops 200000000 | bytes 1048576 | tf_op jit(solution)/shard_map/pallas_call | solution.py:646
  19.7 0.7 %broadcast_in_dim.30 = f16[32,24,128]{2,1,0:T(8,128)(2,1)} broadcast(f16[24,128]{1,0:T(8,128)(2,1)S(1)} %convert_element_type.38), dimensions={1,2} | broadcast | bytes 202752 | tf_op jit(solution)/shard_map/broadcast_in_dim | solution.py:562
  20.4 6.2 %all-to-all-start = ((f16[32,24,128]{2,1,0:T(8,128)(2,1)}), f16[32,24,128]{2,1,0:T(8,128)(2,1)S(1)}, u32[]{:S(2)}, u32[]{:S(2)}) async-start(f16[32,24,128]{2,1,0:T(8,128)(2,1)} %broadcast_in_dim.30), calls=%async_computation | async-start | bytes 393216 | tf_op jit(solution)/shard_map/all_to_all | solution.py:563
  26.6 4.2 %collective-permute-start.6 = (f32[8,512]{1,0:T(8,128)S(1)}, f32[8,512]{1,0:T(8,128)S(1)}, u32[]{:S(2)}, u32[]{:S(2)}) collective-permute-start(f32[8,512]{1,0:T(8,128)S(1)} %get-tuple-element.100), channel_id=1, source_target_pairs={{4,0},{8,4},{12,8},{16,12},{20,16},{24,20},{28,24},{0,28},{5,1},{9... | collective-permute-start | bytes 49160 | tf_op jit(solution)/shard_map/ppermute | solution.py:654
  30.8 1.9 %shard_map.142 = (bf16[256,512]{1,0:T(8,128)(2,1)}, f32[4,256]{1,0:T(4,128)}, f32[16,512]{1,0:T(8,128)S(1)}) custom-call(f32[256,512]{1,0:T(8,128)S(1)} %get-tuple-element.97.conv_ref, f32[4,512]{1,0:T(4,128)S(1)} %copy-done.1, f32[264,512]{1,0:T(8,128)S(1)} %get-tuple-element.98.states_ref, bf16[256,512]{1,0:T(8,128)(2,1)S(1)} %get-tuple-element.70.xbc_ref, ...), custom_call_target="tpu_custom_call" | custom-call | flops 1000000 | bytes 1048576 | tf_op jit(solution)/shard_map/pallas_call | solution.py:661
  32.7 0.0 collective-permute-done.6.spilled_ref
  32.7 0.7 %shard_map.143 = bf16[256,512]{1,0:T(8,128)(2,1)} custom-call(f32[16,512]{1,0:T(8,128)S(1)} %get-tuple-element.99.end_ref, f32[8,512]{1,0:T(8,128)S(1)} %collective-permute-done.6.spilled_ref, f32[32,256]{1,0:T(8,128)S(1)} %get-tuple-element.66.places_ref, bf16[256,512]{1,0:T(8,128)(2,1)} %get-tuple-element.101.main_hbm), custom_call_target="tpu_custom_call", output_to_operand_aliasing={{}: (3, {})} | custom-call | bytes 1048576 | tf_op jit(solution)/shard_map/pallas_call | solution.py:669
  33.4 2.5 %all-to-all-done = f16[32,24,128]{2,1,0:T(8,128)(2,1)S(1)} async-done(((f16[32,24,128]{2,1,0:T(8,128)(2,1)}), f16[32,24,128]{2,1,0:T(8,128)(2,1)S(1)}, u32[]{:S(2)}, u32[]{:S(2)}) %all-to-all-start) | async-done | bytes 196640 | tf_op jit(solution)/shard_map/all_to_all | solution.py:563
  35.9 0.7 %shard_map.144 = (f32[4,512]{1,0:T(4,128)}, f32[1,512]{1,0:T(1,128)}, f32[1,4]{1,0:T(1,128)}, f32[1,4]{1,0:T(1,128)}, f32[1,4]{1,0:T(1,128)}) custom-call(f32[32,24,128]{2,1,0:T(8,128)S(1)} %convert_element_type.39.parts_ref), custom_call_target="tpu_custom_call" | custom-call | bytes 1048576 | tf_op jit(solution)/shard_map/pallas_call | solution.py:678
  (22 shorter events, 0.2 us)
Async XLA Ops:
  0.6 0.7 %copy-start.5 = (f32[4]{0:T(128)S(1)}, f32[4]{0:T(128)}, u32[]{:S(2)}) copy-start(f32[4]{0:T(128)} %param.14) | copy-start | bytes 52
  0.6 0.7 %copy-start.4 = (f32[4]{0:T(128)S(1)}, f32[4]{0:T(128)}, u32[]{:S(2)}) copy-start(f32[4]{0:T(128)} %param.13) | copy-start | bytes 52
  0.7 0.7 %copy-start.3 = (f32[4]{0:T(128)S(1)}, f32[4]{0:T(128)}, u32[]{:S(2)}) copy-start(f32[4]{0:T(128)} %param.12) | copy-start | bytes 52
  0.7 0.7 %copy-start.2 = (f32[512]{0:T(512)S(1)}, f32[512]{0:T(512)}, u32[]{:S(2)}) copy-start(f32[512]{0:T(512)} %param.10) | copy-start | bytes 6148
  0.7 1.0 %copy-start = (bf16[1,256,512]{2,1,0:T(8,128)(2,1)S(1)}, bf16[1,256,512]{2,1,0:T(8,128)(2,1)}, u32[]{:S(2)}) copy-start(bf16[1,256,512]{2,1,0:T(8,128)(2,1)} %param.8) | copy-start | bytes 786436
  0.7 3.0 %copy-start.1 = (f32[4,512]{1,0:T(4,128)S(1)}, f32[4,512]{1,0:T(4,128)}, u32[]{:S(2)}) copy-start(f32[4,512]{1,0:T(4,128)} %weight_ref.7) | copy-start | bytes 24580
  0.7 3.0 %copy-start.6 = (bf16[1,256,256]{2,1,0:T(8,128)(2,1)S(1)}, bf16[1,256,256]{2,1,0:T(8,128)(2,1)}, u32[]{:S(2)}) copy-start(bf16[1,256,256]{2,1,0:T(8,128)(2,1)} %param.15) | copy-start | bytes 393220
  0.7 3.0 %copy-start.7 = (f32[1,256,4]{1,2,0:T(4,128)S(1)}, f32[1,256,4]{1,2,0:T(4,128)}, u32[]{:S(2)}) copy-start(f32[1,256,4]{1,2,0:T(4,128)} %param.11) | copy-start | bytes 12292
  1.7 6.3 %collective-permute-start.1 = (bf16[16,512]{1,0:T(8,128)(2,1)S(1)}, bf16[16,512]{1,0:T(8,128)(2,1)S(1)}, u32[]{:S(2)}, u32[]{:S(2)}) collective-permute-start(bf16[16,512]{1,0:T(8,128)(2,1)S(1)} %slice.3), channel_id=1, source_target_pairs={{0,4},{4,8},{8,12},{12,16},{16,20},{20,24},{24,28},{28,0},{1,5},{5... | collective-permute-start | bytes 49160 | tf_op jit(solution)/shard_map/ppermute | solution.py:581
  4.8 5.9 %collective-permute-start = (f16[264,256]{1,0:T(8,128)(2,1)S(1)}, f16[264,256]{1,0:T(8,128)(2,1)S(1)}, u32[]{:S(2)}, u32[]{:S(2)}) collective-permute-start(f16[264,256]{1,0:T(8,128)(2,1)S(1)} %convert_element_type.30), channel_id=1, source_target_pairs={{0,4},{4,0},{8,12},{12,8},{16,20},{20,16},{24,28},{28,24},{1,5},{5... | collective-permute-start | bytes 405512 | tf_op jit(solution)/shard_map/ppermute | solution.py:542
  8.0 2.8 %collective-permute-start.2 = (bf16[16,768]{1,0:T(8,128)(2,1)S(1)}, bf16[16,768]{1,0:T(8,128)(2,1)S(1)}, u32[]{:S(2)}, u32[]{:S(2)}) collective-permute-start(bf16[16,768]{1,0:T(8,128)(2,1)S(1)} %get-tuple-element.74.factors_ref), channel_id=1, source_target_pairs={{0,4},{4,0},{8,12},{12,8},{16,20},{20,16},{24,28},{28,24},{1,5},{5... | collective-permute-start | bytes 73736 | tf_op jit(solution)/shard_map/ppermute | solution.py:542
  11.2 3.4 %collective-permute-start.5 = (f16[136,256]{1,0:T(8,128)(2,1)S(1)}, f16[136,256]{1,0:T(8,128)(2,1)S(1)}, u32[]{:S(2)}, u32[]{:S(2)}) collective-permute-start(f16[136,256]{1,0:T(8,128)(2,1)S(1)} %convert_element_type.36), channel_id=1, source_target_pairs={{0,24},{4,28},{8,0},{12,4},{16,8},{20,12},{24,16},{28,20},{1,25},{... | collective-permute-start | bytes 208904 | tf_op jit(solution)/shard_map/ppermute | solution.py:542
  13.3 5.5 %collective-permute-start.4 = (f16[136,256]{1,0:T(8,128)(2,1)S(1)}, f16[136,256]{1,0:T(8,128)(2,1)S(1)}, u32[]{:S(2)}, u32[]{:S(2)}) collective-permute-start(f16[136,256]{1,0:T(8,128)(2,1)S(1)} %convert_element_type.34), channel_id=1, source_target_pairs={{0,16},{4,20},{8,24},{12,28},{16,0},{20,4},{24,8},{28,12},{1,17},{... | collective-permute-start | bytes 208904 | tf_op jit(solution)/shard_map/ppermute | solution.py:542
  13.3 5.5 %collective-permute-start.3 = (f16[136,256]{1,0:T(8,128)(2,1)S(1)}, f16[136,256]{1,0:T(8,128)(2,1)S(1)}, u32[]{:S(2)}, u32[]{:S(2)}) collective-permute-start(f16[136,256]{1,0:T(8,128)(2,1)S(1)} %convert_element_type.32), channel_id=1, source_target_pairs={{0,8},{4,12},{8,16},{12,20},{16,24},{20,28},{24,0},{28,4},{1,9},{5... | collective-permute-start | bytes 208904 | tf_op jit(solution)/shard_map/ppermute | solution.py:542
  20.4 15.5 %all-to-all-start = ((f16[32,24,128]{2,1,0:T(8,128)(2,1)}), f16[32,24,128]{2,1,0:T(8,128)(2,1)S(1)}, u32[]{:S(2)}, u32[]{:S(2)}) async-start(f16[32,24,128]{2,1,0:T(8,128)(2,1)} %broadcast_in_dim.30), calls=%async_computation | async-start | bytes 393216 | tf_op jit(solution)/shard_map/all_to_all | solution.py:563
  26.6 6.1 %collective-permute-start.6 = (f32[8,512]{1,0:T(8,128)S(1)}, f32[8,512]{1,0:T(8,128)S(1)}, u32[]{:S(2)}, u32[]{:S(2)}) collective-permute-start(f32[8,512]{1,0:T(8,128)S(1)} %get-tuple-element.100), channel_id=1, source_target_pairs={{4,0},{8,4},{12,8},{16,12},{20,16},{24,20},{28,24},{0,28},{5,1},{9... | collective-permute-start | bytes 49160 | tf_op jit(solution)/shard_map/ppermute | solution.py:654

commit v10 on v9

--- a/solution.py
+++ b/solution.py
@@ -244,20 +244,24 @@
     weighted_ref[0:FIX_ROWS] = weighted.astype(bf16)
     scaled = scaled_ref[0:FIX_ROWS].astype(f32)
 
-    def placed(low, high):
-        row = iota(low.shape, 0)
-        moved = jnp.concatenate([high[8:], high[:8]], 0)
-        return jnp.where(row < K - 1, low, jnp.where((row >= 8) & (row < 8 + K - 1), moved, 0.0)).astype(bf16)
-
-    zero = jnp.zeros((FIX_ROWS, N), f32)
-    factors_ref[:, : 2 * INNER] = placed(weighted, scaled)
-    factors_ref[:, 2 * INNER : 2 * INNER + N] = placed(xbc[:, INNER : INNER + N], zero)
-    factors_ref[:, 2 * INNER + N :] = placed(zero, xbc[:, INNER + N :])
+    def packed(*parts):
+        row = iota((FIX_ROWS, parts[0].shape[1]), 0)
+        out = jnp.zeros(row.shape, f32)
+        for at, part in enumerate(parts):
+            part = pltpu.roll(part, at * (K - 1), 0) if at else part
+            out = jnp.where((row >= at * (K - 1)) & (row < (at + 1) * (K - 1)), part, out)
+        return out.astype(bf16)
+
+    b_proj, c_proj = xbc[:, INNER : INNER + N], xbc[:, INNER + N :]
+    factors_ref[:, :INNER] = packed(weighted[:, :INNER], weighted[:, INNER:], scaled[:, :INNER], scaled[:, INNER:])
+    factors_ref[:, INNER:] = packed(b_proj, b_proj, c_proj, c_proj)
 
 
 def first_parts(factors_ref):
-    both = dot(factors_ref[:, 2 * INNER :], factors_ref[:, : 2 * INNER], 0, 0)
-    both = both[:, :INNER] + both[:, INNER:]
+    rows = factors_ref[:, INNER:].astype(f32)
+    of_state = iota(rows.shape, 0) < 2 * (K - 1)
+    rows = jnp.concatenate([jnp.where(of_state, rows, 0.0), jnp.where(of_state, 0.0, rows)], 1).astype(bf16)
+    both = dot(rows, factors_ref[:, :INNER], 0, 0)
     return both[:N], both[N:]
 
 
@@ -304,15 +308,11 @@
 
 
 def local_kernel(
-    xbc_ref, cot_ref, rows_ref, logs_ref, raw_ref, halo_ref, places_ref, scaled_ref, until_ref, pre_ref, factors_ref, state_in, grad_in,
-    local_ref, sums_ref, weights_ref, moved_ref, slope_ref, state_ref, grad_ref,
+    xbc_ref, cot_ref, rows_ref, logs_ref, factors_ref, state_in, grad_in, local_ref, sums_ref, state_ref, grad_ref,
 ):
     state, grad = first_parts(factors_ref)
     state_ref[...] = state_in[...] + state
     grad_ref[...] = grad_in[...] + grad
-    pre = pre_ref[...]
-    sigmoid = 1.0 / (1.0 + jnp.exp(-pre))
-    slope_ref[...] = sigmoid * (1.0 + pre * (1.0 - sigmoid))
     tok = xbc_ref.shape[0]
     cot = cot_ref[...]
     values = xbc_ref[:, :INNER]
@@ -347,12 +347,24 @@
     pairs = jnp.zeros((HEAD_ROWS, tok), f32)
     for h in range(H):
         pairs = jnp.where(row == h, sums[h], pairs)
-    left, gate, decay_rate = rows_ref[16:24], rows_ref[32:40], rows_ref[40:48]
     from_values = head_sums(values_f * grad_stepped, pieces3)
-    skip_rows = head_sums(values_f * cot_f)
-    base = pairs - from_values * step
-    sums_ref[0:8] = base
+    sums_ref[0:8] = pairs - from_values * step
     sums_ref[8:16] = from_values
+
+
+def weights_kernel(
+    xbc_ref, cot_ref, rows_ref, raw_ref, halo_ref, places_ref, scaled_ref, until_ref, pre_ref, sums_ref, logs_ref,
+    weights_ref, fixed_ref, moved_ref, slope_ref,
+):
+    tok = xbc_ref.shape[0]
+    pre = pre_ref[...]
+    sigmoid = 1.0 / (1.0 + jnp.exp(-pre))
+    slope_ref[...] = sigmoid * (1.0 + pre * (1.0 - sigmoid))
+    values_f = xbc_ref[:, :INNER].astype(f32)
+    cum, step, left = rows_ref[0:8], rows_ref[8:16], rows_ref[16:24]
+    gate, decay_rate = rows_ref[32:40], rows_ref[40:48]
+    base, from_values = sums_ref[0:8], sums_ref[8:16]
+    skip_rows = head_sums(values_f * cot_ref[...].astype(f32))
 
     bias_weight = decay_rate * unstacked(dot(stacked(gate), until_ref[...]))
     cum_last, bias_last = cum[:, tok - 1 : tok], bias_weight[:, tok - 1 : tok]
@@ -371,7 +383,7 @@
         bias_last, cum_last,
     )):
         fixed = jnp.where(lane == i, column, fixed)
-    sums_ref[16:24] = fixed
+    fixed_ref[...] = fixed
     raw = raw_ref[...].astype(f32)
     halo = real_halo(halo_ref, places_ref)
     for back in range(1, K):
@@ -379,7 +391,7 @@
 
 
 def totals_kernel(
-    t, radix, raw_ref, moved_ref, xbc_ref, slope_ref, scaled_ref, weighted_ref, tail_ref, rows_ref, local_ref, sums_ref, weights_ref,
+    t, radix, raw_ref, moved_ref, xbc_ref, slope_ref, scaled_ref, weighted_ref, tail_ref, rows_ref, local_ref, fixed_ref, weights_ref,
     logs_ref, places_ref, weight_ref, *refs
 ):
     got, refs = refs[: radix - 1], refs[radix - 1 :]
@@ -437,7 +449,7 @@
     )
     through = through * rows_ref[24:32][:, tok - 1 : tok]
     states_ref[tok:] = jnp.broadcast_to(through, (HEAD_ROWS, 2 * INNER))
-    fixed = sums_ref[16:24]
+    fixed = fixed_ref[...]
     row, lane = iota((HEAD_ROWS, 128), 0), iota((HEAD_ROWS, 128), 1)
     small = jnp.zeros((HEAD_ROWS, 128), f32)
     for i, column in enumerate((
@@ -605,31 +617,29 @@
         fix_kernel,
         (
             struct((tok, channels)), struct((tok, channels), bf16), struct((tok, 2 * INNER), bf16),
-            struct((FIX_ROWS, 2 * INNER + 2 * N), bf16),
+            struct((FIX_ROWS, INNER + N), bf16),
         ),
         [VMEM] * 8,
         flops=1_000_000,
         aliases={5: 0, 6: 1, 7: 2},
     )(halo, conv_weight, scaled, tail, places, pre, xbc, weighted)
 
-    local, sums, weights, moved, slope, state, grad = call(
+    local, sums, state, grad = call(
         local_kernel,
-        (
-            struct((tok, channels)), struct((3 * HEAD_ROWS, tok)), struct((tok, 4 * INNER)), struct(((K - 1) * tok, channels)),
-            struct((tok, channels)), state_like, state_like,
-        ),
-        [VMEM] * 13,
+        (struct((tok, channels)), struct((2 * HEAD_ROWS, tok)), state_like, state_like),
+        [VMEM] * 7,
         flops=10**11,
-        aliases={11: 5, 12: 6},
-    )(xbc, cot, rows, logs, raw, halo, places, scaled, until, pre, factors, state, grad)
+        aliases={5: 2, 6: 3},
+    )(xbc, cot, rows, logs, factors, state, grad)
 
     carried = ()
     for t, (size, radix) in enumerate(stages):
         got = states_from_groups(outgoing, slabs, size, radix)
         if t == 0:
-            got, local, sums, weights, moved, slope = lax.optimization_barrier((got, local, sums, weights, moved, slope))
+            got, local, sums = lax.optimization_barrier((got, local, sums))
             carried = from_groups([factors], slabs, size, radix)
         if t == len(stages) - 1:
+            got, weights, fixed, moved, slope = lax.optimization_barrier((got, weights, fixed, moved, slope))
             break
         last = last_radix(t + 1)
         outs = (logs_like, state_like, state_like) + (() if last else (state_like, state_like))
@@ -642,6 +652,15 @@
         carried, outgoing = outgoing[:2], outgoing[2:]
         if not last:
             (state, grad), outgoing = outgoing[:2], outgoing[2:]
+        if t == 0:
+            weights, fixed, moved, slope = call(
+                weights_kernel,
+                (
+                    struct((tok, 4 * INNER)), struct((HEAD_ROWS, tok)), struct(((K - 1) * tok, channels)), struct((tok, channels)),
+                ),
+                [VMEM] * 11,
+                flops=10**11,
+            )(xbc, cot, rows, raw, halo, places, scaled, until, pre, sums, logs)
 
     grad_conv, states, packed, spill = call(
         functools.partial(totals_kernel, len(stages) - 1, radix),
@@ -649,7 +668,7 @@
         [VMEM] * (14 + len(got) + len(carried)),
         scratch=[pltpu.VMEM((TOTAL_ROWS, 128), f32)],
         flops=200_000_000,
-    )(raw, moved, xbc, slope, scaled, weighted, tail, rows, local, sums, weights, logs, places, conv_weight, *got, *carried)
+    )(raw, moved, xbc, slope, scaled, weighted, tail, rows, local, fixed, weights, logs, places, conv_weight, *got, *carried)
 
     spilled = lax.ppermute(spill, "ctx", [((i + 1) % slabs, i) for i in range(slabs)])
     if slabs * contexts <= 64:

time: 36.8 us -> 36.4 us (0.989)
  starting transfers between devices: 16.5 us -> 15.7 us
    all_to_all x1, starting transfers between devices: 6.24 us -> 5.84 us  [everyones(): return lax.all_to_all(packed, axes, 0, 0).astype(f32)]
    pallas_call x1 -> x2, Pallas kernels: 2.53 us -> 2.81 us  [the longest x1 1.97 us: on_device(): call(local_kernel, (struct((tok, channels)), struct((2 * HEAD_ROWS, tok))...]
    unnamed x16 -> x26, local copies, waits for them, and re-layouts: 0.84 us -> 0.86 us
  transfers between devices with their start and end apart: 8 -> 8, of which waited for: 5 -> 5; matrix products, arithmetic and copies ran while one was open for 0% -> 0% of each run, Pallas kernels for 17% -> 18%
where the time goes in v10:
time: 36.4 us; the launch traced here: 36.2 us
  starting transfers between devices  15.7 us (43%)
  waiting for transfers between devices  9.4 us (26%)
  Pallas kernels  8.4 us (23%)
  local copies, waits for them, and re-layouts  1.58 us (4%)
  between operations  0.92 us (3%)
    all_to_all x1, starting transfers between devices, everyones(): return lax.all_to_all(packed, axes, 0, 0).astype(f32)  5.84 us
    ppermute x5, waiting for transfers between devices, from_groups(): got.append(lax.ppermute(message, 'ctx', route))  5.1 us
    ppermute x1, starting transfers between devices, on_device(): lax.ppermute(spill, 'ctx', [((i + 1) % slabs, i) for i in range(slabs)])  4.21 us
    ppermute x5, starting transfers between devices, from_groups(): got.append(lax.ppermute(message, 'ctx', route))  3.65 us
    all_to_all x1, waiting for transfers between devices, everyones(): return lax.all_to_all(packed, axes, 0, 0).astype(f32)  2.48 us
    ppermute x1, starting transfers between devices, on_device(): lax.ppermute(early_raw[tok - HALO_ROWS:], 'ctx', [(i, (i + 1) % slabs) fo...  2.04 us
    pallas_call x1, Pallas kernels, on_device(): call(local_kernel, (struct((tok, channels)), struct((2 * HEAD_ROWS, tok))...  1.97 us
    pallas_call x1, Pallas kernels, on_device(): call(input_kernel, (struct((tok, channels), bf16), struct((H, tok)), stru...  1.86 us
  transfers between devices with their start and end apart: 8, of which 5 were waited for; matrix products, arithmetic and copies ran while one was open for 0% of the time, Pallas kernels for 18%

profile of v10, /device:TPU:1, one launch (start us, length us, event | category | flops | bytes accessed | tf_op | source)
XLA Modules:
  0.0 36.2 jit_solution(8862352295359634452)
XLA Ops:
  0.7 0.0 copy-start.5
  0.7 0.5 %copy-done.10 = f32[4]{0:T(128)S(1)} copy-done((f32[4]{0:T(128)S(1)}, f32[4]{0:T(128)}, u32[]{:S(2)}) %copy-start.10) | copy-done | bytes 40
  1.3 0.0 copy-done.9
  1.3 0.0 copy-done.8
  1.3 0.0 copy-done.7
  1.4 0.1 shard_map.136
  1.4 0.2 copy-done.4
  1.7 2.0 %collective-permute-start = (bf16[16,512]{1,0:T(8,128)(2,1)S(1)}, bf16[16,512]{1,0:T(8,128)(2,1)S(1)}, u32[]{:S(2)}, u32[]{:S(2)}) collective-permute-start(bf16[16,512]{1,0:T(8,128)(2,1)S(1)} %slice.3), channel_id=1, source_target_pairs={{0,4},{4,8},{8,12},{12,16},{16,20},{20,24},{24,28},{28,0},{1,5},{5... | collective-permute-start | bytes 49160 | tf_op jit(solution)/shard_map/ppermute | solution.py:593
  3.7 1.1 %shard_map.137 = (f32[256,512]{1,0:T(8,128)S(1)}, bf16[256,512]{1,0:T(8,128)(2,1)S(1)}, bf16[256,512]{1,0:T(8,128)(2,1)S(1)}, bf16[256,512]{1,0:T(8,128)(2,1)S(1...) custom-call(bf16[256,512]{1,0:T(8,128)(2,1)S(1)} %bitcast.18, ...), custom_call_target="tpu_custom_call" | custom-call | flops 99999997952 | bytes 1048576 | tf_op jit(solution)/shard_map/pallas_call | solution.py:605
  4.8 1.3 %collective-permute-start.1 = (f16[264,256]{1,0:T(8,128)(2,1)S(1)}, f16[264,256]{1,0:T(8,128)(2,1)S(1)}, u32[]{:S(2)}, u32[]{:S(2)}) collective-permute-start(f16[264,256]{1,0:T(8,128)(2,1)S(1)} %convert_element_type.30), channel_id=1, source_target_pairs={{0,4},{4,0},{8,12},{12,8},{16,20},{20,16},{24,28},{28,24},{1,5},{5... | collective-permute-start | bytes 405512 | tf_op jit(solution)/shard_map/ppermute | solution.py:554
  6.1 1.8 %collective-permute-done.halo_ref = bf16[16,512]{1,0:T(8,128)(2,1)S(1)} collective-permute-done((bf16[16,512]{1,0:T(8,128)(2,1)S(1)}, bf16[16,512]{1,0:T(8,128)(2,1)S(1)}, u32[]{:S(2)}, u32[]{:S(2)}) %collective-permute-start) | collective-permute-done | bytes 16416 | tf_op jit(solution)/shard_map/ppermute | solution.py:593
  8.0 0.1 shard_map.138
  8.0 0.0 copy-start.2
  8.1 0.1 collective-permute-start.2
  8.1 2.0 %shard_map.139 = (f32[256,512]{1,0:T(8,128)S(1)}, f32[16,256]{1,0:T(8,128)S(1)}, f32[128,256]{1,0:T(8,128)S(1)}, f32[128,256]{1,0:T(8,128)S(1)}) custom-call(bf16[256,512]{1,0:T(8,128)(2,1)S(1)} %get-tuple-element.74.xbc_ref, bf16[256,256]{1,0:T(8,128)(2,1)S(1)} %bitcast.26, ...), custom_call_target="tpu_custom_call", output_to_operand_aliasing={{2}: (5, {}), {3}: (6, {})} | custom-call | flops 99999997952 | bytes 1048576 | tf_op jit(solution)/shard_map/pallas_call | solution.py:627
  10.1 0.0 collective-permute-done.1
  10.2 0.7 %collective-permute-done.2.refs_1_ = bf16[16,384]{1,0:T(8,128)(2,1)S(1)} collective-permute-done((bf16[16,384]{1,0:T(8,128)(2,1)S(1)}, bf16[16,384]{1,0:T(8,128)(2,1)S(1)}, u32[]{:S(2)}, u32[]{:S(2)}) %collective-permute-start.2) | collective-permute-done | bytes 12320 | tf_op jit(solution)/shard_map/ppermute | solution.py:554
  10.8 0.3 shard_map.140
  11.2 1.8 %collective-permute-start.5 = (f16[136,256]{1,0:T(8,128)(2,1)S(1)}, f16[136,256]{1,0:T(8,128)(2,1)S(1)}, u32[]{:S(2)}, u32[]{:S(2)}) collective-permute-start(f16[136,256]{1,0:T(8,128)(2,1)S(1)} %convert_element_type.36), channel_id=1, source_target_pairs={{0,24},{4,28},{8,0},{12,4},{16,8},{20,12},{24,16},{28,20},{1,25},{... | collective-permute-start | bytes 208904 | tf_op jit(solution)/shard_map/ppermute | solution.py:554
  13.0 0.0 collective-permute-start.4
  13.0 0.4 %collective-permute-start.3 = (f16[136,256]{1,0:T(8,128)(2,1)S(1)}, f16[136,256]{1,0:T(8,128)(2,1)S(1)}, u32[]{:S(2)}, u32[]{:S(2)}) collective-permute-start(f16[136,256]{1,0:T(8,128)(2,1)S(1)} %convert_element_type.32), channel_id=1, source_target_pairs={{0,8},{4,12},{8,16},{12,20},{16,24},{20,28},{24,0},{28,4},{1,9},{5... | collective-permute-start | bytes 208904 | tf_op jit(solution)/shard_map/ppermute | solution.py:554
  13.5 0.8 %shard_map.141 = (f32[256,1024]{1,0:T(8,128)S(1)}, f32[8,256]{1,0:T(8,128)S(1)}, f32[768,512]{1,0:T(8,128)S(1)}, f32[256,512]{1,0:T(8,128)S(1)}) custom-call(bf16[256,512]{1,0:T(8,128)(2,1)S(1)} %get-tuple-element.74.xbc_ref, bf16[256,256]{1,0:T(8,128)(2,1)S(1)} %bitcast.27, f32[48,256]{1,0:T(8,128)S(1)} %get-tuple-element.75.rows_ref, ...), custom_call_target="tpu_custom_call" | custom-call | flops 99999997952 | bytes 1048576 | tf_op jit(solution)/shard_map/pallas_call | solution.py:656
  14.3 0.1 collective-permute-done.5
  14.4 4.3 %collective-permute-done.4 = f16[136,256]{1,0:T(8,128)(2,1)S(1)} collective-permute-done((f16[136,256]{1,0:T(8,128)(2,1)S(1)}, f16[136,256]{1,0:T(8,128)(2,1)S(1)}, u32[]{:S(2)}, u32[]{:S(2)}) %collective-permute-start.4) | collective-permute-done | bytes 69664 | tf_op jit(solution)/shard_map/ppermute | solution.py:554
  18.8 0.8 %shard_map.142 = (f32[256,512]{1,0:T(8,128)S(1)}, f32[264,512]{1,0:T(8,128)S(1)}, f32[24,128]{1,0:T(8,128)S(1)}, f32[8,512]{1,0:T(8,128)S(1)}) custom-call(bf16[256,512]{1,0:T(8,128)(2,1)S(1)} %bitcast.20, f32[768,512]{1,0:T(8,128)S(1)} %get-tuple-element.96.moved_ref, bf16[256,512]{1,0:T(8,128)(2,1)S(1)} %get-tuple-element.74.xbc_ref, ...), custom_call_target="tpu_custom_call" | custom-call | flops 200000000 | bytes 1048576 | tf_op jit(solution)/shard_map/pallas_call | solution.py:665
  19.7 0.7 %broadcast_in_dim.30 = f16[32,24,128]{2,1,0:T(8,128)(2,1)} broadcast(f16[24,128]{1,0:T(8,128)(2,1)S(1)} %convert_element_type.38), dimensions={1,2} | broadcast | bytes 202752 | tf_op jit(solution)/shard_map/broadcast_in_dim | solution.py:574
  20.4 5.8 %all-to-all-start = ((f16[32,24,128]{2,1,0:T(8,128)(2,1)}), f16[32,24,128]{2,1,0:T(8,128)(2,1)S(1)}, u32[]{:S(2)}, u32[]{:S(2)}) async-start(f16[32,24,128]{2,1,0:T(8,128)(2,1)} %broadcast_in_dim.30), calls=%async_computation | async-start | bytes 393216 | tf_op jit(solution)/shard_map/all_to_all | solution.py:575
  26.2 4.2 %collective-permute-start.6 = (f32[8,512]{1,0:T(8,128)S(1)}, f32[8,512]{1,0:T(8,128)S(1)}, u32[]{:S(2)}, u32[]{:S(2)}) collective-permute-start(f32[8,512]{1,0:T(8,128)S(1)} %get-tuple-element.110), channel_id=1, source_target_pairs={{4,0},{8,4},{12,8},{16,12},{20,16},{24,20},{28,24},{0,28},{5,1},{9... | collective-permute-start | bytes 49160 | tf_op jit(solution)/shard_map/ppermute | solution.py:673
  30.4 1.9 %shard_map.143 = (bf16[256,512]{1,0:T(8,128)(2,1)}, f32[4,256]{1,0:T(4,128)}, f32[16,512]{1,0:T(8,128)S(1)}) custom-call(f32[256,512]{1,0:T(8,128)S(1)} %get-tuple-element.107.conv_ref, f32[4,512]{1,0:T(4,128)S(1)} %copy-done.6, f32[264,512]{1,0:T(8,128)S(1)} %get-tuple-element.108.states_ref, bf16[256,512]{1,0:T(8,128)(2,1)S(1)} %get-tuple-element.74.xbc_ref, ...), custom_call_target="tpu_custom_call" | custom-call | flops 1000000 | bytes 1048576 | tf_op jit(solution)/shard_map/pallas_call | solution.py:680
  32.3 0.7 %shard_map.144 = bf16[256,512]{1,0:T(8,128)(2,1)} custom-call(f32[16,512]{1,0:T(8,128)S(1)} %get-tuple-element.109.end_ref, f32[8,512]{1,0:T(8,128)S(1)} %collective-permute-done.6.spilled_ref, f32[32,256]{1,0:T(8,128)S(1)} %get-tuple-element.70.places_ref, bf16[256,512]{1,0:T(8,128)(2,1)} %get-tuple-element.111.main_hbm), custom_call_target="tpu_custom_call", output_to_operand_aliasing={{}: (3, {})} | custom-call | bytes 1048576 | tf_op jit(solution)/shard_map/pallas_call | solution.py:688
  33.0 2.5 %all-to-all-done = f16[32,24,128]{2,1,0:T(8,128)(2,1)S(1)} async-done(((f16[32,24,128]{2,1,0:T(8,128)(2,1)}), f16[32,24,128]{2,1,0:T(8,128)(2,1)S(1)}, u32[]{:S(2)}, u32[]{:S(2)}) %all-to-all-start) | async-done | bytes 196640 | tf_op jit(solution)/shard_map/all_to_all | solution.py:575
  35.5 0.7 %shard_map.145 = (f32[4,512]{1,0:T(4,128)}, f32[1,512]{1,0:T(1,128)}, f32[1,4]{1,0:T(1,128)}, f32[1,4]{1,0:T(1,128)}, f32[1,4]{1,0:T(1,128)}) custom-call(f32[32,24,128]{2,1,0:T(8,128)S(1)} %convert_element_type.39.parts_ref), custom_call_target="tpu_custom_call" | custom-call | bytes 1048576 | tf_op jit(solution)/shard_map/pallas_call | solution.py:697
  (33 shorter events, 0.2 us)
Async XLA Ops:
  0.6 0.7 %copy-start.10 = (f32[4]{0:T(128)S(1)}, f32[4]{0:T(128)}, u32[]{:S(2)}) copy-start(f32[4]{0:T(128)} %param.14) | copy-start | bytes 52
  0.6 0.7 %copy-start.9 = (f32[4]{0:T(128)S(1)}, f32[4]{0:T(128)}, u32[]{:S(2)}) copy-start(f32[4]{0:T(128)} %param.13) | copy-start | bytes 52
  0.7 0.7 %copy-start.8 = (f32[4]{0:T(128)S(1)}, f32[4]{0:T(128)}, u32[]{:S(2)}) copy-start(f32[4]{0:T(128)} %param.12) | copy-start | bytes 52
  0.7 0.7 %copy-start.7 = (f32[512]{0:T(512)S(1)}, f32[512]{0:T(512)}, u32[]{:S(2)}) copy-start(f32[512]{0:T(512)} %param.10) | copy-start | bytes 6148
  0.7 1.0 %copy-start.4 = (bf16[1,256,512]{2,1,0:T(8,128)(2,1)S(1)}, bf16[1,256,512]{2,1,0:T(8,128)(2,1)}, u32[]{:S(2)}) copy-start(bf16[1,256,512]{2,1,0:T(8,128)(2,1)} %param.8) | copy-start | bytes 786436
  0.7 3.0 %copy-start.5 = (f32[4,512]{1,0:T(4,128)S(1)}, f32[4,512]{1,0:T(4,128)}, u32[]{:S(2)}) copy-start(f32[4,512]{1,0:T(4,128)} %weight_ref.7) | copy-start | bytes 24580
  0.7 3.0 %copy-start.11 = (bf16[1,256,256]{2,1,0:T(8,128)(2,1)S(1)}, bf16[1,256,256]{2,1,0:T(8,128)(2,1)}, u32[]{:S(2)}) copy-start(bf16[1,256,256]{2,1,0:T(8,128)(2,1)} %param.15) | copy-start | bytes 393220
  0.7 3.0 %copy-start.12 = (f32[1,256,4]{1,2,0:T(4,128)S(1)}, f32[1,256,4]{1,2,0:T(4,128)}, u32[]{:S(2)}) copy-start(f32[1,256,4]{1,2,0:T(4,128)} %param.11) | copy-start | bytes 12292
  1.7 6.3 %collective-permute-start = (bf16[16,512]{1,0:T(8,128)(2,1)S(1)}, bf16[16,512]{1,0:T(8,128)(2,1)S(1)}, u32[]{:S(2)}, u32[]{:S(2)}) collective-permute-start(bf16[16,512]{1,0:T(8,128)(2,1)S(1)} %slice.3), channel_id=1, source_target_pairs={{0,4},{4,8},{8,12},{12,16},{16,20},{20,24},{24,28},{28,0},{1,5},{5... | collective-permute-start | bytes 49160 | tf_op jit(solution)/shard_map/ppermute | solution.py:593
  4.8 3.3 %copy-start = (f32[256,256]{1,0:T(8,128)}, f32[256,256]{1,0:T(8,128)S(1)}, u32[]{:S(2)}) copy-start(f32[256,256]{1,0:T(8,128)S(1)} %get-tuple-element.69.tail_ref) | copy-start | bytes 786436
  4.8 5.3 %collective-permute-start.1 = (f16[264,256]{1,0:T(8,128)(2,1)S(1)}, f16[264,256]{1,0:T(8,128)(2,1)S(1)}, u32[]{:S(2)}, u32[]{:S(2)}) collective-permute-start(f16[264,256]{1,0:T(8,128)(2,1)S(1)} %convert_element_type.30), channel_id=1, source_target_pairs={{0,4},{4,0},{8,12},{12,8},{16,20},{20,16},{24,28},{28,24},{1,5},{5... | collective-permute-start | bytes 405512 | tf_op jit(solution)/shard_map/ppermute | solution.py:554
  8.0 2.1 %copy-start.2 = (bf16[256,512]{1,0:T(8,128)(2,1)}, bf16[256,512]{1,0:T(8,128)(2,1)S(1)}, u32[]{:S(2)}) copy-start(bf16[256,512]{1,0:T(8,128)(2,1)S(1)} %get-tuple-element.98.weighted_ref) | copy-start | bytes 786436
  8.1 2.8 %collective-permute-start.2 = (bf16[16,384]{1,0:T(8,128)(2,1)S(1)}, bf16[16,384]{1,0:T(8,128)(2,1)S(1)}, u32[]{:S(2)}, u32[]{:S(2)}) collective-permute-start(bf16[16,384]{1,0:T(8,128)(2,1)S(1)} %get-tuple-element.77.factors_ref), channel_id=1, source_target_pairs={{0,4},{4,0},{8,12},{12,8},{16,20},{20,16},{24,28},{28,24},{1,5},{5... | collective-permute-start | bytes 36872 | tf_op jit(solution)/shard_map/ppermute | solution.py:554
  11.2 3.2 %collective-permute-start.5 = (f16[136,256]{1,0:T(8,128)(2,1)S(1)}, f16[136,256]{1,0:T(8,128)(2,1)S(1)}, u32[]{:S(2)}, u32[]{:S(2)}) collective-permute-start(f16[136,256]{1,0:T(8,128)(2,1)S(1)} %convert_element_type.36), channel_id=1, source_target_pairs={{0,24},{4,28},{8,0},{12,4},{16,8},{20,12},{24,16},{28,20},{1,25},{... | collective-permute-start | bytes 208904 | tf_op jit(solution)/shard_map/ppermute | solution.py:554
  13.0 5.7 %collective-permute-start.4 = (f16[136,256]{1,0:T(8,128)(2,1)S(1)}, f16[136,256]{1,0:T(8,128)(2,1)S(1)}, u32[]{:S(2)}, u32[]{:S(2)}) collective-permute-start(f16[136,256]{1,0:T(8,128)(2,1)S(1)} %convert_element_type.34), channel_id=1, source_target_pairs={{0,16},{4,20},{8,24},{12,28},{16,0},{20,4},{24,8},{28,12},{1,17},{... | collective-permute-start | bytes 208904 | tf_op jit(solution)/shard_map/ppermute | solution.py:554
  13.0 5.7 %collective-permute-start.3 = (f16[136,256]{1,0:T(8,128)(2,1)S(1)}, f16[136,256]{1,0:T(8,128)(2,1)S(1)}, u32[]{:S(2)}, u32[]{:S(2)}) collective-permute-start(f16[136,256]{1,0:T(8,128)(2,1)S(1)} %convert_element_type.32), channel_id=1, source_target_pairs={{0,8},{4,12},{8,16},{12,20},{16,24},{20,28},{24,0},{28,4},{1,9},{5... | collective-permute-start | bytes 208904 | tf_op jit(solution)/shard_map/ppermute | solution.py:554
  13.5 5.3 %copy-start.1 = (f32[256,256]{1,0:T(8,128)S(1)}, f32[256,256]{1,0:T(8,128)}, u32[]{:S(2)}) copy-start(f32[256,256]{1,0:T(8,128)} %copy-done) | copy-start | bytes 786436
  13.5 5.3 %copy-start.3 = (bf16[256,512]{1,0:T(8,128)(2,1)S(1)}, bf16[256,512]{1,0:T(8,128)(2,1)}, u32[]{:S(2)}) copy-start(bf16[256,512]{1,0:T(8,128)(2,1)} %copy-done.2) | copy-start | bytes 786436
  13.5 5.4 %copy-start.6 = (f32[4,512]{1,0:T(4,128)S(1)}, f32[4,512]{1,0:T(4,128)}, u32[]{:S(2)}) copy-start(f32[4,512]{1,0:T(4,128)} %weight_ref.7) | copy-start | bytes 24580
  20.4 15.1 %all-to-all-start = ((f16[32,24,128]{2,1,0:T(8,128)(2,1)}), f16[32,24,128]{2,1,0:T(8,128)(2,1)S(1)}, u32[]{:S(2)}, u32[]{:S(2)}) async-start(f16[32,24,128]{2,1,0:T(8,128)(2,1)} %broadcast_in_dim.30), calls=%async_computation | async-start | bytes 393216 | tf_op jit(solution)/shard_map/all_to_all | solution.py:575
  26.2 6.1 %collective-permute-start.6 = (f32[8,512]{1,0:T(8,128)S(1)}, f32[8,512]{1,0:T(8,128)S(1)}, u32[]{:S(2)}, u32[]{:S(2)}) collective-permute-start(f32[8,512]{1,0:T(8,128)S(1)} %get-tuple-element.110), channel_id=1, source_target_pairs={{4,0},{8,4},{12,8},{16,12},{20,16},{24,20},{28,24},{0,28},{5,1},{9... | collective-permute-start | bytes 49160 | tf_op jit(solution)/shard_map/ppermute | solution.py:673

commit v11 on v10

--- a/solution.py
+++ b/solution.py
@@ -63,6 +63,10 @@
 
 def over_channels(rows):
     return dot(stacked(rows), head_selector(4 * HEAD_ROWS), 0, 0)
+
+
+def channel_row(column):
+    return jnp.sum(head_selector(HEAD_ROWS * 2)[:HEAD_ROWS].astype(f32) * column, axis=0, keepdims=True)
 
 
 def pieces3(x):
@@ -192,8 +196,8 @@
     rows_ref[40:48] = decay_rate
     tail = over_channels(left * step)
     tail_ref[...] = tail
-    log_total = over_channels(cum)[tok - 1 : tok]
-    skip = over_channels(heads_ref[16:24])[0:1]
+    log_total = channel_row(cum[:, tok - 1 : tok])
+    skip = channel_row(heads_ref[16:24][:, :1])
     row = iota((8, INNER), 0)
     logs_ref[...] = jnp.where(row == 2, log_total, jnp.where(row == 3, skip, 0.0))
     scaled = jnp.concatenate(split2(cot_ref[...].astype(f32) * over_channels(reach)), 1)

time: 36.4 us -> 36.4 us (level)
  no operation moved by 1% of the time
where the time goes in v11:
time: 36.4 us; the launch traced here: 36.2 us
  starting transfers between devices  15.9 us (44%)
  waiting for transfers between devices  9.37 us (26%)
  Pallas kernels  8.3 us (23%)
  local copies, waits for them, and re-layouts  1.58 us (4%)
  between operations  0.92 us (3%)
    all_to_all x1, starting transfers between devices, everyones(): return lax.all_to_all(packed, axes, 0, 0).astype(f32)  5.99 us
    ppermute x5, waiting for transfers between devices, from_groups(): got.append(lax.ppermute(message, 'ctx', route))  4.96 us
    ppermute x1, starting transfers between devices, on_device(): lax.ppermute(spill, 'ctx', [((i + 1) % slabs, i) for i in range(slabs)])  4.21 us
    ppermute x5, starting transfers between devices, from_groups(): got.append(lax.ppermute(message, 'ctx', route))  3.67 us
    all_to_all x1, waiting for transfers between devices, everyones(): return lax.all_to_all(packed, axes, 0, 0).astype(f32)  2.48 us
    ppermute x1, starting transfers between devices, on_device(): lax.ppermute(early_raw[tok - HALO_ROWS:], 'ctx', [(i, (i + 1) % slabs) fo...  2.04 us
    pallas_call x1, Pallas kernels, on_device(): call(local_kernel, (struct((tok, channels)), struct((2 * HEAD_ROWS, tok))...  1.98 us
    ppermute x1, waiting for transfers between devices, on_device(): lax.ppermute(early_raw[tok - HALO_ROWS:], 'ctx', [(i, (i + 1) % slabs) fo...  1.93 us
  transfers between devices with their start and end apart: 8, of which 5 were waited for; matrix products, arithmetic and copies ran while one was open for 0% of the time, Pallas kernels for 18%

profile of v11, /device:TPU:1, one launch (start us, length us, event | category | flops | bytes accessed | tf_op | source)
XLA Modules:
  0.0 36.2 jit_solution(10682277557496369431)
XLA Ops:
  0.7 0.0 copy-start.5
  0.7 0.5 %copy-done.10 = f32[4]{0:T(128)S(1)} copy-done((f32[4]{0:T(128)S(1)}, f32[4]{0:T(128)}, u32[]{:S(2)}) %copy-start.10) | copy-done | bytes 40
  1.3 0.0 copy-done.9
  1.3 0.0 copy-done.8
  1.3 0.0 copy-done.7
  1.4 0.1 shard_map.136
  1.4 0.2 copy-done.4
  1.7 2.0 %collective-permute-start = (bf16[16,512]{1,0:T(8,128)(2,1)S(1)}, bf16[16,512]{1,0:T(8,128)(2,1)S(1)}, u32[]{:S(2)}, u32[]{:S(2)}) collective-permute-start(bf16[16,512]{1,0:T(8,128)(2,1)S(1)} %slice.3), channel_id=1, source_target_pairs={{0,4},{4,8},{8,12},{12,16},{16,20},{20,24},{24,28},{28,0},{1,5},{5... | collective-permute-start | bytes 49160 | tf_op jit(solution)/shard_map/ppermute | solution.py:597
  3.7 1.0 %shard_map.137 = (f32[256,512]{1,0:T(8,128)S(1)}, bf16[256,512]{1,0:T(8,128)(2,1)S(1)}, bf16[256,512]{1,0:T(8,128)(2,1)S(1)}, bf16[256,512]{1,0:T(8,128)(2,1)S(1...) custom-call(bf16[256,512]{1,0:T(8,128)(2,1)S(1)} %bitcast.18, ...), custom_call_target="tpu_custom_call" | custom-call | flops 99999997952 | bytes 1048576 | tf_op jit(solution)/shard_map/pallas_call | solution.py:609
  4.7 1.3 %collective-permute-start.1 = (f16[264,256]{1,0:T(8,128)(2,1)S(1)}, f16[264,256]{1,0:T(8,128)(2,1)S(1)}, u32[]{:S(2)}, u32[]{:S(2)}) collective-permute-start(f16[264,256]{1,0:T(8,128)(2,1)S(1)} %convert_element_type.30), channel_id=1, source_target_pairs={{0,4},{4,0},{8,12},{12,8},{16,20},{20,16},{24,28},{28,24},{1,5},{5... | collective-permute-start | bytes 405512 | tf_op jit(solution)/shard_map/ppermute | solution.py:558
  6.0 1.9 %collective-permute-done.halo_ref = bf16[16,512]{1,0:T(8,128)(2,1)S(1)} collective-permute-done((bf16[16,512]{1,0:T(8,128)(2,1)S(1)}, bf16[16,512]{1,0:T(8,128)(2,1)S(1)}, u32[]{:S(2)}, u32[]{:S(2)}) %collective-permute-start) | collective-permute-done | bytes 16416 | tf_op jit(solution)/shard_map/ppermute | solution.py:597
  8.0 0.1 shard_map.138
  8.1 0.0 copy-start.2
  8.1 0.1 collective-permute-start.2
  8.1 2.0 %shard_map.139 = (f32[256,512]{1,0:T(8,128)S(1)}, f32[16,256]{1,0:T(8,128)S(1)}, f32[128,256]{1,0:T(8,128)S(1)}, f32[128,256]{1,0:T(8,128)S(1)}) custom-call(bf16[256,512]{1,0:T(8,128)(2,1)S(1)} %get-tuple-element.74.xbc_ref, bf16[256,256]{1,0:T(8,128)(2,1)S(1)} %bitcast.26, ...), custom_call_target="tpu_custom_call", output_to_operand_aliasing={{2}: (5, {}), {3}: (6, {})} | custom-call | flops 99999997952 | bytes 1048576 | tf_op jit(solution)/shard_map/pallas_call | solution.py:631
  10.1 0.0 collective-permute-done.1
  10.2 0.6 %collective-permute-done.2.refs_1_ = bf16[16,384]{1,0:T(8,128)(2,1)S(1)} collective-permute-done((bf16[16,384]{1,0:T(8,128)(2,1)S(1)}, bf16[16,384]{1,0:T(8,128)(2,1)S(1)}, u32[]{:S(2)}, u32[]{:S(2)}) %collective-permute-start.2) | collective-permute-done | bytes 12320 | tf_op jit(solution)/shard_map/ppermute | solution.py:558
  10.7 0.3 shard_map.140
  11.1 1.8 %collective-permute-start.5 = (f16[136,256]{1,0:T(8,128)(2,1)S(1)}, f16[136,256]{1,0:T(8,128)(2,1)S(1)}, u32[]{:S(2)}, u32[]{:S(2)}) collective-permute-start(f16[136,256]{1,0:T(8,128)(2,1)S(1)} %convert_element_type.36), channel_id=1, source_target_pairs={{0,24},{4,28},{8,0},{12,4},{16,8},{20,12},{24,16},{28,20},{1,25},{... | collective-permute-start | bytes 208904 | tf_op jit(solution)/shard_map/ppermute | solution.py:558
  12.9 0.0 collective-permute-start.4
  12.9 0.5 %collective-permute-start.3 = (f16[136,256]{1,0:T(8,128)(2,1)S(1)}, f16[136,256]{1,0:T(8,128)(2,1)S(1)}, u32[]{:S(2)}, u32[]{:S(2)}) collective-permute-start(f16[136,256]{1,0:T(8,128)(2,1)S(1)} %convert_element_type.32), channel_id=1, source_target_pairs={{0,8},{4,12},{8,16},{12,20},{16,24},{20,28},{24,0},{28,4},{1,9},{5... | collective-permute-start | bytes 208904 | tf_op jit(solution)/shard_map/ppermute | solution.py:558
  13.4 0.8 %shard_map.141 = (f32[256,1024]{1,0:T(8,128)S(1)}, f32[8,256]{1,0:T(8,128)S(1)}, f32[768,512]{1,0:T(8,128)S(1)}, f32[256,512]{1,0:T(8,128)S(1)}) custom-call(bf16[256,512]{1,0:T(8,128)(2,1)S(1)} %get-tuple-element.74.xbc_ref, bf16[256,256]{1,0:T(8,128)(2,1)S(1)} %bitcast.27, f32[48,256]{1,0:T(8,128)S(1)} %get-tuple-element.75.rows_ref, ...), custom_call_target="tpu_custom_call" | custom-call | flops 99999997952 | bytes 1048576 | tf_op jit(solution)/shard_map/pallas_call | solution.py:660
  14.2 0.1 collective-permute-done.5
  14.3 4.3 %collective-permute-done.4 = f16[136,256]{1,0:T(8,128)(2,1)S(1)} collective-permute-done((f16[136,256]{1,0:T(8,128)(2,1)S(1)}, f16[136,256]{1,0:T(8,128)(2,1)S(1)}, u32[]{:S(2)}, u32[]{:S(2)}) %collective-permute-start.4) | collective-permute-done | bytes 69664 | tf_op jit(solution)/shard_map/ppermute | solution.py:558
  18.7 0.8 %shard_map.142 = (f32[256,512]{1,0:T(8,128)S(1)}, f32[264,512]{1,0:T(8,128)S(1)}, f32[24,128]{1,0:T(8,128)S(1)}, f32[8,512]{1,0:T(8,128)S(1)}) custom-call(bf16[256,512]{1,0:T(8,128)(2,1)S(1)} %bitcast.20, f32[768,512]{1,0:T(8,128)S(1)} %get-tuple-element.96.moved_ref, bf16[256,512]{1,0:T(8,128)(2,1)S(1)} %get-tuple-element.74.xbc_ref, ...), custom_call_target="tpu_custom_call" | custom-call | flops 200000000 | bytes 1048576 | tf_op jit(solution)/shard_map/pallas_call | solution.py:669
  19.6 0.7 %broadcast_in_dim.30 = f16[32,24,128]{2,1,0:T(8,128)(2,1)} broadcast(f16[24,128]{1,0:T(8,128)(2,1)S(1)} %convert_element_type.38), dimensions={1,2} | broadcast | bytes 202752 | tf_op jit(solution)/shard_map/broadcast_in_dim | solution.py:578
  20.3 6.0 %all-to-all-start = ((f16[32,24,128]{2,1,0:T(8,128)(2,1)}), f16[32,24,128]{2,1,0:T(8,128)(2,1)S(1)}, u32[]{:S(2)}, u32[]{:S(2)}) async-start(f16[32,24,128]{2,1,0:T(8,128)(2,1)} %broadcast_in_dim.30), calls=%async_computation | async-start | bytes 393216 | tf_op jit(solution)/shard_map/all_to_all | solution.py:579
  26.3 4.2 %collective-permute-start.6 = (f32[8,512]{1,0:T(8,128)S(1)}, f32[8,512]{1,0:T(8,128)S(1)}, u32[]{:S(2)}, u32[]{:S(2)}) collective-permute-start(f32[8,512]{1,0:T(8,128)S(1)} %get-tuple-element.110), channel_id=1, source_target_pairs={{4,0},{8,4},{12,8},{16,12},{20,16},{24,20},{28,24},{0,28},{5,1},{9... | collective-permute-start | bytes 49160 | tf_op jit(solution)/shard_map/ppermute | solution.py:677
  30.5 1.9 %shard_map.143 = (bf16[256,512]{1,0:T(8,128)(2,1)}, f32[4,256]{1,0:T(4,128)}, f32[16,512]{1,0:T(8,128)S(1)}) custom-call(f32[256,512]{1,0:T(8,128)S(1)} %get-tuple-element.107.conv_ref, f32[4,512]{1,0:T(4,128)S(1)} %copy-done.6, f32[264,512]{1,0:T(8,128)S(1)} %get-tuple-element.108.states_ref, bf16[256,512]{1,0:T(8,128)(2,1)S(1)} %get-tuple-element.74.xbc_ref, ...), custom_call_target="tpu_custom_call" | custom-call | flops 1000000 | bytes 1048576 | tf_op jit(solution)/shard_map/pallas_call | solution.py:684
  32.4 0.7 %shard_map.144 = bf16[256,512]{1,0:T(8,128)(2,1)} custom-call(f32[16,512]{1,0:T(8,128)S(1)} %get-tuple-element.109.end_ref, f32[8,512]{1,0:T(8,128)S(1)} %collective-permute-done.6.spilled_ref, f32[32,256]{1,0:T(8,128)S(1)} %get-tuple-element.70.places_ref, bf16[256,512]{1,0:T(8,128)(2,1)} %get-tuple-element.111.main_hbm), custom_call_target="tpu_custom_call", output_to_operand_aliasing={{}: (3, {})} | custom-call | bytes 1048576 | tf_op jit(solution)/shard_map/pallas_call | solution.py:692
  33.0 2.5 %all-to-all-done = f16[32,24,128]{2,1,0:T(8,128)(2,1)S(1)} async-done(((f16[32,24,128]{2,1,0:T(8,128)(2,1)}), f16[32,24,128]{2,1,0:T(8,128)(2,1)S(1)}, u32[]{:S(2)}, u32[]{:S(2)}) %all-to-all-start) | async-done | bytes 196640 | tf_op jit(solution)/shard_map/all_to_all | solution.py:579
  35.5 0.7 %shard_map.145 = (f32[4,512]{1,0:T(4,128)}, f32[1,512]{1,0:T(1,128)}, f32[1,4]{1,0:T(1,128)}, f32[1,4]{1,0:T(1,128)}, f32[1,4]{1,0:T(1,128)}) custom-call(f32[32,24,128]{2,1,0:T(8,128)S(1)} %convert_element_type.39.parts_ref), custom_call_target="tpu_custom_call" | custom-call | bytes 1048576 | tf_op jit(solution)/shard_map/pallas_call | solution.py:701
  (33 shorter events, 0.2 us)
Async XLA Ops:
  0.6 0.7 %copy-start.10 = (f32[4]{0:T(128)S(1)}, f32[4]{0:T(128)}, u32[]{:S(2)}) copy-start(f32[4]{0:T(128)} %param.14) | copy-start | bytes 52
  0.6 0.7 %copy-start.9 = (f32[4]{0:T(128)S(1)}, f32[4]{0:T(128)}, u32[]{:S(2)}) copy-start(f32[4]{0:T(128)} %param.13) | copy-start | bytes 52
  0.7 0.7 %copy-start.8 = (f32[4]{0:T(128)S(1)}, f32[4]{0:T(128)}, u32[]{:S(2)}) copy-start(f32[4]{0:T(128)} %param.12) | copy-start | bytes 52
  0.7 0.7 %copy-start.7 = (f32[512]{0:T(512)S(1)}, f32[512]{0:T(512)}, u32[]{:S(2)}) copy-start(f32[512]{0:T(512)} %param.10) | copy-start | bytes 6148
  0.7 1.0 %copy-start.4 = (bf16[1,256,512]{2,1,0:T(8,128)(2,1)S(1)}, bf16[1,256,512]{2,1,0:T(8,128)(2,1)}, u32[]{:S(2)}) copy-start(bf16[1,256,512]{2,1,0:T(8,128)(2,1)} %param.8) | copy-start | bytes 786436
  0.7 3.0 %copy-start.5 = (f32[4,512]{1,0:T(4,128)S(1)}, f32[4,512]{1,0:T(4,128)}, u32[]{:S(2)}) copy-start(f32[4,512]{1,0:T(4,128)} %weight_ref.7) | copy-start | bytes 24580
  0.7 3.0 %copy-start.11 = (bf16[1,256,256]{2,1,0:T(8,128)(2,1)S(1)}, bf16[1,256,256]{2,1,0:T(8,128)(2,1)}, u32[]{:S(2)}) copy-start(bf16[1,256,256]{2,1,0:T(8,128)(2,1)} %param.15) | copy-start | bytes 393220
  0.7 3.0 %copy-start.12 = (f32[1,256,4]{1,2,0:T(4,128)S(1)}, f32[1,256,4]{1,2,0:T(4,128)}, u32[]{:S(2)}) copy-start(f32[1,256,4]{1,2,0:T(4,128)} %param.11) | copy-start | bytes 12292
  1.7 6.3 %collective-permute-start = (bf16[16,512]{1,0:T(8,128)(2,1)S(1)}, bf16[16,512]{1,0:T(8,128)(2,1)S(1)}, u32[]{:S(2)}, u32[]{:S(2)}) collective-permute-start(bf16[16,512]{1,0:T(8,128)(2,1)S(1)} %slice.3), channel_id=1, source_target_pairs={{0,4},{4,8},{8,12},{12,16},{16,20},{20,24},{24,28},{28,0},{1,5},{5... | collective-permute-start | bytes 49160 | tf_op jit(solution)/shard_map/ppermute | solution.py:597
  4.7 3.4 %copy-start = (f32[256,256]{1,0:T(8,128)}, f32[256,256]{1,0:T(8,128)S(1)}, u32[]{:S(2)}) copy-start(f32[256,256]{1,0:T(8,128)S(1)} %get-tuple-element.69.tail_ref) | copy-start | bytes 786436
  4.7 5.4 %collective-permute-start.1 = (f16[264,256]{1,0:T(8,128)(2,1)S(1)}, f16[264,256]{1,0:T(8,128)(2,1)S(1)}, u32[]{:S(2)}, u32[]{:S(2)}) collective-permute-start(f16[264,256]{1,0:T(8,128)(2,1)S(1)} %convert_element_type.30), channel_id=1, source_target_pairs={{0,4},{4,0},{8,12},{12,8},{16,20},{20,16},{24,28},{28,24},{1,5},{5... | collective-permute-start | bytes 405512 | tf_op jit(solution)/shard_map/ppermute | solution.py:558
  8.1 2.1 %copy-start.2 = (bf16[256,512]{1,0:T(8,128)(2,1)}, bf16[256,512]{1,0:T(8,128)(2,1)S(1)}, u32[]{:S(2)}) copy-start(bf16[256,512]{1,0:T(8,128)(2,1)S(1)} %get-tuple-element.98.weighted_ref) | copy-start | bytes 786436
  8.1 2.7 %collective-permute-start.2 = (bf16[16,384]{1,0:T(8,128)(2,1)S(1)}, bf16[16,384]{1,0:T(8,128)(2,1)S(1)}, u32[]{:S(2)}, u32[]{:S(2)}) collective-permute-start(bf16[16,384]{1,0:T(8,128)(2,1)S(1)} %get-tuple-element.77.factors_ref), channel_id=1, source_target_pairs={{0,4},{4,0},{8,12},{12,8},{16,20},{20,16},{24,28},{28,24},{1,5},{5... | collective-permute-start | bytes 36872 | tf_op jit(solution)/shard_map/ppermute | solution.py:558
  11.1 3.2 %collective-permute-start.5 = (f16[136,256]{1,0:T(8,128)(2,1)S(1)}, f16[136,256]{1,0:T(8,128)(2,1)S(1)}, u32[]{:S(2)}, u32[]{:S(2)}) collective-permute-start(f16[136,256]{1,0:T(8,128)(2,1)S(1)} %convert_element_type.36), channel_id=1, source_target_pairs={{0,24},{4,28},{8,0},{12,4},{16,8},{20,12},{24,16},{28,20},{1,25},{... | collective-permute-start | bytes 208904 | tf_op jit(solution)/shard_map/ppermute | solution.py:558
  12.9 5.7 %collective-permute-start.4 = (f16[136,256]{1,0:T(8,128)(2,1)S(1)}, f16[136,256]{1,0:T(8,128)(2,1)S(1)}, u32[]{:S(2)}, u32[]{:S(2)}) collective-permute-start(f16[136,256]{1,0:T(8,128)(2,1)S(1)} %convert_element_type.34), channel_id=1, source_target_pairs={{0,16},{4,20},{8,24},{12,28},{16,0},{20,4},{24,8},{28,12},{1,17},{... | collective-permute-start | bytes 208904 | tf_op jit(solution)/shard_map/ppermute | solution.py:558
  12.9 5.7 %collective-permute-start.3 = (f16[136,256]{1,0:T(8,128)(2,1)S(1)}, f16[136,256]{1,0:T(8,128)(2,1)S(1)}, u32[]{:S(2)}, u32[]{:S(2)}) collective-permute-start(f16[136,256]{1,0:T(8,128)(2,1)S(1)} %convert_element_type.32), channel_id=1, source_target_pairs={{0,8},{4,12},{8,16},{12,20},{16,24},{20,28},{24,0},{28,4},{1,9},{5... | collective-permute-start | bytes 208904 | tf_op jit(solution)/shard_map/ppermute | solution.py:558
  13.4 5.3 %copy-start.1 = (f32[256,256]{1,0:T(8,128)S(1)}, f32[256,256]{1,0:T(8,128)}, u32[]{:S(2)}) copy-start(f32[256,256]{1,0:T(8,128)} %copy-done) | copy-start | bytes 786436
  13.4 5.3 %copy-start.3 = (bf16[256,512]{1,0:T(8,128)(2,1)S(1)}, bf16[256,512]{1,0:T(8,128)(2,1)}, u32[]{:S(2)}) copy-start(bf16[256,512]{1,0:T(8,128)(2,1)} %copy-done.2) | copy-start | bytes 786436
  13.4 5.3 %copy-start.6 = (f32[4,512]{1,0:T(4,128)S(1)}, f32[4,512]{1,0:T(4,128)}, u32[]{:S(2)}) copy-start(f32[4,512]{1,0:T(4,128)} %weight_ref.7) | copy-start | bytes 24580
  20.3 15.2 %all-to-all-start = ((f16[32,24,128]{2,1,0:T(8,128)(2,1)}), f16[32,24,128]{2,1,0:T(8,128)(2,1)S(1)}, u32[]{:S(2)}, u32[]{:S(2)}) async-start(f16[32,24,128]{2,1,0:T(8,128)(2,1)} %broadcast_in_dim.30), calls=%async_computation | async-start | bytes 393216 | tf_op jit(solution)/shard_map/all_to_all | solution.py:579
  26.3 6.1 %collective-permute-start.6 = (f32[8,512]{1,0:T(8,128)S(1)}, f32[8,512]{1,0:T(8,128)S(1)}, u32[]{:S(2)}, u32[]{:S(2)}) collective-permute-start(f32[8,512]{1,0:T(8,128)S(1)} %get-tuple-element.110), channel_id=1, source_target_pairs={{4,0},{8,4},{12,8},{16,12},{20,16},{24,20},{28,24},{0,28},{5,1},{9... | collective-permute-start | bytes 49160 | tf_op jit(solution)/shard_map/ppermute | solution.py:677

commit v12 on v11

--- a/solution.py
+++ b/solution.py
@@ -276,7 +276,7 @@
         prior, after = refs[0][...], refs[1][...]
         refs = refs[2:]
     else:
-        parts, refs = [first_parts(ref) for ref in refs[: radix - 1]], refs[radix - 1 :]
+        parts, refs = [first_parts(ref) for ref in refs[:radix]], refs[radix:]
     logs_out, prior_out, after_out, *refs = refs
     if not next_radix:
         state_out, grad_out, *refs = refs
@@ -287,8 +287,9 @@
     logs = [message_log(ref) for ref in got]
     own_state, own_grad = state_ref[...], grad_ref[...]
     if t == 0:
-        states = [each + part[0] for each, part in zip(states, parts)]
-        grads = [each + part[1] for each, part in zip(grads, parts)]
+        own_state, own_grad = own_state + parts[0][0], own_grad + parts[0][1]
+        states = [each + part[0] for each, part in zip(states, parts[1:])]
+        grads = [each + part[1] for each, part in zip(grads, parts[1:])]
     earlier = [s <= place for s in range(1, radix)]
     later = [s > place for s in range(1, radix)]
     before, log_before = chained(states, logs, earlier)
@@ -312,11 +313,8 @@
 
 
 def local_kernel(
-    xbc_ref, cot_ref, rows_ref, logs_ref, factors_ref, state_in, grad_in, local_ref, sums_ref, state_ref, grad_ref,
+    xbc_ref, cot_ref, rows_ref, logs_ref, merged_logs_ref, local_ref, sums_ref,
 ):
-    state, grad = first_parts(factors_ref)
-    state_ref[...] = state_in[...] + state
-    grad_ref[...] = grad_in[...] + grad
     tok = xbc_ref.shape[0]
     cot = cot_ref[...]
     values = xbc_ref[:, :INNER]
@@ -624,26 +622,18 @@
             struct((FIX_ROWS, INNER + N), bf16),
         ),
         [VMEM] * 8,
-        flops=1_000_000,
+        flops=5 * 10**9,
         aliases={5: 0, 6: 1, 7: 2},
     )(halo, conv_weight, scaled, tail, places, pre, xbc, weighted)
 
-    local, sums, state, grad = call(
-        local_kernel,
-        (struct((tok, channels)), struct((2 * HEAD_ROWS, tok)), state_like, state_like),
-        [VMEM] * 7,
-        flops=10**11,
-        aliases={5: 2, 6: 3},
-    )(xbc, cot, rows, logs, factors, state, grad)
-
+    first_logs = logs
     carried = ()
     for t, (size, radix) in enumerate(stages):
         got = states_from_groups(outgoing, slabs, size, radix)
         if t == 0:
-            got, local, sums = lax.optimization_barrier((got, local, sums))
-            carried = from_groups([factors], slabs, size, radix)
+            carried = [factors] + from_groups([factors], slabs, size, radix)
         if t == len(stages) - 1:
-            got, weights, fixed, moved, slope = lax.optimization_barrier((got, weights, fixed, moved, slope))
+            got, local, weights, fixed, moved, slope = lax.optimization_barrier((got, local, weights, fixed, moved, slope))
             break
         last = last_radix(t + 1)
         outs = (logs_like, state_like, state_like) + (() if last else (state_like, state_like))
@@ -657,6 +647,12 @@
         if not last:
             (state, grad), outgoing = outgoing[:2], outgoing[2:]
         if t == 0:
+            local, sums = call(
+                local_kernel,
+                (struct((tok, channels)), struct((2 * HEAD_ROWS, tok))),
+                [VMEM] * 5,
+                flops=2 * 10**9,
+            )(xbc, cot, rows, first_logs, logs)
             weights, fixed, moved, slope = call(
                 weights_kernel,
                 (

time: 36.4 us -> 36.4 us (level)
    unnamed x26 -> x16, local copies, waits for them, and re-layouts: 0.86 us -> 0.84 us
where the time goes in v12:
time: 36.4 us; the launch traced here: 36.2 us
  starting transfers between devices  15.9 us (44%)
  waiting for transfers between devices  9.35 us (26%)
  Pallas kernels  8.38 us (23%)
  local copies, waits for them, and re-layouts  1.55 us (4%)
  between operations  0.88 us (2%)
    all_to_all x1, starting transfers between devices, everyones(): return lax.all_to_all(packed, axes, 0, 0).astype(f32)  6 us
    ppermute x5, waiting for transfers between devices, from_groups(): got.append(lax.ppermute(message, 'ctx', route))  4.92 us
    ppermute x1, starting transfers between devices, on_device(): lax.ppermute(spill, 'ctx', [((i + 1) % slabs, i) for i in range(slabs)])  4.21 us
    ppermute x5, starting transfers between devices, from_groups(): got.append(lax.ppermute(message, 'ctx', route))  3.67 us
    all_to_all x1, waiting for transfers between devices, everyones(): return lax.all_to_all(packed, axes, 0, 0).astype(f32)  2.48 us
    ppermute x1, starting transfers between devices, on_device(): lax.ppermute(early_raw[tok - HALO_ROWS:], 'ctx', [(i, (i + 1) % slabs) fo...  2.04 us
    pallas_call x1, Pallas kernels, on_device(): call(local_kernel, (struct((tok, channels)), struct((2 * HEAD_ROWS, tok))...  2.01 us
    ppermute x1, waiting for transfers between devices, on_device(): lax.ppermute(early_raw[tok - HALO_ROWS:], 'ctx', [(i, (i + 1) % slabs) fo...  1.94 us
  transfers between devices with their start and end apart: 8, of which 5 were waited for; matrix products, arithmetic and copies ran while one was open for 0% of the time, Pallas kernels for 18%

profile of v12, /device:TPU:1, one launch (start us, length us, event | category | flops | bytes accessed | tf_op | source)
XLA Modules:
  0.0 36.2 jit_solution(5611668917185967883)
XLA Ops:
  0.7 0.5 %copy-done.5 = f32[4]{0:T(128)S(1)} copy-done((f32[4]{0:T(128)S(1)}, f32[4]{0:T(128)}, u32[]{:S(2)}) %copy-start.5) | copy-done | bytes 40
  1.3 0.0 copy-done.4
  1.3 0.0 copy-done.3
  1.3 0.0 copy-done.2
  1.4 0.1 shard_map.136
  1.4 0.2 copy-done
  1.7 2.0 %collective-permute-start.1 = (bf16[16,512]{1,0:T(8,128)(2,1)S(1)}, bf16[16,512]{1,0:T(8,128)(2,1)S(1)}, u32[]{:S(2)}, u32[]{:S(2)}) collective-permute-start(bf16[16,512]{1,0:T(8,128)(2,1)S(1)} %slice.3), channel_id=1, source_target_pairs={{0,4},{4,8},{8,12},{12,16},{16,20},{20,24},{24,28},{28,0},{1,5},{5... | collective-permute-start | bytes 49160 | tf_op jit(solution)/shard_map/ppermute | solution.py:595
  3.7 1.0 %shard_map.137 = (f32[256,512]{1,0:T(8,128)S(1)}, bf16[256,512]{1,0:T(8,128)(2,1)S(1)}, bf16[256,512]{1,0:T(8,128)(2,1)S(1)}, bf16[256,512]{1,0:T(8,128)(2,1)S(1...) custom-call(bf16[256,512]{1,0:T(8,128)(2,1)S(1)} %bitcast.18, ...), custom_call_target="tpu_custom_call" | custom-call | flops 99999997952 | bytes 1048576 | tf_op jit(solution)/shard_map/pallas_call | solution.py:607
  4.7 1.3 %collective-permute-start = (f16[264,256]{1,0:T(8,128)(2,1)S(1)}, f16[264,256]{1,0:T(8,128)(2,1)S(1)}, u32[]{:S(2)}, u32[]{:S(2)}) collective-permute-start(f16[264,256]{1,0:T(8,128)(2,1)S(1)} %convert_element_type.30), channel_id=1, source_target_pairs={{0,4},{4,0},{8,12},{12,8},{16,20},{20,16},{24,28},{28,24},{1,5},{5... | collective-permute-start | bytes 405512 | tf_op jit(solution)/shard_map/ppermute | solution.py:556
  6.0 1.9 %collective-permute-done.1.halo_ref = bf16[16,512]{1,0:T(8,128)(2,1)S(1)} collective-permute-done((bf16[16,512]{1,0:T(8,128)(2,1)S(1)}, bf16[16,512]{1,0:T(8,128)(2,1)S(1)}, u32[]{:S(2)}, u32[]{:S(2)}) %collective-permute-start.1) | collective-permute-done | bytes 16416 | tf_op jit(solution)/shard_map/ppermute | solution.py:595
  8.0 0.1 shard_map.138
  8.0 0.1 collective-permute-start.2
  8.1 1.3 %collective-permute-done = f16[264,256]{1,0:T(8,128)(2,1)S(1)} collective-permute-done((f16[264,256]{1,0:T(8,128)(2,1)S(1)}, f16[264,256]{1,0:T(8,128)(2,1)S(1)}, u32[]{:S(2)}, u32[]{:S(2)}) %collective-permute-start) | collective-permute-done | bytes 135200 | tf_op jit(solution)/shard_map/ppermute | solution.py:556
  9.4 1.3 %collective-permute-done.2.refs_2_ = bf16[16,384]{1,0:T(8,128)(2,1)S(1)} collective-permute-done((bf16[16,384]{1,0:T(8,128)(2,1)S(1)}, bf16[16,384]{1,0:T(8,128)(2,1)S(1)}, u32[]{:S(2)}, u32[]{:S(2)}) %collective-permute-start.2) | collective-permute-done | bytes 12320 | tf_op jit(solution)/shard_map/ppermute | solution.py:556
  10.7 0.3 shard_map.139
  11.1 1.8 %collective-permute-start.5 = (f16[136,256]{1,0:T(8,128)(2,1)S(1)}, f16[136,256]{1,0:T(8,128)(2,1)S(1)}, u32[]{:S(2)}, u32[]{:S(2)}) collective-permute-start(f16[136,256]{1,0:T(8,128)(2,1)S(1)} %convert_element_type.36), channel_id=1, source_target_pairs={{0,24},{4,28},{8,0},{12,4},{16,8},{20,12},{24,16},{28,20},{1,25},{... | collective-permute-start | bytes 208904 | tf_op jit(solution)/shard_map/ppermute | solution.py:556
  12.9 0.0 collective-permute-start.4
  12.9 0.5 %collective-permute-start.3 = (f16[136,256]{1,0:T(8,128)(2,1)S(1)}, f16[136,256]{1,0:T(8,128)(2,1)S(1)}, u32[]{:S(2)}, u32[]{:S(2)}) collective-permute-start(f16[136,256]{1,0:T(8,128)(2,1)S(1)} %convert_element_type.32), channel_id=1, source_target_pairs={{0,8},{4,12},{8,16},{12,20},{16,24},{20,28},{24,0},{28,4},{1,9},{5... | collective-permute-start | bytes 208904 | tf_op jit(solution)/shard_map/ppermute | solution.py:556
  13.4 2.0 %shard_map.140 = (f32[256,512]{1,0:T(8,128)S(1)}, f32[16,256]{1,0:T(8,128)S(1)}) custom-call(bf16[256,512]{1,0:T(8,128)(2,1)S(1)} %get-tuple-element.78.xbc_ref, bf16[256,256]{1,0:T(8,128)(2,1)S(1)} %bitcast.26, f32[48,256]{1,0:T(8,128)S(1)} %get-tuple-element.79.rows_ref, f32[8,256]{1,0:T(8,128)S(1)} %get-tuple-element.65.logs_ref, ...), custom_call_target="tpu_custom_call" | custom-call | flops 2000000000 | bytes 1048576 | tf_op jit(solution)/shard_map/pallas_call | solution.py:650
  15.4 0.9 %shard_map.141 = (f32[256,1024]{1,0:T(8,128)S(1)}, f32[8,256]{1,0:T(8,128)S(1)}, f32[768,512]{1,0:T(8,128)S(1)}, f32[256,512]{1,0:T(8,128)S(1)}) custom-call(bf16[256,512]{1,0:T(8,128)(2,1)S(1)} %get-tuple-element.78.xbc_ref, bf16[256,256]{1,0:T(8,128)(2,1)S(1)} %bitcast.27, f32[48,256]{1,0:T(8,128)S(1)} %get-tuple-element.79.rows_ref, ...), custom_call_target="tpu_custom_call" | custom-call | flops 99999997952 | bytes 1048576 | tf_op jit(solution)/shard_map/pallas_call | solution.py:656
  16.3 0.0 collective-permute-done.5
  16.3 2.4 %collective-permute-done.4 = f16[136,256]{1,0:T(8,128)(2,1)S(1)} collective-permute-done((f16[136,256]{1,0:T(8,128)(2,1)S(1)}, f16[136,256]{1,0:T(8,128)(2,1)S(1)}, u32[]{:S(2)}, u32[]{:S(2)}) %collective-permute-start.4) | collective-permute-done | bytes 69664 | tf_op jit(solution)/shard_map/ppermute | solution.py:556
  18.7 0.0 collective-permute-done.3
  18.7 0.8 %shard_map.142 = (f32[256,512]{1,0:T(8,128)S(1)}, f32[264,512]{1,0:T(8,128)S(1)}, f32[24,128]{1,0:T(8,128)S(1)}, f32[8,512]{1,0:T(8,128)S(1)}) custom-call(bf16[256,512]{1,0:T(8,128)(2,1)S(1)} %bitcast.20, f32[768,512]{1,0:T(8,128)S(1)} %get-tuple-element.88.moved_ref, bf16[256,512]{1,0:T(8,128)(2,1)S(1)} %get-tuple-element.78.xbc_ref, ...), custom_call_target="tpu_custom_call" | custom-call | flops 200000000 | bytes 1048576 | tf_op jit(solution)/shard_map/pallas_call | solution.py:665
  19.5 0.7 %broadcast_in_dim.30 = f16[32,24,128]{2,1,0:T(8,128)(2,1)} broadcast(f16[24,128]{1,0:T(8,128)(2,1)S(1)} %convert_element_type.38), dimensions={1,2} | broadcast | bytes 202752 | tf_op jit(solution)/shard_map/broadcast_in_dim | solution.py:576
  20.2 6.0 %all-to-all-start = ((f16[32,24,128]{2,1,0:T(8,128)(2,1)}), f16[32,24,128]{2,1,0:T(8,128)(2,1)S(1)}, u32[]{:S(2)}, u32[]{:S(2)}) async-start(f16[32,24,128]{2,1,0:T(8,128)(2,1)} %broadcast_in_dim.30), calls=%async_computation | async-start | bytes 393216 | tf_op jit(solution)/shard_map/all_to_all | solution.py:577
  26.3 4.2 %collective-permute-start.6 = (f32[8,512]{1,0:T(8,128)S(1)}, f32[8,512]{1,0:T(8,128)S(1)}, u32[]{:S(2)}, u32[]{:S(2)}) collective-permute-start(f32[8,512]{1,0:T(8,128)S(1)} %get-tuple-element.102), channel_id=1, source_target_pairs={{4,0},{8,4},{12,8},{16,12},{20,16},{24,20},{28,24},{0,28},{5,1},{9... | collective-permute-start | bytes 49160 | tf_op jit(solution)/shard_map/ppermute | solution.py:673
  30.5 1.9 %shard_map.143 = (bf16[256,512]{1,0:T(8,128)(2,1)}, f32[4,256]{1,0:T(4,128)}, f32[16,512]{1,0:T(8,128)S(1)}) custom-call(f32[256,512]{1,0:T(8,128)S(1)} %get-tuple-element.99.conv_ref, f32[4,512]{1,0:T(4,128)S(1)} %copy-done.1, f32[264,512]{1,0:T(8,128)S(1)} %get-tuple-element.100.states_ref, bf16[256,512]{1,0:T(8,128)(2,1)S(1)} %get-tuple-element.78.xbc_ref, ...), custom_call_target="tpu_custom_call" | custom-call | flops 1000000 | bytes 1048576 | tf_op jit(solution)/shard_map/pallas_call | solution.py:680
  32.3 0.0 collective-permute-done.6.spilled_ref
  32.3 0.7 %shard_map.144 = bf16[256,512]{1,0:T(8,128)(2,1)} custom-call(f32[16,512]{1,0:T(8,128)S(1)} %get-tuple-element.101.end_ref, f32[8,512]{1,0:T(8,128)S(1)} %collective-permute-done.6.spilled_ref, f32[32,256]{1,0:T(8,128)S(1)} %get-tuple-element.66.places_ref, bf16[256,512]{1,0:T(8,128)(2,1)} %get-tuple-element.103.main_hbm), custom_call_target="tpu_custom_call", output_to_operand_aliasing={{}: (3, {})} | custom-call | bytes 1048576 | tf_op jit(solution)/shard_map/pallas_call | solution.py:688
  33.0 2.5 %all-to-all-done = f16[32,24,128]{2,1,0:T(8,128)(2,1)S(1)} async-done(((f16[32,24,128]{2,1,0:T(8,128)(2,1)}), f16[32,24,128]{2,1,0:T(8,128)(2,1)S(1)}, u32[]{:S(2)}, u32[]{:S(2)}) %all-to-all-start) | async-done | bytes 196640 | tf_op jit(solution)/shard_map/all_to_all | solution.py:577
  35.5 0.7 %shard_map.145 = (f32[4,512]{1,0:T(4,128)}, f32[1,512]{1,0:T(1,128)}, f32[1,4]{1,0:T(1,128)}, f32[1,4]{1,0:T(1,128)}, f32[1,4]{1,0:T(1,128)}) custom-call(f32[32,24,128]{2,1,0:T(8,128)S(1)} %convert_element_type.39.parts_ref), custom_call_target="tpu_custom_call" | custom-call | bytes 1048576 | tf_op jit(solution)/shard_map/pallas_call | solution.py:697
  (23 shorter events, 0.2 us)
Async XLA Ops:
  0.6 0.7 %copy-start.5 = (f32[4]{0:T(128)S(1)}, f32[4]{0:T(128)}, u32[]{:S(2)}) copy-start(f32[4]{0:T(128)} %param.14) | copy-start | bytes 52
  0.6 0.7 %copy-start.4 = (f32[4]{0:T(128)S(1)}, f32[4]{0:T(128)}, u32[]{:S(2)}) copy-start(f32[4]{0:T(128)} %param.13) | copy-start | bytes 52
  0.7 0.7 %copy-start.3 = (f32[4]{0:T(128)S(1)}, f32[4]{0:T(128)}, u32[]{:S(2)}) copy-start(f32[4]{0:T(128)} %param.12) | copy-start | bytes 52
  0.7 0.7 %copy-start.2 = (f32[512]{0:T(512)S(1)}, f32[512]{0:T(512)}, u32[]{:S(2)}) copy-start(f32[512]{0:T(512)} %param.10) | copy-start | bytes 6148
  0.7 1.0 %copy-start = (bf16[1,256,512]{2,1,0:T(8,128)(2,1)S(1)}, bf16[1,256,512]{2,1,0:T(8,128)(2,1)}, u32[]{:S(2)}) copy-start(bf16[1,256,512]{2,1,0:T(8,128)(2,1)} %param.8) | copy-start | bytes 786436
  0.7 3.0 %copy-start.1 = (f32[4,512]{1,0:T(4,128)S(1)}, f32[4,512]{1,0:T(4,128)}, u32[]{:S(2)}) copy-start(f32[4,512]{1,0:T(4,128)} %weight_ref.7) | copy-start | bytes 24580
  0.7 3.0 %copy-start.6 = (bf16[1,256,256]{2,1,0:T(8,128)(2,1)S(1)}, bf16[1,256,256]{2,1,0:T(8,128)(2,1)}, u32[]{:S(2)}) copy-start(bf16[1,256,256]{2,1,0:T(8,128)(2,1)} %param.15) | copy-start | bytes 393220
  0.7 3.0 %copy-start.7 = (f32[1,256,4]{1,2,0:T(4,128)S(1)}, f32[1,256,4]{1,2,0:T(4,128)}, u32[]{:S(2)}) copy-start(f32[1,256,4]{1,2,0:T(4,128)} %param.11) | copy-start | bytes 12292
  1.7 6.3 %collective-permute-start.1 = (bf16[16,512]{1,0:T(8,128)(2,1)S(1)}, bf16[16,512]{1,0:T(8,128)(2,1)S(1)}, u32[]{:S(2)}, u32[]{:S(2)}) collective-permute-start(bf16[16,512]{1,0:T(8,128)(2,1)S(1)} %slice.3), channel_id=1, source_target_pairs={{0,4},{4,8},{8,12},{12,16},{16,20},{20,24},{24,28},{28,0},{1,5},{5... | collective-permute-start | bytes 49160 | tf_op jit(solution)/shard_map/ppermute | solution.py:595
  4.7 4.7 %collective-permute-start = (f16[264,256]{1,0:T(8,128)(2,1)S(1)}, f16[264,256]{1,0:T(8,128)(2,1)S(1)}, u32[]{:S(2)}, u32[]{:S(2)}) collective-permute-start(f16[264,256]{1,0:T(8,128)(2,1)S(1)} %convert_element_type.30), channel_id=1, source_target_pairs={{0,4},{4,0},{8,12},{12,8},{16,20},{20,16},{24,28},{28,24},{1,5},{5... | collective-permute-start | bytes 405512 | tf_op jit(solution)/shard_map/ppermute | solution.py:556
  8.0 2.7 %collective-permute-start.2 = (bf16[16,384]{1,0:T(8,128)(2,1)S(1)}, bf16[16,384]{1,0:T(8,128)(2,1)S(1)}, u32[]{:S(2)}, u32[]{:S(2)}) collective-permute-start(bf16[16,384]{1,0:T(8,128)(2,1)S(1)} %get-tuple-element.74.refs_1_), channel_id=1, source_target_pairs={{0,4},{4,0},{8,12},{12,8},{16,20},{20,16},{24,28},{28,24},{1,5},{5... | collective-permute-start | bytes 36872 | tf_op jit(solution)/shard_map/ppermute | solution.py:556
  11.1 5.2 %collective-permute-start.5 = (f16[136,256]{1,0:T(8,128)(2,1)S(1)}, f16[136,256]{1,0:T(8,128)(2,1)S(1)}, u32[]{:S(2)}, u32[]{:S(2)}) collective-permute-start(f16[136,256]{1,0:T(8,128)(2,1)S(1)} %convert_element_type.36), channel_id=1, source_target_pairs={{0,24},{4,28},{8,0},{12,4},{16,8},{20,12},{24,16},{28,20},{1,25},{... | collective-permute-start | bytes 208904 | tf_op jit(solution)/shard_map/ppermute | solution.py:556
  12.9 5.7 %collective-permute-start.4 = (f16[136,256]{1,0:T(8,128)(2,1)S(1)}, f16[136,256]{1,0:T(8,128)(2,1)S(1)}, u32[]{:S(2)}, u32[]{:S(2)}) collective-permute-start(f16[136,256]{1,0:T(8,128)(2,1)S(1)} %convert_element_type.34), channel_id=1, source_target_pairs={{0,16},{4,20},{8,24},{12,28},{16,0},{20,4},{24,8},{28,12},{1,17},{... | collective-permute-start | bytes 208904 | tf_op jit(solution)/shard_map/ppermute | solution.py:556
  12.9 5.7 %collective-permute-start.3 = (f16[136,256]{1,0:T(8,128)(2,1)S(1)}, f16[136,256]{1,0:T(8,128)(2,1)S(1)}, u32[]{:S(2)}, u32[]{:S(2)}) collective-permute-start(f16[136,256]{1,0:T(8,128)(2,1)S(1)} %convert_element_type.32), channel_id=1, source_target_pairs={{0,8},{4,12},{8,16},{12,20},{16,24},{20,28},{24,0},{28,4},{1,9},{5... | collective-permute-start | bytes 208904 | tf_op jit(solution)/shard_map/ppermute | solution.py:556
  20.2 15.2 %all-to-all-start = ((f16[32,24,128]{2,1,0:T(8,128)(2,1)}), f16[32,24,128]{2,1,0:T(8,128)(2,1)S(1)}, u32[]{:S(2)}, u32[]{:S(2)}) async-start(f16[32,24,128]{2,1,0:T(8,128)(2,1)} %broadcast_in_dim.30), calls=%async_computation | async-start | bytes 393216 | tf_op jit(solution)/shard_map/all_to_all | solution.py:577
  26.3 6.1 %collective-permute-start.6 = (f32[8,512]{1,0:T(8,128)S(1)}, f32[8,512]{1,0:T(8,128)S(1)}, u32[]{:S(2)}, u32[]{:S(2)}) collective-permute-start(f32[8,512]{1,0:T(8,128)S(1)} %get-tuple-element.102), channel_id=1, source_target_pairs={{4,0},{8,4},{12,8},{16,12},{20,16},{24,20},{28,24},{0,28},{5,1},{9... | collective-permute-start | bytes 49160 | tf_op jit(solution)/shard_map/ppermute | solution.py:673

commit v13 on v11

--- a/solution.py
+++ b/solution.py
@@ -676,7 +676,7 @@
 
     spilled = lax.ppermute(spill, "ctx", [((i + 1) % slabs, i) for i in range(slabs)])
     if slabs * contexts <= 64:
-        parts = everyones(packed, ("ctx", "dp"), slabs * contexts)
+        parts = everyones(packed, ("dp", "ctx"), slabs * contexts)
     else:
         packed = call(repack_kernel, struct((TOTAL_ROWS, 128)), [VMEM])(everyones(packed, "ctx", slabs))
         parts = everyones(packed, "dp", contexts)

time: 36.4 us -> 36 us (0.989); the launches traced: 36.2 us -> 35.4 us
  waiting for transfers between devices: 9.37 us -> 8.59 us
    all_to_all x1, waiting for transfers between devices: 2.48 us -> 1.7 us  [everyones(): return lax.all_to_all(packed, axes, 0, 0).astype(f32)]
where the time goes in v13:
time: 36 us; the launch traced here: 35.4 us
  starting transfers between devices  15.9 us (44%)
  waiting for transfers between devices  8.59 us (24%)
  Pallas kernels  8.3 us (23%)
  local copies, waits for them, and re-layouts  1.58 us (4%)
  between operations  0.92 us (3%)
    all_to_all x1, starting transfers between devices, everyones(): return lax.all_to_all(packed, axes, 0, 0).astype(f32)  5.99 us
    ppermute x5, waiting for transfers between devices, from_groups(): got.append(lax.ppermute(message, 'ctx', route))  4.96 us
    ppermute x1, starting transfers between devices, on_device(): lax.ppermute(spill, 'ctx', [((i + 1) % slabs, i) for i in range(slabs)])  4.21 us
    ppermute x5, starting transfers between devices, from_groups(): got.append(lax.ppermute(message, 'ctx', route))  3.67 us
    ppermute x1, starting transfers between devices, on_device(): lax.ppermute(early_raw[tok - HALO_ROWS:], 'ctx', [(i, (i + 1) % slabs) fo...  2.04 us
    pallas_call x1, Pallas kernels, on_device(): call(local_kernel, (struct((tok, channels)), struct((2 * HEAD_ROWS, tok))...  1.98 us
    ppermute x1, waiting for transfers between devices, on_device(): lax.ppermute(early_raw[tok - HALO_ROWS:], 'ctx', [(i, (i + 1) % slabs) fo...  1.93 us
    pallas_call x1, Pallas kernels, on_device(): call(input_kernel, (struct((tok, channels), bf16), struct((H, tok)), stru...  1.86 us
  transfers between devices with their start and end apart: 8, of which 5 were waited for; matrix products, arithmetic and copies ran while one was open for 0% of the time, Pallas kernels for 18%

profile of v13, /device:TPU:1, one launch (start us, length us, event | category | flops | bytes accessed | tf_op | source)
XLA Modules:
  0.0 35.4 jit_solution(1712970035852492190)
XLA Ops:
  0.7 0.0 copy-start.5
  0.7 0.5 %copy-done.10 = f32[4]{0:T(128)S(1)} copy-done((f32[4]{0:T(128)S(1)}, f32[4]{0:T(128)}, u32[]{:S(2)}) %copy-start.10) | copy-done | bytes 40
  1.3 0.0 copy-done.9
  1.3 0.0 copy-done.8
  1.3 0.0 copy-done.7
  1.4 0.1 shard_map.136
  1.4 0.2 copy-done.4
  1.7 2.0 %collective-permute-start = (bf16[16,512]{1,0:T(8,128)(2,1)S(1)}, bf16[16,512]{1,0:T(8,128)(2,1)S(1)}, u32[]{:S(2)}, u32[]{:S(2)}) collective-permute-start(bf16[16,512]{1,0:T(8,128)(2,1)S(1)} %slice.3), channel_id=1, source_target_pairs={{0,4},{4,8},{8,12},{12,16},{16,20},{20,24},{24,28},{28,0},{1,5},{5... | collective-permute-start | bytes 49160 | tf_op jit(solution)/shard_map/ppermute | solution.py:597
  3.7 1.0 %shard_map.137 = (f32[256,512]{1,0:T(8,128)S(1)}, bf16[256,512]{1,0:T(8,128)(2,1)S(1)}, bf16[256,512]{1,0:T(8,128)(2,1)S(1)}, bf16[256,512]{1,0:T(8,128)(2,1)S(1...) custom-call(bf16[256,512]{1,0:T(8,128)(2,1)S(1)} %bitcast.18, ...), custom_call_target="tpu_custom_call" | custom-call | flops 99999997952 | bytes 1048576 | tf_op jit(solution)/shard_map/pallas_call | solution.py:609
  4.7 1.3 %collective-permute-start.1 = (f16[264,256]{1,0:T(8,128)(2,1)S(1)}, f16[264,256]{1,0:T(8,128)(2,1)S(1)}, u32[]{:S(2)}, u32[]{:S(2)}) collective-permute-start(f16[264,256]{1,0:T(8,128)(2,1)S(1)} %convert_element_type.30), channel_id=1, source_target_pairs={{0,4},{4,0},{8,12},{12,8},{16,20},{20,16},{24,28},{28,24},{1,5},{5... | collective-permute-start | bytes 405512 | tf_op jit(solution)/shard_map/ppermute | solution.py:558
  6.0 1.9 %collective-permute-done.halo_ref = bf16[16,512]{1,0:T(8,128)(2,1)S(1)} collective-permute-done((bf16[16,512]{1,0:T(8,128)(2,1)S(1)}, bf16[16,512]{1,0:T(8,128)(2,1)S(1)}, u32[]{:S(2)}, u32[]{:S(2)}) %collective-permute-start) | collective-permute-done | bytes 16416 | tf_op jit(solution)/shard_map/ppermute | solution.py:597
  8.0 0.1 shard_map.138
  8.1 0.0 copy-start.2
  8.1 0.1 collective-permute-start.2
  8.1 2.0 %shard_map.139 = (f32[256,512]{1,0:T(8,128)S(1)}, f32[16,256]{1,0:T(8,128)S(1)}, f32[128,256]{1,0:T(8,128)S(1)}, f32[128,256]{1,0:T(8,128)S(1)}) custom-call(bf16[256,512]{1,0:T(8,128)(2,1)S(1)} %get-tuple-element.74.xbc_ref, bf16[256,256]{1,0:T(8,128)(2,1)S(1)} %bitcast.26, ...), custom_call_target="tpu_custom_call", output_to_operand_aliasing={{2}: (5, {}), {3}: (6, {})} | custom-call | flops 99999997952 | bytes 1048576 | tf_op jit(solution)/shard_map/pallas_call | solution.py:631
  10.1 0.0 collective-permute-done.1
  10.2 0.6 %collective-permute-done.2.refs_1_ = bf16[16,384]{1,0:T(8,128)(2,1)S(1)} collective-permute-done((bf16[16,384]{1,0:T(8,128)(2,1)S(1)}, bf16[16,384]{1,0:T(8,128)(2,1)S(1)}, u32[]{:S(2)}, u32[]{:S(2)}) %collective-permute-start.2) | collective-permute-done | bytes 12320 | tf_op jit(solution)/shard_map/ppermute | solution.py:558
  10.7 0.3 shard_map.140
  11.1 1.8 %collective-permute-start.5 = (f16[136,256]{1,0:T(8,128)(2,1)S(1)}, f16[136,256]{1,0:T(8,128)(2,1)S(1)}, u32[]{:S(2)}, u32[]{:S(2)}) collective-permute-start(f16[136,256]{1,0:T(8,128)(2,1)S(1)} %convert_element_type.36), channel_id=1, source_target_pairs={{0,24},{4,28},{8,0},{12,4},{16,8},{20,12},{24,16},{28,20},{1,25},{... | collective-permute-start | bytes 208904 | tf_op jit(solution)/shard_map/ppermute | solution.py:558
  12.9 0.0 collective-permute-start.4
  12.9 0.5 %collective-permute-start.3 = (f16[136,256]{1,0:T(8,128)(2,1)S(1)}, f16[136,256]{1,0:T(8,128)(2,1)S(1)}, u32[]{:S(2)}, u32[]{:S(2)}) collective-permute-start(f16[136,256]{1,0:T(8,128)(2,1)S(1)} %convert_element_type.32), channel_id=1, source_target_pairs={{0,8},{4,12},{8,16},{12,20},{16,24},{20,28},{24,0},{28,4},{1,9},{5... | collective-permute-start | bytes 208904 | tf_op jit(solution)/shard_map/ppermute | solution.py:558
  13.4 0.8 %shard_map.141 = (f32[256,1024]{1,0:T(8,128)S(1)}, f32[8,256]{1,0:T(8,128)S(1)}, f32[768,512]{1,0:T(8,128)S(1)}, f32[256,512]{1,0:T(8,128)S(1)}) custom-call(bf16[256,512]{1,0:T(8,128)(2,1)S(1)} %get-tuple-element.74.xbc_ref, bf16[256,256]{1,0:T(8,128)(2,1)S(1)} %bitcast.27, f32[48,256]{1,0:T(8,128)S(1)} %get-tuple-element.75.rows_ref, ...), custom_call_target="tpu_custom_call" | custom-call | flops 99999997952 | bytes 1048576 | tf_op jit(solution)/shard_map/pallas_call | solution.py:660
  14.2 0.1 collective-permute-done.5
  14.3 4.3 %collective-permute-done.4 = f16[136,256]{1,0:T(8,128)(2,1)S(1)} collective-permute-done((f16[136,256]{1,0:T(8,128)(2,1)S(1)}, f16[136,256]{1,0:T(8,128)(2,1)S(1)}, u32[]{:S(2)}, u32[]{:S(2)}) %collective-permute-start.4) | collective-permute-done | bytes 69664 | tf_op jit(solution)/shard_map/ppermute | solution.py:558
  18.7 0.8 %shard_map.142 = (f32[256,512]{1,0:T(8,128)S(1)}, f32[264,512]{1,0:T(8,128)S(1)}, f32[24,128]{1,0:T(8,128)S(1)}, f32[8,512]{1,0:T(8,128)S(1)}) custom-call(bf16[256,512]{1,0:T(8,128)(2,1)S(1)} %bitcast.20, f32[768,512]{1,0:T(8,128)S(1)} %get-tuple-element.96.moved_ref, bf16[256,512]{1,0:T(8,128)(2,1)S(1)} %get-tuple-element.74.xbc_ref, ...), custom_call_target="tpu_custom_call" | custom-call | flops 200000000 | bytes 1048576 | tf_op jit(solution)/shard_map/pallas_call | solution.py:669
  19.6 0.7 %broadcast_in_dim.30 = f16[32,24,128]{2,1,0:T(8,128)(2,1)} broadcast(f16[24,128]{1,0:T(8,128)(2,1)S(1)} %convert_element_type.38), dimensions={1,2} | broadcast | bytes 202752 | tf_op jit(solution)/shard_map/broadcast_in_dim | solution.py:578
  20.3 6.0 %all-to-all-start = ((f16[32,24,128]{2,1,0:T(8,128)(2,1)}), f16[32,24,128]{2,1,0:T(8,128)(2,1)S(1)}, u32[]{:S(2)}, u32[]{:S(2)}) async-start(f16[32,24,128]{2,1,0:T(8,128)(2,1)} %broadcast_in_dim.30), calls=%async_computation | async-start | bytes 393216 | tf_op jit(solution)/shard_map/all_to_all | solution.py:579
  26.3 4.2 %collective-permute-start.6 = (f32[8,512]{1,0:T(8,128)S(1)}, f32[8,512]{1,0:T(8,128)S(1)}, u32[]{:S(2)}, u32[]{:S(2)}) collective-permute-start(f32[8,512]{1,0:T(8,128)S(1)} %get-tuple-element.110), channel_id=1, source_target_pairs={{4,0},{8,4},{12,8},{16,12},{20,16},{24,20},{28,24},{0,28},{5,1},{9... | collective-permute-start | bytes 49160 | tf_op jit(solution)/shard_map/ppermute | solution.py:677
  30.5 1.9 %shard_map.143 = (bf16[256,512]{1,0:T(8,128)(2,1)}, f32[4,256]{1,0:T(4,128)}, f32[16,512]{1,0:T(8,128)S(1)}) custom-call(f32[256,512]{1,0:T(8,128)S(1)} %get-tuple-element.107.conv_ref, f32[4,512]{1,0:T(4,128)S(1)} %copy-done.6, f32[264,512]{1,0:T(8,128)S(1)} %get-tuple-element.108.states_ref, bf16[256,512]{1,0:T(8,128)(2,1)S(1)} %get-tuple-element.74.xbc_ref, ...), custom_call_target="tpu_custom_call" | custom-call | flops 1000000 | bytes 1048576 | tf_op jit(solution)/shard_map/pallas_call | solution.py:684
  32.4 0.7 %shard_map.144 = bf16[256,512]{1,0:T(8,128)(2,1)} custom-call(f32[16,512]{1,0:T(8,128)S(1)} %get-tuple-element.109.end_ref, f32[8,512]{1,0:T(8,128)S(1)} %collective-permute-done.6.spilled_ref, f32[32,256]{1,0:T(8,128)S(1)} %get-tuple-element.70.places_ref, bf16[256,512]{1,0:T(8,128)(2,1)} %get-tuple-element.111.main_hbm), custom_call_target="tpu_custom_call", output_to_operand_aliasing={{}: (3, {})} | custom-call | bytes 1048576 | tf_op jit(solution)/shard_map/pallas_call | solution.py:692
  33.0 1.7 %all-to-all-done = f16[32,24,128]{2,1,0:T(8,128)(2,1)S(1)} async-done(((f16[32,24,128]{2,1,0:T(8,128)(2,1)}), f16[32,24,128]{2,1,0:T(8,128)(2,1)S(1)}, u32[]{:S(2)}, u32[]{:S(2)}) %all-to-all-start) | async-done | bytes 196640 | tf_op jit(solution)/shard_map/all_to_all | solution.py:579
  34.8 0.7 %shard_map.145 = (f32[4,512]{1,0:T(4,128)}, f32[1,512]{1,0:T(1,128)}, f32[1,4]{1,0:T(1,128)}, f32[1,4]{1,0:T(1,128)}, f32[1,4]{1,0:T(1,128)}) custom-call(f32[32,24,128]{2,1,0:T(8,128)S(1)} %convert_element_type.39.parts_ref), custom_call_target="tpu_custom_call" | custom-call | bytes 1048576 | tf_op jit(solution)/shard_map/pallas_call | solution.py:701
  (33 shorter events, 0.2 us)
Async XLA Ops:
  0.6 0.7 %copy-start.10 = (f32[4]{0:T(128)S(1)}, f32[4]{0:T(128)}, u32[]{:S(2)}) copy-start(f32[4]{0:T(128)} %param.14) | copy-start | bytes 52
  0.6 0.7 %copy-start.9 = (f32[4]{0:T(128)S(1)}, f32[4]{0:T(128)}, u32[]{:S(2)}) copy-start(f32[4]{0:T(128)} %param.13) | copy-start | bytes 52
  0.7 0.7 %copy-start.8 = (f32[4]{0:T(128)S(1)}, f32[4]{0:T(128)}, u32[]{:S(2)}) copy-start(f32[4]{0:T(128)} %param.12) | copy-start | bytes 52
  0.7 0.7 %copy-start.7 = (f32[512]{0:T(512)S(1)}, f32[512]{0:T(512)}, u32[]{:S(2)}) copy-start(f32[512]{0:T(512)} %param.10) | copy-start | bytes 6148
  0.7 1.0 %copy-start.4 = (bf16[1,256,512]{2,1,0:T(8,128)(2,1)S(1)}, bf16[1,256,512]{2,1,0:T(8,128)(2,1)}, u32[]{:S(2)}) copy-start(bf16[1,256,512]{2,1,0:T(8,128)(2,1)} %param.8) | copy-start | bytes 786436
  0.7 3.0 %copy-start.5 = (f32[4,512]{1,0:T(4,128)S(1)}, f32[4,512]{1,0:T(4,128)}, u32[]{:S(2)}) copy-start(f32[4,512]{1,0:T(4,128)} %weight_ref.7) | copy-start | bytes 24580
  0.7 3.0 %copy-start.11 = (bf16[1,256,256]{2,1,0:T(8,128)(2,1)S(1)}, bf16[1,256,256]{2,1,0:T(8,128)(2,1)}, u32[]{:S(2)}) copy-start(bf16[1,256,256]{2,1,0:T(8,128)(2,1)} %param.15) | copy-start | bytes 393220
  0.7 3.0 %copy-start.12 = (f32[1,256,4]{1,2,0:T(4,128)S(1)}, f32[1,256,4]{1,2,0:T(4,128)}, u32[]{:S(2)}) copy-start(f32[1,256,4]{1,2,0:T(4,128)} %param.11) | copy-start | bytes 12292
  1.7 6.3 %collective-permute-start = (bf16[16,512]{1,0:T(8,128)(2,1)S(1)}, bf16[16,512]{1,0:T(8,128)(2,1)S(1)}, u32[]{:S(2)}, u32[]{:S(2)}) collective-permute-start(bf16[16,512]{1,0:T(8,128)(2,1)S(1)} %slice.3), channel_id=1, source_target_pairs={{0,4},{4,8},{8,12},{12,16},{16,20},{20,24},{24,28},{28,0},{1,5},{5... | collective-permute-start | bytes 49160 | tf_op jit(solution)/shard_map/ppermute | solution.py:597
  4.7 3.4 %copy-start = (f32[256,256]{1,0:T(8,128)}, f32[256,256]{1,0:T(8,128)S(1)}, u32[]{:S(2)}) copy-start(f32[256,256]{1,0:T(8,128)S(1)} %get-tuple-element.69.tail_ref) | copy-start | bytes 786436
  4.7 5.4 %collective-permute-start.1 = (f16[264,256]{1,0:T(8,128)(2,1)S(1)}, f16[264,256]{1,0:T(8,128)(2,1)S(1)}, u32[]{:S(2)}, u32[]{:S(2)}) collective-permute-start(f16[264,256]{1,0:T(8,128)(2,1)S(1)} %convert_element_type.30), channel_id=1, source_target_pairs={{0,4},{4,0},{8,12},{12,8},{16,20},{20,16},{24,28},{28,24},{1,5},{5... | collective-permute-start | bytes 405512 | tf_op jit(solution)/shard_map/ppermute | solution.py:558
  8.1 2.1 %copy-start.2 = (bf16[256,512]{1,0:T(8,128)(2,1)}, bf16[256,512]{1,0:T(8,128)(2,1)S(1)}, u32[]{:S(2)}) copy-start(bf16[256,512]{1,0:T(8,128)(2,1)S(1)} %get-tuple-element.98.weighted_ref) | copy-start | bytes 786436
  8.1 2.7 %collective-permute-start.2 = (bf16[16,384]{1,0:T(8,128)(2,1)S(1)}, bf16[16,384]{1,0:T(8,128)(2,1)S(1)}, u32[]{:S(2)}, u32[]{:S(2)}) collective-permute-start(bf16[16,384]{1,0:T(8,128)(2,1)S(1)} %get-tuple-element.77.factors_ref), channel_id=1, source_target_pairs={{0,4},{4,0},{8,12},{12,8},{16,20},{20,16},{24,28},{28,24},{1,5},{5... | collective-permute-start | bytes 36872 | tf_op jit(solution)/shard_map/ppermute | solution.py:558
  11.1 3.2 %collective-permute-start.5 = (f16[136,256]{1,0:T(8,128)(2,1)S(1)}, f16[136,256]{1,0:T(8,128)(2,1)S(1)}, u32[]{:S(2)}, u32[]{:S(2)}) collective-permute-start(f16[136,256]{1,0:T(8,128)(2,1)S(1)} %convert_element_type.36), channel_id=1, source_target_pairs={{0,24},{4,28},{8,0},{12,4},{16,8},{20,12},{24,16},{28,20},{1,25},{... | collective-permute-start | bytes 208904 | tf_op jit(solution)/shard_map/ppermute | solution.py:558
  12.9 5.7 %collective-permute-start.4 = (f16[136,256]{1,0:T(8,128)(2,1)S(1)}, f16[136,256]{1,0:T(8,128)(2,1)S(1)}, u32[]{:S(2)}, u32[]{:S(2)}) collective-permute-start(f16[136,256]{1,0:T(8,128)(2,1)S(1)} %convert_element_type.34), channel_id=1, source_target_pairs={{0,16},{4,20},{8,24},{12,28},{16,0},{20,4},{24,8},{28,12},{1,17},{... | collective-permute-start | bytes 208904 | tf_op jit(solution)/shard_map/ppermute | solution.py:558
  12.9 5.7 %collective-permute-start.3 = (f16[136,256]{1,0:T(8,128)(2,1)S(1)}, f16[136,256]{1,0:T(8,128)(2,1)S(1)}, u32[]{:S(2)}, u32[]{:S(2)}) collective-permute-start(f16[136,256]{1,0:T(8,128)(2,1)S(1)} %convert_element_type.32), channel_id=1, source_target_pairs={{0,8},{4,12},{8,16},{12,20},{16,24},{20,28},{24,0},{28,4},{1,9},{5... | collective-permute-start | bytes 208904 | tf_op jit(solution)/shard_map/ppermute | solution.py:558
  13.4 5.3 %copy-start.1 = (f32[256,256]{1,0:T(8,128)S(1)}, f32[256,256]{1,0:T(8,128)}, u32[]{:S(2)}) copy-start(f32[256,256]{1,0:T(8,128)} %copy-done) | copy-start | bytes 786436
  13.4 5.3 %copy-start.3 = (bf16[256,512]{1,0:T(8,128)(2,1)S(1)}, bf16[256,512]{1,0:T(8,128)(2,1)}, u32[]{:S(2)}) copy-start(bf16[256,512]{1,0:T(8,128)(2,1)} %copy-done.2) | copy-start | bytes 786436
  13.4 5.3 %copy-start.6 = (f32[4,512]{1,0:T(4,128)S(1)}, f32[4,512]{1,0:T(4,128)}, u32[]{:S(2)}) copy-start(f32[4,512]{1,0:T(4,128)} %weight_ref.7) | copy-start | bytes 24580
  20.3 14.4 %all-to-all-start = ((f16[32,24,128]{2,1,0:T(8,128)(2,1)}), f16[32,24,128]{2,1,0:T(8,128)(2,1)S(1)}, u32[]{:S(2)}, u32[]{:S(2)}) async-start(f16[32,24,128]{2,1,0:T(8,128)(2,1)} %broadcast_in_dim.30), calls=%async_computation | async-start | bytes 393216 | tf_op jit(solution)/shard_map/all_to_all | solution.py:579
  26.3 6.1 %collective-permute-start.6 = (f32[8,512]{1,0:T(8,128)S(1)}, f32[8,512]{1,0:T(8,128)S(1)}, u32[]{:S(2)}, u32[]{:S(2)}) collective-permute-start(f32[8,512]{1,0:T(8,128)S(1)} %get-tuple-element.110), channel_id=1, source_target_pairs={{4,0},{8,4},{12,8},{16,12},{20,16},{24,20},{28,24},{0,28},{5,1},{9... | collective-permute-start | bytes 49160 | tf_op jit(solution)/shard_map/ppermute | solution.py:677
